TPU v7x, 32 devices: a whole 2x2x4 slice. The times are simulated.
32 devices in a mesh: dp: 2 (over y), seq: 16 (over z, x, core).
Axes of the slice: x: 2, y: 2, z: 4, core: 2. Of those that a mesh axis runs over, the one named last changes fastest.
Arguments:
- tokens: bfloat16 [5120, 768], P(('dp', 'seq')), may hold values from -6 to 6
- segment_ids: int32 [5120], P(('dp', 'seq')), may hold values from 0 to 15, as said below
- pad_mask: int32 [5120], P(('dp', 'seq')), may hold values from 0 to 1, as said below
- w_qkv: float32 [1, 768, 2304], P(None, ('dp', 'seq')), may hold values from -0.21875 to 0.21875
- w_out: float32 [1, 768, 768], P(None, ('dp', 'seq')), may hold values from -2.5 to 2.5
- w_gate: float32 [1, 768, 3072], P(None, ('dp', 'seq')), may hold values from -0.21875 to 0.21875
- w_up: float32 [1, 768, 3072], P(None, ('dp', 'seq')), may hold values from -0.21875 to 0.21875
- w_down: float32 [1, 3072, 768], P(None, ('dp', 'seq')), may hold values from -0.109375 to 0.109375
- ln_gain: float32 [1, 2, 768], P(None, None, ('dp', 'seq')), may hold values from 0.5 to 1.5
- ln_bias: float32 [1, 2, 768], P(None, None, ('dp', 'seq')), may hold values from -2 to 2
- cotangent: bfloat16 [5120, 768], P(('dp', 'seq')), may hold values from -6 to 6
Outputs:
- output: bfloat16 [5120, 768], P(('dp', 'seq'))
- grad_input: float32 [5120, 768], P(('dp', 'seq'))
- grad_qkv: float32 [1, 768, 2304], P(None, ('dp', 'seq'))
- grad_out: float32 [1, 768, 768], P(None, ('dp', 'seq'))
- grad_gate: float32 [1, 768, 3072], P(None, ('dp', 'seq'))
- grad_up: float32 [1, 768, 3072], P(None, ('dp', 'seq'))
- grad_down: float32 [1, 3072, 768], P(None, ('dp', 'seq'))
- grad_gain: float32 [1, 2, 768], P(None, None, ('dp', 'seq'))
- grad_bias: float32 [1, 2, 768], P(None, None, ('dp', 'seq'))
Inputs may be any that keep to these rules, and one draw needn't show every extreme that they name: `segment_ids`: within each sequence of 2560 tokens, tokens with equal ids form one document; the first 4 tokens of every 160 belong to document 0, and the other ids never fall along a sequence. `pad_mask`: 0 exactly on the tokens whose segment id is the largest of their sequence.
All inputs are finite; a program needn't handle non-finite values.
Results may differ from a plain program's by a relative error of at most 0.02.
Values may be sent and summed in bfloat16 or wider, within the bound.
No kernel may reach another device: no remote copies, remote signals or barrier semaphores. Data moves between devices by JAX's collectives and lax.ppermute only.
A program may use at most 384 MiB of HBM per device.

v0:
```python
import jax
import jax.numpy as jnp
from jax import lax
from jax.sharding import PartitionSpec as P

HEADS = 12
LAYERS = 1


epsilon = 1e-05
rope_base = 10000.0


def rope_tables(positions, head_size):
    half_size = head_size // 2
    frequency = jnp.exp(
        -jnp.log(rope_base) * jnp.arange(half_size, dtype=jnp.float32) * (2.0 / head_size)
    )
    angles = positions.astype(jnp.float32)[:, None] * frequency[None, :]
    return (jnp.cos(angles)[:, None, :], jnp.sin(angles)[:, None, :])


def rotate(values, cos_table, sin_table):
    half_size = values.shape[-1] // 2
    leading = values[..., :half_size]
    trailing = values[..., half_size:]
    return jnp.concatenate(
        [leading * cos_table - trailing * sin_table, trailing * cos_table + leading * sin_table],
        axis=-1,
    )


def unrotate(gradient, cos_table, sin_table):
    half_size = gradient.shape[-1] // 2
    leading = gradient[..., :half_size]
    trailing = gradient[..., half_size:]
    return jnp.concatenate(
        [leading * cos_table + trailing * sin_table, trailing * cos_table - leading * sin_table],
        axis=-1,
    )


def normalize(values):
    average = jnp.mean(values, axis=-1, keepdims=True)
    centred = values - average
    factor = lax.rsqrt(jnp.mean(centred * centred, axis=-1, keepdims=True) + epsilon)
    return (centred * factor, factor)


def norm_back(gradient, normed, factor):
    return factor * (
        gradient
        - jnp.mean(gradient, axis=-1, keepdims=True)
        - normed * jnp.mean(gradient * normed, axis=-1, keepdims=True)
    )


def left_product(left, right):
    return lax.dot_general(
        left, right, (((0,), (0,)), ((), ())), preferred_element_type=jnp.float32
    )


def right_product(left, right):
    return lax.dot_general(
        left, right, (((1,), (1,)), ((), ())), preferred_element_type=jnp.float32
    )


def rounded(values):
    return lax.optimization_barrier(values.astype(jnp.bfloat16)).astype(jnp.float32)


def pair_terms(
    queries, grads_out, key_rows, value_rows, query_seg, key_seg, top_log, row_delta, factor
):
    scores = (
        jnp.einsum("qhd,khd->hqk", queries, key_rows, preferred_element_type=jnp.float32) * factor
    )
    allowed = (query_seg[:, None] == key_seg[None, :])[None]
    weights_now = jnp.where(allowed, jnp.exp(scores - top_log[:, :, None]), 0.0)
    prob_grad = jnp.einsum(
        "qhd,khd->hqk", grads_out, value_rows, preferred_element_type=jnp.float32
    )
    score_low = (weights_now * (prob_grad - row_delta[:, :, None])).astype(jnp.bfloat16)
    return (weights_now.astype(jnp.bfloat16), score_low)


def body(
    tokens, segment_ids, pad_mask, w_qkv, w_out, w_gate, w_up, w_down, ln_gain, ln_bias, cotangent
):
    local_rows = tokens.shape[0]
    model_width = tokens.shape[1]
    head_count = HEADS
    head_size = model_width // head_count
    factor = head_size ** (-0.5)
    seg_all = lax.all_gather(segment_ids, "seq", axis=0, tiled=True)
    seq_length = seg_all.shape[0]
    block_rows = min(512, seq_length)
    block_count = seq_length // block_rows
    own_index = lax.axis_index("seq") * local_rows + jnp.arange(local_rows, dtype=jnp.int32)
    all_index = jnp.arange(seq_length, dtype=jnp.int32)
    earlier = (segment_ids[:, None] == seg_all[None, :]) & (all_index[None, :] < own_index[:, None])
    positions = jnp.sum(earlier.astype(jnp.int32), axis=1)
    cos_table, sin_table = rope_tables(positions, head_size)
    keep_rows = pad_mask.astype(jnp.float32)[:, None]

    def local_parts(layer_index):
        return (
            w_qkv[layer_index].astype(jnp.bfloat16),
            w_out[layer_index].astype(jnp.bfloat16),
            w_gate[layer_index].astype(jnp.bfloat16),
            w_up[layer_index].astype(jnp.bfloat16),
            w_down[layer_index].astype(jnp.bfloat16),
            ln_gain[layer_index].astype(jnp.bfloat16),
            ln_bias[layer_index].astype(jnp.bfloat16),
        )

    hidden_in = tokens.astype(jnp.float32)
    gathered = []
    layer_index = 0
    parts = local_parts(layer_index)
    weights = (
        lax.all_gather(parts[0], ("dp", "seq"), axis=0, tiled=True),
        lax.all_gather(parts[1], ("dp", "seq"), axis=0, tiled=True),
        lax.all_gather(parts[2], ("dp", "seq"), axis=0, tiled=True),
        lax.all_gather(parts[3], ("dp", "seq"), axis=0, tiled=True),
        lax.all_gather(parts[4], ("dp", "seq"), axis=0, tiled=True),
        lax.all_gather(parts[5], ("dp", "seq"), axis=1, tiled=True),
        lax.all_gather(parts[6], ("dp", "seq"), axis=1, tiled=True),
    )
    qkv_w, out_w, gate_w, up_w, down_w, gain_rows, bias_rows = weights
    gain_rows = gain_rows.astype(jnp.float32)
    bias_rows = bias_rows.astype(jnp.float32)
    input_low = hidden_in.astype(jnp.bfloat16)
    projected = jnp.dot(input_low, qkv_w, preferred_element_type=jnp.float32)
    shaped = projected.reshape(local_rows, 3, head_count, head_size)
    query_low = rotate(shaped[:, 0], cos_table, sin_table).astype(jnp.bfloat16)
    key_low = rotate(shaped[:, 1], cos_table, sin_table).astype(jnp.bfloat16)
    value_low = shaped[:, 2].astype(jnp.bfloat16)
    key_values = jnp.concatenate(
        [key_low.reshape(local_rows, model_width), value_low.reshape(local_rows, model_width)],
        axis=1,
    )
    absorb_shard_piece = lax.all_gather(key_values, "seq", axis=0, tiled=True)
    running_max = jnp.full((head_count, local_rows), -1e30, jnp.float32)
    row_count = absorb_shard_piece.shape[0]
    absorb_key_rows = absorb_shard_piece[:, :model_width].reshape(row_count, head_count, head_size)
    absorb_value_rows = absorb_shard_piece[:, model_width:].reshape(
        row_count, head_count, head_size
    )
    scores = (
        jnp.einsum("qhd,khd->hqk", query_low, absorb_key_rows, preferred_element_type=jnp.float32)
        * factor
    )
    allowed = (segment_ids[:, None] == seg_all[None, :])[None]
    scores = jnp.where(allowed, scores, -1e30)
    new_max = jnp.maximum(running_max, jnp.max(scores, axis=2))
    weights_now = jnp.where(allowed, jnp.exp(scores - new_max[:, :, None]), 0.0)
    denominator = jnp.sum(weights_now, axis=2)
    weighted = jnp.einsum(
        "hqk,khd->qhd",
        weights_now.astype(jnp.bfloat16),
        absorb_value_rows,
        preferred_element_type=jnp.float32,
    )
    running_max, denominator, weighted = (new_max, denominator, weighted)
    attended = weighted / jnp.transpose(denominator)[:, :, None]
    top_log = running_max + jnp.log(denominator)
    attended_low = attended.reshape(local_rows, model_width).astype(jnp.bfloat16)
    mixed_sum = hidden_in + jnp.dot(attended_low, out_w, preferred_element_type=jnp.float32)
    normed_one, factor_one = normalize(mixed_sum)
    middle = normed_one * gain_rows[0] + bias_rows[0]
    middle_low = middle.astype(jnp.bfloat16)
    gate_vals = jnp.dot(middle_low, gate_w, preferred_element_type=jnp.float32)
    up_vals = jnp.dot(middle_low, up_w, preferred_element_type=jnp.float32)
    hidden_low = (jax.nn.silu(gate_vals) * up_vals).astype(jnp.bfloat16)
    second = middle + jnp.dot(hidden_low, down_w, preferred_element_type=jnp.float32)
    normed_two, factor_two = normalize(second)
    result = (normed_two * gain_rows[1] + bias_rows[1]) * keep_rows
    saved_state = (
        input_low,
        query_low,
        key_values,
        attended,
        top_log,
        attended_low,
        normed_one,
        factor_one,
        middle_low,
        gate_vals,
        up_vals,
        hidden_low,
        normed_two,
        factor_two,
    )
    hidden_in, saved_state = (result, saved_state)
    saved = [saved_state]
    gathered.append(weights)
    gradient = cotangent.astype(jnp.float32)
    collected = [None] * LAYERS
    for layer_index in reversed(range(LAYERS)):
        gather_parts = local_parts(layer_index)
        weights = (
            lax.all_gather(gather_parts[0], ("dp", "seq"), axis=0, tiled=True),
            lax.all_gather(gather_parts[1], ("dp", "seq"), axis=0, tiled=True),
            lax.all_gather(gather_parts[2], ("dp", "seq"), axis=0, tiled=True),
            lax.all_gather(gather_parts[3], ("dp", "seq"), axis=0, tiled=True),
            lax.all_gather(gather_parts[4], ("dp", "seq"), axis=0, tiled=True),
            lax.all_gather(gather_parts[5], ("dp", "seq"), axis=1, tiled=True),
            lax.all_gather(gather_parts[6], ("dp", "seq"), axis=1, tiled=True),
        )
        (
            layer_input_low,
            layer_query_low,
            layer_key_values,
            layer_attended,
            layer_top_log,
            layer_attended_low,
            layer_normed_one,
            layer_factor_one,
            layer_middle_low,
            layer_gate_vals,
            layer_up_vals,
            layer_hidden_low,
            layer_normed_two,
            layer_factor_two,
        ) = saved[layer_index]
        (
            layer_qkv_w,
            layer_out_w,
            layer_gate_w,
            layer_up_w,
            layer_down_w,
            layer_gain_rows,
            layer_bias_rows,
        ) = weights
        layer_gain_rows = layer_gain_rows.astype(jnp.float32)
        masked = gradient * keep_rows
        grad_gain_two = jnp.sum(masked * layer_normed_two, axis=0)
        grad_bias_two = jnp.sum(masked, axis=0)
        second_grad = norm_back(masked * layer_gain_rows[1], layer_normed_two, layer_factor_two)
        second_low = second_grad.astype(jnp.bfloat16)
        grad_down = left_product(layer_hidden_low, second_low)
        hidden_grad = right_product(second_low, layer_down_w)
        sigmoid_gate = jax.nn.sigmoid(layer_gate_vals)
        gate_low = (
            hidden_grad
            * layer_up_vals
            * sigmoid_gate
            * (1.0 + layer_gate_vals * (1.0 - sigmoid_gate))
        ).astype(jnp.bfloat16)
        up_low = (hidden_grad * layer_gate_vals * sigmoid_gate).astype(jnp.bfloat16)
        grad_gate = left_product(layer_middle_low, gate_low)
        grad_up = left_product(layer_middle_low, up_low)
        middle_grad = (
            second_grad + right_product(gate_low, layer_gate_w) + right_product(up_low, layer_up_w)
        )
        grad_gain_one = jnp.sum(middle_grad * layer_normed_one, axis=0)
        grad_bias_one = jnp.sum(middle_grad, axis=0)
        mixed_grad = norm_back(middle_grad * layer_gain_rows[0], layer_normed_one, layer_factor_one)
        mixed_low = mixed_grad.astype(jnp.bfloat16)
        grad_out = left_product(layer_attended_low, mixed_low)
        attended_grad = (
            right_product(mixed_low, layer_out_w)
            .astype(jnp.bfloat16)
            .reshape(local_rows, head_count, head_size)
        )
        row_delta = jnp.transpose(
            jnp.sum(attended_grad.astype(jnp.float32) * layer_attended, axis=2)
        )
        kv_all = lax.all_gather(layer_key_values, "seq", axis=0, tiled=True)

        def key_step(query_grad, block_index):
            offset = block_index * block_rows
            shard_piece = lax.dynamic_slice_in_dim(kv_all, offset, block_rows)
            key_rows = shard_piece[:, :model_width].reshape(block_rows, head_count, head_size)
            value_rows = shard_piece[:, model_width:].reshape(block_rows, head_count, head_size)
            key_seg = lax.dynamic_slice_in_dim(seg_all, offset, block_rows)
            probs_low, score_low = pair_terms(
                layer_query_low,
                attended_grad,
                key_rows,
                value_rows,
                segment_ids,
                key_seg,
                layer_top_log,
                row_delta,
                factor,
            )
            query_grad = query_grad + jnp.einsum(
                "hqk,khd->qhd", score_low, key_rows, preferred_element_type=jnp.float32
            )
            key_grad = (
                jnp.einsum(
                    "hqk,qhd->khd", score_low, layer_query_low, preferred_element_type=jnp.float32
                )
                * factor
            )
            value_grad = jnp.einsum(
                "hqk,qhd->khd", probs_low, attended_grad, preferred_element_type=jnp.float32
            )
            return (
                query_grad,
                jnp.concatenate(
                    [
                        key_grad.reshape(block_rows, model_width),
                        value_grad.reshape(block_rows, model_width),
                    ],
                    axis=1,
                ),
            )

        query_grad, key_terms = lax.scan(
            key_step,
            jnp.zeros((local_rows, head_count, head_size), jnp.float32),
            jnp.arange(block_count, dtype=jnp.int32),
        )
        query_grad = query_grad * factor
        kv_grad = lax.psum_scatter(
            key_terms.reshape(seq_length, 2 * model_width), "seq", scatter_dimension=0, tiled=True
        )
        query_back = unrotate(rounded(query_grad), cos_table, sin_table).reshape(
            local_rows, model_width
        )
        key_back = unrotate(
            rounded(kv_grad[:, :model_width]).reshape(local_rows, head_count, head_size),
            cos_table,
            sin_table,
        ).reshape(local_rows, model_width)
        qkv_low = jnp.concatenate([query_back, key_back, kv_grad[:, model_width:]], axis=1).astype(
            jnp.bfloat16
        )
        grad_qkv = left_product(layer_input_low, qkv_low)
        input_grad = mixed_grad + right_product(qkv_low, layer_qkv_w)
        layer_grads = (
            grad_qkv,
            grad_out,
            grad_gate,
            grad_up,
            grad_down,
            jnp.stack([grad_gain_one, grad_gain_two]),
            jnp.stack([grad_bias_one, grad_bias_two]),
        )
        gradient, layer_grads = (input_grad, layer_grads)
        collected[layer_index] = (
            lax.psum_scatter(layer_grads[0], ("dp", "seq"), scatter_dimension=0, tiled=True),
            lax.psum_scatter(layer_grads[1], ("dp", "seq"), scatter_dimension=0, tiled=True),
            lax.psum_scatter(layer_grads[2], ("dp", "seq"), scatter_dimension=0, tiled=True),
            lax.psum_scatter(layer_grads[3], ("dp", "seq"), scatter_dimension=0, tiled=True),
            lax.psum_scatter(layer_grads[4], ("dp", "seq"), scatter_dimension=0, tiled=True),
            lax.psum_scatter(layer_grads[5], ("dp", "seq"), scatter_dimension=1, tiled=True),
            lax.psum_scatter(layer_grads[6], ("dp", "seq"), scatter_dimension=1, tiled=True),
        )

    def stack_member(member):
        return jnp.stack([collected[0][member]])

    finals = tuple((stack_member(member) for member in range(7)))
    return (
        hidden_in.astype(jnp.bfloat16),
        gradient,
        finals[0],
        finals[1],
        finals[2],
        finals[3],
        finals[4],
        finals[5],
        finals[6],
    )


def solution(mesh):
    placed = (
        P(("dp", "seq"), None),
        P(("dp", "seq")),
        P(("dp", "seq")),
        P(None, ("dp", "seq"), None),
        P(None, ("dp", "seq"), None),
        P(None, ("dp", "seq"), None),
        P(None, ("dp", "seq"), None),
        P(None, ("dp", "seq"), None),
        P(None, None, ("dp", "seq")),
        P(None, None, ("dp", "seq")),
        P(("dp", "seq"), None),
    )
    return jax.shard_map(
        body,
        mesh=mesh,
        in_specs=placed,
        out_specs=(
            P(("dp", "seq"), None),
            P(("dp", "seq"), None),
            P(None, ("dp", "seq"), None),
            P(None, ("dp", "seq"), None),
            P(None, ("dp", "seq"), None),
            P(None, ("dp", "seq"), None),
            P(None, ("dp", "seq"), None),
            P(None, None, ("dp", "seq")),
            P(None, None, ("dp", "seq")),
        ),
        check_vma=False,
    )
```

profile of v0, /device:TPU:0, one launch (start us, length us, event | category | flops | bytes accessed | tf_op | source)
XLA Modules:
  0.0 1374.4 jit_solution(8605554805171509683)
XLA Ops:
  11.7 63.3 %all-reduce = s32[2560]{0:T(1024)} all-reduce(s32[2560]{0:T(1024)S(1)} %dynamic-update-slice), channel_id=1, replica_groups=mesh['dp'=2,'seq'=16] {'seq'}, use_global_device_ids=true, to_apply=%add | all-reduce | flops 2560 | bytes 20480
  76.5 3.7 fusion.31
  85.1 40.0 %all-gather.3 = bf16[1,2,768]{1,0,2:T(2,128)(2,1)S(1)} all-gather(bf16[1,2,24]{1,0,2:T(2,128)(2,1)S(1)} %copy.66), channel_id=5, replica_groups=mesh['dp'=2,'seq'=16] {'dp','seq'}, dimensions={2}, use_global_device_ids=true | all-gather | bytes 3168 | tf_op jit(solution)/shard_map/all_gather | solution.py:130
  125.6 39.6 %all-gather.2 = bf16[1,2,768]{1,0,2:T(2,128)(2,1)S(1)} all-gather(bf16[1,2,24]{1,0,2:T(2,128)(2,1)S(1)} %copy.65), channel_id=4, replica_groups=mesh['dp'=2,'seq'=16] {'dp','seq'}, dimensions={2}, use_global_device_ids=true | all-gather | bytes 3168 | tf_op jit(solution)/shard_map/all_gather | solution.py:129
  165.7 4.6 slice_reduce_fusion
  170.3 4.6 slice_reduce_fusion.1
  176.0 5.5 fusion.71
  181.5 6.3 copy.64
  187.8 6.3 copy.63
  194.1 5.3 fusion.11
  199.4 6.4 fusion.12
  206.1 13.9 %fusion.73 = (bf16[160,12,64]{0,2,1:T(8,128)(2,1)S(1)}, f32[160,12,64]{0,2,1:T(8,128)}) fusion(f32[160,12]{0,1:T(8,128)S(1)} %bitcast.192, bf16[2560,12,64]{0,2,1:T(8,128)(2,1)} %bitcast.184, f32[12,160,2560]{2,1,0:T(8,128)} %copy-done.1, f32[12,160]{1,0:T(8,128)S(1)} %broadcast_maximum_fusion, pred[160,2560]{1,0:T(8,128)(4,1)S(1)} %broadcast_compare_fusion.1), kind=kOutput, calls=%fused_computation.134 | convolution fusion | flops 653967360 | bytes 24755200 | tf_op jit(solution)/shard_map/hqk,khd->qhd/dot_general | solution.py:161
  222.3 53.9 %all-gather.20.cloned.1.call-done = bf16[1,768,3072]{2,1,0:T(8,128)(2,1)} async-done(((bf16[1,24,3072]{2,1,0:T(8,128)(2,1)}), bf16[1,768,3072]{2,1,0:T(8,128)(2,1)}) %all-gather.20.cloned.1.call-update) | async-done | bytes 4718608 | tf_op jit(solution)/shard_map/all_gather | solution.py:126
  276.2 4.6 fusion.27
  280.8 61.1 %all-gather.22.cloned.1.call-done = bf16[1,768,3072]{2,1,0:T(8,128)(2,1)} async-done(((bf16[1,24,3072]{2,1,0:T(8,128)(2,1)}), bf16[1,768,3072]{2,1,0:T(8,128)(2,1)}) %all-gather.22.cloned.1.call-update) | async-done | bytes 4718608 | tf_op jit(solution)/shard_map/all_gather | solution.py:127
  342.0 5.4 multiply_convert_fusion.2
  347.4 60.3 %all-gather.24.cloned.1.call-done = bf16[1,3072,768]{2,1,0:T(8,128)(2,1)} async-done(((bf16[1,96,768]{2,1,0:T(8,128)(2,1)}), bf16[1,3072,768]{2,1,0:T(8,128)(2,1)}) %all-gather.24.cloned.1.call-update) | async-done | bytes 4718608 | tf_op jit(solution)/shard_map/all_gather | solution.py:128
  407.7 3.5 fusion.75
  413.2 4.3 multiply_convert_fusion
  419.5 2.8 multiply_reduce_fusion.2
  424.0 2.0 multiply_reduce_fusion
  426.5 122.4 %while.13 = (s32[]{:T(128)}, f32[160,12,64]{0,2,1:T(8,128)}, f32[5,512,1536]{2,1,0:T(8,128)}, s32[5]{0:T(128)}, bf16[2560,1536]{1,0:T(8,128)(2,1)}, /*index=5*/s...) while((s32[]{:T(128)}, f32[160,12,64]{0,2,1:T(8,128)}, ...), condition=%wide.region_13.14_spmd.clone, body=%wide.region_12.13_spmd.clone.sunk | while | flops 640483328 | bytes 66336152 | solution.py:314
  430.2 2.6 fusion.130
  435.5 4.0 fusion.131
  441.9 2.0 fusion.133
  444.3 2.0 maximum_bitcast_fusion.2
  446.3 2.4 copy.105
  454.2 2.6 fusion.130
  459.6 4.0 fusion.131
  463.6 2.9 fusion.132
  466.5 2.0 fusion.133
  468.9 2.0 maximum_bitcast_fusion.2
  470.9 2.4 copy.105
  478.9 2.6 fusion.130
  484.2 4.0 fusion.131
  488.2 2.9 fusion.132
  491.2 2.0 fusion.133
  493.6 2.0 maximum_bitcast_fusion.2
  495.6 2.4 copy.105
  503.5 2.6 fusion.130
  508.8 4.0 fusion.131
  512.8 2.9 fusion.132
  515.8 2.0 fusion.133
  518.2 2.0 maximum_bitcast_fusion.2
  520.2 2.4 copy.105
  528.1 2.6 fusion.130
  533.4 4.0 fusion.131
  537.4 2.9 fusion.132
  540.3 2.0 fusion.133
  542.7 2.0 maximum_bitcast_fusion.2
  544.7 2.4 copy.105
  550.2 154.6 %reduce-scatter.11.cloned.1.call-done = f32[160,1536]{1,0:T(8,128)} async-done(((f32[2560,1536]{1,0:T(8,128)}), f32[160,1536]{1,0:T(8,128)}) %reduce-scatter.11.cloned.1.call-update) | async-done | bytes 983056 | tf_op jit(solution)/shard_map/reduce_scatter | solution.py:320
  707.0 4.0 convolution_bitcast_fusion.1
  711.1 8.0 copy.75
  722.2 5.1 fusion.77
  728.5 5.0 fusion.78
  735.0 5.3 fusion.61
  741.1 39.8 %all-reduce.3 = (f32[2,768]{1,0:T(2,128)S(1)}, f32[2,768]{1,0:T(2,128)S(1)}) all-reduce(f32[2,768]{1,0:T(2,128)S(1)} %pad_maximum_fusion.8, f32[2,768]{1,0:T(2,128)S(1)} %pad_maximum_fusion.9), channel_id=15, replica_groups=mesh['dp'=2,'seq'=16] {'dp','seq'}, use_global_device_ids=true, to_apply=%region_22.23.clone | all-reduce | flops 3072 | bytes 24576
  782.2 4.1 fusion.37
  786.3 51.9 %reduce-scatter.21.cloned.1.call-done = f32[24,2304]{1,0:T(8,128)} async-done(((f32[768,2304]{1,0:T(8,128)}), f32[24,2304]{1,0:T(8,128)}) %reduce-scatter.21.cloned.1.call-update) | async-done | bytes 221200
  840.5 101.8 %reduce-scatter.13.cloned.1.call-done = f32[24,768]{1,0:T(8,128)} async-done(((f32[768,768]{1,0:T(8,128)}), f32[24,768]{1,0:T(8,128)}) %reduce-scatter.13.cloned.1.call-update) | async-done | bytes 73744 | tf_op jit(solution)/shard_map/reduce_scatter | solution.py:348
  942.3 142.0 %reduce-scatter.15.cloned.1.call-done = f32[24,3072]{1,0:T(8,128)} async-done(((f32[768,3072]{1,0:T(8,128)}), f32[24,3072]{1,0:T(8,128)}) %reduce-scatter.15.cloned.1.call-update) | async-done | bytes 294928 | tf_op jit(solution)/shard_map/reduce_scatter | solution.py:349
  1084.3 141.1 %reduce-scatter.17.cloned.1.call-done = f32[24,3072]{1,0:T(8,128)} async-done(((f32[768,3072]{1,0:T(8,128)}), f32[24,3072]{1,0:T(8,128)}) %reduce-scatter.17.cloned.1.call-update) | async-done | bytes 294928 | tf_op jit(solution)/shard_map/reduce_scatter | solution.py:350
  1225.4 141.9 %reduce-scatter.19.cloned.1.call-done = f32[96,768]{1,0:T(8,128)} async-done(((f32[3072,768]{1,0:T(8,128)}), f32[96,768]{1,0:T(8,128)}) %reduce-scatter.19.cloned.1.call-update) | async-done | bytes 294928 | tf_op jit(solution)/shard_map/reduce_scatter | solution.py:351
  (271 shorter events, 76.0 us)
Async XLA Ops:
  7.2 69.3 %all-gather.16.cloned.1.call-start = ((), (), s32[]{:S(2)}) async-start(), calls=%async_computation.12 | async-start | bytes 3649536 | tf_op jit(solution)/shard_map/all_gather | solution.py:124
  8.8 167.2 %all-gather.14.cloned.1.call-start = ((), (), s32[]{:S(2)}) async-start(), calls=%async_computation.6 | async-start | bytes 8355840 | tf_op jit(solution)/shard_map/all_gather | solution.py:145
  76.4 4.1 copy-start.24
  76.4 4.1 copy-start.26
  80.2 1.7 copy-start.33
  80.2 2.5 copy-start.28
  80.3 3.1 copy-start.29
  80.3 3.8 copy-start.30
  80.4 4.6 copy-start.55
  80.5 45.0 %copy-start.56 = (f32[1,2,24]{2,1,0:T(2,128)S(1)}, f32[1,2,24]{2,1,0:T(2,128)}, u32[]{:S(2)}) copy-start(f32[1,2,24]{2,1,0:T(2,128)} %param.21) | copy-start | bytes 580
  80.8 84.9 %copy-start.54 = (s32[160]{0:T(256)S(1)}, s32[160]{0:T(256)}, u32[]{:S(2)}) copy-start(s32[160]{0:T(256)} %param.15) | copy-start | bytes 1924
  81.9 138.0 %all-gather.18.cloned.1.call-start = ((), (), s32[]{:S(2)}) async-start(), calls=%async_computation.13 | async-start | bytes 1216512 | tf_op jit(solution)/shard_map/all_gather | solution.py:125
  82.6 193.6 %all-gather.20.cloned.1.call-start = ((), (), s32[]{:S(2)}) async-start(), calls=%async_computation.14 | async-start | bytes 4866048 | tf_op jit(solution)/shard_map/all_gather | solution.py:126
  83.4 258.6 %all-gather.22.cloned.1.call-start = ((), (), s32[]{:S(2)}) async-start(), calls=%async_computation.15 | async-start | bytes 4866048 | tf_op jit(solution)/shard_map/all_gather | solution.py:127
  84.1 323.6 %all-gather.24.cloned.1.call-start = ((), (), s32[]{:S(2)}) async-start(), calls=%async_computation.16 | async-start | bytes 4866048 | tf_op jit(solution)/shard_map/all_gather | solution.py:128
  84.9 619.9 %reduce-scatter.11.cloned.1.call-start = ((), (), s32[]{:S(2)}) async-start(), calls=%async_computation.7 | async-start | bytes 16711680 | tf_op jit(solution)/shard_map/reduce_scatter | solution.py:320
  165.7 251.9 %copy-start.44 = (f32[160]{0:T(256)}, f32[160]{0:T(256)S(1)}, u32[]{:S(2)}) copy-start(f32[160]{0:T(256)S(1)} %convert_element_type.163) | copy-start | bytes 1924
  174.9 232.8 %copy-start.31 = (f32[768]{0:T(1024)}, f32[768]{0:T(1024)S(1)}, u32[]{:S(2)}) copy-start(f32[768]{0:T(1024)S(1)} %get-tuple-element.190) | copy-start | bytes 9220
  174.9 242.7 %copy-start.34 = (f32[768]{0:T(1024)}, f32[768]{0:T(1024)S(1)}, u32[]{:S(2)}) copy-start(f32[768]{0:T(1024)S(1)} %get-tuple-element.189) | copy-start | bytes 9220
  199.4 6.7 copy-start.1
  206.0 13.9 %copy-start.17 = (bf16[160,768]{1,0:T(8,128)(2,1)S(1)}, bf16[160,768]{1,0:T(8,128)(2,1)}, u32[]{:S(2)}) copy-start(bf16[160,768]{1,0:T(8,128)(2,1)} %param.13) | copy-start | bytes 737284
  219.9 60.9 %copy-start.22 = (bf16[160,12,64]{0,2,1:T(8,128)(2,1)}, bf16[160,12,64]{0,2,1:T(8,128)(2,1)S(1)}, u32[]{:S(2)}) copy-start(bf16[160,12,64]{0,2,1:T(8,128)(2,1)S(1)} %get-tuple-element.246) | copy-start | bytes 737284
  221.9 185.9 %copy-start.36 = (f32[160]{0:T(256)}, f32[160]{0:T(256)S(1)}, u32[]{:S(2)}) copy-start(f32[160]{0:T(256)S(1)} %broadcast_multiply_fusion.5) | copy-start | bytes 1924
  222.1 185.6 %copy-start.40 = (f32[160]{0:T(256)}, f32[160]{0:T(256)S(1)}, u32[]{:S(2)}) copy-start(f32[160]{0:T(256)S(1)} %add_rsqrt_fusion.1) | copy-start | bytes 1924
  222.3 125.1 %copy-start.15 = (bf16[160,768]{1,0:T(8,128)(2,1)}, bf16[160,768]{1,0:T(8,128)(2,1)S(1)}, u32[]{:S(2)}) copy-start(bf16[160,768]{1,0:T(8,128)(2,1)S(1)} %fusion.57) | copy-start | bytes 737284
  347.4 65.8 %copy-start.5 = (bf16[160,3072]{1,0:T(8,128)(2,1)}, bf16[160,3072]{1,0:T(8,128)(2,1)S(1)}, u32[]{:S(2)}) copy-start(bf16[160,3072]{1,0:T(8,128)(2,1)S(1)} %get-tuple-element.250) | copy-start | bytes 2949124
  347.4 64.1 %copy-start.19 = (bf16[160,768]{1,0:T(8,128)(2,1)S(1)}, bf16[160,768]{1,0:T(8,128)(2,1)}, u32[]{:S(2)}) copy-start(bf16[160,768]{1,0:T(8,128)(2,1)} %param.23) | copy-start | bytes 737284
  407.7 5.5 copy-start.7
  407.7 5.5 copy-start.21
  411.3 6.4 copy-start.3
  411.3 6.3 copy-start.38
  411.5 6.1 copy-start.46
  411.5 6.1 slice-start
  411.6 7.9 slice-start.2
  413.2 4.5 copy-start.50
  413.2 4.5 copy-start.52
  413.2 4.5 slice-start.1
  413.2 6.2 slice-start.3
  417.6 4.8 copy-start.11
  417.6 4.8 copy-start.13
  417.6 1.9 copy-start.32
  417.6 1.9 copy-start.37
  417.6 1.9 copy-start.41
  419.5 3.0 copy-start.8
  422.5 4.0 copy-start.9
  439.5 2.4 copy-start
  463.6 3.0 copy-start
  488.2 3.0 copy-start
  512.8 3.0 copy-start
  537.4 3.0 copy-start
  549.0 157.3 %copy-start.25 = (f32[160,32]{0,1:T(8,128)S(1)}, f32[160,32]{0,1:T(8,128)}, u32[]{:S(2)}) copy-start(f32[160,32]{0,1:T(8,128)} %copy-done.24) | copy-start | bytes 61444
  549.0 157.3 %copy-start.27 = (f32[160,32]{0,1:T(8,128)S(1)}, f32[160,32]{0,1:T(8,128)}, u32[]{:S(2)}) copy-start(f32[160,32]{0,1:T(8,128)} %copy-done.26) | copy-start | bytes 61444
  549.0 289.2 %reduce-scatter.21.cloned.1.call-start = ((), (), s32[]{:S(2)}) async-start(), calls=%async_computation.17 | async-start | bytes 7299072
  719.1 3.1 copy-start.14
  719.1 3.1 copy-start.16
  719.1 223.2 %reduce-scatter.13.cloned.1.call-start = ((), (), s32[]{:S(2)}) async-start(), calls=%async_computation.8 | async-start | bytes 2433024 | tf_op jit(solution)/shard_map/reduce_scatter | solution.py:348
  722.1 362.2 %reduce-scatter.15.cloned.1.call-start = ((), (), s32[]{:S(2)}) async-start(), calls=%async_computation.9 | async-start | bytes 9732096 | tf_op jit(solution)/shard_map/reduce_scatter | solution.py:349
  727.3 498.1 %reduce-scatter.17.cloned.1.call-start = ((), (), s32[]{:S(2)}) async-start(), calls=%async_computation.10 | async-start | bytes 9732096 | tf_op jit(solution)/shard_map/reduce_scatter | solution.py:350
  733.6 1.4 copy-start.20
  733.6 1.4 copy-start.35
  733.6 1.4 copy-start.39
  733.6 1.4 copy-start.45
  733.6 1.4 copy-start.47
  733.7 633.7 %reduce-scatter.19.cloned.1.call-start = ((), (), s32[]{:S(2)}) async-start(), calls=%async_computation.11 | async-start | bytes 9732096 | tf_op jit(solution)/shard_map/reduce_scatter | solution.py:351
  (13 other events, 13.6 us)
Sparse Core Ops, SparseCore 0:
  11.5 62.9 all-gather.15
  82.0 72.5 all-gather.13
  158.0 52.2 all-gather.17
  213.7 62.5 all-gather.19
  279.6 62.3 all-gather.21
  345.3 62.3 all-gather.23
  549.1 155.6 reduce-scatter.10
  719.2 118.8 reduce-scatter.20
  844.0 98.2 reduce-scatter.12
  949.6 134.6 reduce-scatter.14
  1090.8 134.5 reduce-scatter.16
  1232.7 134.5 reduce-scatter.18
where the time goes:
time: 1380 us; the launch traced here: 1370 us
  waiting for transfers between devices  909 us (66%)
  blocking collectives  183 us (13%)
  matrix products  132 us (10%)
  local copies, waits for them, and re-layouts  95.6 us (7%)
  other arithmetic  35.1 us (3%)
  between operations  16.1 us (1%)
    reduce_scatter x1, waiting for transfers between devices, body(): lax.psum_scatter(key_terms.reshape(seq_length, 2 * model_width), 'seq', s...  155 us
    reduce_scatter x1, waiting for transfers between devices, body(): lax.psum_scatter(layer_grads[2], ('dp', 'seq'), scatter_dimension=0, tile...  142 us
    reduce_scatter x1, waiting for transfers between devices, body(): lax.psum_scatter(layer_grads[4], ('dp', 'seq'), scatter_dimension=0, tile...  142 us
    reduce_scatter x1, waiting for transfers between devices, body(): lax.psum_scatter(layer_grads[3], ('dp', 'seq'), scatter_dimension=0, tile...  141 us
    unnamed x2, blocking collectives  103 us
    reduce_scatter x1, waiting for transfers between devices, body(): lax.psum_scatter(layer_grads[1], ('dp', 'seq'), scatter_dimension=0, tile...  102 us
    all_gather x1, waiting for transfers between devices, body(): lax.all_gather(parts[3], ('dp', 'seq'), axis=0, tiled=True)  61.1 us
    all_gather x1, waiting for transfers between devices, body(): lax.all_gather(parts[4], ('dp', 'seq'), axis=0, tiled=True)  60.3 us
  transfers between devices with their start and end apart: 12, of which 9 were waited for; matrix products, arithmetic and copies ran while one was open for 7% of the time, Pallas kernels for 0%

commit v1 on v0

v1 whole, which is shorter than its diff:
```python
import functools

import jax
import jax.numpy as jnp
from jax import lax
from jax.experimental import pallas as pl
from jax.experimental.pallas import tpu as pltpu
from jax.sharding import PartitionSpec as P

HEADS = 12
EPS = 1e-05
BASE = 10000.0
AXES = ("dp", "seq")
BF = jnp.bfloat16
F32 = jnp.float32
FAR = -1e30
ONES = 64


def dot(a, b):
    return jnp.dot(a, b, preferred_element_type=F32)


def dot_t(a, b):
    return lax.dot_general(a, b, (((1,), (1,)), ((), ())), preferred_element_type=F32)


def t_dot(a, b):
    return lax.dot_general(a, b, (((0,), (0,)), ((), ())), preferred_element_type=F32)


def lanes(shape):
    return lax.broadcasted_iota(jnp.int32, shape, len(shape) - 1)


def swap_halves(u):
    width = u.shape[-1]
    low = lanes(u.shape) % 64 < 32
    return jnp.where(low, pltpu.roll(u, width - 32, 1), pltpu.roll(u, 32, 1))


def split3(v):
    hi = v.astype(BF).astype(F32)
    rest = v - hi
    mid = rest.astype(BF).astype(F32)
    return hi, mid, rest - mid


def with_units(base, v):
    at = lanes(base.shape)
    hi, mid, low = split3(v)
    return jnp.where(
        at == ONES,
        -hi,
        jnp.where(at == ONES + 1, -mid, jnp.where(at == ONES + 2, -low, base)),
    )


def project_kernel(x_ref, w_ref, cos_ref, sin_ref, ext_ref, q_ref, k_ref, v_ref):
    x = x_ref[...]
    cos, sin, ext = cos_ref[...], sin_ref[...], ext_ref[...]

    def rope(u):
        return u * cos + swap_halves(u) * sin

    kv = dot(x, w_ref[:, 384:])
    for p in range(3):
        k = rope(kv[:, p * 128 : (p + 1) * 128])
        k_ref[p, :, :128] = k.astype(BF)
        k_ref[p, :, 128:] = ext
        v_ref[p, :, :128] = kv[:, 384 + p * 128 : 384 + (p + 1) * 128].astype(BF)
        v_ref[p, :, 128:] = ext

    @pl.when(pl.program_id(0) == 0)
    def _():
        q = dot(x, w_ref[:, :384])
        for p in range(3):
            r = rope(q[:, p * 128 : (p + 1) * 128]).astype(BF)
            q_ref[:, p * 128 : (p + 1) * 128] = r * jnp.asarray(0.125, BF)


def project(x_all, w, cos, sin, ext, own):
    count, width = x_all.shape
    return pl.pallas_call(
        project_kernel,
        grid=(count // own,),
        in_specs=[
            pl.BlockSpec((own, width), lambda i: (i, 0)),
            pl.BlockSpec((width, 1152), lambda i: (0, 0)),
            pl.BlockSpec((own, 128), lambda i: (i, 0)),
            pl.BlockSpec((own, 128), lambda i: (i, 0)),
            pl.BlockSpec((own, 128), lambda i: (i, 0)),
        ],
        out_specs=[
            pl.BlockSpec((own, 384), lambda i: (0, 0)),
            pl.BlockSpec((3, own, 256), lambda i: (0, i, 0)),
            pl.BlockSpec((3, own, 256), lambda i: (0, i, 0)),
        ],
        out_shape=[
            jax.ShapeDtypeStruct((own, 384), BF),
            jax.ShapeDtypeStruct((3, count, 256), BF),
            jax.ShapeDtypeStruct((3, count, 256), BF),
        ],
        compiler_params=pltpu.CompilerParams(vmem_limit_bytes=32 << 20),
        cost_estimate=pl.CostEstimate(
            flops=2 * count * width * 768, bytes_accessed=count * 5000, transcendentals=0
        ),
        name="project",
    )(x_all, w, cos, sin, ext)


def attend_kernel(q_ref, k_ref, v_ref, ext_ref, att_ref, ob_ref, lse_ref, s_ref, *, chunk):
    keys = k_ref.shape[1]
    q = q_ref[...]
    own = q.shape[0]
    first = lanes(q.shape) < 64
    ext = ext_ref[...]
    parts = []
    for h in range(2):
        qh = jnp.where(first if h == 0 else ~first, q, jnp.zeros_like(q))
        qc = jnp.concatenate([qh, ext], axis=1)
        top = jnp.full((own, 128), FAR, F32)
        for j in range(0, keys, chunk):
            s = dot_t(qc, k_ref[0, j : j + chunk, :])
            s_ref[h, :, j : j + chunk] = s
            for i in range(0, chunk, 128):
                top = jnp.maximum(top, s[:, i : i + 128])
        m = jnp.max(top, axis=1, keepdims=True)
        acc = jnp.zeros((own, 256), F32)
        for j in range(0, keys, chunk):
            e = jnp.exp(s_ref[h, :, j : j + chunk] - m).astype(BF)
            acc = acc + dot(e, v_ref[0, j : j + chunk, :])
        total = acc[:, 128 + ONES : 129 + ONES]
        parts.append(acc[:, :128] / total)
        lse_ref[h] = with_units(ext.astype(F32), m + jnp.log(total)).astype(BF)
    att = jnp.where(first, parts[0], parts[1])
    att_ref[...] = att
    ob_ref[...] = att.astype(BF)


def attend(q, k, v, ext):
    own = q.shape[0]
    keys = k.shape[1]
    return pl.pallas_call(
        functools.partial(attend_kernel, chunk=512),
        grid=(3,),
        in_specs=[
            pl.BlockSpec((own, 128), lambda p: (0, p)),
            pl.BlockSpec((1, keys, 256), lambda p: (p, 0, 0)),
            pl.BlockSpec((1, keys, 256), lambda p: (p, 0, 0)),
            pl.BlockSpec((own, 128), lambda p: (0, 0)),
        ],
        out_specs=[
            pl.BlockSpec((own, 128), lambda p: (0, p)),
            pl.BlockSpec((own, 128), lambda p: (0, p)),
            pl.BlockSpec((2, own, 128), lambda p: (p, 0, 0)),
        ],
        out_shape=[
            jax.ShapeDtypeStruct((own, 384), F32),
            jax.ShapeDtypeStruct((own, 384), BF),
            jax.ShapeDtypeStruct((6, own, 128), BF),
        ],
        scratch_shapes=[pltpu.VMEM((2, own, keys), F32)],
        compiler_params=pltpu.CompilerParams(vmem_limit_bytes=56 << 20),
        cost_estimate=pl.CostEstimate(
            flops=4 * 6 * own * keys * 256,
            bytes_accessed=3 * keys * 1024,
            transcendentals=6 * own * keys,
        ),
        name="attend",
    )(q, k, v, ext)


def attend_back_kernel(
    q_ref, lse_ref, d_ref, att_ref, k_ref, v_ref, cos_ref, sin_ref, cosq_ref, sinq_ref,
    dq_ref, dk_ref, dv_ref, qc_s, dc_s, dq_s,
):
    j = pl.program_id(1)
    own = q_ref.shape[0]

    @pl.when(j == 0)
    def _():
        q, d = q_ref[...], d_ref[...]
        first = lanes(q.shape) < 64
        prod = d.astype(F32) * att_ref[...]
        for h in range(2):
            keep = first if h == 0 else ~first
            rows = slice(h * own, (h + 1) * own)
            qc_s[rows, :128] = jnp.where(keep, q, jnp.zeros_like(q))
            qc_s[rows, 128:] = lse_ref[h]
            dc_s[rows, :128] = jnp.where(keep, d, jnp.zeros_like(d))
            delta = jnp.sum(jnp.where(keep, prod, 0.0), axis=1, keepdims=True)
            dc_s[rows, 128:] = with_units(jnp.zeros((own, 128), F32), delta).astype(BF)
        dq_s[...] = jnp.zeros_like(dq_s)

    k = k_ref[0]
    v = v_ref[0]
    e = jnp.exp(dot_t(k, qc_s[...]))
    ds = (e * dot_t(v, dc_s[...])).astype(BF)
    dv_ref[...] = dot(e.astype(BF), dc_s[:, :128]).astype(BF)
    dk = dot(ds, qc_s[:, :128]).astype(BF).astype(F32)
    dk_ref[...] = (dk * cos_ref[...] - swap_halves(dk) * sin_ref[...]).astype(BF)
    dq_s[...] += t_dot(k[:, :128], ds)

    @pl.when(j == pl.num_programs(1) - 1)
    def _():
        t = dq_s[...].T
        first = lanes((own, 128)) < 64
        dq = jnp.where(first, t[:own], t[own:])
        dq = (dq * 0.125).astype(BF).astype(F32)
        dq_ref[...] = (dq * cosq_ref[...] - swap_halves(dq) * sinq_ref[...]).astype(BF)


def attend_back(q, lse, d, att, k, v, cos, sin):
    own = q.shape[0]
    keys = k.shape[1]
    chunk = 512
    return pl.pallas_call(
        attend_back_kernel,
        grid=(3, keys // chunk),
        in_specs=[
            pl.BlockSpec((own, 128), lambda p, j: (0, p)),
            pl.BlockSpec((2, own, 128), lambda p, j: (p, 0, 0)),
            pl.BlockSpec((own, 128), lambda p, j: (0, p)),
            pl.BlockSpec((own, 128), lambda p, j: (0, p)),
            pl.BlockSpec((1, chunk, 256), lambda p, j: (p, j, 0)),
            pl.BlockSpec((1, chunk, 256), lambda p, j: (p, j, 0)),
            pl.BlockSpec((chunk, 128), lambda p, j: (j, 0)),
            pl.BlockSpec((chunk, 128), lambda p, j: (j, 0)),
            pl.BlockSpec((own, 128), lambda p, j: (0, 0)),
            pl.BlockSpec((own, 128), lambda p, j: (0, 0)),
        ],
        out_specs=[
            pl.BlockSpec((own, 128), lambda p, j: (0, p)),
            pl.BlockSpec((chunk, 128), lambda p, j: (j, p)),
            pl.BlockSpec((chunk, 128), lambda p, j: (j, p)),
        ],
        out_shape=[
            jax.ShapeDtypeStruct((own, 384), BF),
            jax.ShapeDtypeStruct((keys, 384), BF),
            jax.ShapeDtypeStruct((keys, 384), BF),
        ],
        scratch_shapes=[
            pltpu.VMEM((2 * own, 256), BF),
            pltpu.VMEM((2 * own, 256), BF),
            pltpu.VMEM((128, 2 * own), F32),
        ],
        compiler_params=pltpu.CompilerParams(vmem_limit_bytes=32 << 20),
        cost_estimate=pl.CostEstimate(
            flops=10 * 6 * own * keys * 256,
            bytes_accessed=3 * keys * 1600,
            transcendentals=6 * own * keys,
        ),
        name="attend_back",
    )(q, lse, d, att, k, v, cos, sin, cos[:own], sin[:own])


def normalize(values):
    average = jnp.mean(values, axis=-1, keepdims=True)
    centred = values - average
    factor = lax.rsqrt(jnp.mean(centred * centred, axis=-1, keepdims=True) + EPS)
    return centred * factor, factor


def norm_back(gradient, normed, factor):
    return factor * (
        gradient
        - jnp.mean(gradient, axis=-1, keepdims=True)
        - normed * jnp.mean(gradient * normed, axis=-1, keepdims=True)
    )


class Grid:
    def __init__(self, ndp, nseq):
        self.ny, self.nz = ndp, nseq // 4
        self.count = ndp * nseq
        self.ring = [0, 1, 3, 2] if self.nz == 4 else list(range(self.nz))
        self.place = [self.ring.index(z) for z in range(self.nz)]
        step = {z: self.ring[(self.place[z] + 1) % self.nz] for z in range(self.nz)}
        self.across = {
            "c": self.pairs(lambda y, z, x, c: (y, z, x, 1 - c)),
            "x": self.pairs(lambda y, z, x, c: (y, z, 1 - x, c)),
            "y": self.pairs(lambda y, z, x, c: (1 - y, z, x, c)),
            "up": self.pairs(lambda y, z, x, c: (y, step[z], x, c)),
        }
        self.across["down"] = [(b, a) for a, b in self.across["up"]]
        self.across["spread"] = self.pairs(lambda y, z, x, c: (1 - y, z, x, c) if c == y else None)
        self.across["home"] = self.pairs(lambda y, z, x, c: (1 - y, z, x, c) if c != y else None)
        self.across["give"] = self.pairs(lambda y, z, x, c: (y, z, x, 1 - c) if c == y else None)

    def pairs(self, to):
        def index(y, z, x, c):
            return ((y * self.nz + z) * 2 + x) * 2 + c

        made = []
        for y in range(self.ny):
            for z in range(self.nz):
                for x in range(2):
                    for c in range(2):
                        there = to(y, z, x, c)
                        if there is not None:
                            made.append((index(y, z, x, c), index(*there)))
        return made

    def locate(self):
        s = lax.axis_index("seq")
        self.y = lax.axis_index("dp")
        self.z, self.x, self.c = s // 4, (s // 2) % 2, s % 2
        self.p = self.place_of(self.z)

    def place_of(self, z):
        return z ^ (z >> 1) if self.nz == 4 else z

    def move(self, way, a):
        return lax.ppermute(a, AXES, self.across[way])

    def ordered(self, bit, mine, theirs, axis):
        return jnp.where(
            bit == 0,
            jnp.concatenate([mine, theirs], axis=axis),
            jnp.concatenate([theirs, mine], axis=axis),
        )

    def gather(self, shard, order):
        a = shard[None, None, None]
        for axis in order:
            if axis == "z":
                held = [a]
                for _ in range(self.nz - 1):
                    held.append(self.move("up", held[-1]))
                if self.nz == 4:
                    pieces = []
                    for z in range(4):
                        back = (self.p - self.place[z]) % 4
                        pieces.append(
                            jnp.where(
                                back < 2,
                                jnp.where(back == 0, held[0], held[1]),
                                jnp.where(back == 2, held[2], held[3]),
                            )
                        )
                    a = jnp.concatenate(pieces, axis=1)
                else:
                    twice = jnp.concatenate(held[::-1] * 2, axis=1)
                    a = lax.dynamic_slice_in_dim(twice, self.nz - 1 - self.p, self.nz, 1)
            elif axis == "x":
                a = self.ordered(self.x, a, self.move("x", a), 2)
            else:
                a = self.ordered(self.y, a, self.move("y", a), 0)
        return a

    def blocks(self, order, count):
        i = jnp.arange(count, dtype=jnp.int32)
        y, z, x = (jnp.full((count,), v, jnp.int32) for v in (self.y, self.z, self.x))
        size = {"x": 2, "y": 2, "z": self.nz}
        for axis in reversed(order):
            if axis in size:
                d, i = i % size[axis], i // size[axis]
                if axis == "x":
                    x = x ^ d
                elif axis == "y":
                    y = y ^ d
                else:
                    z = self.place_of((self.p - d) % self.nz)
        return y, z, x

    def reduce(self, first, rest, order):
        raise NotImplementedError


def ring_sum(grid, blocks):
    part = blocks[-1]
    for d in range(len(blocks) - 2, -1, -1):
        part = grid.move("down", part.astype(BF)).astype(F32) + blocks[d]
    return part


def pair_sum(grid, axis, mine, theirs):
    return mine + grid.move(axis, theirs.astype(BF)).astype(F32)


def reduce_rows(grid, left, right, order):
    count = left.shape[0]
    head, tail = order[0], order[1:]
    if head == "z":
        whole = dot(left, right)
        size = count // grid.nz
        part = ring_sum(grid, [whole[d * size : (d + 1) * size] for d in range(grid.nz)])
    else:
        theirs = dot(left[count // 2 :], right).astype(BF)
        part = dot(left[: count // 2], right) + grid.move(head, theirs).astype(F32)
    for axis in tail:
        count = part.shape[0]
        if axis == "z":
            size = count // grid.nz
            part = ring_sum(grid, [part[d * size : (d + 1) * size] for d in range(grid.nz)])
        else:
            part = pair_sum(grid, axis, part[: count // 2], part[count // 2 :])
    return part


def body(grid, tokens, segment_ids, pad_mask, w_qkv, w_out, w_gate, w_up, w_down, ln_gain, ln_bias, cotangent):
    grid.locate()
    y, z, x, c = grid.y, grid.z, grid.x, grid.c
    local, width = tokens.shape
    own = 2 * local
    chips = grid.nz * 2
    rows = w_qkv.shape[1]
    down_rows = w_down.shape[1]
    half = width // 2
    ff = w_gate.shape[2] // 2
    move = grid.move

    def side(a, which, size):
        return jnp.where(which == 0, a[:, :size], a[:, size:])

    note = jnp.concatenate([segment_ids[None, :], pad_mask[None, :]], axis=0).astype(BF)
    note = jnp.pad(note, ((0, 6), (0, width - local)))
    message = jnp.concatenate([tokens, note], axis=0)
    held = [message]
    for _ in range(grid.nz - 1):
        held.append(move("up", held[-1]))
    along = jnp.stack(held)
    along = jnp.concatenate([along, move("x", along)], axis=0)
    beside = move("c", along)
    x_all = jnp.stack([along[:, :local], beside[:, :local]], axis=1).reshape(-1, width)
    ids = jnp.stack([along[:, local, :local], beside[:, local, :local]], axis=1)
    ids = ids.reshape(2 * chips, local)
    keep = jnp.concatenate([along[0, local + 1, :local], beside[0, local + 1, :local]])
    keep = keep.astype(F32)[:, None]
    cot = jnp.concatenate([cotangent, move("c", cotangent)], axis=0).astype(F32)

    w3 = [w_qkv[0, :, j * width : (j + 1) * width].astype(BF) for j in range(3)]
    gate_up = [w_gate[0].astype(BF), w_up[0].astype(BF)]
    mine = [side(w, c, half) for w in w3] + [side(w, c, ff) for w in gate_up]
    theirs = [side(w, 1 - c, half) for w in w3] + [side(w, 1 - c, ff) for w in gate_up]
    mine = jnp.concatenate(mine, axis=1)
    shard = grid.ordered(c, mine, move("c", jnp.concatenate(theirs, axis=1)), 0)
    n3 = 3 * half
    qkv_w = grid.gather(shard[:, :n3], "zxy").reshape(width, n3)

    extra = jnp.concatenate([ln_gain[0], ln_bias[0]], axis=0).astype(BF).reshape(1, 4 * rows)
    extra = jnp.pad(extra, ((0, 7), (0, width - 4 * rows)))
    out_shard = jnp.concatenate([w_out[0].astype(BF), extra], axis=0)
    out_half = grid.gather(out_shard, "yxz")
    out_both = grid.ordered(
        c, out_half[:, :, :, None], move("c", out_half)[:, :, :, None], 3
    ).reshape(grid.count, rows + 8, width)
    out_w = out_both[:, :rows].reshape(width, width)
    params = out_both[:, rows, : 4 * rows].reshape(grid.count, 4, rows)
    params = jnp.transpose(params, (1, 0, 2)).reshape(4, width).astype(F32)
    gain_one, gain_two, bias_one, bias_two = (params[i : i + 1] for i in range(4))

    gate_w = grid.gather(shard[:, n3 : n3 + ff], "zxy").reshape(width, ff)
    up_w = grid.gather(shard[:, n3 + ff :], "zyx").reshape(width, ff)
    down = w_down[0].astype(BF)
    down = grid.ordered(c, down, move("c", down), 0)
    down = jnp.where(c == y, down, move("spread", down))
    down_w = grid.gather(down, "zx").reshape(ff, width)

    onehot = (ids[:, :, None] == jnp.arange(64, dtype=jnp.int32).astype(BF)).astype(F32)
    at = jnp.arange(2 * chips, dtype=jnp.int32)
    _, bz, bx = grid.blocks("xz", chips)
    number = (bz * 2 + bx)[:, None] * 2 + jnp.stack([c, 1 - c])[None, :]
    number = number.reshape(2 * chips)
    tri = jnp.arange(local)
    before = jnp.einsum(
        "ij,bjs->bis", (tri[None, :] < tri[:, None]).astype(BF), onehot.astype(BF),
        preferred_element_type=F32,
    )
    counts = jnp.sum(onehot, axis=1)
    earlier = jnp.sum(
        jnp.where((number[None, :] < number[:, None])[:, :, None], counts[None], 0.0), axis=1
    )
    position = jnp.sum(onehot * (before + earlier[:, None, :]), axis=2).reshape(-1)
    del at
    lane = jnp.arange(128, dtype=jnp.int32)
    frequency = jnp.exp(-jnp.log(BASE) * (lane % 32).astype(F32) * (2.0 / 64))
    angle = position[:, None] * frequency[None, :]
    cos = jnp.cos(angle)
    sin = jnp.sin(angle) * jnp.where(lane % 64 < 32, -1.0, 1.0)
    flat = onehot.reshape(-1, 64)
    units = jnp.broadcast_to((jnp.arange(64) < 3).astype(F32), flat.shape)
    key_ext = jnp.concatenate([flat, units], axis=1).astype(BF)
    query_ext = jnp.concatenate(
        [(1.0 - flat[:own]) * FAR, jnp.zeros((own, 64), F32)], axis=1
    ).astype(BF)

    q, k, v = project(x_all, qkv_w, cos, sin, key_ext, own)
    att, ob, lse = attend(q, k, v, query_ext)

    def turned(a):
        return jnp.concatenate([a[local:], a[:local]], axis=0)

    ob_all = grid.ordered(c, ob, turned(move("c", ob)), 1)
    x_own = x_all[:own]
    n1, f1 = normalize(x_own.astype(F32) + dot(ob_all, out_w))
    h1 = n1 * gain_one + bias_one
    h1_low = h1.astype(BF)
    gate = dot(h1_low, gate_w)
    up = dot(h1_low, up_w)
    hidden = (jax.nn.silu(gate) * up).astype(BF)
    part = dot(hidden, down_w)
    n2, f2 = normalize(h1 + part + turned(move("c", part)))
    output = ((n2[:local] * gain_two + bias_two) * keep[:local]).astype(BF)

    masked = cot * keep
    grad_gain_two = jnp.sum(masked * n2, axis=0)
    grad_bias_two = jnp.sum(masked, axis=0)
    dr2 = norm_back(masked * gain_two, n2, f2)
    dm = dr2.astype(BF)
    dh = dot_t(dm, down_w)
    sigmoid = jax.nn.sigmoid(gate)
    dgate = (dh * up * sigmoid * (1.0 + gate * (1.0 - sigmoid))).astype(BF)
    dup = (dh * gate * sigmoid).astype(BF)

    def selector(order, per, size, both):
        blocks = size // per
        by, bz, bx = grid.blocks(order, blocks)
        start = ((by * grid.nz + bz) * 2 + bx) * per
        row = (start[:, None] + jnp.arange(per, dtype=jnp.int32)[None, :]).reshape(-1)
        del both
        return (jnp.arange(size, dtype=jnp.int32)[:, None] == row[None, :]).astype(BF)

    def turned_rows(order, a, per):
        return t_dot(selector(order, per, a.shape[1], True), a.T).astype(BF)

    two = 2 * rows

    size_d = 2 * down_rows
    by, bz, bx = grid.blocks("xz", chips)
    row = ((bz * 2 + bx) * size_d)[:, None] + jnp.arange(size_d, dtype=jnp.int32)[None, :]
    pick = (jnp.arange(ff, dtype=jnp.int32)[:, None] == row.reshape(1, -1)).astype(BF)
    hidden_t = lax.dot_general(
        pick, hidden, (((0,), (1,)), ((), ())), preferred_element_type=F32
    ).astype(BF)
    dd = reduce_rows(grid, hidden_t, dm, "xz")
    dd = dd + move("home", dd.astype(BF)).astype(F32)
    sent = jnp.where(c == 0, dd[down_rows:], dd[:down_rows])
    kept = jnp.where(c == 0, dd[:down_rows], dd[down_rows:])
    grad_down = jnp.where(c == y, kept, move("give", sent))

    def rows_in(order, a):
        sel = selector(order, two, width, True)
        return lax.dot_general(
            sel, a, (((0,), (1,)), ((), ())), preferred_element_type=F32
        ).astype(BF)

    def finish(part, size):
        sent = jnp.where(c == 0, part[rows:], part[:rows])
        kept = jnp.where(c == 0, part[:rows], part[rows:])
        got = move("c", sent)
        pieces = []
        for i in range(0, part.shape[1], size):
            pieces.append(grid.ordered(c, kept[:, i : i + size], got[:, i : i + size], 1))
        return jnp.concatenate(pieces, axis=1)

    h1_yx = rows_in("yxz", h1_low)
    h1_xy = rows_in("xyz", h1_low)
    grad_gate = finish(reduce_rows(grid, h1_yx, dgate, "yxz"), ff)
    grad_up = finish(reduce_rows(grid, h1_xy, dup, "xyz"), ff)

    part = dot_t(dgate, gate_w) + dot_t(dup, up_w)
    dh1 = dr2 + part + turned(move("c", part))
    grad_gain_one = jnp.sum(dh1 * n1, axis=0)
    grad_bias_one = jnp.sum(dh1, axis=0)
    dr1 = norm_back(dh1 * gain_one, n1, f1)
    da = dr1.astype(BF)
    my_out = jnp.where(c == 0, out_w[:half], out_w[half:])
    dob = dot_t(da, my_out).astype(BF)

    dq, dk, dv = attend_back(q, lse, dob, att, k, v, cos, sin)

    by, bz, bx = grid.blocks("yxz", grid.count // 2)
    start = (((by * grid.nz + bz) * 2 + bx) * 2 + c) * rows
    row = (start[:, None] + jnp.arange(rows, dtype=jnp.int32)[None, :]).reshape(1, -1)
    pick = (jnp.arange(width, dtype=jnp.int32)[:, None] == row).astype(BF)
    ob_t = lax.dot_general(
        pick, ob_all, (((0,), (1,)), ((), ())), preferred_element_type=F32
    ).astype(BF)
    do = dot(ob_t, da).reshape(grid.count // 2, rows, width)
    norms = jnp.stack([grad_gain_one, grad_gain_two, grad_bias_one, grad_bias_two])
    hi, mid, low = split3(norms)
    norms = dot(hi.astype(BF), pick) + dot(mid.astype(BF), pick) + dot(low.astype(BF), pick)
    norms = jnp.transpose(norms.reshape(4, grid.count // 2, rows), (1, 0, 2))
    norms = jnp.pad(norms.reshape(-1, 1, 4 * rows), ((0, 0), (0, 7), (0, width - 4 * rows)))
    part = jnp.concatenate([do, norms], axis=1)
    n = part.shape[0]
    part = pair_sum(grid, "y", part[: n // 2], part[n // 2 :])
    part = pair_sum(grid, "x", part[: n // 4], part[n // 4 :])
    part = ring_sum(grid, [part[d] for d in range(grid.nz)])
    grad_out = part[:rows]
    norms = part[rows, : 4 * rows].reshape(2, 2, rows)

    x_t = rows_in("yxz", x_all)
    grad_q = reduce_rows(grid, x_t[:, :own], dq, "yxz")
    dkv = jnp.concatenate([dk, dv], axis=1)
    grad_kv = reduce_rows(grid, x_t, dkv, "yxz")
    grad_qkv = finish(jnp.concatenate([grad_q, grad_kv], axis=1), half)
    dx = dot_t(dkv, qkv_w[:, half:]).reshape(chips, 2, local, width)
    dx_q = dot_t(dq, qkv_w[:, :half]).reshape(2, local, width)
    theirs = jnp.concatenate([dx[:1, 1] + dx_q[1], dx[1:, 1]], axis=0)
    mine = jnp.concatenate([dx[:1, 0] + dx_q[0], dx[1:, 0]], axis=0)
    part = mine + move("c", theirs.astype(BF)).astype(F32)
    part = pair_sum(grid, "x", part[: chips // 2], part[chips // 2 :])
    part = ring_sum(grid, [part[d] for d in range(grid.nz)])
    grad_input = dr1[:local] + part

    return (
        output,
        grad_input,
        grad_qkv[None],
        grad_out[None],
        grad_gate[None],
        grad_up[None],
        grad_down[None],
        norms[0][None],
        norms[1][None],
    )


def solution(mesh):
    grid = Grid(mesh.shape["dp"], mesh.shape["seq"])
    rows = P(AXES, None)
    weight = P(None, AXES, None)
    norm = P(None, None, AXES)
    return jax.shard_map(
        functools.partial(body, grid),
        mesh=mesh,
        in_specs=(rows, P(AXES), P(AXES)) + (weight,) * 5 + (norm,) * 2 + (rows,),
        out_specs=(rows, rows) + (weight,) * 5 + (norm,) * 2,
        check_vma=False,
    )
```

time: 1380 us -> 469 us (0.34)
  waiting for transfers between devices: 909 us -> 167 us
  blocking collectives: 183 us -> 0 us
  starting transfers between devices: 0.67 us -> 84.9 us
  matrix products: 132 us -> 50.2 us
  local copies, waits for them, and re-layouts: 95.6 us -> 52.3 us
  Pallas kernels: 0 us -> 37.8 us
  other arithmetic: 35.1 us -> 68.4 us
    reduce_scatter x5 -> x0, waiting for transfers between devices: 681 us -> none  [the longest x1 155 us: body(): lax.psum_scatter(key_terms.reshape(seq_length, 2 * model_width), 'seq', s...]
    all_gather x6 -> x0, waiting for transfers between devices: 175 us -> none  [the longest x1 61.1 us: body(): lax.all_gather(parts[3], ('dp', 'seq'), axis=0, tiled=True)]
    ppermute x0 -> x76, waiting for transfers between devices: none -> 167 us  [move(): return lax.ppermute(a, AXES, self.across[way])]
    unnamed x2 -> x0, blocking collectives: 103 us -> none
    ppermute x0 -> x76, starting transfers between devices: none -> 84.9 us  [move(): return lax.ppermute(a, AXES, self.across[way])]
    dot_general x42 -> x29, matrix products: 132 us -> 50.2 us  [the longest x18 29.1 us: dot(): return jnp.dot(a, b, preferred_element_type=F32)]
    all_gather x2 -> x0, blocking collectives: 79.7 us -> none  [the longest x1 40 us: body(): lax.all_gather(parts[6], ('dp', 'seq'), axis=1, tiled=True)]
    unnamed x13 -> x0, waiting for transfers between devices: 52.1 us -> none
  transfers between devices with their start and end apart: 12 -> 76, of which waited for: 9 -> 33; matrix products, arithmetic and copies ran while one was open for 7% -> 30% of each run, Pallas kernels for 0% -> 8%
where the time goes in v1:
time: 469 us; the launch traced here: 463 us
  waiting for transfers between devices  167 us (36%)
  starting transfers between devices  84.9 us (18%)
  other arithmetic  68.4 us (15%)
  local copies, waits for them, and re-layouts  52.3 us (11%)
  matrix products  50.2 us (11%)
  Pallas kernels  37.8 us (8%)
    ppermute x76, waiting for transfers between devices, move(): return lax.ppermute(a, AXES, self.across[way])  167 us
    ppermute x76, starting transfers between devices, move(): return lax.ppermute(a, AXES, self.across[way])  84.9 us
    dot_general x18, matrix products, dot(): return jnp.dot(a, b, preferred_element_type=F32)  29.1 us
    unnamed x142, local copies, waits for them, and re-layouts  20.9 us
    select_n x17, other arithmetic, ordered(): jnp.where(bit == 0, jnp.concatenate([mine, theirs], axis=axis), jnp.conca...  19.9 us
    pallas_call x1, Pallas kernels, attend_back(): pl.pallas_call(attend_back_kernel, grid=(3, keys // chunk), in_specs=[pl....  18.9 us
    pallas_call x1, Pallas kernels, attend(): pl.pallas_call(functools.partial(attend_kernel, chunk=512), grid=(3,), in...  12.6 us
    dot_general x6, matrix products, dot_t(): lax.dot_general(a, b, (((1,), (1,)), ((), ())), preferred_element_type=F32)  12.5 us
  transfers between devices with their start and end apart: 76, of which 33 were waited for; matrix products, arithmetic and copies ran while one was open for 30% of the time, Pallas kernels for 8%

profile of v1, /device:TPU:0, one launch (start us, length us, event | category | flops | bytes accessed | tf_op | source)
XLA Modules:
  0.0 463.1 jit_solution(16536477947081671053)
XLA Ops:
  2.4 3.0 collective-permute-start.12
  26.7 2.2 collective-permute-done.13
  29.0 2.6 collective-permute-start.14
  32.7 2.4 collective-permute-start.29
  38.8 4.5 collective-permute-done.6
  43.7 2.7 collective-permute-done.18
  46.4 3.2 collective-permute-done.23
  49.6 7.9 %collective-permute-done.7 = bf16[1,1,1,48,1152]{4,3,2,1,0:T(8,128)(2,1)S(1)} collective-permute-done((bf16[1,1,1,48,1152]{4,3,2,1,0:T(8,128)(2,1)S(1)}, bf16[1,1,1,48,1152]{4,3,2,1,0:T(8,128)(2,1)S(1)}, u32[]{:S(2)}, u32[]{:S(2)}) %collective-permute-start.7) | collective-permute-done | bytes 110624 | tf_op jit(solution)/shard_map/ppermute | solution.py:315
  58.0 6.9 %collective-permute-done.19 = bf16[1,1,1,48,1536]{4,3,2,1,0:T(8,128)(2,1)S(1)} collective-permute-done((bf16[1,1,1,48,1536]{4,3,2,1,0:T(8,128)(2,1)S(1)}, bf16[1,1,1,48,1536]{4,3,2,1,0:T(8,128)(2,1)S(1)}, u32[]{:S(2)}, u32[]{:S(2)}) %collective-permute-start.19) | collective-permute-done | bytes 147488 | tf_op jit(solution)/shard_map/ppermute | solution.py:315
  64.8 3.2 collective-permute-done.24
  72.1 7.7 %collective-permute-done.20 = bf16[1,1,1,48,1536]{4,3,2,1,0:T(8,128)(2,1)S(1)} collective-permute-done((bf16[1,1,1,48,1536]{4,3,2,1,0:T(8,128)(2,1)S(1)}, bf16[1,1,1,48,1536]{4,3,2,1,0:T(8,128)(2,1)S(1)}, u32[]{:S(2)}, u32[]{:S(2)}) %collective-permute-start.20) | collective-permute-done | bytes 147488 | tf_op jit(solution)/shard_map/ppermute | solution.py:315
  80.0 3.0 collective-permute-done.25
  84.7 4.2 collective-permute-done.16
  88.9 2.4 collective-permute-start.26
  95.5 6.4 %collective-permute-done.31 = bf16[1,1,1,192,768]{4,3,2,1,0:T(8,128)(2,1)S(1)} collective-permute-done((bf16[1,1,1,192,768]{4,3,2,1,0:T(8,128)(2,1)S(1)}, bf16[1,1,1,192,768]{4,3,2,1,0:T(8,128)(2,1)S(1)}, u32[]{:S(2)}, u32[]{:S(2)}) %collective-permute-start.31) | collective-permute-done | bytes 294944 | tf_op jit(solution)/shard_map/ppermute | solution.py:315
  101.9 2.6 collective-permute-done.26
  107.7 5.3 %collective-permute-done.32 = bf16[1,1,1,192,768]{4,3,2,1,0:T(8,128)(2,1)S(1)} collective-permute-done((bf16[1,1,1,192,768]{4,3,2,1,0:T(8,128)(2,1)S(1)}, bf16[1,1,1,192,768]{4,3,2,1,0:T(8,128)(2,1)S(1)}, u32[]{:S(2)}, u32[]{:S(2)}) %collective-permute-start.32) | collective-permute-done | bytes 294944 | tf_op jit(solution)/shard_map/ppermute | solution.py:315
  119.7 2.2 constant_dynamic-update-slice_fusion
  123.6 2.9 slice_bitcast_fusion.1
  127.1 2.3 maximum_select_fusion.3
  129.4 14.7 %collective-permute-done.27 = bf16[2,4,1,48,1536]{4,3,2,1,0:T(8,128)(2,1)} collective-permute-done((bf16[2,4,1,48,1536]{4,3,2,1,0:T(8,128)(2,1)S(1)}, bf16[2,4,1,48,1536]{4,3,2,1,0:T(8,128)(2,1)}, u32[]{:S(2)}, u32[]{:S(2)}) %collective-permute-start.27) | collective-permute-done | bytes 1179680 | tf_op jit(solution)/shard_map/ppermute | solution.py:315
  144.1 3.3 maximum_select_fusion.1
  148.7 4.2 maximum_select_fusion
  152.9 16.0 %collective-permute-done.33 = bf16[1,4,1,192,768]{4,3,2,1,0:T(8,128)(2,1)} collective-permute-done((bf16[1,4,1,192,768]{4,3,2,1,0:T(8,128)(2,1)}, bf16[1,4,1,192,768]{4,3,2,1,0:T(8,128)(2,1)}, u32[]{:S(2)}, u32[]{:S(2)}) %collective-permute-start.33) | collective-permute-done | bytes 1179680 | tf_op jit(solution)/shard_map/ppermute | solution.py:315
  168.9 2.8 maximum_select_fusion.2
  178.5 2.2 copy.29
  182.9 5.4 %fusion.16 = (f32[2560,128]{1,0:T(8,128)S(1)}, f32[2560,128]{1,0:T(8,128)S(1)}) fusion(f32[128]{0:T(128)} %get-tuple-element.120, f32[128]{0:T(128)} %get-tuple-element.121, f32[2560]{0:T(1024)} %mul.280), kind=kLoop, calls=%fused_computation.51 | loop fusion | flops 655360 | bytes 2632704 | tf_op jit(solution)/shard_map/mul | solution.py:481
  188.3 6.3 %project.1 = (bf16[320,384]{1,0:T(8,128)(2,1)S(1)}, bf16[3,2560,256]{2,1,0:T(8,128)(2,1)S(1)}, bf16[3,2560,256]{2,1,0:T(8,128)(2,1)S(1)}) custom-call(bf16[2560,768]{1,0:T(8,128)(2,1)S(1)} %bitcast.194, bf16[768,1152]{1,0:T(8,128)(2,1)S(1)} %bitcast.196, f32[2560,128]{1,0:T(8,128)S(1)} %get-tuple-element.109.cos_ref, ...), custom_call_target="tpu_custom_call" | custom-call | flops 3019898880 | bytes 12800000 | tf_op jit(solution)/shard_map/project/pallas_call | solution.py:84
  199.2 12.6 %attend.1 = (f32[320,384]{1,0:T(8,128)}, bf16[320,384]{1,0:T(8,128)(2,1)}, bf16[6,320,128]{2,1,0:T(8,128)(2,1)}) custom-call(bf16[320,384]{1,0:T(8,128)(2,1)} %copy-done.8, bf16[3,2560,256]{2,1,0:T(8,128)(2,1)} %copy-done.4, bf16[3,2560,256]{2,1,0:T(8,128)(2,1)} %copy-done.6, bf16[320,128]{1,0:T(8,128)(2,1)} %concatenate.369.ext_ref), custom_call_target="tpu_custom_call" | custom-call | flops 5033164800 | bytes 7864320 | tf_op jit(solution)/shard_map/attend/pallas_call | solution.py:144
  211.8 4.9 %convolution_convert_fusion = bf16[768,2560]{1,0:T(8,128)(2,1)} fusion(bf16[2560,768]{1,0:T(8,128)(2,1)S(1)} %bitcast.195, s32[768]{0:T(1024)S(1)} %copy-done.59), kind=kOutput, calls=%fused_computation.2 | convolution fusion | flops 3023044608 | bytes 7867392 | tf_op jit(solution)/shard_map/dot_general | solution.py:545
  233.5 2.9 multiply_convert_fusion.1
  238.5 3.1 convolution_convert_fusion.3
  253.4 3.5 fusion.29
  260.9 2.1 copy-done.5
  263.0 2.1 copy-done.7
  268.1 18.9 %attend_back.1 = (bf16[320,384]{1,0:T(8,128)(2,1)S(1)}, bf16[2560,384]{1,0:T(8,128)(2,1)S(1)}, bf16[2560,384]{1,0:T(8,128)(2,1)S(1)}) custom-call(bf16[320,384]{1,0:T(8,128)(2,1)S(1)} %copy-done.9, bf16[6,320,128]{2,1,0:T(8,128)(2,1)S(1)} %copy-done.11, bf16[320,384]{1,0:T(8,128)(2,1)S(1)} %convolution_convert_fusion.6.d_ref, f32[320,384]{1,0:T(8,128)S(1)} %copy-done.10, ...), custom_call_target="tpu_custom_call" | custom-call | flops 12582912000 | bytes 12288000 | tf_op jit(solution)/shard_map/attend_back/pallas_call | solution.py:218
  289.1 2.5 fusion.13
  291.6 5.4 %fusion.21 = f32[2560,768]{1,0:T(8,128)} fusion(bf16[2560,768]{1,0:T(8,128)(2,1)S(1)} %constant_dynamic-update-slice_fusion.11, bf16[768,1152]{1,0:T(8,128)(2,1)S(1)} %bitcast.198), kind=kOutput, calls=%fused_computation.63 | convolution fusion | flops 3019898880 | bytes 12976128 | tf_op jit(solution)/shard_map/dot_general | solution.py:25
  301.2 2.1 fusion.10
  303.4 4.0 copy_bitcast_fusion
  312.3 2.6 convert_add_fusion
  315.0 3.0 convert_add_fusion.1
  318.0 2.9 collective-permute-start.71
  328.4 3.5 collective-permute-done.44
  334.8 14.8 %collective-permute-done.54 = bf16[4,32,768]{2,1,0:T(8,128)(2,1)S(1)} collective-permute-done((bf16[4,32,768]{2,1,0:T(8,128)(2,1)S(1)}, bf16[4,32,768]{2,1,0:T(8,128)(2,1)S(1)}, u32[]{:S(2)}, u32[]{:S(2)}) %collective-permute-start.54) | collective-permute-done | bytes 196640 | tf_op jit(solution)/shard_map/ppermute | solution.py:315
  350.8 2.7 collective-permute-done.45
  353.5 2.5 collective-permute-start.55
  357.7 3.2 collective-permute-start.46
  362.6 3.2 collective-permute-start.56
  365.8 2.2 collective-permute-done.56
  368.0 3.4 collective-permute-start.72
  374.0 2.6 collective-permute-done.57
  376.6 2.4 collective-permute-start.48
  382.2 3.4 collective-permute-start.73
  391.2 3.4 collective-permute-done.66
  394.6 3.4 collective-permute-start.67
  399.0 3.4 collective-permute-start.50
  404.4 3.3 collective-permute-start.51
  412.0 2.3 collective-permute-done.68
  419.6 21.3 %collective-permute-done.38 = bf16[4,160,768]{2,1,0:T(8,128)(2,1)S(1)} collective-permute-done((bf16[4,160,768]{2,1,0:T(8,128)(2,1)S(1)}, bf16[4,160,768]{2,1,0:T(8,128)(2,1)S(1)}, u32[]{:S(2)}, u32[]{:S(2)}) %collective-permute-start.38) | collective-permute-done | bytes 983072 | tf_op jit(solution)/shard_map/ppermute | solution.py:315
  442.8 5.9 %collective-permute-done.39 = bf16[160,768]{1,0:T(8,128)(2,1)S(1)} collective-permute-done((bf16[160,768]{1,0:T(8,128)(2,1)S(1)}, bf16[160,768]{1,0:T(8,128)(2,1)S(1)}, u32[]{:S(2)}, u32[]{:S(2)}) %collective-permute-start.39) | collective-permute-done | bytes 245792 | tf_op jit(solution)/shard_map/ppermute | solution.py:315
  451.4 4.1 collective-permute-done.40
  455.5 2.7 collective-permute-start.41
  459.0 2.9 collective-permute-done.41
  (460 shorter events, 158.5 us)
Async XLA Ops:
  2.4 21.0 %collective-permute-start.12 = (bf16[1,1,1,32,768]{4,3,2,1,0:T(8,128)(2,1)S(1)}, bf16[1,1,1,32,768]{4,3,2,1,0:T(8,128)(2,1)}, u32[]{:S(2)}, u32[]{:S(2)}) collective-permute-start(bf16[1,1,1,32,768]{4,3,2,1,0:T(8,128)(2,1)S(1)} %get-tuple-element.101), channel_id=1, source_target_pairs={{0,16},{1,17},{2,18},{3,19},{4,20},{5,21},{6,22},{7,23},{8,24},{9,... | collective-permute-start | bytes 147464 | tf_op jit(solution)/shard_map/ppermute | solution.py:315
  6.4 25.2 %collective-permute-start.28 = (bf16[96,768]{1,0:T(8,128)(2,1)S(1)}, bf16[96,768]{1,0:T(8,128)(2,1)}, u32[]{:S(2)}, u32[]{:S(2)}) collective-permute-start(bf16[96,768]{1,0:T(8,128)(2,1)S(1)} %convert_bitcast_fusion), channel_id=1, source_target_pairs={{0,1},{1,0},{2,3},{3,2},{4,5},{5,4},{6,7},{7,6},{8,9},{9,8},{10,11... | collective-permute-start | bytes 442376 | tf_op jit(solution)/shard_map/ppermute | solution.py:315
  12.6 22.5 %collective-permute-start.5 = (bf16[24,4224]{1,0:T(8,128)(2,1)}, bf16[24,4224]{1,0:T(8,128)(2,1)}, u32[]{:S(2)}, u32[]{:S(2)}) collective-permute-start(bf16[24,4224]{1,0:T(8,128)(2,1)} %get-tuple-element.88), channel_id=1, source_target_pairs={{0,1},{1,0},{2,3},{3,2},{4,5},{5,4},{6,7},{7,6},{8,9},{9,8},{10,11... | collective-permute-start | bytes 608264 | tf_op jit(solution)/shard_map/ppermute | solution.py:315
  13.2 23.8 %collective-permute-start = (bf16[168,768]{1,0:T(8,128)(2,1)S(1)}, bf16[168,768]{1,0:T(8,128)(2,1)S(1)}, u32[]{:S(2)}, u32[]{:S(2)}) collective-permute-start(bf16[168,768]{1,0:T(8,128)(2,1)S(1)} %get-tuple-element.82), channel_id=1, source_target_pairs={{0,4},{1,5},{2,6},{3,7},{4,12},{5,13},{6,14},{7,15},{8,0},{9,1},{1... | collective-permute-start | bytes 774152 | tf_op jit(solution)/shard_map/ppermute | solution.py:315
  29.0 14.3 %collective-permute-start.14 = (bf16[2,1,2,32,768]{4,3,2,1,0:T(8,128)(2,1)S(1)}, bf16[2,1,2,32,768]{4,3,2,1,0:T(8,128)(2,1)S(1)}, u32[]{:S(2)}, u32[]{:S(2)}) collective-permute-start(bf16[2,1,2,32,768]{4,3,2,1,0:T(8,128)(2,1)S(1)} %maximum_select_fusion.13), channel_id=1, source_target_pairs={{0,4},{1,5},{2,6},{3,7},{4,12},{5,13},{6,14},{7,15},{8,0},{9,1},{1... | collective-permute-start | bytes 589832 | tf_op jit(solution)/shard_map/ppermute | solution.py:315
  32.7 24.8 %collective-permute-start.29 = (bf16[192,768]{1,0:T(8,128)(2,1)S(1)}, bf16[192,768]{1,0:T(8,128)(2,1)S(1)}, u32[]{:S(2)}, u32[]{:S(2)}) collective-permute-start(bf16[192,768]{1,0:T(8,128)(2,1)S(1)} %maximum_select_fusion.10), channel_id=1, source_target_pairs={{0,16},{2,18},{4,20},{6,22},{8,24},{10,26},{12,28},{14,30},{17,1},... | collective-permute-start | bytes 884744 | tf_op jit(solution)/shard_map/ppermute | solution.py:315
  36.3 6.9 %collective-permute-start.6 = (bf16[1,1,1,48,1152]{4,3,2,1,0:T(8,128)(2,1)S(1)}, bf16[1,1,1,48,1152]{4,3,2,1,0:T(8,128)(2,1)S(1)}, u32[]{:S(2)}, u32[]{:S(2)}) collective-permute-start(bf16[1,1,1,48,1152]{4,3,2,1,0:T(8,128)(2,1)S(1)} %slice_bitcast_fusion.9), channel_id=1, source_target_pairs={{0,4},{1,5},{2,6},{3,7},{4,12},{5,13},{6,14},{7,15},{8,0},{9,1},{1... | collective-permute-start | bytes 331784 | tf_op jit(solution)/shard_map/ppermute | solution.py:315
  36.8 9.6 %collective-permute-start.18 = (bf16[1,1,1,48,1536]{4,3,2,1,0:T(8,128)(2,1)S(1)}, bf16[1,1,1,48,1536]{4,3,2,1,0:T(8,128)(2,1)S(1)}, u32[]{:S(2)}, u32[]{:S(2)}) collective-permute-start(bf16[1,1,1,48,1536]{4,3,2,1,0:T(8,128)(2,1)S(1)} %get-tuple-element.75), channel_id=1, source_target_pairs={{0,4},{1,5},{2,6},{3,7},{4,12},{5,13},{6,14},{7,15},{8,0},{9,1},{1... | collective-permute-start | bytes 442376 | tf_op jit(solution)/shard_map/ppermute | solution.py:315
  37.0 12.5 %collective-permute-start.23 = (bf16[1,1,1,48,1536]{4,3,2,1,0:T(8,128)(2,1)S(1)}, bf16[1,1,1,48,1536]{4,3,2,1,0:T(8,128)(2,1)S(1)}, u32[]{:S(2)}, u32[]{:S(2)}) collective-permute-start(bf16[1,1,1,48,1536]{4,3,2,1,0:T(8,128)(2,1)S(1)} %get-tuple-element.76), channel_id=1, source_target_pairs={{0,4},{1,5},{2,6},{3,7},{4,12},{5,13},{6,14},{7,15},{8,0},{9,1},{1... | collective-permute-start | bytes 442376 | tf_op jit(solution)/shard_map/ppermute | solution.py:315
  43.2 24.8 %collective-permute-start.1 = (bf16[168,768]{1,0:T(8,128)(2,1)S(1)}, bf16[168,768]{1,0:T(8,128)(2,1)S(1)}, u32[]{:S(2)}, u32[]{:S(2)}) collective-permute-start(bf16[168,768]{1,0:T(8,128)(2,1)S(1)} %collective-permute-done), channel_id=1, source_target_pairs={{0,4},{1,5},{2,6},{3,7},{4,12},{5,13},{6,14},{7,15},{8,0},{9,1},{1... | collective-permute-start | bytes 774152 | tf_op jit(solution)/shard_map/ppermute | solution.py:315
  43.2 14.2 %collective-permute-start.7 = (bf16[1,1,1,48,1152]{4,3,2,1,0:T(8,128)(2,1)S(1)}, bf16[1,1,1,48,1152]{4,3,2,1,0:T(8,128)(2,1)S(1)}, u32[]{:S(2)}, u32[]{:S(2)}) collective-permute-start(bf16[1,1,1,48,1152]{4,3,2,1,0:T(8,128)(2,1)S(1)} %collective-permute-done.6), channel_id=1, source_target_pairs={{0,4},{1,5},{2,6},{3,7},{4,12},{5,13},{6,14},{7,15},{8,0},{9,1},{1... | collective-permute-start | bytes 331784 | tf_op jit(solution)/shard_map/ppermute | solution.py:315
  46.4 24.1 %collective-permute-start.15 = (bf16[2,1,2,32,768]{4,3,2,1,0:T(8,128)(2,1)S(1)}, bf16[2,1,2,32,768]{4,3,2,1,0:T(8,128)(2,1)S(1)}, u32[]{:S(2)}, u32[]{:S(2)}) collective-permute-start(bf16[2,1,2,32,768]{4,3,2,1,0:T(8,128)(2,1)S(1)} %collective-permute-done.14), channel_id=1, source_target_pairs={{0,4},{1,5},{2,6},{3,7},{4,12},{5,13},{6,14},{7,15},{8,0},{9,1},{1... | collective-permute-start | bytes 589832 | tf_op jit(solution)/shard_map/ppermute | solution.py:315
  49.5 15.3 %collective-permute-start.19 = (bf16[1,1,1,48,1536]{4,3,2,1,0:T(8,128)(2,1)S(1)}, bf16[1,1,1,48,1536]{4,3,2,1,0:T(8,128)(2,1)S(1)}, u32[]{:S(2)}, u32[]{:S(2)}) collective-permute-start(bf16[1,1,1,48,1536]{4,3,2,1,0:T(8,128)(2,1)S(1)} %collective-permute-done.18), channel_id=1, source_target_pairs={{0,4},{1,5},{2,6},{3,7},{4,12},{5,13},{6,14},{7,15},{8,0},{9,1},{1... | collective-permute-start | bytes 442376 | tf_op jit(solution)/shard_map/ppermute | solution.py:315
  57.4 10.5 %collective-permute-start.24 = (bf16[1,1,1,48,1536]{4,3,2,1,0:T(8,128)(2,1)S(1)}, bf16[1,1,1,48,1536]{4,3,2,1,0:T(8,128)(2,1)S(1)}, u32[]{:S(2)}, u32[]{:S(2)}) collective-permute-start(bf16[1,1,1,48,1536]{4,3,2,1,0:T(8,128)(2,1)S(1)} %collective-permute-done.23), channel_id=1, source_target_pairs={{0,4},{1,5},{2,6},{3,7},{4,12},{5,13},{6,14},{7,15},{8,0},{9,1},{1... | collective-permute-start | bytes 442376 | tf_op jit(solution)/shard_map/ppermute | solution.py:315
  57.5 12.9 %collective-permute-start.8 = (bf16[1,1,1,48,1152]{4,3,2,1,0:T(8,128)(2,1)S(1)}, bf16[1,1,1,48,1152]{4,3,2,1,0:T(8,128)(2,1)S(1)}, u32[]{:S(2)}, u32[]{:S(2)}) collective-permute-start(bf16[1,1,1,48,1152]{4,3,2,1,0:T(8,128)(2,1)S(1)} %collective-permute-done.7), channel_id=1, source_target_pairs={{0,4},{1,5},{2,6},{3,7},{4,12},{5,13},{6,14},{7,15},{8,0},{9,1},{1... | collective-permute-start | bytes 331784 | tf_op jit(solution)/shard_map/ppermute | solution.py:315
  64.8 26.7 %collective-permute-start.30 = (bf16[1,1,1,192,768]{4,3,2,1,0:T(8,128)(2,1)S(1)}, bf16[1,1,1,192,768]{4,3,2,1,0:T(8,128)(2,1)S(1)}, u32[]{:S(2)}, u32[]{:S(2)}) collective-permute-start(bf16[1,1,1,192,768]{4,3,2,1,0:T(8,128)(2,1)S(1)} %select_bitcast_fusion.1), channel_id=1, source_target_pairs={{0,4},{1,5},{2,6},{3,7},{4,12},{5,13},{6,14},{7,15},{8,0},{9,1},{1... | collective-permute-start | bytes 884744 | tf_op jit(solution)/shard_map/ppermute | solution.py:315
  68.0 11.8 %collective-permute-start.20 = (bf16[1,1,1,48,1536]{4,3,2,1,0:T(8,128)(2,1)S(1)}, bf16[1,1,1,48,1536]{4,3,2,1,0:T(8,128)(2,1)S(1)}, u32[]{:S(2)}, u32[]{:S(2)}) collective-permute-start(bf16[1,1,1,48,1536]{4,3,2,1,0:T(8,128)(2,1)S(1)} %collective-permute-done.19), channel_id=1, source_target_pairs={{0,4},{1,5},{2,6},{3,7},{4,12},{5,13},{6,14},{7,15},{8,0},{9,1},{1... | collective-permute-start | bytes 442376 | tf_op jit(solution)/shard_map/ppermute | solution.py:315
  68.0 15.0 %collective-permute-start.25 = (bf16[1,1,1,48,1536]{4,3,2,1,0:T(8,128)(2,1)S(1)}, bf16[1,1,1,48,1536]{4,3,2,1,0:T(8,128)(2,1)S(1)}, u32[]{:S(2)}, u32[]{:S(2)}) collective-permute-start(bf16[1,1,1,48,1536]{4,3,2,1,0:T(8,128)(2,1)S(1)} %collective-permute-done.24), channel_id=1, source_target_pairs={{0,4},{1,5},{2,6},{3,7},{4,12},{5,13},{6,14},{7,15},{8,0},{9,1},{1... | collective-permute-start | bytes 442376 | tf_op jit(solution)/shard_map/ppermute | solution.py:315
  70.4 21.3 %collective-permute-start.2 = (bf16[168,768]{1,0:T(8,128)(2,1)S(1)}, bf16[168,768]{1,0:T(8,128)(2,1)S(1)}, u32[]{:S(2)}, u32[]{:S(2)}) collective-permute-start(bf16[168,768]{1,0:T(8,128)(2,1)S(1)} %collective-permute-done.1), channel_id=1, source_target_pairs={{0,4},{1,5},{2,6},{3,7},{4,12},{5,13},{6,14},{7,15},{8,0},{9,1},{1... | collective-permute-start | bytes 774152 | tf_op jit(solution)/shard_map/ppermute | solution.py:315
  70.5 22.3 %collective-permute-start.9 = (bf16[1,4,1,48,1152]{4,3,2,1,0:T(8,128)(2,1)S(1)}, bf16[1,4,1,48,1152]{4,3,2,1,0:T(8,128)(2,1)S(1)}, u32[]{:S(2)}, u32[]{:S(2)}) collective-permute-start(bf16[1,4,1,48,1152]{4,3,2,1,0:T(8,128)(2,1)S(1)} %pad_maximum_fusion.9), channel_id=1, source_target_pairs={{0,2},{1,3},{2,0},{3,1},{4,6},{5,7},{6,4},{7,5},{8,10},{9,11},{10,... | collective-permute-start | bytes 1327112 | tf_op jit(solution)/shard_map/ppermute | solution.py:315
  79.8 9.1 %collective-permute-start.16 = (bf16[2,1,2,32,768]{4,3,2,1,0:T(8,128)(2,1)S(1)}, bf16[2,1,2,32,768]{4,3,2,1,0:T(8,128)(2,1)S(1)}, u32[]{:S(2)}, u32[]{:S(2)}) collective-permute-start(bf16[2,1,2,32,768]{4,3,2,1,0:T(8,128)(2,1)S(1)} %collective-permute-done.15), channel_id=1, source_target_pairs={{0,4},{1,5},{2,6},{3,7},{4,12},{5,13},{6,14},{7,15},{8,0},{9,1},{1... | collective-permute-start | bytes 589832 | tf_op jit(solution)/shard_map/ppermute | solution.py:315
  83.0 22.0 %collective-permute-start.21 = (bf16[1,4,1,48,1536]{4,3,2,1,0:T(8,128)(2,1)S(1)}, bf16[1,4,1,48,1536]{4,3,2,1,0:T(8,128)(2,1)S(1)}, u32[]{:S(2)}, u32[]{:S(2)}) collective-permute-start(bf16[1,4,1,48,1536]{4,3,2,1,0:T(8,128)(2,1)S(1)} %pad_maximum_fusion.6), channel_id=1, source_target_pairs={{0,2},{1,3},{2,0},{3,1},{4,6},{5,7},{6,4},{7,5},{8,10},{9,11},{10,... | collective-permute-start | bytes 1769480 | tf_op jit(solution)/shard_map/ppermute | solution.py:315
  88.9 15.6 %collective-permute-start.26 = (bf16[1,4,1,48,1536]{4,3,2,1,0:T(8,128)(2,1)S(1)}, bf16[1,4,1,48,1536]{4,3,2,1,0:T(8,128)(2,1)S(1)}, u32[]{:S(2)}, u32[]{:S(2)}) collective-permute-start(bf16[1,4,1,48,1536]{4,3,2,1,0:T(8,128)(2,1)S(1)} %pad_maximum_fusion.7), channel_id=1, source_target_pairs={{0,16},{1,17},{2,18},{3,19},{4,20},{5,21},{6,22},{7,23},{8,24},{9,... | collective-permute-start | bytes 1769480 | tf_op jit(solution)/shard_map/ppermute | solution.py:315
  91.5 24.7 %collective-permute-start.17 = (bf16[2,4,2,32,768]{4,3,2,1,0:T(8,128)(2,1)S(1)}, bf16[2,4,2,32,768]{4,3,2,1,0:T(8,128)(2,1)S(1)}, u32[]{:S(2)}, u32[]{:S(2)}) collective-permute-start(bf16[2,4,2,32,768]{4,3,2,1,0:T(8,128)(2,1)S(1)} %get-tuple-element.66), channel_id=1, source_target_pairs={{0,1},{1,0},{2,3},{3,2},{4,5},{5,4},{6,7},{7,6},{8,9},{9,8},{10,11... | collective-permute-start | bytes 2359304 | tf_op jit(solution)/shard_map/ppermute | solution.py:315
  91.6 10.3 %collective-permute-start.31 = (bf16[1,1,1,192,768]{4,3,2,1,0:T(8,128)(2,1)S(1)}, bf16[1,1,1,192,768]{4,3,2,1,0:T(8,128)(2,1)S(1)}, u32[]{:S(2)}, u32[]{:S(2)}) collective-permute-start(bf16[1,1,1,192,768]{4,3,2,1,0:T(8,128)(2,1)S(1)} %collective-permute-done.30), channel_id=1, source_target_pairs={{0,4},{1,5},{2,6},{3,7},{4,12},{5,13},{6,14},{7,15},{8,0},{9,1},{1... | collective-permute-start | bytes 884744 | tf_op jit(solution)/shard_map/ppermute | solution.py:315
  92.8 26.9 %collective-permute-start.3 = (bf16[4,168,768]{2,1,0:T(8,128)(2,1)}, bf16[4,168,768]{2,1,0:T(8,128)(2,1)}, u32[]{:S(2)}, u32[]{:S(2)}) collective-permute-start(bf16[4,168,768]{2,1,0:T(8,128)(2,1)} %pad_maximum_fusion.3), channel_id=1, source_target_pairs={{0,2},{1,3},{2,0},{3,1},{4,6},{5,7},{6,4},{7,5},{8,10},{9,11},{10,... | collective-permute-start | bytes 3096584 | tf_op jit(solution)/shard_map/ppermute | solution.py:315
  101.9 24.6 %collective-permute-start.10 = (bf16[1,4,2,48,1152]{4,3,2,1,0:T(8,128)(2,1)}, bf16[1,4,2,48,1152]{4,3,2,1,0:T(8,128)(2,1)}, u32[]{:S(2)}, u32[]{:S(2)}) collective-permute-start(bf16[1,4,2,48,1152]{4,3,2,1,0:T(8,128)(2,1)} %maximum_select_fusion.7), channel_id=1, source_target_pairs={{0,16},{1,17},{2,18},{3,19},{4,20},{5,21},{6,22},{7,23},{8,24},{9,... | collective-permute-start | bytes 2654216 | tf_op jit(solution)/shard_map/ppermute | solution.py:315
  104.5 8.4 %collective-permute-start.32 = (bf16[1,1,1,192,768]{4,3,2,1,0:T(8,128)(2,1)S(1)}, bf16[1,1,1,192,768]{4,3,2,1,0:T(8,128)(2,1)S(1)}, u32[]{:S(2)}, u32[]{:S(2)}) collective-permute-start(bf16[1,1,1,192,768]{4,3,2,1,0:T(8,128)(2,1)S(1)} %collective-permute-done.31), channel_id=1, source_target_pairs={{0,4},{1,5},{2,6},{3,7},{4,12},{5,13},{6,14},{7,15},{8,0},{9,1},{1... | collective-permute-start | bytes 884744 | tf_op jit(solution)/shard_map/ppermute | solution.py:315
  105.0 39.1 %collective-permute-start.27 = (bf16[2,4,1,48,1536]{4,3,2,1,0:T(8,128)(2,1)S(1)}, bf16[2,4,1,48,1536]{4,3,2,1,0:T(8,128)(2,1)}, u32[]{:S(2)}, u32[]{:S(2)}) collective-permute-start(bf16[2,4,1,48,1536]{4,3,2,1,0:T(8,128)(2,1)S(1)} %maximum_select_fusion.6), channel_id=1, source_target_pairs={{0,2},{1,3},{2,0},{3,1},{4,6},{5,7},{6,4},{7,5},{8,10},{9,11},{10,... | collective-permute-start | bytes 3538952 | tf_op jit(solution)/shard_map/ppermute | solution.py:315
  113.0 35.8 %collective-permute-start.22 = (bf16[1,4,2,48,1536]{4,3,2,1,0:T(8,128)(2,1)}, bf16[1,4,2,48,1536]{4,3,2,1,0:T(8,128)(2,1)}, u32[]{:S(2)}, u32[]{:S(2)}) collective-permute-start(bf16[1,4,2,48,1536]{4,3,2,1,0:T(8,128)(2,1)} %maximum_select_fusion.5), channel_id=1, source_target_pairs={{0,16},{1,17},{2,18},{3,19},{4,20},{5,21},{6,22},{7,23},{8,24},{9,... | collective-permute-start | bytes 3538952 | tf_op jit(solution)/shard_map/ppermute | solution.py:315
  116.3 52.7 %collective-permute-start.33 = (bf16[1,4,1,192,768]{4,3,2,1,0:T(8,128)(2,1)}, bf16[1,4,1,192,768]{4,3,2,1,0:T(8,128)(2,1)}, u32[]{:S(2)}, u32[]{:S(2)}) collective-permute-start(bf16[1,4,1,192,768]{4,3,2,1,0:T(8,128)(2,1)} %pad_maximum_fusion.2), channel_id=1, source_target_pairs={{0,2},{1,3},{2,0},{3,1},{4,6},{5,7},{6,4},{7,5},{8,10},{9,11},{10,... | collective-permute-start | bytes 3538952 | tf_op jit(solution)/shard_map/ppermute | solution.py:315
  122.0 49.8 %collective-permute-start.4 = (bf16[8,168,768]{2,1,0:T(8,128)(2,1)}, bf16[8,168,768]{2,1,0:T(8,128)(2,1)S(1)}, u32[]{:S(2)}, u32[]{:S(2)}) collective-permute-start(bf16[8,168,768]{2,1,0:T(8,128)(2,1)} %constant_dynamic-update-slice_fusion), channel_id=1, source_target_pairs={{0,1},{1,0},{2,3},{3,2},{4,5},{5,4},{6,7},{7,6},{8,9},{9,8},{10,11... | collective-permute-start | bytes 6193160 | tf_op jit(solution)/shard_map/ppermute | solution.py:315
  126.6 105.2 %collective-permute-start.35 = (bf16[160,768]{1,0:T(8,128)(2,1)}, bf16[160,768]{1,0:T(8,128)(2,1)}, u32[]{:S(2)}, u32[]{:S(2)}) collective-permute-start(bf16[160,768]{1,0:T(8,128)(2,1)} %param.21), channel_id=1, source_target_pairs={{0,1},{1,0},{2,3},{3,2},{4,5},{5,4},{6,7},{7,6},{8,9},{9,8},{10,11... | collective-permute-start | bytes 737288 | tf_op jit(solution)/shard_map/ppermute | solution.py:315
  211.8 7.4 %collective-permute-start.11 = (bf16[320,384]{1,0:T(8,128)(2,1)}, bf16[320,384]{1,0:T(8,128)(2,1)S(1)}, u32[]{:S(2)}, u32[]{:S(2)}) collective-permute-start(bf16[320,384]{1,0:T(8,128)(2,1)} %get-tuple-element.21), channel_id=1, source_target_pairs={{0,1},{1,0},{2,3},{3,2},{4,5},{5,4},{6,7},{7,6},{8,9},{9,8},{10,11... | collective-permute-start | bytes 737288 | tf_op jit(solution)/shard_map/ppermute | solution.py:315
  238.3 9.8 %collective-permute-start.36 = (f32[320,768]{1,0:T(8,128)S(1)}, f32[320,768]{1,0:T(8,128)S(1)}, u32[]{:S(2)}, u32[]{:S(2)}) collective-permute-start(f32[320,768]{1,0:T(8,128)S(1)} %convolution_add_fusion.1), channel_id=1, source_target_pairs={{0,1},{1,0},{2,3},{3,2},{4,5},{5,4},{6,7},{7,6},{8,9},{9,8},{10,11... | collective-permute-start | bytes 2949128 | tf_op jit(solution)/shard_map/ppermute | solution.py:315
  241.5 68.6 %collective-permute-start.70 = (bf16[768,768]{1,0:T(8,128)(2,1)}, bf16[768,768]{1,0:T(8,128)(2,1)}, u32[]{:S(2)}, u32[]{:S(2)}) collective-permute-start(bf16[768,768]{1,0:T(8,128)(2,1)} %convolution_convert_fusion.3), channel_id=1, source_target_pairs={{0,2},{1,3},{2,0},{3,1},{4,6},{5,7},{6,4},{7,5},{8,10},{9,11},{10,... | collective-permute-start | bytes 3538952 | tf_op jit(solution)/shard_map/ppermute | solution.py:315
  244.9 70.0 %collective-permute-start.64 = (bf16[384,1536]{1,0:T(8,128)(2,1)}, bf16[384,1536]{1,0:T(8,128)(2,1)}, u32[]{:S(2)}, u32[]{:S(2)}) collective-permute-start(bf16[384,1536]{1,0:T(8,128)(2,1)} %convolution_convert_fusion.1), channel_id=1, source_target_pairs={{0,2},{1,3},{2,0},{3,1},{4,6},{5,7},{6,4},{7,5},{8,10},{9,11},{10,... | collective-permute-start | bytes 3538952 | tf_op jit(solution)/shard_map/ppermute | solution.py:315
  247.4 73.9 %collective-permute-start.58 = (bf16[384,1536]{1,0:T(8,128)(2,1)}, bf16[384,1536]{1,0:T(8,128)(2,1)}, u32[]{:S(2)}, u32[]{:S(2)}) collective-permute-start(bf16[384,1536]{1,0:T(8,128)(2,1)} %convolution_convert_fusion.2), channel_id=1, source_target_pairs={{0,16},{1,17},{2,18},{3,19},{4,20},{5,21},{6,22},{7,23},{8,24},{9,... | collective-permute-start | bytes 3538952 | tf_op jit(solution)/shard_map/ppermute | solution.py:315
  297.6 20.4 %collective-permute-start.42 = (bf16[384,384]{1,0:T(8,128)(2,1)}, bf16[384,384]{1,0:T(8,128)(2,1)S(1)}, u32[]{:S(2)}, u32[]{:S(2)}) collective-permute-start(bf16[384,384]{1,0:T(8,128)(2,1)} %convolution_convert_fusion.4), channel_id=1, source_target_pairs={{0,16},{1,17},{2,18},{3,19},{4,20},{5,21},{6,22},{7,23},{8,24},{9,... | collective-permute-start | bytes 884744 | tf_op jit(solution)/shard_map/ppermute | solution.py:315
  301.1 26.7 %collective-permute-start.53 = (bf16[8,32,768]{2,1,0:T(8,128)(2,1)S(1)}, bf16[8,32,768]{2,1,0:T(8,128)(2,1)S(1)}, u32[]{:S(2)}, u32[]{:S(2)}) collective-permute-start(bf16[8,32,768]{2,1,0:T(8,128)(2,1)S(1)} %slice.919), channel_id=1, source_target_pairs={{0,16},{1,17},{2,18},{3,19},{4,20},{5,21},{6,22},{7,23},{8,24},{9,... | collective-permute-start | bytes 1179656 | tf_op jit(solution)/shard_map/ppermute | solution.py:315
  310.2 61.3 %collective-permute-start.47 = (bf16[384,768]{1,0:T(8,128)(2,1)S(1)}, bf16[384,768]{1,0:T(8,128)(2,1)S(1)}, u32[]{:S(2)}, u32[]{:S(2)}) collective-permute-start(bf16[384,768]{1,0:T(8,128)(2,1)S(1)} %copy-done.63), channel_id=1, source_target_pairs={{0,16},{1,17},{2,18},{3,19},{4,20},{5,21},{6,22},{7,23},{8,24},{9,... | collective-permute-start | bytes 1769480 | tf_op jit(solution)/shard_map/ppermute | solution.py:315
  314.9 99.6 %collective-permute-start.37 = (bf16[8,160,768]{2,1,0:T(8,128)(2,1)}, bf16[8,160,768]{2,1,0:T(8,128)(2,1)}, u32[]{:S(2)}, u32[]{:S(2)}) collective-permute-start(bf16[8,160,768]{2,1,0:T(8,128)(2,1)} %pad_maximum_fusion.1), channel_id=1, source_target_pairs={{0,1},{1,0},{2,3},{3,2},{4,5},{5,4},{6,7},{7,6},{8,9},{9,8},{10,11... | collective-permute-start | bytes 5898248 | tf_op jit(solution)/shard_map/ppermute | solution.py:315
  318.0 15.4 %collective-permute-start.71 = (bf16[192,768]{1,0:T(8,128)(2,1)S(1)}, bf16[192,768]{1,0:T(8,128)(2,1)S(1)}, u32[]{:S(2)}, u32[]{:S(2)}) collective-permute-start(bf16[192,768]{1,0:T(8,128)(2,1)S(1)} %slice.920), channel_id=1, source_target_pairs={{4,0},{5,1},{6,2},{7,3},{12,4},{13,5},{14,6},{15,7},{0,8},{1,9},{2... | collective-permute-start | bytes 884744 | tf_op jit(solution)/shard_map/ppermute | solution.py:315
  321.2 5.5 %collective-permute-start.43 = (bf16[192,384]{1,0:T(8,128)(2,1)S(1)}, bf16[192,384]{1,0:T(8,128)(2,1)S(1)}, u32[]{:S(2)}, u32[]{:S(2)}) collective-permute-start(bf16[192,384]{1,0:T(8,128)(2,1)S(1)} %slice.925), channel_id=1, source_target_pairs={{0,2},{1,3},{2,0},{3,1},{4,6},{5,7},{6,4},{7,5},{8,10},{9,11},{10,... | collective-permute-start | bytes 442376 | tf_op jit(solution)/shard_map/ppermute | solution.py:315
  326.8 58.9 %collective-permute-start.65 = (bf16[192,1536]{1,0:T(8,128)(2,1)}, bf16[192,1536]{1,0:T(8,128)(2,1)}, u32[]{:S(2)}, u32[]{:S(2)}) collective-permute-start(bf16[192,1536]{1,0:T(8,128)(2,1)} %slice.917), channel_id=1, source_target_pairs={{0,16},{1,17},{2,18},{3,19},{4,20},{5,21},{6,22},{7,23},{8,24},{9,... | collective-permute-start | bytes 1769480 | tf_op jit(solution)/shard_map/ppermute | solution.py:315
  331.9 55.4 %collective-permute-start.59 = (bf16[192,1536]{1,0:T(8,128)(2,1)}, bf16[192,1536]{1,0:T(8,128)(2,1)}, u32[]{:S(2)}, u32[]{:S(2)}) collective-permute-start(bf16[192,1536]{1,0:T(8,128)(2,1)} %slice.918), channel_id=1, source_target_pairs={{0,2},{1,3},{2,0},{3,1},{4,6},{5,7},{6,4},{7,5},{8,10},{9,11},{10,... | collective-permute-start | bytes 1769480 | tf_op jit(solution)/shard_map/ppermute | solution.py:315
  333.4 16.1 %collective-permute-start.54 = (bf16[4,32,768]{2,1,0:T(8,128)(2,1)S(1)}, bf16[4,32,768]{2,1,0:T(8,128)(2,1)S(1)}, u32[]{:S(2)}, u32[]{:S(2)}) collective-permute-start(bf16[4,32,768]{2,1,0:T(8,128)(2,1)S(1)} %slice.922), channel_id=1, source_target_pairs={{0,2},{1,3},{2,0},{3,1},{4,6},{5,7},{6,4},{7,5},{8,10},{9,11},{10,... | collective-permute-start | bytes 589832 | tf_op jit(solution)/shard_map/ppermute | solution.py:315
  368.0 13.0 %collective-permute-start.72 = (bf16[192,768]{1,0:T(8,128)(2,1)}, bf16[192,768]{1,0:T(8,128)(2,1)}, u32[]{:S(2)}, u32[]{:S(2)}) collective-permute-start(bf16[192,768]{1,0:T(8,128)(2,1)} %fusion.39), channel_id=1, source_target_pairs={{4,0},{5,1},{6,2},{7,3},{12,4},{13,5},{14,6},{15,7},{0,8},{1,9},{2... | collective-permute-start | bytes 884744 | tf_op jit(solution)/shard_map/ppermute | solution.py:315
  376.6 12.5 %collective-permute-start.48 = (bf16[192,768]{1,0:T(8,128)(2,1)}, bf16[192,768]{1,0:T(8,128)(2,1)}, u32[]{:S(2)}, u32[]{:S(2)}) collective-permute-start(bf16[192,768]{1,0:T(8,128)(2,1)} %slice.921), channel_id=1, source_target_pairs={{0,2},{1,3},{2,0},{3,1},{4,6},{5,7},{6,4},{7,5},{8,10},{9,11},{10,... | collective-permute-start | bytes 884744 | tf_op jit(solution)/shard_map/ppermute | solution.py:315
  382.2 25.6 %collective-permute-start.73 = (bf16[192,768]{1,0:T(8,128)(2,1)S(1)}, bf16[192,768]{1,0:T(8,128)(2,1)S(1)}, u32[]{:S(2)}, u32[]{:S(2)}) collective-permute-start(bf16[192,768]{1,0:T(8,128)(2,1)S(1)} %fusion.38), channel_id=1, source_target_pairs={{4,0},{5,1},{6,2},{7,3},{12,4},{13,5},{14,6},{15,7},{0,8},{1,9},{2... | collective-permute-start | bytes 884744 | tf_op jit(solution)/shard_map/ppermute | solution.py:315
  387.2 7.4 %collective-permute-start.66 = (bf16[48,1536]{1,0:T(8,128)(2,1)S(1)}, bf16[48,1536]{1,0:T(8,128)(2,1)S(1)}, u32[]{:S(2)}, u32[]{:S(2)}) collective-permute-start(bf16[48,1536]{1,0:T(8,128)(2,1)S(1)} %slice.923), channel_id=1, source_target_pairs={{4,0},{5,1},{6,2},{7,3},{12,4},{13,5},{14,6},{15,7},{0,8},{1,9},{2... | collective-permute-start | bytes 442376 | tf_op jit(solution)/shard_map/ppermute | solution.py:315
  388.6 13.8 %collective-permute-start.60 = (bf16[48,1536]{1,0:T(8,128)(2,1)S(1)}, bf16[48,1536]{1,0:T(8,128)(2,1)S(1)}, u32[]{:S(2)}, u32[]{:S(2)}) collective-permute-start(bf16[48,1536]{1,0:T(8,128)(2,1)S(1)} %slice.924), channel_id=1, source_target_pairs={{4,0},{5,1},{6,2},{7,3},{12,4},{13,5},{14,6},{15,7},{0,8},{1,9},{2... | collective-permute-start | bytes 442376 | tf_op jit(solution)/shard_map/ppermute | solution.py:315
  390.2 8.8 %collective-permute-start.49 = (bf16[48,768]{1,0:T(8,128)(2,1)S(1)}, bf16[48,768]{1,0:T(8,128)(2,1)S(1)}, u32[]{:S(2)}, u32[]{:S(2)}) collective-permute-start(bf16[48,768]{1,0:T(8,128)(2,1)S(1)} %slice.926), channel_id=1, source_target_pairs={{4,0},{5,1},{6,2},{7,3},{12,4},{13,5},{14,6},{15,7},{0,8},{1,9},{2... | collective-permute-start | bytes 221192 | tf_op jit(solution)/shard_map/ppermute | solution.py:315
  394.6 14.5 %collective-permute-start.67 = (bf16[48,1536]{1,0:T(8,128)(2,1)S(1)}, bf16[48,1536]{1,0:T(8,128)(2,1)S(1)}, u32[]{:S(2)}, u32[]{:S(2)}) collective-permute-start(bf16[48,1536]{1,0:T(8,128)(2,1)S(1)} %fusion.67), channel_id=1, source_target_pairs={{4,0},{5,1},{6,2},{7,3},{12,4},{13,5},{14,6},{15,7},{0,8},{1,9},{2... | collective-permute-start | bytes 442376 | tf_op jit(solution)/shard_map/ppermute | solution.py:315
  402.5 6.8 %collective-permute-start.61 = (bf16[48,1536]{1,0:T(8,128)(2,1)S(1)}, bf16[48,1536]{1,0:T(8,128)(2,1)S(1)}, u32[]{:S(2)}, u32[]{:S(2)}) collective-permute-start(bf16[48,1536]{1,0:T(8,128)(2,1)S(1)} %fusion.69), channel_id=1, source_target_pairs={{4,0},{5,1},{6,2},{7,3},{12,4},{13,5},{14,6},{15,7},{0,8},{1,9},{2... | collective-permute-start | bytes 442376 | tf_op jit(solution)/shard_map/ppermute | solution.py:315
  407.8 9.6 %collective-permute-start.74 = (bf16[192,768]{1,0:T(8,128)(2,1)S(1)}, bf16[192,768]{1,0:T(8,128)(2,1)S(1)}, u32[]{:S(2)}, u32[]{:S(2)}) collective-permute-start(bf16[192,768]{1,0:T(8,128)(2,1)S(1)} %fusion.65), channel_id=1, source_target_pairs={{1,17},{3,19},{5,21},{7,23},{9,25},{11,27},{13,29},{15,31},{16,0},... | collective-permute-start | bytes 884744 | tf_op jit(solution)/shard_map/ppermute | solution.py:315
  409.3 7.6 %collective-permute-start.62 = (bf16[48,1536]{1,0:T(8,128)(2,1)S(1)}, bf16[48,1536]{1,0:T(8,128)(2,1)S(1)}, u32[]{:S(2)}, u32[]{:S(2)}) collective-permute-start(bf16[48,1536]{1,0:T(8,128)(2,1)S(1)} %fusion.68), channel_id=1, source_target_pairs={{4,0},{5,1},{6,2},{7,3},{12,4},{13,5},{14,6},{15,7},{0,8},{1,9},{2... | collective-permute-start | bytes 442376 | tf_op jit(solution)/shard_map/ppermute | solution.py:315
  414.4 27.7 %collective-permute-start.69 = (f32[24,1536]{1,0:T(8,128)S(1)}, f32[24,1536]{1,0:T(8,128)S(1)}, u32[]{:S(2)}, u32[]{:S(2)}) collective-permute-start(f32[24,1536]{1,0:T(8,128)S(1)} %get-tuple-element.78), channel_id=1, source_target_pairs={{0,1},{1,0},{2,3},{3,2},{4,5},{5,4},{6,7},{7,6},{8,9},{9,8},{10,11... | collective-permute-start | bytes 442376 | tf_op jit(solution)/shard_map/ppermute | solution.py:315
  416.7 24.2 %collective-permute-start.38 = (bf16[4,160,768]{2,1,0:T(8,128)(2,1)S(1)}, bf16[4,160,768]{2,1,0:T(8,128)(2,1)S(1)}, u32[]{:S(2)}, u32[]{:S(2)}) collective-permute-start(bf16[4,160,768]{2,1,0:T(8,128)(2,1)S(1)} %slice.916), channel_id=1, source_target_pairs={{0,2},{1,3},{2,0},{3,1},{4,6},{5,7},{6,4},{7,5},{8,10},{9,11},{10,... | collective-permute-start | bytes 2949128 | tf_op jit(solution)/shard_map/ppermute | solution.py:315
  417.0 33.7 %collective-permute-start.63 = (f32[24,1536]{1,0:T(8,128)S(1)}, f32[24,1536]{1,0:T(8,128)S(1)}, u32[]{:S(2)}, u32[]{:S(2)}) collective-permute-start(f32[24,1536]{1,0:T(8,128)S(1)} %get-tuple-element.80), channel_id=1, source_target_pairs={{0,1},{1,0},{2,3},{3,2},{4,5},{5,4},{6,7},{7,6},{8,9},{9,8},{10,11... | collective-permute-start | bytes 442376 | tf_op jit(solution)/shard_map/ppermute | solution.py:315
  417.5 40.7 %collective-permute-start.75 = (f32[96,768]{1,0:T(8,128)S(1)}, f32[96,768]{1,0:T(8,128)S(1)}, u32[]{:S(2)}, u32[]{:S(2)}) collective-permute-start(f32[96,768]{1,0:T(8,128)S(1)} %slice_select_fusion.1), channel_id=1, source_target_pairs={{0,1},{2,3},{4,5},{6,7},{8,9},{10,11},{12,13},{14,15},{17,16},{19,... | collective-permute-start | bytes 884744 | tf_op jit(solution)/shard_map/ppermute | solution.py:315
  441.1 7.6 %collective-permute-start.39 = (bf16[160,768]{1,0:T(8,128)(2,1)S(1)}, bf16[160,768]{1,0:T(8,128)(2,1)S(1)}, u32[]{:S(2)}, u32[]{:S(2)}) collective-permute-start(bf16[160,768]{1,0:T(8,128)(2,1)S(1)} %fusion.78), channel_id=1, source_target_pairs={{4,0},{5,1},{6,2},{7,3},{12,4},{13,5},{14,6},{15,7},{0,8},{1,9},{2... | collective-permute-start | bytes 737288 | tf_op jit(solution)/shard_map/ppermute | solution.py:315
  448.8 6.7 %collective-permute-start.40 = (bf16[160,768]{1,0:T(8,128)(2,1)S(1)}, bf16[160,768]{1,0:T(8,128)(2,1)S(1)}, u32[]{:S(2)}, u32[]{:S(2)}) collective-permute-start(bf16[160,768]{1,0:T(8,128)(2,1)S(1)} %fusion.59), channel_id=1, source_target_pairs={{4,0},{5,1},{6,2},{7,3},{12,4},{13,5},{14,6},{15,7},{0,8},{1,9},{2... | collective-permute-start | bytes 737288 | tf_op jit(solution)/shard_map/ppermute | solution.py:315
  455.5 6.4 %collective-permute-start.41 = (bf16[160,768]{1,0:T(8,128)(2,1)S(1)}, bf16[160,768]{1,0:T(8,128)(2,1)S(1)}, u32[]{:S(2)}, u32[]{:S(2)}) collective-permute-start(bf16[160,768]{1,0:T(8,128)(2,1)S(1)} %fusion.57), channel_id=1, source_target_pairs={{4,0},{5,1},{6,2},{7,3},{12,4},{13,5},{14,6},{15,7},{0,8},{1,9},{2... | collective-permute-start | bytes 737288 | tf_op jit(solution)/shard_map/ppermute | solution.py:315
  (82 other events, 553.5 us)

commit v2 on v1

v2 whole, which is shorter than its diff:
```python
import functools

import jax
import jax.numpy as jnp
import numpy as np
from jax import lax
from jax.experimental import pallas as pl
from jax.experimental.pallas import tpu as pltpu
from jax.sharding import PartitionSpec as P

HEADS = 12
EPS = 1e-05
BASE = 10000.0
AXES = ("dp", "seq")
BF = jnp.bfloat16
F32 = jnp.float32
FAR = -1e30
ONES = 64


ORDERS = {"X": "hx", "Q": "Zyx", "U": "hyx", "G": "xzy", "D": "xz", "d": "xZ", "g": "yzx", "u": "yxz", "q": "yxh", "r": "xyZ", "x": "h"}
STREAMS = "XPQUGDCdguqx"
SEQUENCE = [
    1, 2, 81, 17, 82, 18, 83, -82, 49, 33, -2, 11, 34, -33, -83, 65, 97, -97,
    84, 43, 4, -84, 58, 66, 85, -34, -35, -50, 51, 36, -4, -36, 37, 67, 5, -5,
    -51, 52, -67, 86, 76, 200, -37, 201, 69, 202, 203, -86, 95, -203, -68, -203, -52, -203,
    53, 204, -69, 205, -53, -87, 206, 207, -207, 208, -207, 209, -207, 210, 212, 213, 145, 211,
    129, 113, 214, -113, -145, 114, 115, 146, 177, 178, -177, 124, -114, -115, 147, 161, -146, -116,
    -129, 130, 148, -147, -130, 131, -178, 157, -161, 162, 179, -162, -131, -149, 163, 140, 117, 172,
    -179, 188, -132, -163, 133, -164, -133, 150, 134, 165, -117, -134, 118, -150, -118, -165, -148,
]


def dot(a, b):
    return jnp.dot(a, b, preferred_element_type=F32)


def dot_t(a, b):
    return lax.dot_general(a, b, (((1,), (1,)), ((), ())), preferred_element_type=F32)


def t_dot(a, b):
    return lax.dot_general(a, b, (((0,), (0,)), ((), ())), preferred_element_type=F32)


def lanes(shape):
    return lax.broadcasted_iota(jnp.int32, shape, len(shape) - 1)


def swap_halves(u):
    width = u.shape[-1]
    low = lanes(u.shape) % 64 < 32
    return jnp.where(low, pltpu.roll(u, width - 32, 1), pltpu.roll(u, 32, 1))


def split3(v):
    hi = v.astype(BF).astype(F32)
    rest = v - hi
    mid = rest.astype(BF).astype(F32)
    return hi, mid, rest - mid


def with_units(base, v):
    at = lanes(base.shape)
    hi, mid, low = split3(v)
    return jnp.where(
        at == ONES,
        -hi,
        jnp.where(at == ONES + 1, -mid, jnp.where(at == ONES + 2, -low, base)),
    )


def fill(target, pieces, places, per):
    n = 0
    for piece in pieces:
        for i in range(piece.shape[0]):
            target[pl.ds(pl.multiple_of(places[n] * per, 16), per), :] = piece[i]
            n += 1


def whole(shape):
    return pl.BlockSpec(shape, lambda *_: (0,) * len(shape))


def scalars():
    return pl.BlockSpec(memory_space=pltpu.SMEM)


def params(mib):
    return pltpu.CompilerParams(vmem_limit_bytes=mib << 20)


def like(*shape, dtype=F32):
    return jax.ShapeDtypeStruct(shape, dtype)


def far(*shape, dtype=F32):
    return pltpu.HBM(shape, dtype)


def kept_far(*arrays):
    return [pltpu.with_memory_space_constraint(a, pltpu.HBM) for a in arrays]


def message_kernel(x_ref, ids_ref, mask_ref, out_ref):
    local, width = x_ref.shape
    out_ref[:local] = x_ref[...]
    out_ref[local:] = jnp.zeros((8, width), BF)
    out_ref[local : local + 1, :local] = ids_ref[...].astype(F32).astype(BF)
    out_ref[local + 1 : local + 2, :local] = mask_ref[...].astype(F32).astype(BF)


def make_message(tokens, ids, mask):
    local, width = tokens.shape
    return pl.pallas_call(
        message_kernel,
        out_shape=like(local + 8, width, dtype=BF),
        compiler_params=params(8),
        cost_estimate=pl.CostEstimate(flops=1, bytes_accessed=1, transcendentals=0),
        name="message",
    )(tokens, ids.reshape(1, local), mask.reshape(1, local))


def columns_kernel(me_ref, qkv_ref, up_ref, out_w_ref, gate_ref, gain_ref, bias_ref, mine_ref, theirs_ref):
    c = me_ref[3]
    rows = qkv_ref.shape[1]

    def halves(ref, start, size, to):
        for target, which in ((mine_ref, c), (theirs_ref, 1 - c)):
            at = pl.ds(pl.multiple_of(start + which * size, 128), size)
            target[:, to : to + size] = ref[0, :, at].astype(BF)

    for j in range(3):
        halves(qkv_ref, j * 768, 384, j * 384)
    ff = up_ref.shape[2] // 2
    to = 1152
    halves(up_ref, 0, ff, to)
    halves(out_w_ref, 0, 384, to + ff)
    halves(gate_ref, 0, ff, to + ff + 512)
    for target in (mine_ref, theirs_ref):
        ext = slice(to + ff + 384, to + ff + 512)
        target[:, ext] = jnp.zeros((rows, 128), BF)
        target[0:2, to + ff + 384 : to + ff + 384 + rows] = gain_ref[0].astype(BF)
        target[2:4, to + ff + 384 : to + ff + 384 + rows] = bias_ref[0].astype(BF)


def make_columns(me, qkv, up, out_w, gate, gain, bias):
    rows = qkv.shape[1]
    shape = like(rows, 1152 + up.shape[2] + 512, dtype=BF)
    args = [qkv, up, out_w, gate, gain, bias]
    return pl.pallas_call(
        columns_kernel,
        grid=(1,),
        in_specs=[scalars()] + [whole(a.shape) for a in args],
        out_specs=[whole(shape.shape)] * 2,
        out_shape=[shape] * 2,
        compiler_params=params(12),
        cost_estimate=pl.CostEstimate(flops=1, bytes_accessed=1, transcendentals=0),
        name="columns",
    )(me, *args)


def angle_table(count, stride):
    angle = np.arange(count)[:, None] * float(stride) * BASE ** (-2.0 * (np.arange(128) % 32) / 64)[None, :]
    rest = np.concatenate([np.cos(angle), np.sin(angle)], axis=1)
    parts = []
    for _ in range(3):
        part = rest.astype(jnp.bfloat16)
        parts.append(part)
        rest = rest - part.astype(np.float64)
    return np.concatenate(parts, axis=0)


def rank_kernel(
    me_ref, along_ref, beside_ref, note_a_ref, note_b_ref, fine_ref, coarse_ref,
    t_ref, cos_ref, sin_ref, ext_ref, keep_ref, ext_s, count_s, before_s, *, numbers, coarse,
):
    local = cos_ref.shape[0] // 4
    chips = note_a_ref.shape[0]
    step = pl.program_id(0)
    lane = lanes((local, 128))

    @pl.when(step == 0)
    def _():
        def one(i, _):
            for h, ref in enumerate((note_a_ref, note_b_ref)):
                note = ref[i].astype(F32)[:, :256].T
                own = jnp.where(note[:local, 0:1] == lane.astype(F32), 1.0, 0.0)
                ext = jnp.where(lane < 64, own, jnp.where(lane < ONES + 3, 1.0, 0.0))
                ext_s[2 * i + h] = ext.astype(BF)
                count_s[pl.ds(2 * i + h, 1), :] = jnp.sum(own, axis=0, keepdims=True)
            return 0

        lax.fori_loop(0, chips, one, 0)
        for h, ref in enumerate((note_a_ref, note_b_ref)):
            note = ref[0].astype(F32)[:, :256].T
            keep_ref[h * local : (h + 1) * local] = jnp.broadcast_to(note[:local, 1:2], (local, 128))
        blocks = 2 * chips
        mine = numbers(lax.broadcasted_iota(jnp.int32, (blocks, blocks), 0), me_ref)
        other = numbers(lax.broadcasted_iota(jnp.int32, (blocks, blocks), 1), me_ref)
        before_s[...] = dot(jnp.where(other < mine, 1.0, 0.0).astype(BF), count_s[...].astype(BF))

    x = jnp.concatenate([r[i, :local] for i in range(2) for r in (along_ref, beside_ref)], axis=0)
    t_ref[...] = x.T
    up = lax.broadcasted_iota(jnp.int32, (local, local), 0) > lax.broadcasted_iota(jnp.int32, (local, local), 1)
    up = jnp.where(up, 1.0, 0.0).astype(BF)
    for b in range(4):
        block = 4 * step + b
        ext = ext_s[block]
        rank = dot(up, ext) + before_s[pl.ds(block, 1), :]
        position = jnp.sum(jnp.where(lane < 64, ext.astype(F32) * rank, 0.0), axis=1, keepdims=True)
        high = jnp.floor(position * (1.0 / 64))

        def pick(value, size, table_ref):
            at = lanes((local, 3 * size)) & (size - 1)
            chosen = jnp.where(at.astype(F32) == value, 1.0, 0.0).astype(BF)
            return dot(chosen, table_ref[...])

        low = pick(position - 64 * high, 64, fine_ref)
        high = pick(high, coarse, coarse_ref)
        cos = low[:, :128] * high[:, :128] - low[:, 128:] * high[:, 128:]
        sin = low[:, 128:] * high[:, :128] + low[:, :128] * high[:, 128:]
        rows = slice(b * local, (b + 1) * local)
        cos_ref[rows] = cos
        sin_ref[rows] = jnp.where(lane % 64 < 32, -sin, sin)
        ext_ref[rows] = ext


def rank(me, numbers, along, beside):
    chips, padded, width = along.shape
    local = padded - 8
    count = chips * 2 * local
    step = 4 * local
    coarse = max(64, 1 << (-(-count // 64) - 1).bit_length())
    note = pl.BlockSpec((chips, 8, width), lambda i: (0, local // 8, 0))
    rows = pl.BlockSpec((step, 128), lambda i: (i, 0))
    return pl.pallas_call(
        functools.partial(rank_kernel, numbers=numbers, coarse=coarse),
        grid=(chips // 2,),
        in_specs=[scalars()]
        + [pl.BlockSpec((2, padded, width), lambda i: (i, 0, 0))] * 2
        + [note, note, whole((192, 256)), whole((3 * coarse, 256))],
        out_specs=[pl.BlockSpec((width, step), lambda i: (0, i)), rows, rows, rows, whole((2 * local, 128))],
        out_shape=[
            far(width, count, dtype=BF), far(count, 128), far(count, 128), far(count, 128, dtype=BF),
            like(2 * local, 128),
        ],
        scratch_shapes=[
            pltpu.VMEM((2 * chips, local, 128), BF),
            pltpu.VMEM((2 * chips, 128), F32),
            pltpu.VMEM((2 * chips, 128), F32),
        ],
        compiler_params=params(16),
        cost_estimate=pl.CostEstimate(flops=1, bytes_accessed=1, transcendentals=0),
        name="rank",
    )(
        me, along, beside, along, beside,
        jnp.asarray(angle_table(64, 1)), jnp.asarray(angle_table(coarse, 64)),
    )


def project_kernel(me_ref, *refs, places, per, n):
    pieces = refs[:n]
    along_ref, beside_ref, cos_ref, sin_ref, q_ref, k_ref, v_ref, w_ref = refs[n:]
    local = cos_ref.shape[0] // 4
    first = pl.program_id(0) == 0

    @pl.when(first)
    def _():
        fill(w_ref, pieces, places(me_ref), per)

    x = jnp.concatenate([r[i, :local] for i in range(2) for r in (along_ref, beside_ref)], axis=0)
    cos, sin = cos_ref[...], sin_ref[...]
    kv = dot(x, w_ref[:, 384:])
    for p in range(3):
        at = slice(p * 128, p * 128 + 128)
        u = kv[:, at]
        k_ref[p] = (u * cos + swap_halves(u) * sin).astype(BF)
        v_ref[p] = kv[:, 384 + p * 128 : 512 + p * 128].astype(BF)

    @pl.when(first)
    def _():
        q = dot(x[: 2 * local], w_ref[:, :384])
        for p in range(3):
            at = slice(p * 128, p * 128 + 128)
            u = q[:, at]
            r = (u * cos[: 2 * local] + swap_halves(u) * sin[: 2 * local]).astype(BF)
            q_ref[:, at] = r * jnp.asarray(0.125, BF)


def project(me, pieces, places, per, along, beside, cos, sin):
    chips, padded, width = along.shape
    count = cos.shape[0]
    step = 2 * (count // chips)
    rows = pl.BlockSpec((step, 128), lambda i: (i, 0))
    heads = pl.BlockSpec((3, step, 128), lambda i: (0, i, 0))
    return pl.pallas_call(
        functools.partial(project_kernel, places=places, per=per, n=len(pieces)),
        grid=(chips // 2,),
        in_specs=[scalars()]
        + [whole(p.shape) for p in pieces]
        + [pl.BlockSpec((2, padded, width), lambda i: (i, 0, 0))] * 2
        + [rows] * 2,
        out_specs=[whole((step // 2, 384)), heads, heads, whole((width, 1152))],
        out_shape=[
            far(step // 2, 384, dtype=BF), far(3, count, 128, dtype=BF), far(3, count, 128, dtype=BF),
            far(width, 1152, dtype=BF),
        ],
        compiler_params=params(24),
        cost_estimate=pl.CostEstimate(flops=1, bytes_accessed=1, transcendentals=0),
        name="project",
    )(me, *pieces, along, beside, *kept_far(cos, sin))


def attend_kernel(q_ref, k_ref, v_ref, ext_ref, att_ref, ob_ref, lse_ref, *, chunk):
    keys = k_ref.shape[1]
    q = q_ref[...]
    own = q.shape[0]
    first = lanes(q.shape) < 64
    ext = ext_ref[:own].astype(F32)
    ext = jnp.where(lanes(ext.shape) < 64, (1.0 - ext) * FAR, 0.0).astype(BF)
    parts = []
    for h in range(2):
        qh = jnp.where(first if h == 0 else ~first, q, jnp.zeros_like(q))
        qc = jnp.concatenate([qh, ext], axis=1)
        top = jnp.full((own, 1), FAR, F32)
        acc = jnp.zeros((own, 256), F32)
        for j in range(0, keys, chunk):
            rows = slice(j, j + chunk)
            s = dot_t(qc, jnp.concatenate([k_ref[0, rows], ext_ref[rows]], axis=1))
            above = jnp.maximum(top, jnp.max(s, axis=1, keepdims=True))
            e = jnp.exp(s - above).astype(BF)
            acc = acc * jnp.exp(top - above) + dot(e, jnp.concatenate([v_ref[0, rows], ext_ref[rows]], axis=1))
            top = above
        total = acc[:, 128 + ONES : 129 + ONES]
        parts.append(acc[:, :128] / total)
        lse_ref[h] = with_units(ext.astype(F32), top + jnp.log(total)).astype(BF)
    att = jnp.where(first, parts[0], parts[1])
    att_ref[...] = att
    ob_ref[...] = att.astype(BF)


def attend(q, k, v, ext):
    own = q.shape[0]
    keys = k.shape[1]
    return pl.pallas_call(
        functools.partial(attend_kernel, chunk=512),
        grid=(3,),
        in_specs=[
            pl.BlockSpec((own, 128), lambda p: (0, p)),
            pl.BlockSpec((1, keys, 128), lambda p: (p, 0, 0)),
            pl.BlockSpec((1, keys, 128), lambda p: (p, 0, 0)),
            whole(ext.shape),
        ],
        out_specs=[
            pl.BlockSpec((own, 128), lambda p: (0, p)),
            pl.BlockSpec((own, 128), lambda p: (0, p)),
            pl.BlockSpec((2, own, 128), lambda p: (p, 0, 0)),
        ],
        out_shape=[
            far(own, 384),
            like(own, 384, dtype=BF),
            far(6, own, 128, dtype=BF),
        ],
        compiler_params=params(20 if keys <= 4096 else 60),
        cost_estimate=pl.CostEstimate(
            flops=4 * 6 * own * keys * 256,
            bytes_accessed=3 * keys * 1024,
            transcendentals=6 * own * keys,
        ),
        name="attend",
    )(*kept_far(q, k, v, ext))


def normalize(values):
    average = jnp.mean(values, axis=-1, keepdims=True)
    centred = values - average
    factor = lax.rsqrt(jnp.mean(centred * centred, axis=-1, keepdims=True) + EPS)
    return centred * factor, factor


def norm_back(gradient, normed, factor):
    return factor * (
        gradient
        - jnp.mean(gradient, axis=-1, keepdims=True)
        - normed * jnp.mean(gradient * normed, axis=-1, keepdims=True)
    )


def turned(a):
    half = a.shape[0] // 2
    return jnp.concatenate([a[half:], a[:half]], axis=0)


def silu_parts(gate):
    sigmoid = 1.0 / (1.0 + jnp.exp(-gate))
    return sigmoid, gate * sigmoid


def mid_kernel(me_ref, *refs, places, per, n, share_rows):
    pieces = refs[:n]
    ob_ref, got_ref, sib_ref, along_ref, beside_ref = refs[n : n + 5]
    n1_ref, f1_ref, h1_ref, up_ref, all_ref, out_ref, up_w_ref, norm_ref = refs[n + 5 :]
    local = along_ref.shape[1] - 8
    c = me_ref[3]
    ff = up_ref.shape[1]
    at = places(me_ref)
    done = 0
    norm = jnp.zeros(norm_ref.shape, F32)
    width = norm.shape[1]
    for piece in pieces:
        for i in range(piece.shape[0]):
            rows = pl.ds(pl.multiple_of(at[done] * per, 16), per)
            for d in range(per // share_rows):
                ext = piece[i, d * share_rows : d * share_rows + 4, ff + 384 : ff + 512].astype(F32)
                ext = jnp.concatenate([ext, jnp.zeros((4, width - 128), F32)], axis=1)
                ext = jnp.concatenate([ext, jnp.zeros((4, width), F32)], axis=0)
                norm = norm + pltpu.roll(ext, (at[done] * (per // share_rows) + d) * share_rows, 1)
            up_w_ref[rows, :] = piece[i, :, :ff]
            out_ref[c, rows, :] = piece[i, :, ff : ff + 384]
            out_ref[1 - c, rows, :] = sib_ref[done]
            done += 1
    norm_ref[...] = norm
    all_ref[c] = ob_ref[...]
    all_ref[1 - c] = turned(got_ref[...])
    halves = [dot(all_ref[0], out_ref[i, :384]) + dot(all_ref[1], out_ref[i, 384:]) for i in range(2)]
    n1, f1 = normalize(
        jnp.concatenate([along_ref[0, :local], beside_ref[0, :local]], axis=0).astype(F32)
        + jnp.concatenate(halves, axis=1)
    )
    low = (n1 * norm_ref[0:1] + norm_ref[2:3]).astype(BF)
    n1_ref[...] = n1
    f1_ref[...] = jnp.broadcast_to(f1, f1_ref.shape)
    h1_ref[...] = low
    up_ref[...] = dot(low, up_w_ref[...])


def mid(me, pieces, places, per, ob, got, sib, along, beside, ff, share_rows):
    own, width = ob.shape[0], along.shape[2]
    small = [ob, got, sib, along, beside]
    one = pl.BlockSpec((1, *along.shape[1:]), lambda *_: (0, 0, 0))
    return pl.pallas_call(
        functools.partial(mid_kernel, places=places, per=per, n=len(pieces), share_rows=share_rows),
        in_specs=[scalars()]
        + [whole(a.shape) for a in pieces + small[:3]]
        + [one, one],
        out_specs=[
            whole((own, width)), whole((own, 128)), whole((own, width)), whole((own, ff)),
            whole((2, own, 384)), whole((2, width, 384)), whole((width, ff)), whole((8, width)),
        ],
        out_shape=[
            like(own, width), like(own, 128), like(own, width, dtype=BF), like(own, ff),
            like(2, own, 384, dtype=BF), like(2, width, 384, dtype=BF), like(width, ff, dtype=BF), like(8, width),
        ],
        grid=(1,),
        compiler_params=params(22),
        cost_estimate=pl.CostEstimate(flops=2 * own * width * 2304, bytes_accessed=12 << 20, transcendentals=0),
        name="mid",
    )(me, *pieces, *small)


def gate_kernel(me_ref, *refs, places, per, n):
    pieces = refs[:n]
    h1_ref, up_ref, gate_ref, hidden_ref, w_ref = refs[n:]
    fill(w_ref, pieces, places(me_ref), per)
    gate = dot(h1_ref[...], w_ref[...])
    gate_ref[...] = gate
    hidden_ref[...] = (silu_parts(gate)[1] * up_ref[...]).astype(BF)


def gate_up(me, pieces, places, per, h1, up):
    own, ff = up.shape
    width = h1.shape[1]
    return pl.pallas_call(
        functools.partial(gate_kernel, places=places, per=per, n=len(pieces)),
        grid=(1,),
        in_specs=[scalars()] + [whole(a.shape) for a in [*pieces, h1, up]],
        out_specs=[whole((own, ff)), whole((own, ff)), whole((width, ff))],
        out_shape=[like(own, ff), like(own, ff, dtype=BF), like(width, ff, dtype=BF)],
        compiler_params=params(20),
        cost_estimate=pl.CostEstimate(flops=2 * own * width * ff, bytes_accessed=10 << 20, transcendentals=own * ff),
        name="gate_up",
    )(me, *pieces, h1, up)


def down_kernel(me_ref, *refs, places, per, n):
    pieces = refs[:n]
    hidden_ref, part_ref, w_ref = refs[n:]
    fill(w_ref, pieces, places(me_ref), per)
    part_ref[...] = dot(hidden_ref[...], w_ref[...])


def down(me, pieces, places, per, hidden):
    own, ff = hidden.shape
    width = pieces[0].shape[2]
    return pl.pallas_call(
        functools.partial(down_kernel, places=places, per=per, n=len(pieces)),
        grid=(1,),
        in_specs=[scalars()] + [whole(a.shape) for a in [*pieces, hidden]],
        out_specs=[whole((own, width)), whole((ff, width))],
        out_shape=[like(own, width), like(ff, width, dtype=BF)],
        compiler_params=params(14),
        cost_estimate=pl.CostEstimate(flops=2 * own * width * ff, bytes_accessed=8 << 20, transcendentals=0),
        name="down",
    )(me, *pieces, hidden)


def turn_kernel(
    part_ref, got_ref, n1_ref, norm_ref, cot_ref, cot_got_ref, keep_ref, gate_ref, up_ref, gate_w_ref, up_w_ref, down_w_ref,
    out_ref, dr2_ref, dm_ref, dgate_ref, dup_ref, back_ref, sums_ref,
):
    local = out_ref.shape[0]
    h1 = n1_ref[...] * norm_ref[0:1] + norm_ref[2:3]
    n2, f2 = normalize(h1 + part_ref[...] + turned(got_ref[...]))
    keep = keep_ref[:, :1]
    gain = norm_ref[1:2]
    out_ref[...] = ((n2[:local] * gain + norm_ref[3:4]) * keep[:local]).astype(BF)
    masked = jnp.concatenate([cot_ref[...], cot_got_ref[...]], axis=0).astype(F32) * keep
    sums_ref[0:1] = jnp.sum(masked * n2, axis=0, keepdims=True)
    sums_ref[1:2] = jnp.sum(masked, axis=0, keepdims=True)
    sums_ref[2:] = jnp.zeros((6, sums_ref.shape[1]), F32)
    dr2 = norm_back(masked * gain, n2, f2)
    dr2_ref[...] = dr2
    dm = dr2.astype(BF)
    dm_ref[...] = dm
    ff = gate_ref.shape[1]
    step = 512
    back = jnp.zeros(dr2.shape, F32)
    for j in range(0, ff, step):
        at = slice(j, j + step)
        dh = dot_t(dm, down_w_ref[at, :])
        gate = gate_ref[:, at]
        sigmoid, silu = silu_parts(gate)
        dgate = (dh * up_ref[:, at] * sigmoid * (1.0 + gate * (1.0 - sigmoid))).astype(BF)
        dup = (dh * silu).astype(BF)
        dgate_ref[:, at] = dgate
        dup_ref[:, at] = dup
        back = back + dot_t(dgate, gate_w_ref[:, at]) + dot_t(dup, up_w_ref[:, at])
    back_ref[...] = back


def turn(part, got, n1, norm, cot, cot_got, keep, gate, up, gate_w, up_w, down_w):
    own, width = part.shape
    ff = gate.shape[1]
    args = [part, got, n1, norm, cot, cot_got, keep, gate, up, gate_w, up_w, down_w]
    return pl.pallas_call(
        turn_kernel,
        grid=(1,),
        in_specs=[whole(a.shape) for a in args],
        out_specs=[
            whole((own // 2, width)), whole((own, width)), whole((own, width)), whole((own, ff)),
            whole((own, ff)), whole((own, width)), whole((8, width)),
        ],
        out_shape=[
            like(own // 2, width, dtype=BF), like(own, width), like(own, width, dtype=BF),
            like(own, ff, dtype=BF), like(own, ff, dtype=BF), like(own, width), like(8, width),
        ],
        compiler_params=params(34),
        cost_estimate=pl.CostEstimate(flops=6 * own * width * ff, bytes_accessed=20 << 20, transcendentals=own * ff),
        name="turn",
    )(*args)


def back_kernel(me_ref, dr2_ref, part_ref, got_ref, n1_ref, f1_ref, norm_ref, w_ref, dr1_ref, da_ref, dob_ref, sums_ref):
    dh1 = dr2_ref[...] + part_ref[...] + turned(got_ref[...])
    n1 = n1_ref[...]
    sums_ref[0:1] = jnp.sum(dh1 * n1, axis=0, keepdims=True)
    sums_ref[1:2] = jnp.sum(dh1, axis=0, keepdims=True)
    sums_ref[2:] = jnp.zeros((6, n1.shape[1]), F32)
    dr1 = norm_back(dh1 * norm_ref[0:1], n1, f1_ref[:, :1])
    dr1_ref[...] = dr1[: dr1_ref.shape[0]]
    da = dr1.astype(BF)
    da_ref[...] = da
    rows = pl.ds(pl.multiple_of(me_ref[3] * 384, 128), 384)
    dob_ref[...] = (dot_t(da[:, :384], w_ref[0, rows, :]) + dot_t(da[:, 384:], w_ref[1, rows, :])).astype(BF)


def back(me, dr2, part, got, n1, f1, norm, out_w):
    own, width = dr2.shape
    args = [dr2, part, got, n1, f1, norm, out_w]
    return pl.pallas_call(
        back_kernel,
        grid=(1,),
        in_specs=[scalars()] + [whole(a.shape) for a in args],
        out_specs=[whole((own // 2, width)), whole((own, width)), whole((own, 384)), whole((8, width))],
        out_shape=[like(own // 2, width), like(own, width, dtype=BF), like(own, 384, dtype=BF), like(8, width)],
        compiler_params=params(14),
        cost_estimate=pl.CostEstimate(flops=2 * own * width * 384, bytes_accessed=7 << 20, transcendentals=0),
        name="back",
    )(me, *args)


def share(whole_ref, at, per, mine_ref, theirs_ref):
    half = mine_ref.shape[0]
    for i in range(2 * half):
        block = whole_ref[pl.ds(pl.multiple_of(at[i] * per, 16), per), :]
        if i < half:
            mine_ref[i, :, : block.shape[1]] = block
        else:
            theirs_ref[i - half, :, : block.shape[1]] = block.astype(BF)


def grad_kernel(me_ref, left_ref, right_ref, mine_ref, theirs_ref, acc_ref, *, places, per):
    acc_ref[...] = t_dot(left_ref[...], right_ref[...])
    share(acc_ref, places(me_ref), per, mine_ref, theirs_ref)


def grad(me, places, per, left, right):
    own, rows = left.shape
    cols = right.shape[1]
    half = rows // per // 2
    step = 768 if cols % 768 == 0 else cols
    return pl.pallas_call(
        functools.partial(grad_kernel, places=places, per=per),
        grid=(cols // step,),
        in_specs=[scalars(), whole(left.shape), pl.BlockSpec((own, step), lambda j: (0, j))],
        out_specs=[pl.BlockSpec((half, per, step), lambda j: (0, 0, j))] * 2,
        out_shape=[like(half, per, cols), like(half, per, cols, dtype=BF)],
        scratch_shapes=[pltpu.VMEM((rows, step), F32)],
        compiler_params=params(18),
        cost_estimate=pl.CostEstimate(flops=2 * own * rows * cols, bytes_accessed=6 * rows * cols, transcendentals=0),
        name="grad",
    )(me, left, right)


def grad_up_kernel(
    me_ref, h1_ref, dup_ref, ob_ref, da_ref, one_ref, two_ref, mine_ref, theirs_ref, acc_ref, sums_s, *, places, per, share_rows
):
    width, ff = h1_ref.shape[1], dup_ref.shape[1]
    at = places(me_ref)
    acc_ref[:, :ff] = t_dot(h1_ref[...], dup_ref[...])
    columns = pl.ds(pl.multiple_of(me_ref[3] * 384, 128), 384)
    da = da_ref[:, columns]
    acc_ref[:384, ff:] = t_dot(ob_ref[0], da)
    acc_ref[384:, ff:] = t_dot(ob_ref[1], da)
    share(acc_ref, at, per, mine_ref, theirs_ref)
    for j in range(2):
        sums_s[2 * j : 2 * j + 1] = one_ref[j : j + 1]
        sums_s[2 * j + 1 : 2 * j + 2] = two_ref[j : j + 1]
    sums_s[4:] = jnp.zeros((4, width), F32)
    sums = sums_s[...]
    half = mine_ref.shape[0]
    lane = lanes((4, 128))
    for i in range(2 * half):
        ref, k = (mine_ref, i) if i < half else (theirs_ref, i - half)
        ref[k, :, ff + 384 :] = jnp.zeros((per, 128), ref.dtype)
        for d in range(per // share_rows):
            device = at[i] * (per // share_rows) + d
            turn = pltpu.roll(sums, width - device * share_rows, 1)[:4, :128]
            block = jnp.where(lane < share_rows, turn, 0.0)
            ref[k, d * share_rows : d * share_rows + 4, ff + 384 :] = block.astype(ref.dtype)


def grad_up(me, places, per, share_rows, h1, dup, ob_all, da, one, two):
    width, ff = h1.shape[1], dup.shape[1]
    cols = ff + 512
    half = width // per // 2
    args = [h1, dup, ob_all, da, one, two]
    return pl.pallas_call(
        functools.partial(grad_up_kernel, places=places, per=per, share_rows=share_rows),
        grid=(1,),
        in_specs=[scalars()] + [whole(a.shape) for a in args],
        out_specs=[whole((half, per, cols))] * 2,
        out_shape=[like(half, per, cols), like(half, per, cols, dtype=BF)],
        scratch_shapes=[pltpu.VMEM((width, ff + 384), F32), pltpu.VMEM((8, width), F32)],
        compiler_params=params(24),
        cost_estimate=pl.CostEstimate(flops=1, bytes_accessed=1, transcendentals=0),
        name="grad_up",
    )(me, *args)


def attend_back_kernel(
    me_ref, q_ref, lse_ref, d_ref, att_ref, k_ref, v_ref, ext_ref, cos_ref, sin_ref, cosq_ref, sinq_ref, t_ref, w_ref,
    dx_ref, dx_go_ref, dw_ref, dw_go_ref, qc_s, dc_s, dq_s, dkv_s, dw_s, *, places, per,
):
    j = pl.program_id(0)
    own = q_ref.shape[0]
    local = own // 2
    first = lanes((own, 128)) < 64

    @pl.when(j == 0)
    def _():
        for p in range(3):
            at = slice(p * 128, p * 128 + 128)
            q, d = q_ref[:, at], d_ref[:, at]
            prod = d.astype(F32) * att_ref[:, at]
            for h in range(2):
                keep = first if h == 0 else ~first
                rows = slice(h * own, (h + 1) * own)
                qc_s[p, rows, :128] = jnp.where(keep, q, jnp.zeros_like(q))
                qc_s[p, rows, 128:] = lse_ref[2 * p + h]
                dc_s[p, rows, :128] = jnp.where(keep, d, jnp.zeros_like(d))
                delta = jnp.sum(jnp.where(keep, prod, 0.0), axis=1, keepdims=True)
                dc_s[p, rows, 128:] = with_units(jnp.zeros((own, 128), F32), delta).astype(BF)
        dq_s[...] = jnp.zeros_like(dq_s)
        dw_s[...] = jnp.zeros_like(dw_s)

    ext = ext_ref[...]
    for p in range(3):
        k = k_ref[p]
        e = jnp.exp(dot_t(jnp.concatenate([k, ext], axis=1), qc_s[p]))
        ds = (e * dot_t(jnp.concatenate([v_ref[p], ext], axis=1), dc_s[p])).astype(BF)
        dkv_s[:, 384 + p * 128 : 512 + p * 128] = dot(e.astype(BF), dc_s[p, :, :128]).astype(BF)
        dk = dot(ds, qc_s[p, :, :128]).astype(BF).astype(F32)
        dk = dk * cos_ref[...] - swap_halves(dk) * sin_ref[...]
        dkv_s[:, p * 128 : p * 128 + 128] = dk.astype(BF)
        dq_s[p] += t_dot(k, ds)
    dkv = dkv_s[...]
    dw_s[:, 384:] += dot(t_ref[...], dkv)
    dx = dot_t(dkv, w_ref[:, 384:])

    def put(dx):
        for i in range(dx_ref.shape[0]):
            dx_ref[i] = dx[2 * i * local : (2 * i + 1) * local]
            dx_go_ref[i] = dx[(2 * i + 1) * local : (2 * i + 2) * local].astype(BF)

    last = j == pl.num_programs(0) - 1

    @pl.when(~last)
    def _():
        put(dx)

    @pl.when(last)
    def _():
        dqs = []
        for p in range(3):
            t = dq_s[p].T
            dq = jnp.where(first, t[:own], t[own:])
            dq = (dq * 0.125).astype(BF).astype(F32)
            dqs.append((dq * cosq_ref[...] - swap_halves(dq) * sinq_ref[...]).astype(BF))
        dq = jnp.concatenate(dqs, axis=1)
        dw_s[:, :384] = dot(t_ref[:, :own], dq)
        put(jnp.concatenate([dx[:own] + dot_t(dq, w_ref[:, :384]), dx[own:]], axis=0))
        share(dw_s, places(me_ref), per, dw_ref, dw_go_ref)


def attend_back(me, places, per, q, lse, d, att, k, v, ext, cos, sin, t, w):
    own = q.shape[0]
    keys = k.shape[1]
    width = w.shape[0]
    chunk = 2 * own
    steps = keys // chunk
    half = width // per // 2
    return pl.pallas_call(
        functools.partial(attend_back_kernel, places=places, per=per),
        grid=(steps,),
        in_specs=[
            scalars(),
            whole(q.shape),
            whole(lse.shape),
            whole(d.shape),
            whole(att.shape),
            pl.BlockSpec((3, chunk, 128), lambda j: (0, steps - 1 - j, 0)),
            pl.BlockSpec((3, chunk, 128), lambda j: (0, steps - 1 - j, 0)),
            pl.BlockSpec((chunk, 128), lambda j: (steps - 1 - j, 0)),
            pl.BlockSpec((chunk, 128), lambda j: (steps - 1 - j, 0)),
            pl.BlockSpec((chunk, 128), lambda j: (steps - 1 - j, 0)),
            pl.BlockSpec((own, 128), lambda j: (0, 0)),
            pl.BlockSpec((own, 128), lambda j: (0, 0)),
            pl.BlockSpec((width, chunk), lambda j: (0, steps - 1 - j)),
            whole(w.shape),
        ],
        out_specs=[
            pl.BlockSpec((2, own // 2, width), lambda j: (steps - 1 - j, 0, 0)),
            pl.BlockSpec((2, own // 2, width), lambda j: (steps - 1 - j, 0, 0)),
            whole((half, per, 1152)),
            whole((half, per, 1152)),
        ],
        out_shape=[
            like(keys // own, own // 2, width),
            like(keys // own, own // 2, width, dtype=BF),
            like(half, per, 1152),
            like(half, per, 1152, dtype=BF),
        ],
        scratch_shapes=[
            pltpu.VMEM((3, 2 * own, 256), BF),
            pltpu.VMEM((3, 2 * own, 256), BF),
            pltpu.VMEM((3, 128, 2 * own), F32),
            pltpu.VMEM((chunk, 768), BF),
            pltpu.VMEM((width, 1152), F32),
        ],
        compiler_params=params(40),
        cost_estimate=pl.CostEstimate(
            flops=16 * 6 * own * keys * 256,
            bytes_accessed=3 * keys * 1600,
            transcendentals=6 * own * keys,
        ),
        name="attend_back",
    )(me, *kept_far(q, lse), d, *kept_far(att, k, v, ext, cos, sin, cos, sin, t, w))


class Grid:
    def __init__(self, ndp, nseq):
        self.ny, self.nz = ndp, nseq // 4
        self.count = ndp * nseq
        self.ring = [0, 1, 3, 2] if self.nz == 4 else list(range(self.nz))
        self.place = [self.ring.index(z) for z in range(self.nz)]
        step = {z: self.ring[(self.place[z] + 1) % self.nz] for z in range(self.nz)}
        self.across = {
            "c": self.pairs(lambda y, z, x, c: (y, z, x, 1 - c)),
            "x": self.pairs(lambda y, z, x, c: (y, z, 1 - x, c)),
            "y": self.pairs(lambda y, z, x, c: (1 - y, z, x, c)),
            "up": self.pairs(lambda y, z, x, c: (y, step[z], x, c)),
        }
        self.across["down"] = [(b, a) for a, b in self.across["up"]]
        for k in range(1, self.nz):
            by = {z: self.ring[(self.place[z] + k) % self.nz] for z in range(self.nz)}
            self.across[f"up{k}"] = self.pairs(lambda y, z, x, c, by=by: (y, by[z], x, c))
            self.across[f"down{k}"] = [(b, a) for a, b in self.across[f"up{k}"]]
        self.bits = [1 << i for i in range(self.nz.bit_length() - 1)]
        for bit in self.bits:
            self.across[f"z{bit}"] = self.pairs(lambda y, z, x, c, bit=bit: (y, z ^ bit, x, c))
        self.across["spread"] = self.pairs(lambda y, z, x, c: (1 - y, z, x, c) if c == y else None)
        self.across["home"] = self.pairs(lambda y, z, x, c: (1 - y, z, x, c) if c != y else None)
        self.across["give"] = self.pairs(lambda y, z, x, c: (y, z, x, 1 - c) if c == y else None)

    def pairs(self, to):
        def index(y, z, x, c):
            return ((y * self.nz + z) * 2 + x) * 2 + c

        made = []
        for y in range(self.ny):
            for z in range(self.nz):
                for x in range(2):
                    for c in range(2):
                        there = to(y, z, x, c)
                        if there is not None:
                            made.append((index(y, z, x, c), index(*there)))
        return made

    def locate(self):
        s = lax.axis_index("seq")
        self.arrived, self.moved = [], {}
        self.latest, self.streams, self.waiting, self.results = [None, None], {}, {}, {}
        self.y = lax.axis_index("dp")
        self.z, self.x, self.c = s // 4, (s // 2) % 2, s % 2
        return jnp.stack([self.y, self.z, self.x, self.c]).astype(jnp.int32)

    def back_by(self, axis, z, d):
        if axis == "h":
            moved = sum(jnp.where(d & other != 0, bit, 0) for bit, other in zip(self.bits, reversed(self.bits)))
            return z ^ moved
        return self.place_of((self.place_of(z) + self.nz - d) & (self.nz - 1))

    def place_of(self, z):
        return z ^ (z >> 1) if self.nz == 4 else z

    def places(self, order, me):
        size = {"x": 2, "y": self.ny, "z": self.nz, "Z": self.nz, "h": self.nz}
        total = 1
        for axis in order:
            total *= size[axis]
        found = []
        for i in range(total):
            y, z, x = me[0], me[1], me[2]
            for axis in reversed(order):
                d, i = i % size[axis], i // size[axis]
                if d == 0:
                    continue
                if axis == "x":
                    x = 1 - x
                elif axis == "y":
                    y = 1 - y
                elif axis == "h":
                    z = z ^ sum(bit for bit, other in zip(self.bits, reversed(self.bits)) if d & other)
                else:
                    z = self.place_of((self.place_of(z) + self.nz - d) % self.nz)
            if "y" not in order:
                y = 0
            found.append((y * self.nz + z) * 2 + x)
        return found

    def tie(self, arrays):
        tokens = [t for t in self.latest if t is not None] + self.arrived
        self.arrived = []
        if not tokens:
            return list(arrays)
        return list(lax.optimization_barrier((*arrays, *tokens))[: len(arrays)])

    def move(self, way, a):
        a = self.tie([a])[0]
        self.latest[0] = a
        got = self.moved[self.label] = lax.ppermute(a, AXES, self.across[way])
        return got

    def work(self, f, *arrays):
        made = f(*self.tie(arrays))
        self.latest[1] = jax.tree.leaves(made)[0]
        return made

    def advance(self, name, whole_ring):
        while True:
            kind, *what = self.waiting[name]
            value = self.move(*what) if kind == "move" else self.work(*what)
            self.send(name, value)
            if not whole_ring or name not in self.waiting or self.waiting[name][1][0] not in "udz":
                return

    def send(self, name, value):
        try:
            self.waiting[name] = self.streams[name].send(value)
        except StopIteration as stop:
            self.waiting.pop(name, None)
            self.results[name] = stop.value

    def start(self, name, stream):
        self.streams[name] = stream
        self.send(name, None)

    def ways(self, axis):
        return [f"z{bit}" for bit in self.bits] if axis == "h" else [axis]

    def ordered(self, bit, mine, theirs, axis):
        return jnp.where(
            bit == 0,
            jnp.concatenate([mine, theirs], axis=axis),
            jnp.concatenate([theirs, mine], axis=axis),
        )

    def gather(self, shard, order):
        held = [shard[None]]
        for axis in order:
            a = held[0] if len(held) == 1 else jnp.concatenate(held, axis=0)
            if axis == "z":
                held = [a]
                for _ in range(self.nz - 1):
                    held.append((yield "move", "up", held[-1]))
            elif axis == "Z":
                held = [a]
                for k in range(1, self.nz):
                    held.append((yield "move", f"up{k}", a))
            elif axis == "h":
                held = [a]
                for bit in reversed(self.bits):
                    a = held[0] if len(held) == 1 else jnp.concatenate(held, axis=0)
                    held = [a, (yield "move", f"z{bit}", a)]
            else:
                held = [a, (yield "move", axis, a)]
        return held


def sum_blocks(grid, axis, blocks):
    if axis == "z":
        part = blocks[-1]
        for d in range(len(blocks) - 2, -1, -1):
            part = (yield "move", "down", part.astype(BF)).astype(F32) + blocks[d]
        return part
    arrived = []
    for d in range(1, len(blocks)):
        arrived.append((yield "move", f"down{d}", blocks[d].astype(BF)))
    return sum((piece.astype(F32) for piece in arrived), blocks[0])


def halve(grid, ways, part):
    for way in ways:
        n = part.shape[0]
        part = part[: n // 2] + (yield "move", way, part[n // 2 :].astype(BF)).astype(F32)
    return part


def reduce_axes(grid, part, axes):
    for axis in axes:
        if axis in "zZ":
            part = yield from sum_blocks(grid, axis, jnp.split(part, grid.nz))
        else:
            part = yield from halve(grid, grid.ways(axis), part)
    return part[0]


def reduce_shared(grid, mine, theirs, order):
    axis = order[0]
    if axis in "zZ":
        blocks = jnp.split(mine, grid.nz // 2) + jnp.split(theirs, grid.nz // 2)
        part = yield from sum_blocks(grid, axis, blocks)
    else:
        ways = grid.ways(axis)
        part = mine + (yield "move", ways[0], theirs).astype(F32)
        part = yield from halve(grid, ways[1:], part)
    return (yield from reduce_axes(grid, part, order[1:]))


def body(grid, tokens, segment_ids, pad_mask, w_qkv, w_out, w_gate, w_up, w_down, ln_gain, ln_bias, cotangent):
    me = grid.locate()
    y, c = grid.y, grid.c
    local, width = tokens.shape
    own = 2 * local
    chips = grid.nz * 2
    rows = w_qkv.shape[1]
    two = 2 * rows
    down_rows = w_down.shape[1]
    ff = w_gate.shape[2] // 2
    direct = two % 16 == 0

    def tokens_task():
        message = yield "work", make_message, tokens, segment_ids, pad_mask
        along = jnp.concatenate((yield from grid.gather(message, orders["X"])), axis=0)
        return along, (yield "move", "c", along)

    def columns_task():
        mine, theirs = yield "work", functools.partial(make_columns, me), w_qkv, w_up, w_out, w_gate, ln_gain, ln_bias
        return mine, (yield "move", "c", theirs)

    def shard(start, size):
        mine, theirs = grid.results["P"]
        return grid.ordered(c, mine[:, start : start + size], theirs[:, start : start + size], 0)

    def up_task(order):
        pieces = yield from grid.gather(shard(1152, ff + 512), order)
        outs = jnp.concatenate([p[:, :, ff : ff + 384] for p in pieces], axis=0)
        return pieces, (yield "move", "c", outs)

    def down_task(order):
        part = yield "work", lambda w: w.astype(BF), w_down[0]
        part = grid.ordered(c, part, (yield "move", "c", part), 0)
        part = jnp.where(c == y, part, (yield "move", "spread", part))
        return (yield from grid.gather(part, order))

    def cot_task():
        return (yield "move", "c", cotangent)

    def placed(pieces, order):
        per = pieces[0].shape[1]
        at = functools.partial(grid.places, order[::-1])
        if direct:
            return pieces, at, per
        blocks = jnp.concatenate(pieces, axis=0)
        table = jnp.stack(at(me))
        blocks = jnp.zeros_like(blocks).at[table].set(blocks)
        return [blocks.reshape(1, -1, blocks.shape[2])], lambda _: [0], blocks.shape[0] * per

    def numbers(index, me):
        chip, side = index >> 1, index & 1
        order = orders["X"][::-1]
        inner = grid.nz if order[1] != "x" else 2
        d = chip & (inner - 1), chip >> (inner.bit_length() - 1)
        dz, dx = d if order[1] != "x" else d[::-1]
        z = grid.back_by(order.replace("x", ""), me[1], dz)
        return ((z * 2 + (me[2] ^ dx)) << 1) + (me[3] ^ side)

    def shared(made, order, per):
        if direct:
            return made
        blocks = jnp.concatenate([made[0][0], made[1][0].astype(F32)], axis=0)
        blocks = blocks.reshape(-1, per, blocks.shape[1])[jnp.stack(grid.places(order, me))]
        half = blocks.shape[0] // 2
        return blocks[:half], blocks[half:].astype(BF)

    def places_of(order, per, total):
        if direct:
            return functools.partial(grid.places, order), per
        return (lambda _: [0, 1]), total // 2

    def down_grad(made, order):
        per = 2 * down_rows
        part = yield from reduce_shared(grid, *shared(made, order, per), order)
        part = part + (yield "move", "home", part.astype(BF)).astype(F32)
        sent = jnp.where(c == 0, part[down_rows:], part[:down_rows])
        kept = jnp.where(c == 0, part[:down_rows], part[down_rows:])
        return jnp.where(c == y, kept, (yield "move", "give", sent))

    def columns_grad(made, order, cuts):
        part = yield from reduce_shared(grid, *shared(made, order, two), order)
        sent = jnp.where(c == 0, part[rows:], part[:rows])
        kept = jnp.where(c == 0, part[:rows], part[rows:])
        got = yield "move", "c", sent[:, : cuts[-1]]
        return [
            grid.ordered(c, kept[:, i:j], got[:, i:j], 1) for i, j in zip(cuts, cuts[1:])
        ] + [kept[:4, cuts[-1] : cuts[-1] + rows]]

    def input_grad(dx, dx_go, dr1, order):
        part = dx + (yield "move", "c", dx_go).astype(F32)
        part = yield from reduce_axes(grid, part, order)
        return dr1 + part

    orders = ORDERS
    got, start = grid.results, grid.start

    def rank_():
        got["rank"] = grid.work(functools.partial(rank, me, numbers), *got["X"])

    def project_():
        pieces, at, per = placed(got["Q"], orders["Q"])
        got["project"] = grid.work(
            lambda *a: project(me, list(a[:-4]), at, per, *a[-4:]), *pieces, *got["X"], *got["rank"][1:3]
        )

    def attend_():
        q, k, v = got["project"][:3]
        got["attend"] = grid.work(attend, q, k, v, got["rank"][3])

    def ob_move():
        got["ob"] = grid.move("c", got["attend"][1])

    def mid_():
        pieces, out_sib = got["U"]
        if not direct:
            table = jnp.stack(grid.places(orders["U"][::-1], me))
            out_sib = jnp.zeros_like(out_sib).at[table].set(out_sib).reshape(1, width, 384)
        pieces, at, per = placed(pieces, orders["U"])
        args = [got["attend"][1], got["ob"], out_sib, *got["X"]]
        got["mid"] = grid.work(lambda *a: mid(me, list(a[:-5]), at, per, *a[-5:], ff, rows), *pieces, *args)
        got["norm"] = got["mid"][7]

    def gate_():
        pieces, at, per = placed(got["G"], orders["G"])
        h1, up = got["mid"][2:4]
        got["gate"] = grid.work(lambda *a: gate_up(me, list(a[:-2]), at, per, *a[-2:]), *pieces, h1, up)

    def down_():
        pieces, at, per = placed(got["D"], orders["D"])
        got["down"] = grid.work(lambda *a: down(me, list(a[:-1]), at, per, a[-1]), *pieces, got["gate"][1])

    def part_move():
        got["part"] = grid.move("c", got["down"][0])

    def turn_():
        n1, _, _, up, _, _, up_w, _ = got["mid"]
        gate, _, gate_w = got["gate"]
        part, down_w = got["down"]
        got["turn"] = grid.work(
            turn, part, got["part"], n1, got["norm"], cotangent, got["C"], got["rank"][4], gate, up, gate_w, up_w, down_w
        )

    def back_move():
        got["back_part"] = grid.move("c", got["turn"][5])

    def grad_d():
        order = orders["d"]
        at, per = places_of(order, 2 * down_rows, ff)
        made = grid.work(functools.partial(grad, me, at, per), got["gate"][1], got["turn"][2])
        start("d", down_grad(made, order))

    def grad_g():
        order = orders["g"]
        at, per = places_of(order, two, width)
        made = grid.work(functools.partial(grad, me, at, per), got["mid"][2], got["turn"][3])
        start("g", columns_grad(made, order, [0, ff]))

    def back_():
        n1, f1 = got["mid"][:2]
        got["back"] = grid.work(
            functools.partial(back, me), got["turn"][1], got["turn"][5], got["back_part"], n1, f1, got["norm"], got["mid"][5]
        )

    def grad_u():
        order = orders["u"]
        at, per = places_of(order, two, width)
        made = grid.work(
            functools.partial(grad_up, me, at, per, rows),
            got["mid"][2], got["turn"][4], got["mid"][4], got["back"][1], got["back"][3], got["turn"][6],
        )
        start("u", columns_grad(made, order, [0, ff, ff + 384]))

    def attend_back_():
        q, k, v, qkv_w = got["project"]
        x_t, cos, sin, ext = got["rank"][:4]
        att, _, lse = got["attend"]
        order = orders["q"]
        at, per = places_of(order, two, width)
        dx, dx_go, *made = grid.work(
            functools.partial(attend_back, me, at, per), q, lse, got["back"][2], att, k, v, ext, cos, sin, x_t, qkv_w
        )
        start("q", columns_grad(made, order, [0, 384, 768, 1152]))
        start("x", input_grad(dx, dx_go, got["back"][0], "x" + orders["x"][-1]))

    start("X", tokens_task())
    start("P", columns_task())
    later = {
        "Q": lambda: grid.gather(shard(0, 1152), orders["Q"]),
        "U": lambda: up_task(orders["U"]),
        "G": lambda: grid.gather(shard(1152 + ff + 512, ff), orders["G"]),
    }
    start("D", down_task(orders["D"]))
    start("C", cot_task())
    single = [
        rank_, project_, attend_, ob_move, mid_, gate_, down_, part_move, turn_, back_move, grad_d, grad_g,
        back_, grad_u, attend_back_,
    ]
    for code in SEQUENCE:
        if code < 0:
            grid.arrived.append(grid.moved[-code])
            continue
        grid.label = code if code >= 200 else code & ~8
        if code >= 200:
            single[code - 200]()
            continue
        name = STREAMS[code >> 4]
        if name in later:
            start(name, later.pop(name)())
        grid.advance(name, bool(code & 8))
    norms = got["u"][2].reshape(2, 2, rows)
    return (
        got["turn"][0],
        got["x"],
        jnp.concatenate(got["q"][:3], axis=1)[None],
        got["u"][1][None],
        got["g"][0][None],
        got["u"][0][None],
        got["d"][None],
        norms[0][None],
        norms[1][None],
    )


def solution(mesh):
    grid = Grid(mesh.shape["dp"], mesh.shape["seq"])
    rows = P(AXES, None)
    weight = P(None, AXES, None)
    norm = P(None, None, AXES)
    return jax.shard_map(
        functools.partial(body, grid),
        mesh=mesh,
        in_specs=(rows, P(AXES), P(AXES)) + (weight,) * 5 + (norm,) * 2 + (rows,),
        out_specs=(rows, rows) + (weight,) * 5 + (norm,) * 2,
        check_vma=False,
    )
```

time: 469 us -> 300 us (0.64)
  other arithmetic: 68.4 us -> 9.91 us
  matrix products: 50.2 us -> 0 us
  local copies, waits for them, and re-layouts: 52.3 us -> 8.8 us
  waiting for transfers between devices: 167 us -> 129 us
  Pallas kernels: 37.8 us -> 75.1 us
  starting transfers between devices: 84.9 us -> 72.9 us
    dot_general x29 -> x0, matrix products: 50.2 us -> none  [the longest x18 29.1 us: dot(): return jnp.dot(a, b, preferred_element_type=F32)]
    pallas_call x2 -> x13, Pallas kernels: 25.2 us -> 64.8 us  [the longest x1 26.9 us: attend_back(): pl.pallas_call(functools.partial(attend_back_kernel, places=places, per=p...]
    ppermute x76 -> x57, waiting for transfers between devices: 167 us -> 129 us  [move(): got = self.moved[self.label] = lax.ppermute(a, AXES, self.across[way])]
    select_n x17 -> x7, other arithmetic: 19.9 us -> 2.23 us  [ordered(): jnp.where(bit == 0, jnp.concatenate([mine, theirs], axis=axis), jnp.conca...]
    unnamed x142 -> x30, local copies, waits for them, and re-layouts: 20.9 us -> 7.51 us
    ppermute x76 -> x57, starting transfers between devices: 84.9 us -> 72.9 us  [move(): got = self.moved[self.label] = lax.ppermute(a, AXES, self.across[way])]
    slice x28 -> x13, local copies, waits for them, and re-layouts: 8.63 us -> 0.47 us  [the longest x8 0.39 us: halve(): part[n // 2:].astype(BF)]
    mul x5 -> x0, other arithmetic: 7.7 us -> none  [the longest x1 5.35 us: body(): sin = jnp.sin(angle) * jnp.where(lane % 64 < 32, -1.0, 1.0)]
  transfers between devices with their start and end apart: 76 -> 57, of which waited for: 33 -> 29; matrix products, arithmetic and copies ran while one was open for 30% -> 3% of each run, Pallas kernels for 8% -> 22%
where the time goes in v2:
time: 300 us; the launch traced here: 297 us
  waiting for transfers between devices  129 us (43%)
  Pallas kernels  75.1 us (25%)
  starting transfers between devices  72.9 us (24%)
  other arithmetic  9.91 us (3%)
  local copies, waits for them, and re-layouts  8.8 us (3%)
    ppermute x57, waiting for transfers between devices, move(): got = self.moved[self.label] = lax.ppermute(a, AXES, self.across[way])  129 us
    ppermute x57, starting transfers between devices, move(): got = self.moved[self.label] = lax.ppermute(a, AXES, self.across[way])  72.9 us
    pallas_call x1, Pallas kernels, attend_back(): pl.pallas_call(functools.partial(attend_back_kernel, places=places, per=p...  26.9 us
    pallas_call x1, Pallas kernels, attend(): pl.pallas_call(functools.partial(attend_kernel, chunk=512), grid=(3,), in...  10.3 us
    pallas_call x1, Pallas kernels, rank(): pl.pallas_call(functools.partial(rank_kernel, numbers=numbers, coarse=coa...  8.88 us
    pallas_call x1, Pallas kernels, project(): pl.pallas_call(functools.partial(project_kernel, places=places, per=per,...  8.2 us
    unnamed x30, local copies, waits for them, and re-layouts  7.51 us
  transfers between devices with their start and end apart: 57, of which 29 were waited for; matrix products, arithmetic and copies ran while one was open for 3% of the time, Pallas kernels for 22%

profile of v2, /device:TPU:0, one launch (start us, length us, event | category | flops | bytes accessed | tf_op | source)
XLA Modules:
  0.0 296.9 jit_solution(15071109325502190808)
XLA Ops:
  3.0 4.1 %collective-permute-start.3 = (bf16[1,168,768]{2,1,0:T(8,128)(2,1)S(1)}, bf16[1,168,768]{2,1,0:T(8,128)(2,1)S(1)}, u32[]{:S(2)}, u32[]{:S(2)}) collective-permute-start(bf16[1,168,768]{2,1,0:T(8,128)(2,1)S(1)} %bitcast.59), channel_id=1, source_target_pairs={{0,8},{1,9},{2,10},{3,11},{4,12},{5,13},{6,14},{7,15},{8,0},{9,1},... | collective-permute-start | bytes 774152 | tf_op jit(solution)/shard_map/ppermute | solution.py:883
  15.4 3.4 %collective-permute-start.1 = (bf16[192,768]{1,0:T(8,128)(2,1)S(1)}, bf16[192,768]{1,0:T(8,128)(2,1)S(1)}, u32[]{:S(2)}, u32[]{:S(2)}) collective-permute-start(bf16[192,768]{1,0:T(8,128)(2,1)S(1)} %maximum_select_fusion), channel_id=1, source_target_pairs={{0,16},{2,18},{4,20},{6,22},{8,24},{10,26},{12,28},{14,30},{17,1},... | collective-permute-start | bytes 884744 | tf_op jit(solution)/shard_map/ppermute | solution.py:883
  19.3 1.7 collective-permute-start.4
  21.1 2.6 collective-permute-start.9
  24.8 7.7 %collective-permute-done.4 = bf16[1,48,1152]{2,1,0:T(8,128)(2,1)S(1)} collective-permute-done((bf16[1,48,1152]{2,1,0:T(8,128)(2,1)S(1)}, bf16[1,48,1152]{2,1,0:T(8,128)(2,1)S(1)}, u32[]{:S(2)}, u32[]{:S(2)}) %collective-permute-start.4) | collective-permute-done | bytes 110624 | tf_op jit(solution)/shard_map/ppermute | solution.py:883
  32.5 1.6 collective-permute-start.7
  34.1 1.5 collective-permute-done.5.cot_got_ref
  36.2 5.2 %collective-permute-done.9 = bf16[2,168,768]{2,1,0:T(8,128)(2,1)S(1)} collective-permute-done((bf16[2,168,768]{2,1,0:T(8,128)(2,1)S(1)}, bf16[2,168,768]{2,1,0:T(8,128)(2,1)S(1)}, u32[]{:S(2)}, u32[]{:S(2)}) %collective-permute-start.9) | collective-permute-done | bytes 516128 | tf_op jit(solution)/shard_map/ppermute | solution.py:883
  41.5 3.1 %collective-permute-done.6 = bf16[1,192,768]{2,1,0:T(8,128)(2,1)S(1)} collective-permute-done((bf16[1,192,768]{2,1,0:T(8,128)(2,1)S(1)}, bf16[1,192,768]{2,1,0:T(8,128)(2,1)S(1)}, u32[]{:S(2)}, u32[]{:S(2)}) %collective-permute-start.6) | collective-permute-done | bytes 294944 | tf_op jit(solution)/shard_map/ppermute | solution.py:883
  45.7 9.2 %collective-permute-done.11 = bf16[2,48,2048]{2,1,0:T(8,128)(2,1)S(1)} collective-permute-done((bf16[2,48,2048]{2,1,0:T(8,128)(2,1)S(1)}, bf16[2,48,2048]{2,1,0:T(8,128)(2,1)S(1)}, u32[]{:S(2)}, u32[]{:S(2)}) %collective-permute-start.11) | collective-permute-done | bytes 393248 | tf_op jit(solution)/shard_map/ppermute | solution.py:883
  55.0 1.4 collective-permute-start.17
  56.8 11.9 %collective-permute-done.15 = bf16[4,168,768]{2,1,0:T(8,128)(2,1)S(1)} collective-permute-done((bf16[4,168,768]{2,1,0:T(8,128)(2,1)S(1)}, bf16[4,168,768]{2,1,0:T(8,128)(2,1)S(1)}, u32[]{:S(2)}, u32[]{:S(2)}) %collective-permute-start.15) | collective-permute-done | bytes 1032224 | tf_op jit(solution)/shard_map/ppermute | solution.py:883
  69.1 1.4 collective-permute-start.14
  70.5 1.7 collective-permute-start.10
  72.3 1.4 collective-permute-start.21
  73.7 15.4 %collective-permute-done.14 = bf16[4,48,2048]{2,1,0:T(8,128)(2,1)S(1)} collective-permute-done((bf16[4,48,2048]{2,1,0:T(8,128)(2,1)S(1)}, bf16[4,48,2048]{2,1,0:T(8,128)(2,1)S(1)}, u32[]{:S(2)}, u32[]{:S(2)}) %collective-permute-start.14) | collective-permute-done | bytes 786464 | tf_op jit(solution)/shard_map/ppermute | solution.py:883
  89.2 1.3 collective-permute-start.25
  90.6 2.5 collective-permute-done.19
  94.0 1.2 collective-permute-start.20
  95.3 8.9 %rank.1 = (bf16[768,2560]{1,0:T(8,128)(2,1)}, f32[2560,128]{1,0:T(8,128)}, f32[2560,128]{1,0:T(8,128)}, bf16[2560,128]{1,0:T(8,128)(2,1)}, f32[320,128]{1,0:T(8,128)S(1)}) custom-call(s32[4]{0:T(128)S(1)} %pad_add_fusion.me_ref, bf16[8,168,768]{2,1,0:T(8,128)(2,1)S(1)} %pad_maximum_fusion.along_ref.note_a_ref.refs_2_.refs_5_, ...), custom_call_target="tpu_custom_call" | custom-call | flops 1 | bytes 1 | tf_op jit(solution)/shard_map/rank/pallas_call | solution.py:237
  104.1 8.2 %project.1 = (bf16[320,384]{1,0:T(8,128)(2,1)}, bf16[3,2560,128]{2,1,0:T(8,128)(2,1)}, bf16[3,2560,128]{2,1,0:T(8,128)(2,1)}, bf16[768,1152]{1,0:T(8,128)(2,1)}) custom-call(s32[4]{0:T(128)S(1)} %pad_add_fusion.me_ref, bf16[8,48,1152]{2,1,0:T(8,128)(2,1)S(1)} %constant_dynamic-update-slice_fusion.refs_0_, ...), custom_call_target="tpu_custom_call" | custom-call | flops 1 | bytes 1 | tf_op jit(solution)/shard_map/project/pallas_call | solution.py:297
  112.4 1.4 collective-permute-start.24
  113.7 10.3 %attend.1 = (f32[320,384]{1,0:T(8,128)}, bf16[320,384]{1,0:T(8,128)(2,1)S(1)}, bf16[6,320,128]{2,1,0:T(8,128)(2,1)}) custom-call(bf16[320,384]{1,0:T(8,128)(2,1)} %get-tuple-element.330.q_ref, bf16[3,2560,128]{2,1,0:T(8,128)(2,1)} %get-tuple-element.334.k_ref, bf16[3,2560,128]{2,1,0:T(8,128)(2,1)} %get-tuple-element.335.v_ref, ...), custom_call_target="tpu_custom_call" | custom-call | flops 5033164800 | bytes 7864320 | tf_op jit(solution)/shard_map/attend/pallas_call | solution.py:346
  124.1 3.4 %collective-permute-done.25.refs_1_ = bf16[8,48,2048]{2,1,0:T(8,128)(2,1)S(1)} collective-permute-done((bf16[8,48,2048]{2,1,0:T(8,128)(2,1)S(1)}, bf16[8,48,2048]{2,1,0:T(8,128)(2,1)S(1)}, u32[]{:S(2)}, u32[]{:S(2)}) %collective-permute-start.25) | collective-permute-done | bytes 1572896 | tf_op jit(solution)/shard_map/ppermute | solution.py:883
  127.6 1.7 collective-permute-start.23
  129.6 2.8 mid.1
  132.4 7.0 %collective-permute-done.24.refs_1_ = bf16[8,48,1536]{2,1,0:T(8,128)(2,1)S(1)} collective-permute-done((bf16[8,48,1536]{2,1,0:T(8,128)(2,1)S(1)}, bf16[8,48,1536]{2,1,0:T(8,128)(2,1)S(1)}, u32[]{:S(2)}, u32[]{:S(2)}) %collective-permute-start.24) | collective-permute-done | bytes 1179680 | tf_op jit(solution)/shard_map/ppermute | solution.py:883
  139.4 1.8 gate_up.1
  141.2 3.1 %collective-permute-done.23.refs_3_ = bf16[2,192,768]{2,1,0:T(8,128)(2,1)S(1)} collective-permute-done((bf16[2,192,768]{2,1,0:T(8,128)(2,1)S(1)}, bf16[2,192,768]{2,1,0:T(8,128)(2,1)S(1)}, u32[]{:S(2)}, u32[]{:S(2)}) %collective-permute-start.23) | collective-permute-done | bytes 589856 | tf_op jit(solution)/shard_map/ppermute | solution.py:883
  144.3 1.6 down.1
  146.0 2.6 collective-permute-done.28.got_ref
  148.5 4.7 %turn.1 = (bf16[160,768]{1,0:T(8,128)(2,1)}, f32[320,768]{1,0:T(8,128)S(1)}, bf16[320,768]{1,0:T(8,128)(2,1)S(1)}, bf16[320,1536]{1,0:T(8,128)(2,1)S(1)}, bf16[3...) custom-call(f32[320,768]{1,0:T(8,128)S(1)} %get-tuple-element.275.part_ref, ...), custom_call_target="tpu_custom_call" | custom-call | flops 2264924160 | bytes 20971520 | tf_op jit(solution)/shard_map/turn/pallas_call | solution.py:546
  153.4 2.2 grad.2
  155.8 1.7 back.1
  157.4 2.7 grad_up.1
  160.1 1.3 collective-permute-start.30
  161.5 2.8 grad.3
  164.2 1.5 collective-permute-start.31
  165.7 26.9 %attend_back.1 = (f32[8,160,768]{2,1,0:T(8,128)S(1)}, bf16[8,160,768]{2,1,0:T(8,128)(2,1)S(1)}, f32[8,48,1152]{2,1,0:T(8,128)S(1)}, bf16[8,48,1152]{2,1,0:T(8,128)(2,1)S(1)}) custom-call(s32[4]{0:T(128)S(1)} %pad_add_fusion.me_ref, bf16[320,384]{1,0:T(8,128)(2,1)} %get-tuple-element.330.q_ref, bf16[6,320,128]{2,1,0:T(8,128)(2,1)} %get-tuple-element.331.lse_ref, ...), custom_call_target="tpu_custom_call" | custom-call | flops 20132659200 | bytes 12288000 | tf_op jit(solution)/shard_map/attend_back/pallas_call | solution.py:744
  193.1 3.6 %collective-permute-done.30 = bf16[8,48,2048]{2,1,0:T(8,128)(2,1)S(1)} collective-permute-done((bf16[8,48,2048]{2,1,0:T(8,128)(2,1)S(1)}, bf16[8,48,2048]{2,1,0:T(8,128)(2,1)S(1)}, u32[]{:S(2)}, u32[]{:S(2)}) %collective-permute-start.30) | collective-permute-done | bytes 1572896 | tf_op jit(solution)/shard_map/ppermute | solution.py:883
  197.3 1.4 collective-permute-start.34
  198.7 1.3 collective-permute-start.39
  200.1 1.6 collective-permute-start.36
  202.3 15.0 %collective-permute-done.34 = bf16[4,48,2048]{2,1,0:T(8,128)(2,1)S(1)} collective-permute-done((bf16[4,48,2048]{2,1,0:T(8,128)(2,1)S(1)}, bf16[4,48,2048]{2,1,0:T(8,128)(2,1)S(1)}, u32[]{:S(2)}, u32[]{:S(2)}) %collective-permute-start.34) | collective-permute-done | bytes 786464 | tf_op jit(solution)/shard_map/ppermute | solution.py:883
  218.8 3.7 %collective-permute-start.38 = (bf16[1,48,2048]{2,1,0:T(8,128)(2,1)S(1)}, bf16[1,48,2048]{2,1,0:T(8,128)(2,1)S(1)}, u32[]{:S(2)}, u32[]{:S(2)}) collective-permute-start(bf16[1,48,2048]{2,1,0:T(8,128)(2,1)S(1)} %split.93), channel_id=1, source_target_pairs={{4,0},{5,1},{6,2},{7,3},{12,4},{13,5},{14,6},{15,7},{0,8},{1,9},{2... | collective-permute-start | bytes 589832 | tf_op jit(solution)/shard_map/ppermute | solution.py:883
  222.5 4.3 %collective-permute-done.39 = bf16[8,48,1536]{2,1,0:T(8,128)(2,1)S(1)} collective-permute-done((bf16[8,48,1536]{2,1,0:T(8,128)(2,1)S(1)}, bf16[8,48,1536]{2,1,0:T(8,128)(2,1)S(1)}, u32[]{:S(2)}, u32[]{:S(2)}) %collective-permute-start.39) | collective-permute-done | bytes 1179680 | tf_op jit(solution)/shard_map/ppermute | solution.py:883
  227.9 1.3 collective-permute-start.37
  229.2 8.4 %collective-permute-done.40 = bf16[1,192,768]{2,1,0:T(8,128)(2,1)S(1)} collective-permute-done((bf16[1,192,768]{2,1,0:T(8,128)(2,1)S(1)}, bf16[1,192,768]{2,1,0:T(8,128)(2,1)S(1)}, u32[]{:S(2)}, u32[]{:S(2)}) %collective-permute-start.40) | collective-permute-done | bytes 294944 | tf_op jit(solution)/shard_map/ppermute | solution.py:883
  237.6 2.6 collective-permute-start.41
  240.4 4.2 %collective-permute-done.42 = bf16[2,48,1536]{2,1,0:T(8,128)(2,1)S(1)} collective-permute-done((bf16[2,48,1536]{2,1,0:T(8,128)(2,1)S(1)}, bf16[2,48,1536]{2,1,0:T(8,128)(2,1)S(1)}, u32[]{:S(2)}, u32[]{:S(2)}) %collective-permute-start.42) | collective-permute-done | bytes 294944 | tf_op jit(solution)/shard_map/ppermute | solution.py:883
  244.6 1.2 collective-permute-start.45
  246.7 4.8 %collective-permute-done.45 = bf16[2,48,1536]{2,1,0:T(8,128)(2,1)S(1)} collective-permute-done((bf16[2,48,1536]{2,1,0:T(8,128)(2,1)S(1)}, bf16[2,48,1536]{2,1,0:T(8,128)(2,1)S(1)}, u32[]{:S(2)}, u32[]{:S(2)}) %collective-permute-start.45) | collective-permute-done | bytes 294944 | tf_op jit(solution)/shard_map/ppermute | solution.py:883
  251.8 2.3 collective-permute-start.46
  254.1 9.5 %collective-permute-start.44 = (bf16[4,48,1152]{2,1,0:T(8,128)(2,1)S(1)}, bf16[4,48,1152]{2,1,0:T(8,128)(2,1)S(1)}, u32[]{:S(2)}, u32[]{:S(2)}) collective-permute-start(bf16[4,48,1152]{2,1,0:T(8,128)(2,1)S(1)} %slice.306), channel_id=1, source_target_pairs={{0,2},{1,3},{2,0},{3,1},{4,6},{5,7},{6,4},{7,5},{8,10},{9,11},{10,... | collective-permute-start | bytes 1327112 | tf_op jit(solution)/shard_map/ppermute | solution.py:883
  265.2 4.7 %collective-permute-done.44 = bf16[4,48,1152]{2,1,0:T(8,128)(2,1)S(1)} collective-permute-done((bf16[4,48,1152]{2,1,0:T(8,128)(2,1)S(1)}, bf16[4,48,1152]{2,1,0:T(8,128)(2,1)S(1)}, u32[]{:S(2)}, u32[]{:S(2)}) %collective-permute-start.44) | collective-permute-done | bytes 442400 | tf_op jit(solution)/shard_map/ppermute | solution.py:883
  270.6 2.8 collective-permute-start.50
  273.5 1.3 collective-permute-start.55
  274.8 1.8 collective-permute-done.43
  276.7 2.2 collective-permute-done.47
  280.1 1.9 collective-permute-start.48
  282.4 2.7 collective-permute-start.51
  285.9 2.4 collective-permute-done.51
  289.0 2.1 collective-permute-done.48
  292.7 1.3 collective-permute-start.56
  (172 shorter events, 32.5 us)
Async XLA Ops:
  0.6 0.9 copy-start.2
  3.0 18.0 %collective-permute-start.3 = (bf16[1,168,768]{2,1,0:T(8,128)(2,1)S(1)}, bf16[1,168,768]{2,1,0:T(8,128)(2,1)S(1)}, u32[]{:S(2)}, u32[]{:S(2)}) collective-permute-start(bf16[1,168,768]{2,1,0:T(8,128)(2,1)S(1)} %bitcast.59), channel_id=1, source_target_pairs={{0,8},{1,9},{2,10},{3,11},{4,12},{5,13},{6,14},{7,15},{8,0},{9,1},... | collective-permute-start | bytes 774152 | tf_op jit(solution)/shard_map/ppermute | solution.py:883
  8.2 1.0 copy-start
  9.1 1.0 copy-start.1
  10.1 0.9 copy-start.4
  13.9 1.4 collective-permute-start
  13.9 4.9 %collective-permute-start.2 = (bf16[24,4736]{1,0:T(8,128)(2,1)S(1)}, bf16[24,4736]{1,0:T(8,128)(2,1)S(1)}, u32[]{:S(2)}, u32[]{:S(2)}) collective-permute-start(bf16[24,4736]{1,0:T(8,128)(2,1)S(1)} %get-tuple-element.200), channel_id=1, source_target_pairs={{0,1},{1,0},{2,3},{3,2},{4,5},{5,4},{6,7},{7,6},{8,9},{9,8},{10,11... | collective-permute-start | bytes 681992 | tf_op jit(solution)/shard_map/ppermute | solution.py:883
  14.5 19.6 %copy-start.3 = (bf16[160,768]{1,0:T(8,128)(2,1)S(1)}, bf16[160,768]{1,0:T(8,128)(2,1)}, u32[]{:S(2)}) copy-start(bf16[160,768]{1,0:T(8,128)(2,1)} %cot_ref) | copy-start | bytes 737284
  15.4 17.1 %collective-permute-start.1 = (bf16[192,768]{1,0:T(8,128)(2,1)S(1)}, bf16[192,768]{1,0:T(8,128)(2,1)S(1)}, u32[]{:S(2)}, u32[]{:S(2)}) collective-permute-start(bf16[192,768]{1,0:T(8,128)(2,1)S(1)} %maximum_select_fusion), channel_id=1, source_target_pairs={{0,16},{2,18},{4,20},{6,22},{8,24},{10,26},{12,28},{14,30},{17,1},... | collective-permute-start | bytes 884744 | tf_op jit(solution)/shard_map/ppermute | solution.py:883
  18.9 17.2 %collective-permute-start.8 = (bf16[1,48,2048]{2,1,0:T(8,128)(2,1)S(1)}, bf16[1,48,2048]{2,1,0:T(8,128)(2,1)S(1)}, u32[]{:S(2)}, u32[]{:S(2)}) collective-permute-start(bf16[1,48,2048]{2,1,0:T(8,128)(2,1)S(1)} %maximum_select_fusion.3), channel_id=1, source_target_pairs={{0,8},{1,9},{2,10},{3,11},{4,12},{5,13},{6,14},{7,15},{8,0},{9,1},... | collective-permute-start | bytes 589832 | tf_op jit(solution)/shard_map/ppermute | solution.py:883
  19.3 13.1 %collective-permute-start.4 = (bf16[1,48,1152]{2,1,0:T(8,128)(2,1)S(1)}, bf16[1,48,1152]{2,1,0:T(8,128)(2,1)S(1)}, u32[]{:S(2)}, u32[]{:S(2)}) collective-permute-start(bf16[1,48,1152]{2,1,0:T(8,128)(2,1)S(1)} %get-tuple-element.209), channel_id=1, source_target_pairs={{0,4},{1,5},{2,6},{3,7},{4,12},{5,13},{6,14},{7,15},{8,0},{9,1},{1... | collective-permute-start | bytes 331784 | tf_op jit(solution)/shard_map/ppermute | solution.py:883
  21.1 20.3 %collective-permute-start.9 = (bf16[2,168,768]{2,1,0:T(8,128)(2,1)S(1)}, bf16[2,168,768]{2,1,0:T(8,128)(2,1)S(1)}, u32[]{:S(2)}, u32[]{:S(2)}) collective-permute-start(bf16[2,168,768]{2,1,0:T(8,128)(2,1)S(1)} %pad_maximum_fusion.6), channel_id=1, source_target_pairs={{0,4},{1,5},{2,6},{3,7},{4,0},{5,1},{6,2},{7,3},{8,12},{9,13},{10,... | collective-permute-start | bytes 1548296 | tf_op jit(solution)/shard_map/ppermute | solution.py:883
  23.7 21.9 %collective-permute-start.12 = (bf16[1,48,1152]{2,1,0:T(8,128)(2,1)S(1)}, bf16[1,48,1152]{2,1,0:T(8,128)(2,1)S(1)}, u32[]{:S(2)}, u32[]{:S(2)}) collective-permute-start(bf16[1,48,1152]{2,1,0:T(8,128)(2,1)S(1)} %get-tuple-element.209), channel_id=1, source_target_pairs={{0,12},{1,13},{2,14},{3,15},{4,8},{5,9},{6,10},{7,11},{8,4},{9,5},... | collective-permute-start | bytes 331784 | tf_op jit(solution)/shard_map/ppermute | solution.py:883
  32.5 12.1 %collective-permute-start.7 = (bf16[1,48,1536]{2,1,0:T(8,128)(2,1)S(1)}, bf16[1,48,1536]{2,1,0:T(8,128)(2,1)S(1)}, u32[]{:S(2)}, u32[]{:S(2)}) collective-permute-start(bf16[1,48,1536]{2,1,0:T(8,128)(2,1)S(1)} %get-tuple-element.206), channel_id=1, source_target_pairs={{0,2},{1,3},{2,0},{3,1},{4,6},{5,7},{6,4},{7,5},{8,10},{9,11},{10,... | collective-permute-start | bytes 442376 | tf_op jit(solution)/shard_map/ppermute | solution.py:883
  34.0 1.5 collective-permute-start.5
  35.5 9.1 %collective-permute-start.6 = (bf16[1,192,768]{2,1,0:T(8,128)(2,1)S(1)}, bf16[1,192,768]{2,1,0:T(8,128)(2,1)S(1)}, u32[]{:S(2)}, u32[]{:S(2)}) collective-permute-start(bf16[1,192,768]{2,1,0:T(8,128)(2,1)S(1)} %select_bitcast_fusion.1), channel_id=1, source_target_pairs={{0,2},{1,3},{2,0},{3,1},{4,6},{5,7},{6,4},{7,5},{8,10},{9,11},{10,... | collective-permute-start | bytes 884744 | tf_op jit(solution)/shard_map/ppermute | solution.py:883
  36.1 9.5 %collective-permute-start.13 = (bf16[1,48,1152]{2,1,0:T(8,128)(2,1)S(1)}, bf16[1,48,1152]{2,1,0:T(8,128)(2,1)S(1)}, u32[]{:S(2)}, u32[]{:S(2)}) collective-permute-start(bf16[1,48,1152]{2,1,0:T(8,128)(2,1)S(1)} %get-tuple-element.209), channel_id=1, source_target_pairs={{0,8},{1,9},{2,10},{3,11},{4,0},{5,1},{6,2},{7,3},{8,12},{9,13},{1... | collective-permute-start | bytes 331784 | tf_op jit(solution)/shard_map/ppermute | solution.py:883
  44.6 10.3 %collective-permute-start.11 = (bf16[2,48,2048]{2,1,0:T(8,128)(2,1)S(1)}, bf16[2,48,2048]{2,1,0:T(8,128)(2,1)S(1)}, u32[]{:S(2)}, u32[]{:S(2)}) collective-permute-start(bf16[2,48,2048]{2,1,0:T(8,128)(2,1)S(1)} %pad_maximum_fusion.8), channel_id=1, source_target_pairs={{0,4},{1,5},{2,6},{3,7},{4,0},{5,1},{6,2},{7,3},{8,12},{9,13},{10,... | collective-permute-start | bytes 1179656 | tf_op jit(solution)/shard_map/ppermute | solution.py:883
  44.6 24.1 %collective-permute-start.15 = (bf16[4,168,768]{2,1,0:T(8,128)(2,1)S(1)}, bf16[4,168,768]{2,1,0:T(8,128)(2,1)S(1)}, u32[]{:S(2)}, u32[]{:S(2)}) collective-permute-start(bf16[4,168,768]{2,1,0:T(8,128)(2,1)S(1)} %pad_maximum_fusion.2), channel_id=1, source_target_pairs={{0,2},{1,3},{2,0},{3,1},{4,6},{5,7},{6,4},{7,5},{8,10},{9,11},{10,... | collective-permute-start | bytes 3096584 | tf_op jit(solution)/shard_map/ppermute | solution.py:883
  55.0 13.9 %collective-permute-start.17 = (bf16[4,48,1152]{2,1,0:T(8,128)(2,1)S(1)}, bf16[4,48,1152]{2,1,0:T(8,128)(2,1)S(1)}, u32[]{:S(2)}, u32[]{:S(2)}) collective-permute-start(bf16[4,48,1152]{2,1,0:T(8,128)(2,1)S(1)} %pad_maximum_fusion.7), channel_id=1, source_target_pairs={{0,16},{1,17},{2,18},{3,19},{4,20},{5,21},{6,22},{7,23},{8,24},{9,... | collective-permute-start | bytes 1327112 | tf_op jit(solution)/shard_map/ppermute | solution.py:883
  56.4 12.6 %collective-permute-start.16 = (bf16[2,48,1536]{2,1,0:T(8,128)(2,1)S(1)}, bf16[2,48,1536]{2,1,0:T(8,128)(2,1)S(1)}, u32[]{:S(2)}, u32[]{:S(2)}) collective-permute-start(bf16[2,48,1536]{2,1,0:T(8,128)(2,1)S(1)} %pad_maximum_fusion.9), channel_id=1, source_target_pairs={{0,4},{1,5},{2,6},{3,7},{4,12},{5,13},{6,14},{7,15},{8,0},{9,1},{1... | collective-permute-start | bytes 884744 | tf_op jit(solution)/shard_map/ppermute | solution.py:883
  69.0 26.3 %copy-start.5 = (bf16[192,256]{1,0:T(8,128)(2,1)S(1)}, bf16[192,256]{1,0:T(8,128)(2,1)}, u32[]{:S(2)}) copy-start(bf16[192,256]{1,0:T(8,128)(2,1)} %constant.53.clone.coarse_ref) | copy-start | bytes 294916
  69.0 26.3 %copy-start.6 = (bf16[192,256]{1,0:T(8,128)(2,1)S(1)}, bf16[192,256]{1,0:T(8,128)(2,1)}, u32[]{:S(2)}) copy-start(bf16[192,256]{1,0:T(8,128)(2,1)} %constant.52.clone.fine_ref) | copy-start | bytes 294916
  69.0 20.2 %collective-permute-start.18 = (bf16[8,168,768]{2,1,0:T(8,128)(2,1)S(1)}, bf16[8,168,768]{2,1,0:T(8,128)(2,1)S(1)}, u32[]{:S(2)}, u32[]{:S(2)}) collective-permute-start(bf16[8,168,768]{2,1,0:T(8,128)(2,1)S(1)} %pad_maximum_fusion.along_ref.note_a_ref.refs_2_.refs_5_), channel_id=1, source_target_pairs={{0,1},{1,0},{2,3},{3,2},{4,5},{5,4},{6,7},{7,6},{8,9},{9,8},{10,11... | collective-permute-start | bytes 6193160 | tf_op jit(solution)/shard_map/ppermute | solution.py:883
  69.1 20.0 %collective-permute-start.14 = (bf16[4,48,2048]{2,1,0:T(8,128)(2,1)S(1)}, bf16[4,48,2048]{2,1,0:T(8,128)(2,1)S(1)}, u32[]{:S(2)}, u32[]{:S(2)}) collective-permute-start(bf16[4,48,2048]{2,1,0:T(8,128)(2,1)S(1)} %pad_maximum_fusion.3), channel_id=1, source_target_pairs={{0,16},{1,17},{2,18},{3,19},{4,20},{5,21},{6,22},{7,23},{8,24},{9,... | collective-permute-start | bytes 2359304 | tf_op jit(solution)/shard_map/ppermute | solution.py:883
  70.5 20.1 %collective-permute-start.10 = (bf16[2,192,768]{2,1,0:T(8,128)(2,1)S(1)}, bf16[2,192,768]{2,1,0:T(8,128)(2,1)S(1)}, u32[]{:S(2)}, u32[]{:S(2)}) collective-permute-start(bf16[2,192,768]{2,1,0:T(8,128)(2,1)S(1)} %pad_maximum_fusion.4.refs_0_), channel_id=1, source_target_pairs={{0,4},{1,5},{2,6},{3,7},{4,12},{5,13},{6,14},{7,15},{8,0},{9,1},{1... | collective-permute-start | bytes 1769480 | tf_op jit(solution)/shard_map/ppermute | solution.py:883
  72.3 20.9 %collective-permute-start.19 = (bf16[2,48,1536]{2,1,0:T(8,128)(2,1)S(1)}, bf16[2,48,1536]{2,1,0:T(8,128)(2,1)S(1)}, u32[]{:S(2)}, u32[]{:S(2)}) collective-permute-start(bf16[2,48,1536]{2,1,0:T(8,128)(2,1)S(1)} %collective-permute-done.16), channel_id=1, source_target_pairs={{0,4},{1,5},{2,6},{3,7},{4,12},{5,13},{6,14},{7,15},{8,0},{9,1},{1... | collective-permute-start | bytes 884744 | tf_op jit(solution)/shard_map/ppermute | solution.py:883
  72.3 31.8 %collective-permute-start.21 = (bf16[8,48,1152]{2,1,0:T(8,128)(2,1)S(1)}, bf16[8,48,1152]{2,1,0:T(8,128)(2,1)S(1)}, u32[]{:S(2)}, u32[]{:S(2)}) collective-permute-start(bf16[8,48,1152]{2,1,0:T(8,128)(2,1)S(1)} %constant_dynamic-update-slice_fusion.refs_0_), channel_id=1, source_target_pairs={{0,2},{1,3},{2,0},{3,1},{4,6},{5,7},{6,4},{7,5},{8,10},{9,11},{10,... | collective-permute-start | bytes 2654216 | tf_op jit(solution)/shard_map/ppermute | solution.py:883
  89.2 38.2 %collective-permute-start.25 = (bf16[8,48,2048]{2,1,0:T(8,128)(2,1)S(1)}, bf16[8,48,2048]{2,1,0:T(8,128)(2,1)S(1)}, u32[]{:S(2)}, u32[]{:S(2)}) collective-permute-start(bf16[8,48,2048]{2,1,0:T(8,128)(2,1)S(1)} %pad_maximum_fusion.1.refs_0_), channel_id=1, source_target_pairs={{0,2},{1,3},{2,0},{3,1},{4,6},{5,7},{6,4},{7,5},{8,10},{9,11},{10,... | collective-permute-start | bytes 4718600 | tf_op jit(solution)/shard_map/ppermute | solution.py:883
  93.1 19.2 %collective-permute-start.22 = (bf16[2,48,1536]{2,1,0:T(8,128)(2,1)S(1)}, bf16[2,48,1536]{2,1,0:T(8,128)(2,1)S(1)}, u32[]{:S(2)}, u32[]{:S(2)}) collective-permute-start(bf16[2,48,1536]{2,1,0:T(8,128)(2,1)S(1)} %collective-permute-done.19), channel_id=1, source_target_pairs={{0,4},{1,5},{2,6},{3,7},{4,12},{5,13},{6,14},{7,15},{8,0},{9,1},{1... | collective-permute-start | bytes 884744 | tf_op jit(solution)/shard_map/ppermute | solution.py:883
  94.0 30.0 %collective-permute-start.20 = (bf16[2,192,768]{2,1,0:T(8,128)(2,1)S(1)}, bf16[2,192,768]{2,1,0:T(8,128)(2,1)S(1)}, u32[]{:S(2)}, u32[]{:S(2)}) collective-permute-start(bf16[2,192,768]{2,1,0:T(8,128)(2,1)S(1)} %collective-permute-done.10.refs_1_), channel_id=1, source_target_pairs={{0,4},{1,5},{2,6},{3,7},{4,12},{5,13},{6,14},{7,15},{8,0},{9,1},{1... | collective-permute-start | bytes 1769480 | tf_op jit(solution)/shard_map/ppermute | solution.py:883
  112.4 27.0 %collective-permute-start.24 = (bf16[8,48,1536]{2,1,0:T(8,128)(2,1)S(1)}, bf16[8,48,1536]{2,1,0:T(8,128)(2,1)S(1)}, u32[]{:S(2)}, u32[]{:S(2)}) collective-permute-start(bf16[8,48,1536]{2,1,0:T(8,128)(2,1)S(1)} %constant_dynamic-update-slice_fusion.5.refs_0_), channel_id=1, source_target_pairs={{0,16},{1,17},{2,18},{3,19},{4,20},{5,21},{6,22},{7,23},{8,24},{9,... | collective-permute-start | bytes 3538952 | tf_op jit(solution)/shard_map/ppermute | solution.py:883
  124.0 3.5 %collective-permute-start.26 = (bf16[320,384]{1,0:T(8,128)(2,1)S(1)}, bf16[320,384]{1,0:T(8,128)(2,1)S(1)}, u32[]{:S(2)}, u32[]{:S(2)}) collective-permute-start(bf16[320,384]{1,0:T(8,128)(2,1)S(1)} %get-tuple-element.249.refs_2_), channel_id=1, source_target_pairs={{0,1},{1,0},{2,3},{3,2},{4,5},{5,4},{6,7},{7,6},{8,9},{9,8},{10,11... | collective-permute-start | bytes 737288 | tf_op jit(solution)/shard_map/ppermute | solution.py:883
  127.6 2.1 collective-permute-start.27
  127.6 16.6 %collective-permute-start.23 = (bf16[2,192,768]{2,1,0:T(8,128)(2,1)S(1)}, bf16[2,192,768]{2,1,0:T(8,128)(2,1)S(1)}, u32[]{:S(2)}, u32[]{:S(2)}) collective-permute-start(bf16[2,192,768]{2,1,0:T(8,128)(2,1)S(1)} %collective-permute-done.20.refs_2_), channel_id=1, source_target_pairs={{0,4},{1,5},{2,6},{3,7},{4,12},{5,13},{6,14},{7,15},{8,0},{9,1},{1... | collective-permute-start | bytes 1769480 | tf_op jit(solution)/shard_map/ppermute | solution.py:883
  145.9 2.6 collective-permute-start.28
  153.2 2.6 collective-permute-start.29
  160.1 36.6 %collective-permute-start.30 = (bf16[8,48,2048]{2,1,0:T(8,128)(2,1)S(1)}, bf16[8,48,2048]{2,1,0:T(8,128)(2,1)S(1)}, u32[]{:S(2)}, u32[]{:S(2)}) collective-permute-start(bf16[8,48,2048]{2,1,0:T(8,128)(2,1)S(1)} %get-tuple-element.323), channel_id=1, source_target_pairs={{0,16},{1,17},{2,18},{3,19},{4,20},{5,21},{6,22},{7,23},{8,24},{9,... | collective-permute-start | bytes 4718600 | tf_op jit(solution)/shard_map/ppermute | solution.py:883
  164.2 28.4 %collective-permute-start.31 = (bf16[4,192,768]{2,1,0:T(8,128)(2,1)S(1)}, bf16[4,192,768]{2,1,0:T(8,128)(2,1)S(1)}, u32[]{:S(2)}, u32[]{:S(2)}) collective-permute-start(bf16[4,192,768]{2,1,0:T(8,128)(2,1)S(1)} %get-tuple-element.329), channel_id=1, source_target_pairs={{0,2},{1,3},{2,0},{3,1},{4,6},{5,7},{6,4},{7,5},{8,10},{9,11},{10,... | collective-permute-start | bytes 3538952 | tf_op jit(solution)/shard_map/ppermute | solution.py:883
  197.3 20.3 %collective-permute-start.32 = (bf16[8,160,768]{2,1,0:T(8,128)(2,1)S(1)}, bf16[8,160,768]{2,1,0:T(8,128)(2,1)S(1)}, u32[]{:S(2)}, u32[]{:S(2)}) collective-permute-start(bf16[8,160,768]{2,1,0:T(8,128)(2,1)S(1)} %get-tuple-element.346), channel_id=1, source_target_pairs={{0,1},{1,0},{2,3},{3,2},{4,5},{5,4},{6,7},{7,6},{8,9},{9,8},{10,11... | collective-permute-start | bytes 5898248 | tf_op jit(solution)/shard_map/ppermute | solution.py:883
  197.3 20.0 %collective-permute-start.34 = (bf16[4,48,2048]{2,1,0:T(8,128)(2,1)S(1)}, bf16[4,48,2048]{2,1,0:T(8,128)(2,1)S(1)}, u32[]{:S(2)}, u32[]{:S(2)}) collective-permute-start(bf16[4,48,2048]{2,1,0:T(8,128)(2,1)S(1)} %slice.304), channel_id=1, source_target_pairs={{0,2},{1,3},{2,0},{3,1},{4,6},{5,7},{6,4},{7,5},{8,10},{9,11},{10,... | collective-permute-start | bytes 2359304 | tf_op jit(solution)/shard_map/ppermute | solution.py:883
  198.7 28.0 %collective-permute-start.39 = (bf16[8,48,1536]{2,1,0:T(8,128)(2,1)S(1)}, bf16[8,48,1536]{2,1,0:T(8,128)(2,1)S(1)}, u32[]{:S(2)}, u32[]{:S(2)}) collective-permute-start(bf16[8,48,1536]{2,1,0:T(8,128)(2,1)S(1)} %get-tuple-element.328), channel_id=1, source_target_pairs={{0,16},{1,17},{2,18},{3,19},{4,20},{5,21},{6,22},{7,23},{8,24},{9,... | collective-permute-start | bytes 3538952 | tf_op jit(solution)/shard_map/ppermute | solution.py:883
  200.1 18.8 %collective-permute-start.36 = (bf16[1,192,768]{2,1,0:T(8,128)(2,1)S(1)}, bf16[1,192,768]{2,1,0:T(8,128)(2,1)S(1)}, u32[]{:S(2)}, u32[]{:S(2)}) collective-permute-start(bf16[1,192,768]{2,1,0:T(8,128)(2,1)S(1)} %get-tuple-element.344), channel_id=1, source_target_pairs={{12,0},{13,1},{14,2},{15,3},{8,4},{9,5},{10,6},{11,7},{4,8},{5,9},... | collective-permute-start | bytes 884744 | tf_op jit(solution)/shard_map/ppermute | solution.py:883
  201.7 17.1 %collective-permute-start.35 = (bf16[1,192,768]{2,1,0:T(8,128)(2,1)S(1)}, bf16[1,192,768]{2,1,0:T(8,128)(2,1)S(1)}, u32[]{:S(2)}, u32[]{:S(2)}) collective-permute-start(bf16[1,192,768]{2,1,0:T(8,128)(2,1)S(1)} %get-tuple-element.343), channel_id=1, source_target_pairs={{4,0},{5,1},{6,2},{7,3},{12,4},{13,5},{14,6},{15,7},{0,8},{1,9},{2... | collective-permute-start | bytes 884744 | tf_op jit(solution)/shard_map/ppermute | solution.py:883
  218.2 19.4 %collective-permute-start.40 = (bf16[1,192,768]{2,1,0:T(8,128)(2,1)S(1)}, bf16[1,192,768]{2,1,0:T(8,128)(2,1)S(1)}, u32[]{:S(2)}, u32[]{:S(2)}) collective-permute-start(bf16[1,192,768]{2,1,0:T(8,128)(2,1)S(1)} %get-tuple-element.350), channel_id=1, source_target_pairs={{8,0},{9,1},{10,2},{11,3},{0,4},{1,5},{2,6},{3,7},{12,8},{13,9},{1... | collective-permute-start | bytes 884744 | tf_op jit(solution)/shard_map/ppermute | solution.py:883
  218.8 18.8 %collective-permute-start.38 = (bf16[1,48,2048]{2,1,0:T(8,128)(2,1)S(1)}, bf16[1,48,2048]{2,1,0:T(8,128)(2,1)S(1)}, u32[]{:S(2)}, u32[]{:S(2)}) collective-permute-start(bf16[1,48,2048]{2,1,0:T(8,128)(2,1)S(1)} %split.93), channel_id=1, source_target_pairs={{4,0},{5,1},{6,2},{7,3},{12,4},{13,5},{14,6},{15,7},{0,8},{1,9},{2... | collective-permute-start | bytes 589832 | tf_op jit(solution)/shard_map/ppermute | solution.py:883
  227.1 24.6 %collective-permute-start.33 = (bf16[4,160,768]{2,1,0:T(8,128)(2,1)S(1)}, bf16[4,160,768]{2,1,0:T(8,128)(2,1)S(1)}, u32[]{:S(2)}, u32[]{:S(2)}) collective-permute-start(bf16[4,160,768]{2,1,0:T(8,128)(2,1)S(1)} %slice.303), channel_id=1, source_target_pairs={{0,2},{1,3},{2,0},{3,1},{4,6},{5,7},{6,4},{7,5},{8,10},{9,11},{10,... | collective-permute-start | bytes 2949128 | tf_op jit(solution)/shard_map/ppermute | solution.py:883
  227.9 23.6 %collective-permute-start.37 = (bf16[8,48,1152]{2,1,0:T(8,128)(2,1)S(1)}, bf16[8,48,1152]{2,1,0:T(8,128)(2,1)S(1)}, u32[]{:S(2)}, u32[]{:S(2)}) collective-permute-start(bf16[8,48,1152]{2,1,0:T(8,128)(2,1)S(1)} %get-tuple-element.352), channel_id=1, source_target_pairs={{0,16},{1,17},{2,18},{3,19},{4,20},{5,21},{6,22},{7,23},{8,24},{9,... | collective-permute-start | bytes 2654216 | tf_op jit(solution)/shard_map/ppermute | solution.py:883
  237.6 6.9 %collective-permute-start.42 = (bf16[2,48,1536]{2,1,0:T(8,128)(2,1)S(1)}, bf16[2,48,1536]{2,1,0:T(8,128)(2,1)S(1)}, u32[]{:S(2)}, u32[]{:S(2)}) collective-permute-start(bf16[2,48,1536]{2,1,0:T(8,128)(2,1)S(1)} %split.92), channel_id=1, source_target_pairs={{4,0},{5,1},{6,2},{7,3},{12,4},{13,5},{14,6},{15,7},{0,8},{1,9},{2... | collective-permute-start | bytes 884744 | tf_op jit(solution)/shard_map/ppermute | solution.py:883
  237.6 9.0 %collective-permute-start.41 = (bf16[1,48,2048]{2,1,0:T(8,128)(2,1)S(1)}, bf16[1,48,2048]{2,1,0:T(8,128)(2,1)S(1)}, u32[]{:S(2)}, u32[]{:S(2)}) collective-permute-start(bf16[1,48,2048]{2,1,0:T(8,128)(2,1)S(1)} %fusion.8), channel_id=1, source_target_pairs={{4,0},{5,1},{6,2},{7,3},{12,4},{13,5},{14,6},{15,7},{0,8},{1,9},{2... | collective-permute-start | bytes 589832 | tf_op jit(solution)/shard_map/ppermute | solution.py:883
  244.6 6.9 %collective-permute-start.45 = (bf16[2,48,1536]{2,1,0:T(8,128)(2,1)S(1)}, bf16[2,48,1536]{2,1,0:T(8,128)(2,1)S(1)}, u32[]{:S(2)}, u32[]{:S(2)}) collective-permute-start(bf16[2,48,1536]{2,1,0:T(8,128)(2,1)S(1)} %fusion.4), channel_id=1, source_target_pairs={{4,0},{5,1},{6,2},{7,3},{12,4},{13,5},{14,6},{15,7},{0,8},{1,9},{2... | collective-permute-start | bytes 884744 | tf_op jit(solution)/shard_map/ppermute | solution.py:883
  251.8 12.8 %collective-permute-start.46 = (bf16[1,48,2048]{2,1,0:T(8,128)(2,1)S(1)}, bf16[1,48,2048]{2,1,0:T(8,128)(2,1)S(1)}, u32[]{:S(2)}, u32[]{:S(2)}) collective-permute-start(bf16[1,48,2048]{2,1,0:T(8,128)(2,1)S(1)} %fusion.7), channel_id=1, source_target_pairs={{4,0},{5,1},{6,2},{7,3},{12,4},{13,5},{14,6},{15,7},{0,8},{1,9},{2... | collective-permute-start | bytes 589832 | tf_op jit(solution)/shard_map/ppermute | solution.py:883
  254.1 15.8 %collective-permute-start.44 = (bf16[4,48,1152]{2,1,0:T(8,128)(2,1)S(1)}, bf16[4,48,1152]{2,1,0:T(8,128)(2,1)S(1)}, u32[]{:S(2)}, u32[]{:S(2)}) collective-permute-start(bf16[4,48,1152]{2,1,0:T(8,128)(2,1)S(1)} %slice.306), channel_id=1, source_target_pairs={{0,2},{1,3},{2,0},{3,1},{4,6},{5,7},{6,4},{7,5},{8,10},{9,11},{10,... | collective-permute-start | bytes 1327112 | tf_op jit(solution)/shard_map/ppermute | solution.py:883
  263.9 12.6 %collective-permute-start.43 = (bf16[2,160,768]{2,1,0:T(8,128)(2,1)S(1)}, bf16[2,160,768]{2,1,0:T(8,128)(2,1)S(1)}, u32[]{:S(2)}, u32[]{:S(2)}) collective-permute-start(bf16[2,160,768]{2,1,0:T(8,128)(2,1)S(1)} %slice.305), channel_id=1, source_target_pairs={{0,4},{1,5},{2,6},{3,7},{4,0},{5,1},{6,2},{7,3},{8,12},{9,13},{10,... | collective-permute-start | bytes 1474568 | tf_op jit(solution)/shard_map/ppermute | solution.py:883
  270.0 8.9 %collective-permute-start.47 = (bf16[2,48,1152]{2,1,0:T(8,128)(2,1)S(1)}, bf16[2,48,1152]{2,1,0:T(8,128)(2,1)S(1)}, u32[]{:S(2)}, u32[]{:S(2)}) collective-permute-start(bf16[2,48,1152]{2,1,0:T(8,128)(2,1)S(1)} %slice.308), channel_id=1, source_target_pairs={{0,4},{1,5},{2,6},{3,7},{4,0},{5,1},{6,2},{7,3},{8,12},{9,13},{10,... | collective-permute-start | bytes 663560 | tf_op jit(solution)/shard_map/ppermute | solution.py:883
  270.6 11.6 %collective-permute-start.50 = (bf16[2,48,1536]{2,1,0:T(8,128)(2,1)S(1)}, bf16[2,48,1536]{2,1,0:T(8,128)(2,1)S(1)}, u32[]{:S(2)}, u32[]{:S(2)}) collective-permute-start(bf16[2,48,1536]{2,1,0:T(8,128)(2,1)S(1)} %fusion), channel_id=1, source_target_pairs={{4,0},{5,1},{6,2},{7,3},{12,4},{13,5},{14,6},{15,7},{0,8},{1,9},{2... | collective-permute-start | bytes 884744 | tf_op jit(solution)/shard_map/ppermute | solution.py:883
  273.5 8.6 %collective-permute-start.55 = (bf16[192,768]{1,0:T(8,128)(2,1)S(1)}, bf16[192,768]{1,0:T(8,128)(2,1)S(1)}, u32[]{:S(2)}, u32[]{:S(2)}) collective-permute-start(bf16[192,768]{1,0:T(8,128)(2,1)S(1)} %fusion.9), channel_id=1, source_target_pairs={{1,17},{3,19},{5,21},{7,23},{9,25},{11,27},{13,29},{15,31},{16,0},... | collective-permute-start | bytes 884744 | tf_op jit(solution)/shard_map/ppermute | solution.py:883
  279.0 6.8 %collective-permute-start.49 = (bf16[1,48,1152]{2,1,0:T(8,128)(2,1)S(1)}, bf16[1,48,1152]{2,1,0:T(8,128)(2,1)S(1)}, u32[]{:S(2)}, u32[]{:S(2)}) collective-permute-start(bf16[1,48,1152]{2,1,0:T(8,128)(2,1)S(1)} %slice.310), channel_id=1, source_target_pairs={{0,8},{1,9},{2,10},{3,11},{4,12},{5,13},{6,14},{7,15},{8,0},{9,1},... | collective-permute-start | bytes 331784 | tf_op jit(solution)/shard_map/ppermute | solution.py:883
  280.1 10.9 %collective-permute-start.48 = (bf16[1,160,768]{2,1,0:T(8,128)(2,1)S(1)}, bf16[1,160,768]{2,1,0:T(8,128)(2,1)S(1)}, u32[]{:S(2)}, u32[]{:S(2)}) collective-permute-start(bf16[1,160,768]{2,1,0:T(8,128)(2,1)S(1)} %slice.307), channel_id=1, source_target_pairs={{0,8},{1,9},{2,10},{3,11},{4,12},{5,13},{6,14},{7,15},{8,0},{9,1},... | collective-permute-start | bytes 737288 | tf_op jit(solution)/shard_map/ppermute | solution.py:883
  282.4 5.8 %collective-permute-start.51 = (bf16[1,48,1536]{2,1,0:T(8,128)(2,1)S(1)}, bf16[1,48,1536]{2,1,0:T(8,128)(2,1)S(1)}, u32[]{:S(2)}, u32[]{:S(2)}) collective-permute-start(bf16[1,48,1536]{2,1,0:T(8,128)(2,1)S(1)} %slice.309), channel_id=1, source_target_pairs={{0,2},{1,3},{2,0},{3,1},{4,6},{5,7},{6,4},{7,5},{8,10},{9,11},{10,... | collective-permute-start | bytes 442376 | tf_op jit(solution)/shard_map/ppermute | solution.py:883
  288.3 6.5 %collective-permute-start.53 = (f32[24,1920]{1,0:T(8,128)S(1)}, f32[24,1920]{1,0:T(8,128)S(1)}, u32[]{:S(2)}, u32[]{:S(2)}) collective-permute-start(f32[24,1920]{1,0:T(8,128)S(1)} %slice.241), channel_id=1, source_target_pairs={{0,1},{1,0},{2,3},{3,2},{4,5},{5,4},{6,7},{7,6},{8,9},{9,8},{10,11... | collective-permute-start | bytes 552968 | tf_op jit(solution)/shard_map/ppermute | solution.py:883
  288.3 4.4 %collective-permute-start.54 = (f32[24,1536]{1,0:T(8,128)S(1)}, f32[24,1536]{1,0:T(8,128)S(1)}, u32[]{:S(2)}, u32[]{:S(2)}) collective-permute-start(f32[24,1536]{1,0:T(8,128)S(1)} %get-tuple-element.366), channel_id=1, source_target_pairs={{0,1},{1,0},{2,3},{3,2},{4,5},{5,4},{6,7},{7,6},{8,9},{9,8},{10,11... | collective-permute-start | bytes 442376 | tf_op jit(solution)/shard_map/ppermute | solution.py:883
  288.9 3.0 %collective-permute-start.52 = (f32[24,1152]{1,0:T(8,128)S(1)}, f32[24,1152]{1,0:T(8,128)S(1)}, u32[]{:S(2)}, u32[]{:S(2)}) collective-permute-start(f32[24,1152]{1,0:T(8,128)S(1)} %get-tuple-element.367), channel_id=1, source_target_pairs={{0,1},{1,0},{2,3},{3,2},{4,5},{5,4},{6,7},{7,6},{8,9},{9,8},{10,11... | collective-permute-start | bytes 331784 | tf_op jit(solution)/shard_map/ppermute | solution.py:883
  292.7 3.4 %collective-permute-start.56 = (f32[96,768]{1,0:T(8,128)S(1)}, f32[96,768]{1,0:T(8,128)S(1)}, u32[]{:S(2)}, u32[]{:S(2)}) collective-permute-start(f32[96,768]{1,0:T(8,128)S(1)} %slice_select_fusion), channel_id=1, source_target_pairs={{0,1},{2,3},{4,5},{6,7},{8,9},{10,11},{12,13},{14,15},{17,16},{19,... | collective-permute-start | bytes 884744 | tf_op jit(solution)/shard_map/ppermute | solution.py:883
  (5 other events, 3.6 us)

commit v3 on v2

--- a/solution.py
+++ b/solution.py
@@ -15,19 +15,20 @@
 BF = jnp.bfloat16
 F32 = jnp.float32
 FAR = -1e30
+NOTE = 16
 ONES = 64
 
 
 ORDERS = {"X": "hx", "Q": "Zyx", "U": "hyx", "G": "xzy", "D": "xz", "d": "xZ", "g": "yzx", "u": "yxz", "q": "yxh", "r": "xyZ", "x": "h"}
 STREAMS = "XPQUGDCdguqx"
 SEQUENCE = [
-    1, 2, 81, 17, 82, 18, 83, -82, 49, 33, -2, 11, 34, -33, -83, 65, 97, -97,
-    84, 43, 4, -84, 58, 66, 85, -34, -35, -50, 51, 36, -4, -36, 37, 67, 5, -5,
-    -51, 52, -67, 86, 76, 200, -37, 201, 69, 202, 203, -86, 95, -203, -68, -203, -52, -203,
-    53, 204, -69, 205, -53, -87, 206, 207, -207, 208, -207, 209, -207, 210, 212, 213, 145, 211,
-    129, 113, 214, -113, -145, 114, 115, 146, 177, 178, -177, 124, -114, -115, 147, 161, -146, -116,
-    -129, 130, 148, -147, -130, 131, -178, 157, -161, 162, 179, -162, -131, -149, 163, 140, 117, 172,
-    -179, 188, -132, -163, 133, -164, -133, 150, 134, 165, -117, -134, 118, -150, -118, -165, -148,
+    1, 2, 81, 17, 18, 82, 83, -82, 49, 11, 33, -83, 65, 97, 34, -49, -97, 84,
+    43, 4, 58, -50, -84, 66, 85, -34, -35, 51, 36, 37, 67, 5, -36, -4, 52, 86,
+    -67, -5, 76, 200, 201, 95, 69, 202, 203, -203, -52, -203, -68, 53, 204, -85, -53, 205,
+    206, -87, -69, 207, 208, -207, 209, -207, 212, 213, 145, 210, 211, 129, 113, 214, -145, 114,
+    -113, 115, 146, 177, -177, 124, 178, -114, -115, 147, 161, -146, -116, -129, 130, 148, -147, 131,
+    -178, 157, 162, 179, -162, -131, -149, 163, -130, 140, 117, 172, -179, 188, 133, -132, -163, 165,
+    150, -133, 134, 118, -150, -134, -165, -117, -148,
 ]
 
 
@@ -102,26 +103,33 @@
     return [pltpu.with_memory_space_constraint(a, pltpu.HBM) for a in arrays]
 
 
-def message_kernel(x_ref, ids_ref, mask_ref, out_ref):
-    local, width = x_ref.shape
+def message_kernel(x_ref, ids_ref, mask_ref, down_ref, out_ref, low_ref, note_s):
+    local = x_ref.shape[0]
+    note_s[...] = jnp.zeros(note_s.shape, F32)
+    note_s[0:1, :local] = ids_ref[...].astype(F32)
+    note_s[1:2, :local] = mask_ref[...].astype(F32)
     out_ref[:local] = x_ref[...]
-    out_ref[local:] = jnp.zeros((8, width), BF)
-    out_ref[local : local + 1, :local] = ids_ref[...].astype(F32).astype(BF)
-    out_ref[local + 1 : local + 2, :local] = mask_ref[...].astype(F32).astype(BF)
-
-
-def make_message(tokens, ids, mask):
+    out_ref[local:] = note_s[...].astype(BF)
+    low_ref[...] = down_ref[0].astype(BF)
+
+
+def make_message(tokens, ids, mask, down):
     local, width = tokens.shape
+    args = [tokens, ids.reshape(1, local), mask.reshape(1, local), down]
     return pl.pallas_call(
         message_kernel,
-        out_shape=like(local + 8, width, dtype=BF),
+        grid=(1,),
+        in_specs=[whole(a.shape) for a in args],
+        out_specs=[whole((local + NOTE, width)), whole(down.shape[1:])],
+        out_shape=[like(local + NOTE, width, dtype=BF), like(*down.shape[1:], dtype=BF)],
+        scratch_shapes=[pltpu.VMEM((NOTE, width), F32)],
         compiler_params=params(8),
         cost_estimate=pl.CostEstimate(flops=1, bytes_accessed=1, transcendentals=0),
         name="message",
-    )(tokens, ids.reshape(1, local), mask.reshape(1, local))
-
-
-def columns_kernel(me_ref, qkv_ref, up_ref, out_w_ref, gate_ref, gain_ref, bias_ref, mine_ref, theirs_ref):
+    )(*kept_far(*args))
+
+
+def columns_kernel(me_ref, qkv_ref, up_ref, out_w_ref, gate_ref, gain_ref, bias_ref, mine_ref, theirs_ref, ext_s):
     c = me_ref[3]
     rows = qkv_ref.shape[1]
 
@@ -137,11 +145,11 @@
     halves(up_ref, 0, ff, to)
     halves(out_w_ref, 0, 384, to + ff)
     halves(gate_ref, 0, ff, to + ff + 512)
+    ext_s[...] = jnp.zeros(ext_s.shape, F32)
+    ext_s[0:2, :rows] = gain_ref[0]
+    ext_s[2:4, :rows] = bias_ref[0]
     for target in (mine_ref, theirs_ref):
-        ext = slice(to + ff + 384, to + ff + 512)
-        target[:, ext] = jnp.zeros((rows, 128), BF)
-        target[0:2, to + ff + 384 : to + ff + 384 + rows] = gain_ref[0].astype(BF)
-        target[2:4, to + ff + 384 : to + ff + 384 + rows] = bias_ref[0].astype(BF)
+        target[:, to + ff + 384 : to + ff + 512] = ext_s[...].astype(BF)
 
 
 def make_columns(me, qkv, up, out_w, gate, gain, bias):
@@ -154,10 +162,11 @@
         in_specs=[scalars()] + [whole(a.shape) for a in args],
         out_specs=[whole(shape.shape)] * 2,
         out_shape=[shape] * 2,
+        scratch_shapes=[pltpu.VMEM((rows, 128), F32)],
         compiler_params=params(12),
         cost_estimate=pl.CostEstimate(flops=1, bytes_accessed=1, transcendentals=0),
         name="columns",
-    )(me, *args)
+    )(me, *kept_far(*args))
 
 
 def angle_table(count, stride):
@@ -228,11 +237,11 @@
 
 def rank(me, numbers, along, beside):
     chips, padded, width = along.shape
-    local = padded - 8
+    local = padded - NOTE
     count = chips * 2 * local
     step = 4 * local
     coarse = max(64, 1 << (-(-count // 64) - 1).bit_length())
-    note = pl.BlockSpec((chips, 8, width), lambda i: (0, local // 8, 0))
+    note = pl.BlockSpec((chips, NOTE, width), lambda i: (0, local // NOTE, 0))
     rows = pl.BlockSpec((step, 128), lambda i: (i, 0))
     return pl.pallas_call(
         functools.partial(rank_kernel, numbers=numbers, coarse=coarse),
@@ -401,7 +410,7 @@
     pieces = refs[:n]
     ob_ref, got_ref, sib_ref, along_ref, beside_ref = refs[n : n + 5]
     n1_ref, f1_ref, h1_ref, up_ref, all_ref, out_ref, up_w_ref, norm_ref = refs[n + 5 :]
-    local = along_ref.shape[1] - 8
+    local = along_ref.shape[1] - NOTE
     c = me_ref[3]
     ff = up_ref.shape[1]
     at = places(me_ref)
@@ -411,10 +420,10 @@
     for piece in pieces:
         for i in range(piece.shape[0]):
             rows = pl.ds(pl.multiple_of(at[done] * per, 16), per)
+            block = piece[i, :, ff + 384 : ff + 512].astype(F32)
             for d in range(per // share_rows):
-                ext = piece[i, d * share_rows : d * share_rows + 4, ff + 384 : ff + 512].astype(F32)
-                ext = jnp.concatenate([ext, jnp.zeros((4, width - 128), F32)], axis=1)
-                ext = jnp.concatenate([ext, jnp.zeros((4, width), F32)], axis=0)
+                ext = jnp.concatenate([block[d * share_rows :][:4], jnp.zeros((4, 128), F32)], axis=0)
+                ext = jnp.concatenate([ext, jnp.zeros((8, width - 128), F32)], axis=1)
                 norm = norm + pltpu.roll(ext, (at[done] * (per // share_rows) + d) * share_rows, 1)
             up_w_ref[rows, :] = piece[i, :, :ff]
             out_ref[c, rows, :] = piece[i, :, ff : ff + 384]
@@ -643,12 +652,12 @@
     lane = lanes((4, 128))
     for i in range(2 * half):
         ref, k = (mine_ref, i) if i < half else (theirs_ref, i - half)
-        ref[k, :, ff + 384 :] = jnp.zeros((per, 128), ref.dtype)
+        blocks = []
         for d in range(per // share_rows):
             device = at[i] * (per // share_rows) + d
             turn = pltpu.roll(sums, width - device * share_rows, 1)[:4, :128]
-            block = jnp.where(lane < share_rows, turn, 0.0)
-            ref[k, d * share_rows : d * share_rows + 4, ff + 384 :] = block.astype(ref.dtype)
+            blocks += [jnp.where(lane < share_rows, turn, 0.0), jnp.zeros((share_rows - 4, 128), F32)]
+        ref[k, :, ff + 384 :] = jnp.concatenate(blocks, axis=0).astype(ref.dtype)
 
 
 def grad_up(me, places, per, share_rows, h1, dup, ob_all, da, one, two):
@@ -992,7 +1001,7 @@
     direct = two % 16 == 0
 
     def tokens_task():
-        message = yield "work", make_message, tokens, segment_ids, pad_mask
+        message, grid.results["down"] = yield "work", make_message, tokens, segment_ids, pad_mask, w_down
         along = jnp.concatenate((yield from grid.gather(message, orders["X"])), axis=0)
         return along, (yield "move", "c", along)
 
@@ -1010,7 +1019,7 @@
         return pieces, (yield "move", "c", outs)
 
     def down_task(order):
-        part = yield "work", lambda w: w.astype(BF), w_down[0]
+        part = yield "work", lambda w: w, grid.results["down"]
         part = grid.ordered(c, part, (yield "move", "c", part), 0)
         part = jnp.where(c == y, part, (yield "move", "spread", part))
         return (yield from grid.gather(part, order))
@@ -1166,11 +1175,11 @@
     start("X", tokens_task())
     start("P", columns_task())
     later = {
+        "D": lambda: down_task(orders["D"]),
         "Q": lambda: grid.gather(shard(0, 1152), orders["Q"]),
         "U": lambda: up_task(orders["U"]),
         "G": lambda: grid.gather(shard(1152 + ff + 512, ff), orders["G"]),
     }
-    start("D", down_task(orders["D"]))
     start("C", cot_task())
     single = [
         rank_, project_, attend_, ob_move, mid_, gate_, down_, part_move, turn_, back_move, grad_d, grad_g,

time: 300 us -> 301 us (level); the launches traced: 297 us -> 301 us
  waiting for transfers between devices: 129 us -> 149 us
  starting transfers between devices: 72.9 us -> 63.6 us
  local copies, waits for them, and re-layouts: 8.8 us -> 1.41 us
    ppermute x57, waiting for transfers between devices: 129 us -> 149 us  [move(): got = self.moved[self.label] = lax.ppermute(a, AXES, self.across[way])]
    ppermute x57, starting transfers between devices: 72.9 us -> 63.6 us  [move(): got = self.moved[self.label] = lax.ppermute(a, AXES, self.across[way])]
    unnamed x30 -> x12, local copies, waits for them, and re-layouts: 7.51 us -> 0.12 us
  transfers between devices with their start and end apart: 57 -> 57, of which waited for: 29 -> 30; matrix products, arithmetic and copies ran while one was open for 3% -> 3% of each run, Pallas kernels for 22% -> 22%
where the time goes in v3:
time: 301 us
  waiting for transfers between devices  149 us (50%)
  Pallas kernels  76.6 us (25%)
  starting transfers between devices  63.6 us (21%)
  other arithmetic  8.95 us (3%)
    ppermute x57, waiting for transfers between devices, move(): got = self.moved[self.label] = lax.ppermute(a, AXES, self.across[way])  149 us
    ppermute x57, starting transfers between devices, move(): got = self.moved[self.label] = lax.ppermute(a, AXES, self.across[way])  63.6 us
    pallas_call x1, Pallas kernels, attend_back(): pl.pallas_call(functools.partial(attend_back_kernel, places=places, per=p...  26.9 us
    pallas_call x1, Pallas kernels, attend(): pl.pallas_call(functools.partial(attend_kernel, chunk=512), grid=(3,), in...  10.3 us
    pallas_call x1, Pallas kernels, rank(): pl.pallas_call(functools.partial(rank_kernel, numbers=numbers, coarse=coa...  8.45 us
    pallas_call x1, Pallas kernels, project(): pl.pallas_call(functools.partial(project_kernel, places=places, per=per,...  8.21 us
  transfers between devices with their start and end apart: 57, of which 30 were waited for; matrix products, arithmetic and copies ran while one was open for 3% of the time, Pallas kernels for 22%

profile of v3, /device:TPU:0, one launch (start us, length us, event | category | flops | bytes accessed | tf_op | source)
XLA Modules:
  0.0 301.0 jit_solution(7609024271746146784)
XLA Ops:
  1.8 4.1 %collective-permute-start.3 = (bf16[1,176,768]{2,1,0:T(8,128)(2,1)S(1)}, bf16[1,176,768]{2,1,0:T(8,128)(2,1)S(1)}, u32[]{:S(2)}, u32[]{:S(2)}) collective-permute-start(bf16[1,176,768]{2,1,0:T(8,128)(2,1)S(1)} %bitcast.58), channel_id=1, source_target_pairs={{0,8},{1,9},{2,10},{3,11},{4,12},{5,13},{6,14},{7,15},{8,0},{9,1},... | collective-permute-start | bytes 811016 | tf_op jit(solution)/shard_map/ppermute | solution.py:892
  6.0 1.2 columns.1
  9.0 3.4 %collective-permute-start.1 = (bf16[192,768]{1,0:T(8,128)(2,1)S(1)}, bf16[192,768]{1,0:T(8,128)(2,1)S(1)}, u32[]{:S(2)}, u32[]{:S(2)}) collective-permute-start(bf16[192,768]{1,0:T(8,128)(2,1)S(1)} %maximum_select_fusion), channel_id=1, source_target_pairs={{0,16},{2,18},{4,20},{6,22},{8,24},{10,26},{12,28},{14,30},{17,1},... | collective-permute-start | bytes 884744 | tf_op jit(solution)/shard_map/ppermute | solution.py:892
  13.0 10.2 %collective-permute-done.3 = bf16[1,176,768]{2,1,0:T(8,128)(2,1)S(1)} collective-permute-done((bf16[1,176,768]{2,1,0:T(8,128)(2,1)S(1)}, bf16[1,176,768]{2,1,0:T(8,128)(2,1)S(1)}, u32[]{:S(2)}, u32[]{:S(2)}) %collective-permute-start.3) | collective-permute-done | bytes 270368 | tf_op jit(solution)/shard_map/ppermute | solution.py:892
  23.4 3.4 %collective-permute-start.8 = (bf16[2,176,768]{2,1,0:T(8,128)(2,1)S(1)}, bf16[2,176,768]{2,1,0:T(8,128)(2,1)S(1)}, u32[]{:S(2)}, u32[]{:S(2)}) collective-permute-start(bf16[2,176,768]{2,1,0:T(8,128)(2,1)S(1)} %pad_maximum_fusion.6), channel_id=1, source_target_pairs={{0,4},{1,5},{2,6},{3,7},{4,0},{5,1},{6,2},{7,3},{8,12},{9,13},{10,... | collective-permute-start | bytes 1622024 | tf_op jit(solution)/shard_map/ppermute | solution.py:892
  26.8 2.3 collective-permute-done.16
  29.2 1.9 collective-permute-start.7
  31.0 3.2 %collective-permute-start.11 = (bf16[1,48,1152]{2,1,0:T(8,128)(2,1)S(1)}, bf16[1,48,1152]{2,1,0:T(8,128)(2,1)S(1)}, u32[]{:S(2)}, u32[]{:S(2)}) collective-permute-start(bf16[1,48,1152]{2,1,0:T(8,128)(2,1)S(1)} %get-tuple-element.213), channel_id=1, source_target_pairs={{0,12},{1,13},{2,14},{3,15},{4,8},{5,9},{6,10},{7,11},{8,4},{9,5},... | collective-permute-start | bytes 331784 | tf_op jit(solution)/shard_map/ppermute | solution.py:892
  34.9 6.3 %collective-permute-done.8 = bf16[2,176,768]{2,1,0:T(8,128)(2,1)S(1)} collective-permute-done((bf16[2,176,768]{2,1,0:T(8,128)(2,1)S(1)}, bf16[2,176,768]{2,1,0:T(8,128)(2,1)S(1)}, u32[]{:S(2)}, u32[]{:S(2)}) %collective-permute-start.8) | collective-permute-done | bytes 540704 | tf_op jit(solution)/shard_map/ppermute | solution.py:892
  42.2 1.6 collective-permute-start.14
  44.0 1.4 collective-permute-done.12
  45.5 8.2 %collective-permute-done.9 = bf16[2,48,2048]{2,1,0:T(8,128)(2,1)S(1)} collective-permute-done((bf16[2,48,2048]{2,1,0:T(8,128)(2,1)S(1)}, bf16[2,48,2048]{2,1,0:T(8,128)(2,1)S(1)}, u32[]{:S(2)}, u32[]{:S(2)}) %collective-permute-start.9) | collective-permute-done | bytes 393248 | tf_op jit(solution)/shard_map/ppermute | solution.py:892
  53.8 1.6 collective-permute-start.17
  55.5 10.4 %collective-permute-done.17 = bf16[4,48,1152]{2,1,0:T(8,128)(2,1)S(1)} collective-permute-done((bf16[4,48,1152]{2,1,0:T(8,128)(2,1)S(1)}, bf16[4,48,1152]{2,1,0:T(8,128)(2,1)S(1)}, u32[]{:S(2)}, u32[]{:S(2)}) %collective-permute-start.17) | collective-permute-done | bytes 442400 | tf_op jit(solution)/shard_map/ppermute | solution.py:892
  67.3 1.3 collective-permute-start.13
  68.6 1.7 collective-permute-start.10
  70.3 4.8 %collective-permute-start.19 = (bf16[2,48,1536]{2,1,0:T(8,128)(2,1)S(1)}, bf16[2,48,1536]{2,1,0:T(8,128)(2,1)S(1)}, u32[]{:S(2)}, u32[]{:S(2)}) collective-permute-start(bf16[2,48,1536]{2,1,0:T(8,128)(2,1)S(1)} %collective-permute-done.15), channel_id=1, source_target_pairs={{0,4},{1,5},{2,6},{3,7},{4,12},{5,13},{6,14},{7,15},{8,0},{9,1},{1... | collective-permute-start | bytes 884744 | tf_op jit(solution)/shard_map/ppermute | solution.py:892
  75.0 1.5 collective-permute-start.21
  76.5 10.7 %collective-permute-done.13 = bf16[4,48,2048]{2,1,0:T(8,128)(2,1)S(1)} collective-permute-done((bf16[4,48,2048]{2,1,0:T(8,128)(2,1)S(1)}, bf16[4,48,2048]{2,1,0:T(8,128)(2,1)S(1)}, u32[]{:S(2)}, u32[]{:S(2)}) %collective-permute-start.13) | collective-permute-done | bytes 786464 | tf_op jit(solution)/shard_map/ppermute | solution.py:892
  87.4 1.2 collective-permute-start.25
  88.8 1.5 collective-permute-start.18
  90.4 4.3 %collective-permute-done.19 = bf16[2,48,1536]{2,1,0:T(8,128)(2,1)S(1)} collective-permute-done((bf16[2,48,1536]{2,1,0:T(8,128)(2,1)S(1)}, bf16[2,48,1536]{2,1,0:T(8,128)(2,1)S(1)}, u32[]{:S(2)}, u32[]{:S(2)}) %collective-permute-start.19) | collective-permute-done | bytes 294944 | tf_op jit(solution)/shard_map/ppermute | solution.py:892
  95.3 8.5 %rank.1 = (bf16[768,2560]{1,0:T(8,128)(2,1)}, f32[2560,128]{1,0:T(8,128)}, f32[2560,128]{1,0:T(8,128)}, bf16[2560,128]{1,0:T(8,128)(2,1)}, f32[320,128]{1,0:T(8,128)S(1)}) custom-call(s32[4]{0:T(128)S(1)} %pad_add_fusion.me_ref, bf16[8,176,768]{2,1,0:T(8,128)(2,1)S(1)} %pad_maximum_fusion.along_ref.note_a_ref.refs_2_.refs_5_, ...), custom_call_target="tpu_custom_call" | custom-call | flops 1 | bytes 1 | tf_op jit(solution)/shard_map/rank/pallas_call | solution.py:246
  103.7 8.2 %project.1 = (bf16[320,384]{1,0:T(8,128)(2,1)}, bf16[3,2560,128]{2,1,0:T(8,128)(2,1)}, bf16[3,2560,128]{2,1,0:T(8,128)(2,1)}, bf16[768,1152]{1,0:T(8,128)(2,1)}) custom-call(s32[4]{0:T(128)S(1)} %pad_add_fusion.me_ref, bf16[8,48,1152]{2,1,0:T(8,128)(2,1)S(1)} %constant_dynamic-update-slice_fusion.refs_0_, ...), custom_call_target="tpu_custom_call" | custom-call | flops 1 | bytes 1 | tf_op jit(solution)/shard_map/project/pallas_call | solution.py:306
  112.0 2.0 collective-permute-done.23
  114.0 1.6 collective-permute-start.24
  115.6 10.3 %attend.1 = (f32[320,384]{1,0:T(8,128)}, bf16[320,384]{1,0:T(8,128)(2,1)S(1)}, bf16[6,320,128]{2,1,0:T(8,128)(2,1)}) custom-call(bf16[320,384]{1,0:T(8,128)(2,1)} %get-tuple-element.334.q_ref, bf16[3,2560,128]{2,1,0:T(8,128)(2,1)} %get-tuple-element.338.k_ref, bf16[3,2560,128]{2,1,0:T(8,128)(2,1)} %get-tuple-element.339.v_ref, ...), custom_call_target="tpu_custom_call" | custom-call | flops 5033164800 | bytes 7864320 | tf_op jit(solution)/shard_map/attend/pallas_call | solution.py:355
  125.9 4.0 %collective-permute-done.25.refs_1_ = bf16[8,48,2048]{2,1,0:T(8,128)(2,1)S(1)} collective-permute-done((bf16[8,48,2048]{2,1,0:T(8,128)(2,1)S(1)}, bf16[8,48,2048]{2,1,0:T(8,128)(2,1)S(1)}, u32[]{:S(2)}, u32[]{:S(2)}) %collective-permute-start.25) | collective-permute-done | bytes 1572896 | tf_op jit(solution)/shard_map/ppermute | solution.py:892
  130.1 2.0 collective-permute-start.22
  132.1 2.8 mid.1
  134.9 5.9 %collective-permute-done.24.refs_1_ = bf16[8,48,1536]{2,1,0:T(8,128)(2,1)S(1)} collective-permute-done((bf16[8,48,1536]{2,1,0:T(8,128)(2,1)S(1)}, bf16[8,48,1536]{2,1,0:T(8,128)(2,1)S(1)}, u32[]{:S(2)}, u32[]{:S(2)}) %collective-permute-start.24) | collective-permute-done | bytes 1179680 | tf_op jit(solution)/shard_map/ppermute | solution.py:892
  140.7 1.8 gate_up.1
  142.5 4.2 %collective-permute-done.22.refs_3_ = bf16[2,192,768]{2,1,0:T(8,128)(2,1)S(1)} collective-permute-done((bf16[2,192,768]{2,1,0:T(8,128)(2,1)S(1)}, bf16[2,192,768]{2,1,0:T(8,128)(2,1)S(1)}, u32[]{:S(2)}, u32[]{:S(2)}) %collective-permute-start.22) | collective-permute-done | bytes 589856 | tf_op jit(solution)/shard_map/ppermute | solution.py:892
  146.7 1.6 down.1
  148.4 2.6 collective-permute-done.28.got_ref
  151.0 4.7 %turn.1 = (bf16[160,768]{1,0:T(8,128)(2,1)}, f32[320,768]{1,0:T(8,128)S(1)}, bf16[320,768]{1,0:T(8,128)(2,1)S(1)}, bf16[320,1536]{1,0:T(8,128)(2,1)S(1)}, bf16[3...) custom-call(f32[320,768]{1,0:T(8,128)S(1)} %get-tuple-element.279.part_ref, ...), custom_call_target="tpu_custom_call" | custom-call | flops 2264924160 | bytes 20971520 | tf_op jit(solution)/shard_map/turn/pallas_call | solution.py:555
  155.8 2.4 collective-permute-done.29.got_ref
  158.3 1.7 back.1
  159.9 2.7 grad_up.1
  163.2 2.2 grad.2
  165.4 3.0 grad.3
  168.4 1.6 collective-permute-start.31
  170.0 26.9 %attend_back.1 = (f32[8,160,768]{2,1,0:T(8,128)S(1)}, bf16[8,160,768]{2,1,0:T(8,128)(2,1)S(1)}, f32[8,48,1152]{2,1,0:T(8,128)S(1)}, bf16[8,48,1152]{2,1,0:T(8,128)(2,1)S(1)}) custom-call(s32[4]{0:T(128)S(1)} %pad_add_fusion.me_ref, bf16[320,384]{1,0:T(8,128)(2,1)} %get-tuple-element.334.q_ref, bf16[6,320,128]{2,1,0:T(8,128)(2,1)} %get-tuple-element.335.lse_ref, ...), custom_call_target="tpu_custom_call" | custom-call | flops 20132659200 | bytes 12288000 | tf_op jit(solution)/shard_map/attend_back/pallas_call | solution.py:753
  197.4 1.7 collective-permute-done.30
  199.8 1.6 collective-permute-start.34
  201.8 1.5 collective-permute-start.36
  204.1 15.6 %collective-permute-done.34 = bf16[4,48,2048]{2,1,0:T(8,128)(2,1)S(1)} collective-permute-done((bf16[4,48,2048]{2,1,0:T(8,128)(2,1)S(1)}, bf16[4,48,2048]{2,1,0:T(8,128)(2,1)S(1)}, u32[]{:S(2)}, u32[]{:S(2)}) %collective-permute-start.34) | collective-permute-done | bytes 786464 | tf_op jit(solution)/shard_map/ppermute | solution.py:892
  221.5 2.3 collective-permute-start.38
  223.8 5.5 %collective-permute-done.39 = bf16[8,48,1536]{2,1,0:T(8,128)(2,1)S(1)} collective-permute-done((bf16[8,48,1536]{2,1,0:T(8,128)(2,1)S(1)}, bf16[8,48,1536]{2,1,0:T(8,128)(2,1)S(1)}, u32[]{:S(2)}, u32[]{:S(2)}) %collective-permute-start.39) | collective-permute-done | bytes 1179680 | tf_op jit(solution)/shard_map/ppermute | solution.py:892
  230.9 14.8 %collective-permute-done.40 = bf16[1,192,768]{2,1,0:T(8,128)(2,1)S(1)} collective-permute-done((bf16[1,192,768]{2,1,0:T(8,128)(2,1)S(1)}, bf16[1,192,768]{2,1,0:T(8,128)(2,1)S(1)}, u32[]{:S(2)}, u32[]{:S(2)}) %collective-permute-start.40) | collective-permute-done | bytes 294944 | tf_op jit(solution)/shard_map/ppermute | solution.py:892
  246.0 6.4 %collective-permute-done.42 = bf16[2,48,1536]{2,1,0:T(8,128)(2,1)S(1)} collective-permute-done((bf16[2,48,1536]{2,1,0:T(8,128)(2,1)S(1)}, bf16[2,48,1536]{2,1,0:T(8,128)(2,1)S(1)}, u32[]{:S(2)}, u32[]{:S(2)}) %collective-permute-start.42) | collective-permute-done | bytes 294944 | tf_op jit(solution)/shard_map/ppermute | solution.py:892
  253.4 1.7 collective-permute-done.41
  255.2 7.3 %collective-permute-done.45 = bf16[2,48,1536]{2,1,0:T(8,128)(2,1)S(1)} collective-permute-done((bf16[2,48,1536]{2,1,0:T(8,128)(2,1)S(1)}, bf16[2,48,1536]{2,1,0:T(8,128)(2,1)S(1)}, u32[]{:S(2)}, u32[]{:S(2)}) %collective-permute-start.45) | collective-permute-done | bytes 294944 | tf_op jit(solution)/shard_map/ppermute | solution.py:892
  262.8 2.1 collective-permute-start.46
  266.6 4.4 %collective-permute-done.46 = bf16[1,48,2048]{2,1,0:T(8,128)(2,1)S(1)} collective-permute-done((bf16[1,48,2048]{2,1,0:T(8,128)(2,1)S(1)}, bf16[1,48,2048]{2,1,0:T(8,128)(2,1)S(1)}, u32[]{:S(2)}, u32[]{:S(2)}) %collective-permute-start.46) | collective-permute-done | bytes 196640 | tf_op jit(solution)/shard_map/ppermute | solution.py:892
  271.6 1.6 collective-permute-done.44
  273.6 1.3 collective-permute-start.50
  274.9 1.3 collective-permute-start.55
  276.2 5.6 %collective-permute-done.43 = bf16[2,160,768]{2,1,0:T(8,128)(2,1)S(1)} collective-permute-done((bf16[2,160,768]{2,1,0:T(8,128)(2,1)S(1)}, bf16[2,160,768]{2,1,0:T(8,128)(2,1)S(1)}, u32[]{:S(2)}, u32[]{:S(2)}) %collective-permute-start.43) | collective-permute-done | bytes 491552 | tf_op jit(solution)/shard_map/ppermute | solution.py:892
  281.9 2.2 collective-permute-done.47
  285.3 1.9 collective-permute-start.48
  287.5 1.2 collective-permute-start.53
  288.7 4.5 %collective-permute-done.49 = bf16[1,48,1152]{2,1,0:T(8,128)(2,1)S(1)} collective-permute-done((bf16[1,48,1152]{2,1,0:T(8,128)(2,1)S(1)}, bf16[1,48,1152]{2,1,0:T(8,128)(2,1)S(1)}, u32[]{:S(2)}, u32[]{:S(2)}) %collective-permute-start.49) | collective-permute-done | bytes 110624 | tf_op jit(solution)/shard_map/ppermute | solution.py:892
  294.1 2.3 collective-permute-start.56
  (153 shorter events, 26.0 us)
Async XLA Ops:
  1.8 21.4 %collective-permute-start.3 = (bf16[1,176,768]{2,1,0:T(8,128)(2,1)S(1)}, bf16[1,176,768]{2,1,0:T(8,128)(2,1)S(1)}, u32[]{:S(2)}, u32[]{:S(2)}) collective-permute-start(bf16[1,176,768]{2,1,0:T(8,128)(2,1)S(1)} %bitcast.58), channel_id=1, source_target_pairs={{0,8},{1,9},{2,10},{3,11},{4,12},{5,13},{6,14},{7,15},{8,0},{9,1},... | collective-permute-start | bytes 811016 | tf_op jit(solution)/shard_map/ppermute | solution.py:892
  7.2 5.3 %collective-permute-start.2 = (bf16[24,4736]{1,0:T(8,128)(2,1)S(1)}, bf16[24,4736]{1,0:T(8,128)(2,1)S(1)}, u32[]{:S(2)}, u32[]{:S(2)}) collective-permute-start(bf16[24,4736]{1,0:T(8,128)(2,1)S(1)} %get-tuple-element.203), channel_id=1, source_target_pairs={{0,1},{1,0},{2,3},{3,2},{4,5},{5,4},{6,7},{7,6},{8,9},{9,8},{10,11... | collective-permute-start | bytes 681992 | tf_op jit(solution)/shard_map/ppermute | solution.py:892
  7.3 1.7 collective-permute-start
  9.0 20.2 %collective-permute-start.1 = (bf16[192,768]{1,0:T(8,128)(2,1)S(1)}, bf16[192,768]{1,0:T(8,128)(2,1)S(1)}, u32[]{:S(2)}, u32[]{:S(2)}) collective-permute-start(bf16[192,768]{1,0:T(8,128)(2,1)S(1)} %maximum_select_fusion), channel_id=1, source_target_pairs={{0,16},{2,18},{4,20},{6,22},{8,24},{10,26},{12,28},{14,30},{17,1},... | collective-permute-start | bytes 884744 | tf_op jit(solution)/shard_map/ppermute | solution.py:892
  12.5 18.5 %copy-start = (bf16[160,768]{1,0:T(8,128)(2,1)S(1)}, bf16[160,768]{1,0:T(8,128)(2,1)}, u32[]{:S(2)}) copy-start(bf16[160,768]{1,0:T(8,128)(2,1)} %cot_ref) | copy-start | bytes 737284
  12.5 16.6 %collective-permute-start.4 = (bf16[1,48,2048]{2,1,0:T(8,128)(2,1)S(1)}, bf16[1,48,2048]{2,1,0:T(8,128)(2,1)S(1)}, u32[]{:S(2)}, u32[]{:S(2)}) collective-permute-start(bf16[1,48,2048]{2,1,0:T(8,128)(2,1)S(1)} %maximum_select_fusion.3), channel_id=1, source_target_pairs={{0,8},{1,9},{2,10},{3,11},{4,12},{5,13},{6,14},{7,15},{8,0},{9,1},... | collective-permute-start | bytes 589832 | tf_op jit(solution)/shard_map/ppermute | solution.py:892
  23.3 5.8 %collective-permute-start.16 = (bf16[1,48,1152]{2,1,0:T(8,128)(2,1)S(1)}, bf16[1,48,1152]{2,1,0:T(8,128)(2,1)S(1)}, u32[]{:S(2)}, u32[]{:S(2)}) collective-permute-start(bf16[1,48,1152]{2,1,0:T(8,128)(2,1)S(1)} %get-tuple-element.213), channel_id=1, source_target_pairs={{0,4},{1,5},{2,6},{3,7},{4,12},{5,13},{6,14},{7,15},{8,0},{9,1},{1... | collective-permute-start | bytes 331784 | tf_op jit(solution)/shard_map/ppermute | solution.py:892
  23.4 17.8 %collective-permute-start.8 = (bf16[2,176,768]{2,1,0:T(8,128)(2,1)S(1)}, bf16[2,176,768]{2,1,0:T(8,128)(2,1)S(1)}, u32[]{:S(2)}, u32[]{:S(2)}) collective-permute-start(bf16[2,176,768]{2,1,0:T(8,128)(2,1)S(1)} %pad_maximum_fusion.6), channel_id=1, source_target_pairs={{0,4},{1,5},{2,6},{3,7},{4,0},{5,1},{6,2},{7,3},{8,12},{9,13},{10,... | collective-permute-start | bytes 1622024 | tf_op jit(solution)/shard_map/ppermute | solution.py:892
  29.2 13.0 %collective-permute-start.7 = (bf16[1,48,1536]{2,1,0:T(8,128)(2,1)S(1)}, bf16[1,48,1536]{2,1,0:T(8,128)(2,1)S(1)}, u32[]{:S(2)}, u32[]{:S(2)}) collective-permute-start(bf16[1,48,1536]{2,1,0:T(8,128)(2,1)S(1)} %get-tuple-element.209), channel_id=1, source_target_pairs={{0,2},{1,3},{2,0},{3,1},{4,6},{5,7},{6,4},{7,5},{8,10},{9,11},{10,... | collective-permute-start | bytes 442376 | tf_op jit(solution)/shard_map/ppermute | solution.py:892
  31.0 3.3 %collective-permute-start.5 = (bf16[160,768]{1,0:T(8,128)(2,1)S(1)}, bf16[160,768]{1,0:T(8,128)(2,1)S(1)}, u32[]{:S(2)}, u32[]{:S(2)}) collective-permute-start(bf16[160,768]{1,0:T(8,128)(2,1)S(1)} %copy-done), channel_id=1, source_target_pairs={{0,1},{1,0},{2,3},{3,2},{4,5},{5,4},{6,7},{7,6},{8,9},{9,8},{10,11... | collective-permute-start | bytes 737288 | tf_op jit(solution)/shard_map/ppermute | solution.py:892
  31.0 12.9 %collective-permute-start.11 = (bf16[1,48,1152]{2,1,0:T(8,128)(2,1)S(1)}, bf16[1,48,1152]{2,1,0:T(8,128)(2,1)S(1)}, u32[]{:S(2)}, u32[]{:S(2)}) collective-permute-start(bf16[1,48,1152]{2,1,0:T(8,128)(2,1)S(1)} %get-tuple-element.213), channel_id=1, source_target_pairs={{0,12},{1,13},{2,14},{3,15},{4,8},{5,9},{6,10},{7,11},{8,4},{9,5},... | collective-permute-start | bytes 331784 | tf_op jit(solution)/shard_map/ppermute | solution.py:892
  34.3 11.2 %collective-permute-start.6 = (bf16[1,192,768]{2,1,0:T(8,128)(2,1)S(1)}, bf16[1,192,768]{2,1,0:T(8,128)(2,1)S(1)}, u32[]{:S(2)}, u32[]{:S(2)}) collective-permute-start(bf16[1,192,768]{2,1,0:T(8,128)(2,1)S(1)} %select_bitcast_fusion.1), channel_id=1, source_target_pairs={{0,2},{1,3},{2,0},{3,1},{4,6},{5,7},{6,4},{7,5},{8,10},{9,11},{10,... | collective-permute-start | bytes 884744 | tf_op jit(solution)/shard_map/ppermute | solution.py:892
  34.9 10.5 %collective-permute-start.12 = (bf16[1,48,1152]{2,1,0:T(8,128)(2,1)S(1)}, bf16[1,48,1152]{2,1,0:T(8,128)(2,1)S(1)}, u32[]{:S(2)}, u32[]{:S(2)}) collective-permute-start(bf16[1,48,1152]{2,1,0:T(8,128)(2,1)S(1)} %get-tuple-element.213), channel_id=1, source_target_pairs={{0,8},{1,9},{2,10},{3,11},{4,0},{5,1},{6,2},{7,3},{8,12},{9,13},{1... | collective-permute-start | bytes 331784 | tf_op jit(solution)/shard_map/ppermute | solution.py:892
  41.3 12.4 %collective-permute-start.9 = (bf16[2,48,2048]{2,1,0:T(8,128)(2,1)S(1)}, bf16[2,48,2048]{2,1,0:T(8,128)(2,1)S(1)}, u32[]{:S(2)}, u32[]{:S(2)}) collective-permute-start(bf16[2,48,2048]{2,1,0:T(8,128)(2,1)S(1)} %pad_maximum_fusion.8), channel_id=1, source_target_pairs={{0,4},{1,5},{2,6},{3,7},{4,0},{5,1},{6,2},{7,3},{8,12},{9,13},{10,... | collective-permute-start | bytes 1179656 | tf_op jit(solution)/shard_map/ppermute | solution.py:892
  42.2 24.8 %collective-permute-start.14 = (bf16[4,176,768]{2,1,0:T(8,128)(2,1)S(1)}, bf16[4,176,768]{2,1,0:T(8,128)(2,1)S(1)}, u32[]{:S(2)}, u32[]{:S(2)}) collective-permute-start(bf16[4,176,768]{2,1,0:T(8,128)(2,1)S(1)} %pad_maximum_fusion.2), channel_id=1, source_target_pairs={{0,2},{1,3},{2,0},{3,1},{4,6},{5,7},{6,4},{7,5},{8,10},{9,11},{10,... | collective-permute-start | bytes 3244040 | tf_op jit(solution)/shard_map/ppermute | solution.py:892
  53.8 12.2 %collective-permute-start.17 = (bf16[4,48,1152]{2,1,0:T(8,128)(2,1)S(1)}, bf16[4,48,1152]{2,1,0:T(8,128)(2,1)S(1)}, u32[]{:S(2)}, u32[]{:S(2)}) collective-permute-start(bf16[4,48,1152]{2,1,0:T(8,128)(2,1)S(1)} %pad_maximum_fusion.7), channel_id=1, source_target_pairs={{0,16},{1,17},{2,18},{3,19},{4,20},{5,21},{6,22},{7,23},{8,24},{9,... | collective-permute-start | bytes 1327112 | tf_op jit(solution)/shard_map/ppermute | solution.py:892
  55.5 10.6 %collective-permute-start.15 = (bf16[2,48,1536]{2,1,0:T(8,128)(2,1)S(1)}, bf16[2,48,1536]{2,1,0:T(8,128)(2,1)S(1)}, u32[]{:S(2)}, u32[]{:S(2)}) collective-permute-start(bf16[2,48,1536]{2,1,0:T(8,128)(2,1)S(1)} %pad_maximum_fusion.9), channel_id=1, source_target_pairs={{0,4},{1,5},{2,6},{3,7},{4,12},{5,13},{6,14},{7,15},{8,0},{9,1},{1... | collective-permute-start | bytes 884744 | tf_op jit(solution)/shard_map/ppermute | solution.py:892
  67.2 28.1 %copy-start.1 = (bf16[192,256]{1,0:T(8,128)(2,1)S(1)}, bf16[192,256]{1,0:T(8,128)(2,1)}, u32[]{:S(2)}) copy-start(bf16[192,256]{1,0:T(8,128)(2,1)} %constant.53.clone.coarse_ref) | copy-start | bytes 294916
  67.2 28.1 %copy-start.2 = (bf16[192,256]{1,0:T(8,128)(2,1)S(1)}, bf16[192,256]{1,0:T(8,128)(2,1)}, u32[]{:S(2)}) copy-start(bf16[192,256]{1,0:T(8,128)(2,1)} %constant.52.clone.fine_ref) | copy-start | bytes 294916
  67.2 27.5 %collective-permute-start.20 = (bf16[8,176,768]{2,1,0:T(8,128)(2,1)S(1)}, bf16[8,176,768]{2,1,0:T(8,128)(2,1)S(1)}, u32[]{:S(2)}, u32[]{:S(2)}) collective-permute-start(bf16[8,176,768]{2,1,0:T(8,128)(2,1)S(1)} %pad_maximum_fusion.along_ref.note_a_ref.refs_2_.refs_5_), channel_id=1, source_target_pairs={{0,1},{1,0},{2,3},{3,2},{4,5},{5,4},{6,7},{7,6},{8,9},{9,8},{10,11... | collective-permute-start | bytes 6488072 | tf_op jit(solution)/shard_map/ppermute | solution.py:892
  67.3 20.0 %collective-permute-start.13 = (bf16[4,48,2048]{2,1,0:T(8,128)(2,1)S(1)}, bf16[4,48,2048]{2,1,0:T(8,128)(2,1)S(1)}, u32[]{:S(2)}, u32[]{:S(2)}) collective-permute-start(bf16[4,48,2048]{2,1,0:T(8,128)(2,1)S(1)} %pad_maximum_fusion.3), channel_id=1, source_target_pairs={{0,16},{1,17},{2,18},{3,19},{4,20},{5,21},{6,22},{7,23},{8,24},{9,... | collective-permute-start | bytes 2359304 | tf_op jit(solution)/shard_map/ppermute | solution.py:892
  68.6 20.2 %collective-permute-start.10 = (bf16[2,192,768]{2,1,0:T(8,128)(2,1)S(1)}, bf16[2,192,768]{2,1,0:T(8,128)(2,1)S(1)}, u32[]{:S(2)}, u32[]{:S(2)}) collective-permute-start(bf16[2,192,768]{2,1,0:T(8,128)(2,1)S(1)} %pad_maximum_fusion.4.refs_0_), channel_id=1, source_target_pairs={{0,4},{1,5},{2,6},{3,7},{4,12},{5,13},{6,14},{7,15},{8,0},{9,1},{1... | collective-permute-start | bytes 1769480 | tf_op jit(solution)/shard_map/ppermute | solution.py:892
  70.3 24.4 %collective-permute-start.19 = (bf16[2,48,1536]{2,1,0:T(8,128)(2,1)S(1)}, bf16[2,48,1536]{2,1,0:T(8,128)(2,1)S(1)}, u32[]{:S(2)}, u32[]{:S(2)}) collective-permute-start(bf16[2,48,1536]{2,1,0:T(8,128)(2,1)S(1)} %collective-permute-done.15), channel_id=1, source_target_pairs={{0,4},{1,5},{2,6},{3,7},{4,12},{5,13},{6,14},{7,15},{8,0},{9,1},{1... | collective-permute-start | bytes 884744 | tf_op jit(solution)/shard_map/ppermute | solution.py:892
  75.0 28.7 %collective-permute-start.21 = (bf16[8,48,1152]{2,1,0:T(8,128)(2,1)S(1)}, bf16[8,48,1152]{2,1,0:T(8,128)(2,1)S(1)}, u32[]{:S(2)}, u32[]{:S(2)}) collective-permute-start(bf16[8,48,1152]{2,1,0:T(8,128)(2,1)S(1)} %constant_dynamic-update-slice_fusion.refs_0_), channel_id=1, source_target_pairs={{0,2},{1,3},{2,0},{3,1},{4,6},{5,7},{6,4},{7,5},{8,10},{9,11},{10,... | collective-permute-start | bytes 2654216 | tf_op jit(solution)/shard_map/ppermute | solution.py:892
  87.4 42.5 %collective-permute-start.25 = (bf16[8,48,2048]{2,1,0:T(8,128)(2,1)S(1)}, bf16[8,48,2048]{2,1,0:T(8,128)(2,1)S(1)}, u32[]{:S(2)}, u32[]{:S(2)}) collective-permute-start(bf16[8,48,2048]{2,1,0:T(8,128)(2,1)S(1)} %pad_maximum_fusion.1.refs_0_), channel_id=1, source_target_pairs={{0,2},{1,3},{2,0},{3,1},{4,6},{5,7},{6,4},{7,5},{8,10},{9,11},{10,... | collective-permute-start | bytes 4718600 | tf_op jit(solution)/shard_map/ppermute | solution.py:892
  88.8 23.1 %collective-permute-start.18 = (bf16[2,192,768]{2,1,0:T(8,128)(2,1)S(1)}, bf16[2,192,768]{2,1,0:T(8,128)(2,1)S(1)}, u32[]{:S(2)}, u32[]{:S(2)}) collective-permute-start(bf16[2,192,768]{2,1,0:T(8,128)(2,1)S(1)} %collective-permute-done.10.refs_1_), channel_id=1, source_target_pairs={{0,4},{1,5},{2,6},{3,7},{4,12},{5,13},{6,14},{7,15},{8,0},{9,1},{1... | collective-permute-start | bytes 1769480 | tf_op jit(solution)/shard_map/ppermute | solution.py:892
  94.7 19.3 %collective-permute-start.23 = (bf16[2,48,1536]{2,1,0:T(8,128)(2,1)S(1)}, bf16[2,48,1536]{2,1,0:T(8,128)(2,1)S(1)}, u32[]{:S(2)}, u32[]{:S(2)}) collective-permute-start(bf16[2,48,1536]{2,1,0:T(8,128)(2,1)S(1)} %collective-permute-done.19), channel_id=1, source_target_pairs={{0,4},{1,5},{2,6},{3,7},{4,12},{5,13},{6,14},{7,15},{8,0},{9,1},{1... | collective-permute-start | bytes 884744 | tf_op jit(solution)/shard_map/ppermute | solution.py:892
  114.0 26.7 %collective-permute-start.24 = (bf16[8,48,1536]{2,1,0:T(8,128)(2,1)S(1)}, bf16[8,48,1536]{2,1,0:T(8,128)(2,1)S(1)}, u32[]{:S(2)}, u32[]{:S(2)}) collective-permute-start(bf16[8,48,1536]{2,1,0:T(8,128)(2,1)S(1)} %constant_dynamic-update-slice_fusion.5.refs_0_), channel_id=1, source_target_pairs={{0,16},{1,17},{2,18},{3,19},{4,20},{5,21},{6,22},{7,23},{8,24},{9,... | collective-permute-start | bytes 3538952 | tf_op jit(solution)/shard_map/ppermute | solution.py:892
  125.9 4.1 %collective-permute-start.26 = (bf16[320,384]{1,0:T(8,128)(2,1)S(1)}, bf16[320,384]{1,0:T(8,128)(2,1)S(1)}, u32[]{:S(2)}, u32[]{:S(2)}) collective-permute-start(bf16[320,384]{1,0:T(8,128)(2,1)S(1)} %get-tuple-element.253.refs_2_), channel_id=1, source_target_pairs={{0,1},{1,0},{2,3},{3,2},{4,5},{5,4},{6,7},{7,6},{8,9},{9,8},{10,11... | collective-permute-start | bytes 737288 | tf_op jit(solution)/shard_map/ppermute | solution.py:892
  130.0 2.1 collective-permute-start.27
  130.1 16.6 %collective-permute-start.22 = (bf16[2,192,768]{2,1,0:T(8,128)(2,1)S(1)}, bf16[2,192,768]{2,1,0:T(8,128)(2,1)S(1)}, u32[]{:S(2)}, u32[]{:S(2)}) collective-permute-start(bf16[2,192,768]{2,1,0:T(8,128)(2,1)S(1)} %collective-permute-done.18.refs_2_), channel_id=1, source_target_pairs={{0,4},{1,5},{2,6},{3,7},{4,12},{5,13},{6,14},{7,15},{8,0},{9,1},{1... | collective-permute-start | bytes 1769480 | tf_op jit(solution)/shard_map/ppermute | solution.py:892
  148.4 2.6 collective-permute-start.28
  155.7 2.6 collective-permute-start.29
  162.6 36.5 %collective-permute-start.30 = (bf16[8,48,2048]{2,1,0:T(8,128)(2,1)S(1)}, bf16[8,48,2048]{2,1,0:T(8,128)(2,1)S(1)}, u32[]{:S(2)}, u32[]{:S(2)}) collective-permute-start(bf16[8,48,2048]{2,1,0:T(8,128)(2,1)S(1)} %get-tuple-element.322), channel_id=1, source_target_pairs={{0,16},{1,17},{2,18},{3,19},{4,20},{5,21},{6,22},{7,23},{8,24},{9,... | collective-permute-start | bytes 4718600 | tf_op jit(solution)/shard_map/ppermute | solution.py:892
  168.4 28.5 %collective-permute-start.31 = (bf16[4,192,768]{2,1,0:T(8,128)(2,1)S(1)}, bf16[4,192,768]{2,1,0:T(8,128)(2,1)S(1)}, u32[]{:S(2)}, u32[]{:S(2)}) collective-permute-start(bf16[4,192,768]{2,1,0:T(8,128)(2,1)S(1)} %get-tuple-element.333), channel_id=1, source_target_pairs={{0,2},{1,3},{2,0},{3,1},{4,6},{5,7},{6,4},{7,5},{8,10},{9,11},{10,... | collective-permute-start | bytes 3538952 | tf_op jit(solution)/shard_map/ppermute | solution.py:892
  199.7 20.3 %collective-permute-start.32 = (bf16[8,160,768]{2,1,0:T(8,128)(2,1)S(1)}, bf16[8,160,768]{2,1,0:T(8,128)(2,1)S(1)}, u32[]{:S(2)}, u32[]{:S(2)}) collective-permute-start(bf16[8,160,768]{2,1,0:T(8,128)(2,1)S(1)} %get-tuple-element.350), channel_id=1, source_target_pairs={{0,1},{1,0},{2,3},{3,2},{4,5},{5,4},{6,7},{7,6},{8,9},{9,8},{10,11... | collective-permute-start | bytes 5898248 | tf_op jit(solution)/shard_map/ppermute | solution.py:892
  199.8 20.0 %collective-permute-start.34 = (bf16[4,48,2048]{2,1,0:T(8,128)(2,1)S(1)}, bf16[4,48,2048]{2,1,0:T(8,128)(2,1)S(1)}, u32[]{:S(2)}, u32[]{:S(2)}) collective-permute-start(bf16[4,48,2048]{2,1,0:T(8,128)(2,1)S(1)} %slice.304), channel_id=1, source_target_pairs={{0,2},{1,3},{2,0},{3,1},{4,6},{5,7},{6,4},{7,5},{8,10},{9,11},{10,... | collective-permute-start | bytes 2359304 | tf_op jit(solution)/shard_map/ppermute | solution.py:892
  201.3 28.0 %collective-permute-start.39 = (bf16[8,48,1536]{2,1,0:T(8,128)(2,1)S(1)}, bf16[8,48,1536]{2,1,0:T(8,128)(2,1)S(1)}, u32[]{:S(2)}, u32[]{:S(2)}) collective-permute-start(bf16[8,48,1536]{2,1,0:T(8,128)(2,1)S(1)} %get-tuple-element.332), channel_id=1, source_target_pairs={{0,16},{1,17},{2,18},{3,19},{4,20},{5,21},{6,22},{7,23},{8,24},{9,... | collective-permute-start | bytes 3538952 | tf_op jit(solution)/shard_map/ppermute | solution.py:892
  201.8 19.7 %collective-permute-start.36 = (bf16[1,192,768]{2,1,0:T(8,128)(2,1)S(1)}, bf16[1,192,768]{2,1,0:T(8,128)(2,1)S(1)}, u32[]{:S(2)}, u32[]{:S(2)}) collective-permute-start(bf16[1,192,768]{2,1,0:T(8,128)(2,1)S(1)} %get-tuple-element.348), channel_id=1, source_target_pairs={{12,0},{13,1},{14,2},{15,3},{8,4},{9,5},{10,6},{11,7},{4,8},{5,9},... | collective-permute-start | bytes 884744 | tf_op jit(solution)/shard_map/ppermute | solution.py:892
  203.3 18.2 %collective-permute-start.35 = (bf16[1,192,768]{2,1,0:T(8,128)(2,1)S(1)}, bf16[1,192,768]{2,1,0:T(8,128)(2,1)S(1)}, u32[]{:S(2)}, u32[]{:S(2)}) collective-permute-start(bf16[1,192,768]{2,1,0:T(8,128)(2,1)S(1)} %get-tuple-element.347), channel_id=1, source_target_pairs={{4,0},{5,1},{6,2},{7,3},{12,4},{13,5},{14,6},{15,7},{0,8},{1,9},{2... | collective-permute-start | bytes 884744 | tf_op jit(solution)/shard_map/ppermute | solution.py:892
  219.9 25.7 %collective-permute-start.40 = (bf16[1,192,768]{2,1,0:T(8,128)(2,1)S(1)}, bf16[1,192,768]{2,1,0:T(8,128)(2,1)S(1)}, u32[]{:S(2)}, u32[]{:S(2)}) collective-permute-start(bf16[1,192,768]{2,1,0:T(8,128)(2,1)S(1)} %get-tuple-element.351), channel_id=1, source_target_pairs={{8,0},{9,1},{10,2},{11,3},{0,4},{1,5},{2,6},{3,7},{12,8},{13,9},{1... | collective-permute-start | bytes 884744 | tf_op jit(solution)/shard_map/ppermute | solution.py:892
  221.5 24.2 %collective-permute-start.38 = (bf16[1,48,2048]{2,1,0:T(8,128)(2,1)S(1)}, bf16[1,48,2048]{2,1,0:T(8,128)(2,1)S(1)}, u32[]{:S(2)}, u32[]{:S(2)}) collective-permute-start(bf16[1,48,2048]{2,1,0:T(8,128)(2,1)S(1)} %split.93), channel_id=1, source_target_pairs={{4,0},{5,1},{6,2},{7,3},{12,4},{13,5},{14,6},{15,7},{0,8},{1,9},{2... | collective-permute-start | bytes 589832 | tf_op jit(solution)/shard_map/ppermute | solution.py:892
  229.8 33.0 %collective-permute-start.33 = (bf16[4,160,768]{2,1,0:T(8,128)(2,1)S(1)}, bf16[4,160,768]{2,1,0:T(8,128)(2,1)S(1)}, u32[]{:S(2)}, u32[]{:S(2)}) collective-permute-start(bf16[4,160,768]{2,1,0:T(8,128)(2,1)S(1)} %slice.303), channel_id=1, source_target_pairs={{0,2},{1,3},{2,0},{3,1},{4,6},{5,7},{6,4},{7,5},{8,10},{9,11},{10,... | collective-permute-start | bytes 2949128 | tf_op jit(solution)/shard_map/ppermute | solution.py:892
  230.4 32.2 %collective-permute-start.37 = (bf16[8,48,1152]{2,1,0:T(8,128)(2,1)S(1)}, bf16[8,48,1152]{2,1,0:T(8,128)(2,1)S(1)}, u32[]{:S(2)}, u32[]{:S(2)}) collective-permute-start(bf16[8,48,1152]{2,1,0:T(8,128)(2,1)S(1)} %get-tuple-element.356), channel_id=1, source_target_pairs={{0,16},{1,17},{2,18},{3,19},{4,20},{5,21},{6,22},{7,23},{8,24},{9,... | collective-permute-start | bytes 2654216 | tf_op jit(solution)/shard_map/ppermute | solution.py:892
  245.7 6.7 %collective-permute-start.42 = (bf16[2,48,1536]{2,1,0:T(8,128)(2,1)S(1)}, bf16[2,48,1536]{2,1,0:T(8,128)(2,1)S(1)}, u32[]{:S(2)}, u32[]{:S(2)}) collective-permute-start(bf16[2,48,1536]{2,1,0:T(8,128)(2,1)S(1)} %split.92), channel_id=1, source_target_pairs={{4,0},{5,1},{6,2},{7,3},{12,4},{13,5},{14,6},{15,7},{0,8},{1,9},{2... | collective-permute-start | bytes 884744 | tf_op jit(solution)/shard_map/ppermute | solution.py:892
  245.7 9.4 %collective-permute-start.41 = (bf16[1,48,2048]{2,1,0:T(8,128)(2,1)S(1)}, bf16[1,48,2048]{2,1,0:T(8,128)(2,1)S(1)}, u32[]{:S(2)}, u32[]{:S(2)}) collective-permute-start(bf16[1,48,2048]{2,1,0:T(8,128)(2,1)S(1)} %fusion.8), channel_id=1, source_target_pairs={{4,0},{5,1},{6,2},{7,3},{12,4},{13,5},{14,6},{15,7},{0,8},{1,9},{2... | collective-permute-start | bytes 589832 | tf_op jit(solution)/shard_map/ppermute | solution.py:892
  252.5 10.0 %collective-permute-start.45 = (bf16[2,48,1536]{2,1,0:T(8,128)(2,1)S(1)}, bf16[2,48,1536]{2,1,0:T(8,128)(2,1)S(1)}, u32[]{:S(2)}, u32[]{:S(2)}) collective-permute-start(bf16[2,48,1536]{2,1,0:T(8,128)(2,1)S(1)} %fusion.4), channel_id=1, source_target_pairs={{4,0},{5,1},{6,2},{7,3},{12,4},{13,5},{14,6},{15,7},{0,8},{1,9},{2... | collective-permute-start | bytes 884744 | tf_op jit(solution)/shard_map/ppermute | solution.py:892
  262.8 8.2 %collective-permute-start.46 = (bf16[1,48,2048]{2,1,0:T(8,128)(2,1)S(1)}, bf16[1,48,2048]{2,1,0:T(8,128)(2,1)S(1)}, u32[]{:S(2)}, u32[]{:S(2)}) collective-permute-start(bf16[1,48,2048]{2,1,0:T(8,128)(2,1)S(1)} %fusion.7), channel_id=1, source_target_pairs={{4,0},{5,1},{6,2},{7,3},{12,4},{13,5},{14,6},{15,7},{0,8},{1,9},{2... | collective-permute-start | bytes 589832 | tf_op jit(solution)/shard_map/ppermute | solution.py:892
  264.9 8.3 %collective-permute-start.44 = (bf16[4,48,1152]{2,1,0:T(8,128)(2,1)S(1)}, bf16[4,48,1152]{2,1,0:T(8,128)(2,1)S(1)}, u32[]{:S(2)}, u32[]{:S(2)}) collective-permute-start(bf16[4,48,1152]{2,1,0:T(8,128)(2,1)S(1)} %slice.306), channel_id=1, source_target_pairs={{0,2},{1,3},{2,0},{3,1},{4,6},{5,7},{6,4},{7,5},{8,10},{9,11},{10,... | collective-permute-start | bytes 1327112 | tf_op jit(solution)/shard_map/ppermute | solution.py:892
  266.3 15.5 %collective-permute-start.43 = (bf16[2,160,768]{2,1,0:T(8,128)(2,1)S(1)}, bf16[2,160,768]{2,1,0:T(8,128)(2,1)S(1)}, u32[]{:S(2)}, u32[]{:S(2)}) collective-permute-start(bf16[2,160,768]{2,1,0:T(8,128)(2,1)S(1)} %slice.305), channel_id=1, source_target_pairs={{0,4},{1,5},{2,6},{3,7},{4,0},{5,1},{6,2},{7,3},{8,12},{9,13},{10,... | collective-permute-start | bytes 1474568 | tf_op jit(solution)/shard_map/ppermute | solution.py:892
  273.3 10.8 %collective-permute-start.47 = (bf16[2,48,1152]{2,1,0:T(8,128)(2,1)S(1)}, bf16[2,48,1152]{2,1,0:T(8,128)(2,1)S(1)}, u32[]{:S(2)}, u32[]{:S(2)}) collective-permute-start(bf16[2,48,1152]{2,1,0:T(8,128)(2,1)S(1)} %slice.308), channel_id=1, source_target_pairs={{0,4},{1,5},{2,6},{3,7},{4,0},{5,1},{6,2},{7,3},{8,12},{9,13},{10,... | collective-permute-start | bytes 663560 | tf_op jit(solution)/shard_map/ppermute | solution.py:892
  273.6 13.8 %collective-permute-start.50 = (bf16[2,48,1536]{2,1,0:T(8,128)(2,1)S(1)}, bf16[2,48,1536]{2,1,0:T(8,128)(2,1)S(1)}, u32[]{:S(2)}, u32[]{:S(2)}) collective-permute-start(bf16[2,48,1536]{2,1,0:T(8,128)(2,1)S(1)} %fusion), channel_id=1, source_target_pairs={{4,0},{5,1},{6,2},{7,3},{12,4},{13,5},{14,6},{15,7},{0,8},{1,9},{2... | collective-permute-start | bytes 884744 | tf_op jit(solution)/shard_map/ppermute | solution.py:892
  274.9 12.3 %collective-permute-start.55 = (bf16[192,768]{1,0:T(8,128)(2,1)S(1)}, bf16[192,768]{1,0:T(8,128)(2,1)S(1)}, u32[]{:S(2)}, u32[]{:S(2)}) collective-permute-start(bf16[192,768]{1,0:T(8,128)(2,1)S(1)} %fusion.9), channel_id=1, source_target_pairs={{1,17},{3,19},{5,21},{7,23},{9,25},{11,27},{13,29},{15,31},{16,0},... | collective-permute-start | bytes 884744 | tf_op jit(solution)/shard_map/ppermute | solution.py:892
  284.2 9.0 %collective-permute-start.49 = (bf16[1,48,1152]{2,1,0:T(8,128)(2,1)S(1)}, bf16[1,48,1152]{2,1,0:T(8,128)(2,1)S(1)}, u32[]{:S(2)}, u32[]{:S(2)}) collective-permute-start(bf16[1,48,1152]{2,1,0:T(8,128)(2,1)S(1)} %slice.310), channel_id=1, source_target_pairs={{0,8},{1,9},{2,10},{3,11},{4,12},{5,13},{6,14},{7,15},{8,0},{9,1},... | collective-permute-start | bytes 331784 | tf_op jit(solution)/shard_map/ppermute | solution.py:892
  285.3 11.9 %collective-permute-start.48 = (bf16[1,160,768]{2,1,0:T(8,128)(2,1)S(1)}, bf16[1,160,768]{2,1,0:T(8,128)(2,1)S(1)}, u32[]{:S(2)}, u32[]{:S(2)}) collective-permute-start(bf16[1,160,768]{2,1,0:T(8,128)(2,1)S(1)} %slice.307), channel_id=1, source_target_pairs={{0,8},{1,9},{2,10},{3,11},{4,12},{5,13},{6,14},{7,15},{8,0},{9,1},... | collective-permute-start | bytes 737288 | tf_op jit(solution)/shard_map/ppermute | solution.py:892
  287.5 6.3 %collective-permute-start.53 = (bf16[1,48,1536]{2,1,0:T(8,128)(2,1)S(1)}, bf16[1,48,1536]{2,1,0:T(8,128)(2,1)S(1)}, u32[]{:S(2)}, u32[]{:S(2)}) collective-permute-start(bf16[1,48,1536]{2,1,0:T(8,128)(2,1)S(1)} %slice.309), channel_id=1, source_target_pairs={{0,2},{1,3},{2,0},{3,1},{4,6},{5,7},{6,4},{7,5},{8,10},{9,11},{10,... | collective-permute-start | bytes 442376 | tf_op jit(solution)/shard_map/ppermute | solution.py:892
  293.3 3.2 %collective-permute-start.51 = (f32[24,1152]{1,0:T(8,128)S(1)}, f32[24,1152]{1,0:T(8,128)S(1)}, u32[]{:S(2)}, u32[]{:S(2)}) collective-permute-start(f32[24,1152]{1,0:T(8,128)S(1)} %get-tuple-element.369), channel_id=1, source_target_pairs={{0,1},{1,0},{2,3},{3,2},{4,5},{5,4},{6,7},{7,6},{8,9},{9,8},{10,11... | collective-permute-start | bytes 331784 | tf_op jit(solution)/shard_map/ppermute | solution.py:892
  293.4 4.7 %collective-permute-start.52 = (f32[24,1920]{1,0:T(8,128)S(1)}, f32[24,1920]{1,0:T(8,128)S(1)}, u32[]{:S(2)}, u32[]{:S(2)}) collective-permute-start(f32[24,1920]{1,0:T(8,128)S(1)} %slice.244), channel_id=1, source_target_pairs={{0,1},{1,0},{2,3},{3,2},{4,5},{5,4},{6,7},{7,6},{8,9},{9,8},{10,11... | collective-permute-start | bytes 552968 | tf_op jit(solution)/shard_map/ppermute | solution.py:892
  293.9 5.5 %collective-permute-start.54 = (f32[24,1536]{1,0:T(8,128)S(1)}, f32[24,1536]{1,0:T(8,128)S(1)}, u32[]{:S(2)}, u32[]{:S(2)}) collective-permute-start(f32[24,1536]{1,0:T(8,128)S(1)} %get-tuple-element.371), channel_id=1, source_target_pairs={{0,1},{1,0},{2,3},{3,2},{4,5},{5,4},{6,7},{7,6},{8,9},{9,8},{10,11... | collective-permute-start | bytes 442376 | tf_op jit(solution)/shard_map/ppermute | solution.py:892
  294.1 6.1 %collective-permute-start.56 = (f32[96,768]{1,0:T(8,128)S(1)}, f32[96,768]{1,0:T(8,128)S(1)}, u32[]{:S(2)}, u32[]{:S(2)}) collective-permute-start(f32[96,768]{1,0:T(8,128)S(1)} %slice_select_fusion), channel_id=1, source_target_pairs={{0,1},{2,3},{4,5},{6,7},{8,9},{10,11},{12,13},{14,15},{17,16},{19,... | collective-permute-start | bytes 884744 | tf_op jit(solution)/shard_map/ppermute | solution.py:892

commit v4 on v3

--- a/solution.py
+++ b/solution.py
@@ -19,16 +19,17 @@
 ONES = 64
 
 
-ORDERS = {"X": "hx", "Q": "Zyx", "U": "hyx", "G": "xzy", "D": "xz", "d": "xZ", "g": "yzx", "u": "yxz", "q": "yxh", "r": "xyZ", "x": "h"}
+ORDERS = {"X": "zx", "x": "Z", "Q": "zxy", "U": "xzy", "G": "hyx", "D": "zx", "d": "zx", "g": "yxZ", "u": "xyz", "q": "yxz"}
 STREAMS = "XPQUGDCdguqx"
 SEQUENCE = [
-    1, 2, 81, 17, 18, 82, 83, -82, 49, 11, 33, -83, 65, 97, 34, -49, -97, 84,
-    43, 4, 58, -50, -84, 66, 85, -34, -35, 51, 36, 37, 67, 5, -36, -4, 52, 86,
-    -67, -5, 76, 200, 201, 95, 69, 202, 203, -203, -52, -203, -68, 53, 204, -85, -53, 205,
-    206, -87, -69, 207, 208, -207, 209, -207, 212, 213, 145, 210, 211, 129, 113, 214, -145, 114,
-    -113, 115, 146, 177, -177, 124, 178, -114, -115, 147, 161, -146, -116, -129, 130, 148, -147, 131,
-    -178, 157, 162, 179, -162, -131, -149, 163, -130, 140, 117, 172, -179, 188, 133, -132, -163, 165,
-    150, -133, 134, 118, -150, -134, -165, -117, -148,
+    1, 17, 18, -18, 33, 65, 81, 49, 34, 82, 2, -49, 43, 74, -33, -34, 83, -2,
+    3, -65, -35, 36, 50, 67, -36, 12, -66, -83, 37, -50, 51, -4, 5, -3, -67, 68,
+    84, -51, 60, -37, -84, 97, 85, -97, -52, 53, -5, 6, -85, -6, 94, 200, -68, -86,
+    87, 201, 202, 203, -203, -53, 54, 204, 205, 206, 207, -207, 208, 209, 211, 212, 129, 213,
+    145, -54, 210, 113, 214, -113, 161, -209, 130, -145, 114, 146, -130, 131, 177, -129, -114, 123,
+    -161, 162, -177, 132, -131, 178, -162, 163, -115, 147, -163, 141, -132, -146, 148, 164, 116, -133,
+    -178, -164, 179, -148, 173, 157, -116, 180, 117, 166, -166, 189, 150, -149, -117, 118, 134, -118,
+    -134, -180, -150,
 ]
 
 
@@ -1001,7 +1002,7 @@
     direct = two % 16 == 0
 
     def tokens_task():
-        message, grid.results["down"] = yield "work", make_message, tokens, segment_ids, pad_mask, w_down
+        message, grid.results["low_down"] = yield "work", make_message, tokens, segment_ids, pad_mask, w_down
         along = jnp.concatenate((yield from grid.gather(message, orders["X"])), axis=0)
         return along, (yield "move", "c", along)
 
@@ -1019,7 +1020,7 @@
         return pieces, (yield "move", "c", outs)
 
     def down_task(order):
-        part = yield "work", lambda w: w, grid.results["down"]
+        part = yield "work", lambda w: w, grid.results["low_down"]
         part = grid.ordered(c, part, (yield "move", "c", part), 0)
         part = jnp.where(c == y, part, (yield "move", "spread", part))
         return (yield from grid.gather(part, order))

time: 301 us -> 293 us (0.973)
  waiting for transfers between devices: 149 us -> 120 us
  starting transfers between devices: 63.6 us -> 83 us
    ppermute x57 -> x60, waiting for transfers between devices: 149 us -> 120 us  [move(): got = self.moved[self.label] = lax.ppermute(a, AXES, self.across[way])]
    ppermute x57 -> x60, starting transfers between devices: 63.6 us -> 83 us  [move(): got = self.moved[self.label] = lax.ppermute(a, AXES, self.across[way])]
  transfers between devices with their start and end apart: 57 -> 60, of which waited for: 30 -> 25; matrix products, arithmetic and copies ran while one was open for 3% -> 4% of each run, Pallas kernels for 22% -> 23%
where the time goes in v4:
time: 293 us
  waiting for transfers between devices  120 us (41%)
  starting transfers between devices  83 us (28%)
  Pallas kernels  76.2 us (26%)
  other arithmetic  9.77 us (3%)
    ppermute x60, waiting for transfers between devices, move(): got = self.moved[self.label] = lax.ppermute(a, AXES, self.across[way])  120 us
    ppermute x60, starting transfers between devices, move(): got = self.moved[self.label] = lax.ppermute(a, AXES, self.across[way])  83 us
    pallas_call x1, Pallas kernels, attend_back(): pl.pallas_call(functools.partial(attend_back_kernel, places=places, per=p...  26.8 us
    pallas_call x1, Pallas kernels, attend(): pl.pallas_call(functools.partial(attend_kernel, chunk=512), grid=(3,), in...  10.3 us
    pallas_call x1, Pallas kernels, rank(): pl.pallas_call(functools.partial(rank_kernel, numbers=numbers, coarse=coa...  8.43 us
    pallas_call x1, Pallas kernels, project(): pl.pallas_call(functools.partial(project_kernel, places=places, per=per,...  8.17 us
  transfers between devices with their start and end apart: 60, of which 25 were waited for; matrix products, arithmetic and copies ran while one was open for 4% of the time, Pallas kernels for 23%

profile of v4, /device:TPU:0, one launch (start us, length us, event | category | flops | bytes accessed | tf_op | source)
XLA Modules:
  0.0 292.8 jit_solution(18090411217793370776)
XLA Ops:
  4.8 3.0 %collective-permute-start.1 = (bf16[1,48,1152]{2,1,0:T(8,128)(2,1)S(1)}, bf16[1,48,1152]{2,1,0:T(8,128)(2,1)S(1)}, u32[]{:S(2)}, u32[]{:S(2)}) collective-permute-start(bf16[1,48,1152]{2,1,0:T(8,128)(2,1)S(1)} %get-tuple-element.203), channel_id=1, source_target_pairs={{0,4},{1,5},{2,6},{3,7},{4,12},{5,13},{6,14},{7,15},{8,0},{9,1},{1... | collective-permute-start | bytes 331784 | tf_op jit(solution)/shard_map/ppermute | solution.py:893
  9.0 1.9 collective-permute-start.5
  10.9 1.8 collective-permute-done.1
  12.7 4.1 %collective-permute-start.4 = (bf16[1,48,1152]{2,1,0:T(8,128)(2,1)S(1)}, bf16[1,48,1152]{2,1,0:T(8,128)(2,1)S(1)}, u32[]{:S(2)}, u32[]{:S(2)}) collective-permute-start(bf16[1,48,1152]{2,1,0:T(8,128)(2,1)S(1)} %collective-permute-done.1), channel_id=1, source_target_pairs={{0,4},{1,5},{2,6},{3,7},{4,12},{5,13},{6,14},{7,15},{8,0},{9,1},{1... | collective-permute-start | bytes 331784 | tf_op jit(solution)/shard_map/ppermute | solution.py:893
  16.8 3.4 %collective-permute-start.9 = (bf16[1,176,768]{2,1,0:T(8,128)(2,1)S(1)}, bf16[1,176,768]{2,1,0:T(8,128)(2,1)S(1)}, u32[]{:S(2)}, u32[]{:S(2)}) collective-permute-start(bf16[1,176,768]{2,1,0:T(8,128)(2,1)S(1)} %bitcast.59), channel_id=1, source_target_pairs={{0,4},{1,5},{2,6},{3,7},{4,12},{5,13},{6,14},{7,15},{8,0},{9,1},{1... | collective-permute-start | bytes 811016 | tf_op jit(solution)/shard_map/ppermute | solution.py:893
  20.9 2.7 collective-permute-start.8
  23.6 3.5 %collective-permute-start.7 = (bf16[2,48,1536]{2,1,0:T(8,128)(2,1)S(1)}, bf16[2,48,1536]{2,1,0:T(8,128)(2,1)S(1)}, u32[]{:S(2)}, u32[]{:S(2)}) collective-permute-start(bf16[2,48,1536]{2,1,0:T(8,128)(2,1)S(1)} %pad_maximum_fusion.7), channel_id=1, source_target_pairs={{0,4},{1,5},{2,6},{3,7},{4,0},{5,1},{6,2},{7,3},{8,12},{9,13},{10,... | collective-permute-start | bytes 884744 | tf_op jit(solution)/shard_map/ppermute | solution.py:893
  27.1 3.4 %collective-permute-start.6 = (bf16[192,768]{1,0:T(8,128)(2,1)S(1)}, bf16[192,768]{1,0:T(8,128)(2,1)S(1)}, u32[]{:S(2)}, u32[]{:S(2)}) collective-permute-start(bf16[192,768]{1,0:T(8,128)(2,1)S(1)} %maximum_select_fusion), channel_id=1, source_target_pairs={{0,16},{2,18},{4,20},{6,22},{8,24},{10,26},{12,28},{14,30},{17,1},... | collective-permute-start | bytes 884744 | tf_op jit(solution)/shard_map/ppermute | solution.py:893
  30.7 1.6 collective-permute-start.12
  32.3 1.2 collective-permute-start.11
  33.5 2.1 collective-permute-start.14
  35.6 13.9 %collective-permute-done.7 = bf16[2,48,1536]{2,1,0:T(8,128)(2,1)S(1)} collective-permute-done((bf16[2,48,1536]{2,1,0:T(8,128)(2,1)S(1)}, bf16[2,48,1536]{2,1,0:T(8,128)(2,1)S(1)}, u32[]{:S(2)}, u32[]{:S(2)}) %collective-permute-start.7) | collective-permute-done | bytes 294944 | tf_op jit(solution)/shard_map/ppermute | solution.py:893
  49.6 1.6 collective-permute-start.10
  51.9 4.8 %collective-permute-start.16 = (bf16[2,48,2048]{2,1,0:T(8,128)(2,1)S(1)}, bf16[2,48,2048]{2,1,0:T(8,128)(2,1)S(1)}, u32[]{:S(2)}, u32[]{:S(2)}) collective-permute-start(bf16[2,48,2048]{2,1,0:T(8,128)(2,1)S(1)} %collective-permute-done.14), channel_id=1, source_target_pairs={{0,4},{1,5},{2,6},{3,7},{4,12},{5,13},{6,14},{7,15},{8,0},{9,1},{1... | collective-permute-start | bytes 1179656 | tf_op jit(solution)/shard_map/ppermute | solution.py:893
  56.7 4.8 %collective-permute-done.13 = bf16[1,176,768]{2,1,0:T(8,128)(2,1)S(1)} collective-permute-done((bf16[1,176,768]{2,1,0:T(8,128)(2,1)S(1)}, bf16[1,176,768]{2,1,0:T(8,128)(2,1)S(1)}, u32[]{:S(2)}, u32[]{:S(2)}) %collective-permute-start.13) | collective-permute-done | bytes 270368 | tf_op jit(solution)/shard_map/ppermute | solution.py:893
  61.7 1.6 collective-permute-start.19
  63.3 2.6 collective-permute-done.10
  66.1 3.5 %collective-permute-done.16 = bf16[2,48,2048]{2,1,0:T(8,128)(2,1)S(1)} collective-permute-done((bf16[2,48,2048]{2,1,0:T(8,128)(2,1)S(1)}, bf16[2,48,2048]{2,1,0:T(8,128)(2,1)S(1)}, u32[]{:S(2)}, u32[]{:S(2)}) %collective-permute-start.16) | collective-permute-done | bytes 393248 | tf_op jit(solution)/shard_map/ppermute | solution.py:893
  69.6 1.3 collective-permute-start.20
  70.9 6.0 %collective-permute-done.15 = bf16[1,192,768]{2,1,0:T(8,128)(2,1)S(1)} collective-permute-done((bf16[1,192,768]{2,1,0:T(8,128)(2,1)S(1)}, bf16[1,192,768]{2,1,0:T(8,128)(2,1)S(1)}, u32[]{:S(2)}, u32[]{:S(2)}) %collective-permute-start.15) | collective-permute-done | bytes 294944 | tf_op jit(solution)/shard_map/ppermute | solution.py:893
  76.9 7.0 %collective-permute-done.17.refs_1_ = bf16[8,48,1152]{2,1,0:T(8,128)(2,1)S(1)} collective-permute-done((bf16[8,48,1152]{2,1,0:T(8,128)(2,1)S(1)}, bf16[8,48,1152]{2,1,0:T(8,128)(2,1)S(1)}, u32[]{:S(2)}, u32[]{:S(2)}) %collective-permute-start.17) | collective-permute-done | bytes 884768 | tf_op jit(solution)/shard_map/ppermute | solution.py:893
  84.0 1.4 collective-permute-done.21.cot_got_ref
  85.7 1.6 collective-permute-start.24
  87.3 1.5 collective-permute-start.26
  88.8 9.6 %collective-permute-done.18 = bf16[1,192,768]{2,1,0:T(8,128)(2,1)S(1)} collective-permute-done((bf16[1,192,768]{2,1,0:T(8,128)(2,1)S(1)}, bf16[1,192,768]{2,1,0:T(8,128)(2,1)S(1)}, u32[]{:S(2)}, u32[]{:S(2)}) %collective-permute-start.18) | collective-permute-done | bytes 294944 | tf_op jit(solution)/shard_map/ppermute | solution.py:893
  98.4 1.3 collective-permute-start.23
  99.7 8.4 %rank.1 = (bf16[768,2560]{1,0:T(8,128)(2,1)}, f32[2560,128]{1,0:T(8,128)}, f32[2560,128]{1,0:T(8,128)}, bf16[2560,128]{1,0:T(8,128)(2,1)}, f32[320,128]{1,0:T(8,128)S(1)}) custom-call(s32[4]{0:T(128)S(1)} %pad_add_fusion.me_ref, bf16[8,176,768]{2,1,0:T(8,128)(2,1)S(1)} %constant_dynamic-update-slice_fusion.5.along_ref.note_a_ref.refs_2_.refs_5_, ...), custom_call_target="tpu_custom_call" | custom-call | flops 1 | bytes 1 | tf_op jit(solution)/shard_map/rank/pallas_call | solution.py:247
  108.3 5.6 %collective-permute-done.24.refs_1_ = bf16[8,48,1536]{2,1,0:T(8,128)(2,1)S(1)} collective-permute-done((bf16[8,48,1536]{2,1,0:T(8,128)(2,1)S(1)}, bf16[8,48,1536]{2,1,0:T(8,128)(2,1)S(1)}, u32[]{:S(2)}, u32[]{:S(2)}) %collective-permute-start.24) | collective-permute-done | bytes 1179680 | tf_op jit(solution)/shard_map/ppermute | solution.py:893
  114.0 1.5 collective-permute-start.25
  115.5 8.2 %project.1 = (bf16[320,384]{1,0:T(8,128)(2,1)}, bf16[3,2560,128]{2,1,0:T(8,128)(2,1)}, bf16[3,2560,128]{2,1,0:T(8,128)(2,1)}, bf16[768,1152]{1,0:T(8,128)(2,1)}) custom-call(s32[4]{0:T(128)S(1)} %pad_add_fusion.me_ref, bf16[8,48,1152]{2,1,0:T(8,128)(2,1)S(1)} %constant_dynamic-update-slice_fusion.refs_0_, ...), custom_call_target="tpu_custom_call" | custom-call | flops 1 | bytes 1 | tf_op jit(solution)/shard_map/project/pallas_call | solution.py:307
  123.7 10.3 %attend.1 = (f32[320,384]{1,0:T(8,128)}, bf16[320,384]{1,0:T(8,128)(2,1)S(1)}, bf16[6,320,128]{2,1,0:T(8,128)(2,1)}) custom-call(bf16[320,384]{1,0:T(8,128)(2,1)} %get-tuple-element.334.q_ref, bf16[3,2560,128]{2,1,0:T(8,128)(2,1)} %get-tuple-element.338.k_ref, bf16[3,2560,128]{2,1,0:T(8,128)(2,1)} %get-tuple-element.339.v_ref, ...), custom_call_target="tpu_custom_call" | custom-call | flops 5033164800 | bytes 7864320 | tf_op jit(solution)/shard_map/attend/pallas_call | solution.py:356
  134.1 1.4 collective-permute-done.27.refs_3_
  135.6 1.9 collective-permute-done.28.refs_4_
  137.5 2.8 mid.1
  140.2 1.8 gate_up.1
  142.1 1.6 down.1
  143.9 2.4 collective-permute-done.29.got_ref
  146.3 4.7 %turn.1 = (bf16[160,768]{1,0:T(8,128)(2,1)}, f32[320,768]{1,0:T(8,128)S(1)}, bf16[320,768]{1,0:T(8,128)(2,1)S(1)}, bf16[320,1536]{1,0:T(8,128)(2,1)S(1)}, bf16[3...) custom-call(f32[320,768]{1,0:T(8,128)S(1)} %get-tuple-element.279.part_ref, ...), custom_call_target="tpu_custom_call" | custom-call | flops 2264924160 | bytes 20971520 | tf_op jit(solution)/shard_map/turn/pallas_call | solution.py:556
  151.2 2.8 grad.2
  153.9 1.6 back.1
  155.6 1.6 collective-permute-start.31
  157.2 2.7 grad_up.1
  160.8 2.2 grad.3
  163.9 2.2 collective-permute-start.32
  166.1 26.8 %attend_back.1 = (f32[8,160,768]{2,1,0:T(8,128)S(1)}, bf16[8,160,768]{2,1,0:T(8,128)(2,1)S(1)}, f32[8,48,1152]{2,1,0:T(8,128)S(1)}, bf16[8,48,1152]{2,1,0:T(8,128)(2,1)S(1)}) custom-call(s32[4]{0:T(128)S(1)} %pad_add_fusion.me_ref, bf16[320,384]{1,0:T(8,128)(2,1)} %get-tuple-element.334.q_ref, bf16[6,320,128]{2,1,0:T(8,128)(2,1)} %get-tuple-element.335.lse_ref, ...), custom_call_target="tpu_custom_call" | custom-call | flops 20132659200 | bytes 12288000 | tf_op jit(solution)/shard_map/attend_back/pallas_call | solution.py:754
  195.2 1.2 collective-permute-start.33
  197.1 2.5 collective-permute-start.37
  199.7 1.5 collective-permute-start.43
  201.2 8.5 %collective-permute-done.33 = bf16[4,48,1536]{2,1,0:T(8,128)(2,1)S(1)} collective-permute-done((bf16[4,48,1536]{2,1,0:T(8,128)(2,1)S(1)}, bf16[4,48,1536]{2,1,0:T(8,128)(2,1)S(1)}, u32[]{:S(2)}, u32[]{:S(2)}) %collective-permute-start.33) | collective-permute-done | bytes 589856 | tf_op jit(solution)/shard_map/ppermute | solution.py:893
  210.0 5.6 %collective-permute-done.36 = bf16[8,48,1152]{2,1,0:T(8,128)(2,1)S(1)} collective-permute-done((bf16[8,48,1152]{2,1,0:T(8,128)(2,1)S(1)}, bf16[8,48,1152]{2,1,0:T(8,128)(2,1)S(1)}, u32[]{:S(2)}, u32[]{:S(2)}) %collective-permute-start.36) | collective-permute-done | bytes 884768 | tf_op jit(solution)/shard_map/ppermute | solution.py:893
  215.8 2.5 collective-permute-start.38
  219.9 11.0 %collective-permute-done.43 = bf16[4,48,2048]{2,1,0:T(8,128)(2,1)S(1)} collective-permute-done((bf16[4,48,2048]{2,1,0:T(8,128)(2,1)S(1)}, bf16[4,48,2048]{2,1,0:T(8,128)(2,1)S(1)}, u32[]{:S(2)}, u32[]{:S(2)}) %collective-permute-start.43) | collective-permute-done | bytes 786464 | tf_op jit(solution)/shard_map/ppermute | solution.py:893
  231.9 2.5 collective-permute-start.42
  238.1 6.5 %collective-permute-done.44 = bf16[1,48,2048]{2,1,0:T(8,128)(2,1)S(1)} collective-permute-done((bf16[1,48,2048]{2,1,0:T(8,128)(2,1)S(1)}, bf16[1,48,2048]{2,1,0:T(8,128)(2,1)S(1)}, u32[]{:S(2)}, u32[]{:S(2)}) %collective-permute-start.44) | collective-permute-done | bytes 196640 | tf_op jit(solution)/shard_map/ppermute | solution.py:893
  244.6 4.9 %collective-permute-start.49 = (bf16[1,48,2048]{2,1,0:T(8,128)(2,1)S(1)}, bf16[1,48,2048]{2,1,0:T(8,128)(2,1)S(1)}, u32[]{:S(2)}, u32[]{:S(2)}) collective-permute-start(bf16[1,48,2048]{2,1,0:T(8,128)(2,1)S(1)} %fusion.6), channel_id=1, source_target_pairs={{4,0},{5,1},{6,2},{7,3},{12,4},{13,5},{14,6},{15,7},{0,8},{1,9},{2... | collective-permute-start | bytes 589832 | tf_op jit(solution)/shard_map/ppermute | solution.py:893
  250.8 6.0 %collective-permute-done.47 = bf16[1,48,1152]{2,1,0:T(8,128)(2,1)S(1)} collective-permute-done((bf16[1,48,1152]{2,1,0:T(8,128)(2,1)S(1)}, bf16[1,48,1152]{2,1,0:T(8,128)(2,1)S(1)}, u32[]{:S(2)}, u32[]{:S(2)}) %collective-permute-start.47) | collective-permute-done | bytes 110624 | tf_op jit(solution)/shard_map/ppermute | solution.py:893
  256.9 2.6 collective-permute-done.39
  260.8 2.5 collective-permute-done.50
  264.3 2.9 collective-permute-start.55
  267.8 1.3 collective-permute-start.57
  269.2 6.0 %collective-permute-done.55 = bf16[1,48,2048]{2,1,0:T(8,128)(2,1)S(1)} collective-permute-done((bf16[1,48,2048]{2,1,0:T(8,128)(2,1)S(1)}, bf16[1,48,2048]{2,1,0:T(8,128)(2,1)S(1)}, u32[]{:S(2)}, u32[]{:S(2)}) %collective-permute-start.55) | collective-permute-done | bytes 196640 | tf_op jit(solution)/shard_map/ppermute | solution.py:893
  276.0 3.1 %collective-permute-start.54 = (bf16[1,160,768]{2,1,0:T(8,128)(2,1)S(1)}, bf16[1,160,768]{2,1,0:T(8,128)(2,1)S(1)}, u32[]{:S(2)}, u32[]{:S(2)}) collective-permute-start(bf16[1,160,768]{2,1,0:T(8,128)(2,1)S(1)} %get-tuple-element.371), channel_id=1, source_target_pairs={{8,0},{9,1},{10,2},{11,3},{0,4},{1,5},{2,6},{3,7},{12,8},{13,9},{1... | collective-permute-start | bytes 737288 | tf_op jit(solution)/shard_map/ppermute | solution.py:893
  280.0 2.4 collective-permute-start.59
  284.7 6.4 %collective-permute-done.54 = bf16[1,160,768]{2,1,0:T(8,128)(2,1)S(1)} collective-permute-done((bf16[1,160,768]{2,1,0:T(8,128)(2,1)S(1)}, bf16[1,160,768]{2,1,0:T(8,128)(2,1)S(1)}, u32[]{:S(2)}, u32[]{:S(2)}) %collective-permute-start.54) | collective-permute-done | bytes 245792 | tf_op jit(solution)/shard_map/ppermute | solution.py:893
  (161 shorter events, 29.4 us)
Async XLA Ops:
  3.1 1.6 collective-permute-start
  4.8 7.9 %collective-permute-start.1 = (bf16[1,48,1152]{2,1,0:T(8,128)(2,1)S(1)}, bf16[1,48,1152]{2,1,0:T(8,128)(2,1)S(1)}, u32[]{:S(2)}, u32[]{:S(2)}) collective-permute-start(bf16[1,48,1152]{2,1,0:T(8,128)(2,1)S(1)} %get-tuple-element.203), channel_id=1, source_target_pairs={{0,4},{1,5},{2,6},{3,7},{4,12},{5,13},{6,14},{7,15},{8,0},{9,1},{1... | collective-permute-start | bytes 331784 | tf_op jit(solution)/shard_map/ppermute | solution.py:893
  7.8 12.3 %collective-permute-start.3 = (bf16[1,48,1536]{2,1,0:T(8,128)(2,1)S(1)}, bf16[1,48,1536]{2,1,0:T(8,128)(2,1)S(1)}, u32[]{:S(2)}, u32[]{:S(2)}) collective-permute-start(bf16[1,48,1536]{2,1,0:T(8,128)(2,1)S(1)} %maximum_select_fusion.4), channel_id=1, source_target_pairs={{0,8},{1,9},{2,10},{3,11},{4,12},{5,13},{6,14},{7,15},{8,0},{9,1},... | collective-permute-start | bytes 442376 | tf_op jit(solution)/shard_map/ppermute | solution.py:893
  9.0 11.2 %collective-permute-start.5 = (bf16[1,48,2048]{2,1,0:T(8,128)(2,1)S(1)}, bf16[1,48,2048]{2,1,0:T(8,128)(2,1)S(1)}, u32[]{:S(2)}, u32[]{:S(2)}) collective-permute-start(bf16[1,48,2048]{2,1,0:T(8,128)(2,1)S(1)} %get-tuple-element.206), channel_id=1, source_target_pairs={{0,2},{1,3},{2,0},{3,1},{4,6},{5,7},{6,4},{7,5},{8,10},{9,11},{10,... | collective-permute-start | bytes 589832 | tf_op jit(solution)/shard_map/ppermute | solution.py:893
  12.7 8.2 %collective-permute-start.4 = (bf16[1,48,1152]{2,1,0:T(8,128)(2,1)S(1)}, bf16[1,48,1152]{2,1,0:T(8,128)(2,1)S(1)}, u32[]{:S(2)}, u32[]{:S(2)}) collective-permute-start(bf16[1,48,1152]{2,1,0:T(8,128)(2,1)S(1)} %collective-permute-done.1), channel_id=1, source_target_pairs={{0,4},{1,5},{2,6},{3,7},{4,12},{5,13},{6,14},{7,15},{8,0},{9,1},{1... | collective-permute-start | bytes 331784 | tf_op jit(solution)/shard_map/ppermute | solution.py:893
  16.8 10.3 %collective-permute-start.2 = (bf16[96,768]{1,0:T(8,128)(2,1)S(1)}, bf16[96,768]{1,0:T(8,128)(2,1)S(1)}, u32[]{:S(2)}, u32[]{:S(2)}) collective-permute-start(bf16[96,768]{1,0:T(8,128)(2,1)S(1)} %get-tuple-element.208), channel_id=1, source_target_pairs={{0,1},{1,0},{2,3},{3,2},{4,5},{5,4},{6,7},{7,6},{8,9},{9,8},{10,11... | collective-permute-start | bytes 442376 | tf_op jit(solution)/shard_map/ppermute | solution.py:893
  16.8 13.9 %collective-permute-start.9 = (bf16[1,176,768]{2,1,0:T(8,128)(2,1)S(1)}, bf16[1,176,768]{2,1,0:T(8,128)(2,1)S(1)}, u32[]{:S(2)}, u32[]{:S(2)}) collective-permute-start(bf16[1,176,768]{2,1,0:T(8,128)(2,1)S(1)} %bitcast.59), channel_id=1, source_target_pairs={{0,4},{1,5},{2,6},{3,7},{4,12},{5,13},{6,14},{7,15},{8,0},{9,1},{1... | collective-permute-start | bytes 811016 | tf_op jit(solution)/shard_map/ppermute | solution.py:893
  20.9 9.7 %collective-permute-start.8 = (bf16[1,48,1152]{2,1,0:T(8,128)(2,1)S(1)}, bf16[1,48,1152]{2,1,0:T(8,128)(2,1)S(1)}, u32[]{:S(2)}, u32[]{:S(2)}) collective-permute-start(bf16[1,48,1152]{2,1,0:T(8,128)(2,1)S(1)} %collective-permute-done.4), channel_id=1, source_target_pairs={{0,4},{1,5},{2,6},{3,7},{4,12},{5,13},{6,14},{7,15},{8,0},{9,1},{1... | collective-permute-start | bytes 331784 | tf_op jit(solution)/shard_map/ppermute | solution.py:893
  23.6 26.0 %collective-permute-start.7 = (bf16[2,48,1536]{2,1,0:T(8,128)(2,1)S(1)}, bf16[2,48,1536]{2,1,0:T(8,128)(2,1)S(1)}, u32[]{:S(2)}, u32[]{:S(2)}) collective-permute-start(bf16[2,48,1536]{2,1,0:T(8,128)(2,1)S(1)} %pad_maximum_fusion.7), channel_id=1, source_target_pairs={{0,4},{1,5},{2,6},{3,7},{4,0},{5,1},{6,2},{7,3},{8,12},{9,13},{10,... | collective-permute-start | bytes 884744 | tf_op jit(solution)/shard_map/ppermute | solution.py:893
  27.1 24.2 %collective-permute-start.6 = (bf16[192,768]{1,0:T(8,128)(2,1)S(1)}, bf16[192,768]{1,0:T(8,128)(2,1)S(1)}, u32[]{:S(2)}, u32[]{:S(2)}) collective-permute-start(bf16[192,768]{1,0:T(8,128)(2,1)S(1)} %maximum_select_fusion), channel_id=1, source_target_pairs={{0,16},{2,18},{4,20},{6,22},{8,24},{10,26},{12,28},{14,30},{17,1},... | collective-permute-start | bytes 884744 | tf_op jit(solution)/shard_map/ppermute | solution.py:893
  30.7 20.6 %collective-permute-start.12 = (bf16[4,48,1152]{2,1,0:T(8,128)(2,1)S(1)}, bf16[4,48,1152]{2,1,0:T(8,128)(2,1)S(1)}, u32[]{:S(2)}, u32[]{:S(2)}) collective-permute-start(bf16[4,48,1152]{2,1,0:T(8,128)(2,1)S(1)} %pad_maximum_fusion.5), channel_id=1, source_target_pairs={{0,2},{1,3},{2,0},{3,1},{4,6},{5,7},{6,4},{7,5},{8,10},{9,11},{10,... | collective-permute-start | bytes 1327112 | tf_op jit(solution)/shard_map/ppermute | solution.py:893
  32.3 19.0 %collective-permute-start.11 = (bf16[1,176,768]{2,1,0:T(8,128)(2,1)S(1)}, bf16[1,176,768]{2,1,0:T(8,128)(2,1)S(1)}, u32[]{:S(2)}, u32[]{:S(2)}) collective-permute-start(bf16[1,176,768]{2,1,0:T(8,128)(2,1)S(1)} %collective-permute-done.9), channel_id=1, source_target_pairs={{0,4},{1,5},{2,6},{3,7},{4,12},{5,13},{6,14},{7,15},{8,0},{9,1},{1... | collective-permute-start | bytes 811016 | tf_op jit(solution)/shard_map/ppermute | solution.py:893
  33.5 18.4 %collective-permute-start.14 = (bf16[2,48,2048]{2,1,0:T(8,128)(2,1)S(1)}, bf16[2,48,2048]{2,1,0:T(8,128)(2,1)S(1)}, u32[]{:S(2)}, u32[]{:S(2)}) collective-permute-start(bf16[2,48,2048]{2,1,0:T(8,128)(2,1)S(1)} %pad_maximum_fusion.6), channel_id=1, source_target_pairs={{0,4},{1,5},{2,6},{3,7},{4,12},{5,13},{6,14},{7,15},{8,0},{9,1},{1... | collective-permute-start | bytes 1179656 | tf_op jit(solution)/shard_map/ppermute | solution.py:893
  49.6 16.3 %collective-permute-start.10 = (bf16[4,48,1536]{2,1,0:T(8,128)(2,1)S(1)}, bf16[4,48,1536]{2,1,0:T(8,128)(2,1)S(1)}, u32[]{:S(2)}, u32[]{:S(2)}) collective-permute-start(bf16[4,48,1536]{2,1,0:T(8,128)(2,1)S(1)} %pad_maximum_fusion.3), channel_id=1, source_target_pairs={{0,16},{1,17},{2,18},{3,19},{4,20},{5,21},{6,22},{7,23},{8,24},{9,... | collective-permute-start | bytes 1769480 | tf_op jit(solution)/shard_map/ppermute | solution.py:893
  51.3 10.3 %collective-permute-start.13 = (bf16[1,176,768]{2,1,0:T(8,128)(2,1)S(1)}, bf16[1,176,768]{2,1,0:T(8,128)(2,1)S(1)}, u32[]{:S(2)}, u32[]{:S(2)}) collective-permute-start(bf16[1,176,768]{2,1,0:T(8,128)(2,1)S(1)} %collective-permute-done.11), channel_id=1, source_target_pairs={{0,4},{1,5},{2,6},{3,7},{4,12},{5,13},{6,14},{7,15},{8,0},{9,1},{1... | collective-permute-start | bytes 811016 | tf_op jit(solution)/shard_map/ppermute | solution.py:893
  51.4 32.6 %collective-permute-start.17 = (bf16[8,48,1152]{2,1,0:T(8,128)(2,1)S(1)}, bf16[8,48,1152]{2,1,0:T(8,128)(2,1)S(1)}, u32[]{:S(2)}, u32[]{:S(2)}) collective-permute-start(bf16[8,48,1152]{2,1,0:T(8,128)(2,1)S(1)} %constant_dynamic-update-slice_fusion.refs_0_), channel_id=1, source_target_pairs={{0,16},{1,17},{2,18},{3,19},{4,20},{5,21},{6,22},{7,23},{8,24},{9,... | collective-permute-start | bytes 2654216 | tf_op jit(solution)/shard_map/ppermute | solution.py:893
  51.9 17.7 %collective-permute-start.16 = (bf16[2,48,2048]{2,1,0:T(8,128)(2,1)S(1)}, bf16[2,48,2048]{2,1,0:T(8,128)(2,1)S(1)}, u32[]{:S(2)}, u32[]{:S(2)}) collective-permute-start(bf16[2,48,2048]{2,1,0:T(8,128)(2,1)S(1)} %collective-permute-done.14), channel_id=1, source_target_pairs={{0,4},{1,5},{2,6},{3,7},{4,12},{5,13},{6,14},{7,15},{8,0},{9,1},{1... | collective-permute-start | bytes 1179656 | tf_op jit(solution)/shard_map/ppermute | solution.py:893
  61.7 22.2 %copy-start = (bf16[160,768]{1,0:T(8,128)(2,1)S(1)}, bf16[160,768]{1,0:T(8,128)(2,1)}, u32[]{:S(2)}) copy-start(bf16[160,768]{1,0:T(8,128)(2,1)} %cot_ref) | copy-start | bytes 737284
  61.7 23.7 %collective-permute-start.19 = (bf16[4,176,768]{2,1,0:T(8,128)(2,1)S(1)}, bf16[4,176,768]{2,1,0:T(8,128)(2,1)S(1)}, u32[]{:S(2)}, u32[]{:S(2)}) collective-permute-start(bf16[4,176,768]{2,1,0:T(8,128)(2,1)S(1)} %pad_maximum_fusion.2), channel_id=1, source_target_pairs={{0,2},{1,3},{2,0},{3,1},{4,6},{5,7},{6,4},{7,5},{8,10},{9,11},{10,... | collective-permute-start | bytes 3244040 | tf_op jit(solution)/shard_map/ppermute | solution.py:893
  66.0 10.9 %collective-permute-start.15 = (bf16[1,192,768]{2,1,0:T(8,128)(2,1)S(1)}, bf16[1,192,768]{2,1,0:T(8,128)(2,1)S(1)}, u32[]{:S(2)}, u32[]{:S(2)}) collective-permute-start(bf16[1,192,768]{2,1,0:T(8,128)(2,1)S(1)} %select_bitcast_fusion.1), channel_id=1, source_target_pairs={{0,4},{1,5},{2,6},{3,7},{4,12},{5,13},{6,14},{7,15},{8,0},{9,1},{1... | collective-permute-start | bytes 884744 | tf_op jit(solution)/shard_map/ppermute | solution.py:893
  69.6 14.4 %collective-permute-start.20 = (bf16[2,48,2048]{2,1,0:T(8,128)(2,1)S(1)}, bf16[2,48,2048]{2,1,0:T(8,128)(2,1)S(1)}, u32[]{:S(2)}, u32[]{:S(2)}) collective-permute-start(bf16[2,48,2048]{2,1,0:T(8,128)(2,1)S(1)} %collective-permute-done.16), channel_id=1, source_target_pairs={{0,4},{1,5},{2,6},{3,7},{4,12},{5,13},{6,14},{7,15},{8,0},{9,1},{1... | collective-permute-start | bytes 1179656 | tf_op jit(solution)/shard_map/ppermute | solution.py:893
  83.9 1.5 collective-permute-start.21
  84.0 15.8 %copy-start.1 = (bf16[192,256]{1,0:T(8,128)(2,1)S(1)}, bf16[192,256]{1,0:T(8,128)(2,1)}, u32[]{:S(2)}) copy-start(bf16[192,256]{1,0:T(8,128)(2,1)} %constant.52.clone.fine_ref) | copy-start | bytes 294916
  84.0 15.8 %copy-start.2 = (bf16[192,256]{1,0:T(8,128)(2,1)S(1)}, bf16[192,256]{1,0:T(8,128)(2,1)}, u32[]{:S(2)}) copy-start(bf16[192,256]{1,0:T(8,128)(2,1)} %constant.53.clone.coarse_ref) | copy-start | bytes 294916
  85.5 12.9 %collective-permute-start.22 = (bf16[8,176,768]{2,1,0:T(8,128)(2,1)S(1)}, bf16[8,176,768]{2,1,0:T(8,128)(2,1)S(1)}, u32[]{:S(2)}, u32[]{:S(2)}) collective-permute-start(bf16[8,176,768]{2,1,0:T(8,128)(2,1)S(1)} %constant_dynamic-update-slice_fusion.5.along_ref.note_a_ref.refs_2_.refs_5_), channel_id=1, source_target_pairs={{0,1},{1,0},{2,3},{3,2},{4,5},{5,4},{6,7},{7,6},{8,9},{9,8},{10,11... | collective-permute-start | bytes 6488072 | tf_op jit(solution)/shard_map/ppermute | solution.py:893
  85.7 28.2 %collective-permute-start.24 = (bf16[8,48,1536]{2,1,0:T(8,128)(2,1)S(1)}, bf16[8,48,1536]{2,1,0:T(8,128)(2,1)S(1)}, u32[]{:S(2)}, u32[]{:S(2)}) collective-permute-start(bf16[8,48,1536]{2,1,0:T(8,128)(2,1)S(1)} %pad_maximum_fusion.refs_0_), channel_id=1, source_target_pairs={{0,2},{1,3},{2,0},{3,1},{4,6},{5,7},{6,4},{7,5},{8,10},{9,11},{10,... | collective-permute-start | bytes 3538952 | tf_op jit(solution)/shard_map/ppermute | solution.py:893
  87.3 46.7 %collective-permute-start.26 = (bf16[8,48,2048]{2,1,0:T(8,128)(2,1)S(1)}, bf16[8,48,2048]{2,1,0:T(8,128)(2,1)S(1)}, u32[]{:S(2)}, u32[]{:S(2)}) collective-permute-start(bf16[8,48,2048]{2,1,0:T(8,128)(2,1)S(1)} %constant_dynamic-update-slice_fusion.10.refs_0_), channel_id=1, source_target_pairs={{0,16},{1,17},{2,18},{3,19},{4,20},{5,21},{6,22},{7,23},{8,24},{9,... | collective-permute-start | bytes 4718600 | tf_op jit(solution)/shard_map/ppermute | solution.py:893
  88.8 9.6 %collective-permute-start.18 = (bf16[1,192,768]{2,1,0:T(8,128)(2,1)S(1)}, bf16[1,192,768]{2,1,0:T(8,128)(2,1)S(1)}, u32[]{:S(2)}, u32[]{:S(2)}) collective-permute-start(bf16[1,192,768]{2,1,0:T(8,128)(2,1)S(1)} %collective-permute-done.15), channel_id=1, source_target_pairs={{0,4},{1,5},{2,6},{3,7},{4,12},{5,13},{6,14},{7,15},{8,0},{9,1},{1... | collective-permute-start | bytes 884744 | tf_op jit(solution)/shard_map/ppermute | solution.py:893
  98.4 9.8 %collective-permute-start.23 = (bf16[1,192,768]{2,1,0:T(8,128)(2,1)S(1)}, bf16[1,192,768]{2,1,0:T(8,128)(2,1)S(1)}, u32[]{:S(2)}, u32[]{:S(2)}) collective-permute-start(bf16[1,192,768]{2,1,0:T(8,128)(2,1)S(1)} %collective-permute-done.18), channel_id=1, source_target_pairs={{0,4},{1,5},{2,6},{3,7},{4,12},{5,13},{6,14},{7,15},{8,0},{9,1},{1... | collective-permute-start | bytes 884744 | tf_op jit(solution)/shard_map/ppermute | solution.py:893
  114.0 28.1 %collective-permute-start.25 = (bf16[4,192,768]{2,1,0:T(8,128)(2,1)S(1)}, bf16[4,192,768]{2,1,0:T(8,128)(2,1)S(1)}, u32[]{:S(2)}, u32[]{:S(2)}) collective-permute-start(bf16[4,192,768]{2,1,0:T(8,128)(2,1)S(1)} %pad_maximum_fusion.1.refs_0_), channel_id=1, source_target_pairs={{0,2},{1,3},{2,0},{3,1},{4,6},{5,7},{6,4},{7,5},{8,10},{9,11},{10,... | collective-permute-start | bytes 3538952 | tf_op jit(solution)/shard_map/ppermute | solution.py:893
  134.0 1.5 collective-permute-start.27
  135.5 2.0 collective-permute-start.28
  143.7 2.6 collective-permute-start.29
  151.0 2.9 collective-permute-start.30
  155.6 39.2 %collective-permute-start.31 = (bf16[8,48,1536]{2,1,0:T(8,128)(2,1)S(1)}, bf16[8,48,1536]{2,1,0:T(8,128)(2,1)S(1)}, u32[]{:S(2)}, u32[]{:S(2)}) collective-permute-start(bf16[8,48,1536]{2,1,0:T(8,128)(2,1)S(1)} %get-tuple-element.319), channel_id=1, source_target_pairs={{0,16},{1,17},{2,18},{3,19},{4,20},{5,21},{6,22},{7,23},{8,24},{9,... | collective-permute-start | bytes 3538952 | tf_op jit(solution)/shard_map/ppermute | solution.py:893
  159.9 36.5 %collective-permute-start.34 = (bf16[8,48,2048]{2,1,0:T(8,128)(2,1)S(1)}, bf16[8,48,2048]{2,1,0:T(8,128)(2,1)S(1)}, u32[]{:S(2)}, u32[]{:S(2)}) collective-permute-start(bf16[8,48,2048]{2,1,0:T(8,128)(2,1)S(1)} %get-tuple-element.328), channel_id=1, source_target_pairs={{0,2},{1,3},{2,0},{3,1},{4,6},{5,7},{6,4},{7,5},{8,10},{9,11},{10,... | collective-permute-start | bytes 4718600 | tf_op jit(solution)/shard_map/ppermute | solution.py:893
  163.9 29.1 %collective-permute-start.32 = (bf16[2,192,768]{2,1,0:T(8,128)(2,1)}, bf16[2,192,768]{2,1,0:T(8,128)(2,1)}, u32[]{:S(2)}, u32[]{:S(2)}) collective-permute-start(bf16[2,192,768]{2,1,0:T(8,128)(2,1)} %split.68), channel_id=1, source_target_pairs={{4,0},{5,1},{6,2},{7,3},{12,4},{13,5},{14,6},{15,7},{0,8},{1,9},{2... | collective-permute-start | bytes 1769480 | tf_op jit(solution)/shard_map/ppermute | solution.py:893
  193.0 22.6 %collective-permute-start.36 = (bf16[8,48,1152]{2,1,0:T(8,128)(2,1)S(1)}, bf16[8,48,1152]{2,1,0:T(8,128)(2,1)S(1)}, u32[]{:S(2)}, u32[]{:S(2)}) collective-permute-start(bf16[8,48,1152]{2,1,0:T(8,128)(2,1)S(1)} %get-tuple-element.348), channel_id=1, source_target_pairs={{0,16},{1,17},{2,18},{3,19},{4,20},{5,21},{6,22},{7,23},{8,24},{9,... | collective-permute-start | bytes 2654216 | tf_op jit(solution)/shard_map/ppermute | solution.py:893
  195.2 14.5 %collective-permute-start.33 = (bf16[4,48,1536]{2,1,0:T(8,128)(2,1)S(1)}, bf16[4,48,1536]{2,1,0:T(8,128)(2,1)S(1)}, u32[]{:S(2)}, u32[]{:S(2)}) collective-permute-start(bf16[4,48,1536]{2,1,0:T(8,128)(2,1)S(1)} %slice.268), channel_id=1, source_target_pairs={{0,2},{1,3},{2,0},{3,1},{4,6},{5,7},{6,4},{7,5},{8,10},{9,11},{10,... | collective-permute-start | bytes 1769480 | tf_op jit(solution)/shard_map/ppermute | solution.py:893
  197.1 21.2 %collective-permute-start.37 = (bf16[2,192,768]{2,1,0:T(8,128)(2,1)S(1)}, bf16[2,192,768]{2,1,0:T(8,128)(2,1)S(1)}, u32[]{:S(2)}, u32[]{:S(2)}) collective-permute-start(bf16[2,192,768]{2,1,0:T(8,128)(2,1)S(1)} %add_convert_fusion.1), channel_id=1, source_target_pairs={{4,0},{5,1},{6,2},{7,3},{12,4},{13,5},{14,6},{15,7},{0,8},{1,9},{2... | collective-permute-start | bytes 1769480 | tf_op jit(solution)/shard_map/ppermute | solution.py:893
  199.7 31.3 %collective-permute-start.43 = (bf16[4,48,2048]{2,1,0:T(8,128)(2,1)S(1)}, bf16[4,48,2048]{2,1,0:T(8,128)(2,1)S(1)}, u32[]{:S(2)}, u32[]{:S(2)}) collective-permute-start(bf16[4,48,2048]{2,1,0:T(8,128)(2,1)S(1)} %slice.267), channel_id=1, source_target_pairs={{0,16},{1,17},{2,18},{3,19},{4,20},{5,21},{6,22},{7,23},{8,24},{9,... | collective-permute-start | bytes 2359304 | tf_op jit(solution)/shard_map/ppermute | solution.py:893
  209.9 21.4 %collective-permute-start.35 = (bf16[8,160,768]{2,1,0:T(8,128)(2,1)S(1)}, bf16[8,160,768]{2,1,0:T(8,128)(2,1)S(1)}, u32[]{:S(2)}, u32[]{:S(2)}) collective-permute-start(bf16[8,160,768]{2,1,0:T(8,128)(2,1)S(1)} %get-tuple-element.353), channel_id=1, source_target_pairs={{0,1},{1,0},{2,3},{3,2},{4,5},{5,4},{6,7},{7,6},{8,9},{9,8},{10,11... | collective-permute-start | bytes 5898248 | tf_op jit(solution)/shard_map/ppermute | solution.py:893
  215.8 16.1 %collective-permute-start.38 = (bf16[1,48,1536]{2,1,0:T(8,128)(2,1)S(1)}, bf16[1,48,1536]{2,1,0:T(8,128)(2,1)S(1)}, u32[]{:S(2)}, u32[]{:S(2)}) collective-permute-start(bf16[1,48,1536]{2,1,0:T(8,128)(2,1)S(1)} %get-tuple-element.352), channel_id=1, source_target_pairs={{4,0},{5,1},{6,2},{7,3},{12,4},{13,5},{14,6},{15,7},{0,8},{1,9},{2... | collective-permute-start | bytes 442376 | tf_op jit(solution)/shard_map/ppermute | solution.py:893
  218.5 16.0 %collective-permute-start.40 = (bf16[2,192,768]{2,1,0:T(8,128)(2,1)S(1)}, bf16[2,192,768]{2,1,0:T(8,128)(2,1)S(1)}, u32[]{:S(2)}, u32[]{:S(2)}) collective-permute-start(bf16[2,192,768]{2,1,0:T(8,128)(2,1)S(1)} %add_convert_fusion), channel_id=1, source_target_pairs={{4,0},{5,1},{6,2},{7,3},{12,4},{13,5},{14,6},{15,7},{0,8},{1,9},{2... | collective-permute-start | bytes 1769480 | tf_op jit(solution)/shard_map/ppermute | solution.py:893
  218.8 12.5 %collective-permute-start.41 = (bf16[4,48,1152]{2,1,0:T(8,128)(2,1)S(1)}, bf16[4,48,1152]{2,1,0:T(8,128)(2,1)S(1)}, u32[]{:S(2)}, u32[]{:S(2)}) collective-permute-start(bf16[4,48,1152]{2,1,0:T(8,128)(2,1)S(1)} %slice.269), channel_id=1, source_target_pairs={{0,2},{1,3},{2,0},{3,1},{4,6},{5,7},{6,4},{7,5},{8,10},{9,11},{10,... | collective-permute-start | bytes 1327112 | tf_op jit(solution)/shard_map/ppermute | solution.py:893
  231.9 6.1 %collective-permute-start.42 = (bf16[1,48,1152]{2,1,0:T(8,128)(2,1)S(1)}, bf16[1,48,1152]{2,1,0:T(8,128)(2,1)S(1)}, u32[]{:S(2)}, u32[]{:S(2)}) collective-permute-start(bf16[1,48,1152]{2,1,0:T(8,128)(2,1)S(1)} %split.138), channel_id=1, source_target_pairs={{4,0},{5,1},{6,2},{7,3},{12,4},{13,5},{14,6},{15,7},{0,8},{1,9},{2... | collective-permute-start | bytes 331784 | tf_op jit(solution)/shard_map/ppermute | solution.py:893
  234.6 10.0 %collective-permute-start.45 = (bf16[1,48,1536]{2,1,0:T(8,128)(2,1)S(1)}, bf16[1,48,1536]{2,1,0:T(8,128)(2,1)S(1)}, u32[]{:S(2)}, u32[]{:S(2)}) collective-permute-start(bf16[1,48,1536]{2,1,0:T(8,128)(2,1)S(1)} %get-tuple-element.357), channel_id=1, source_target_pairs={{12,0},{13,1},{14,2},{15,3},{8,4},{9,5},{10,6},{11,7},{4,8},{5,9},... | collective-permute-start | bytes 442376 | tf_op jit(solution)/shard_map/ppermute | solution.py:893
  234.7 24.8 %collective-permute-start.39 = (bf16[4,160,768]{2,1,0:T(8,128)(2,1)S(1)}, bf16[4,160,768]{2,1,0:T(8,128)(2,1)S(1)}, u32[]{:S(2)}, u32[]{:S(2)}) collective-permute-start(bf16[4,160,768]{2,1,0:T(8,128)(2,1)S(1)} %slice.266), channel_id=1, source_target_pairs={{0,2},{1,3},{2,0},{3,1},{4,6},{5,7},{6,4},{7,5},{8,10},{9,11},{10,... | collective-permute-start | bytes 2949128 | tf_op jit(solution)/shard_map/ppermute | solution.py:893
  235.9 8.6 %collective-permute-start.44 = (bf16[1,48,2048]{2,1,0:T(8,128)(2,1)S(1)}, bf16[1,48,2048]{2,1,0:T(8,128)(2,1)S(1)}, u32[]{:S(2)}, u32[]{:S(2)}) collective-permute-start(bf16[1,48,2048]{2,1,0:T(8,128)(2,1)S(1)} %split.137), channel_id=1, source_target_pairs={{4,0},{5,1},{6,2},{7,3},{12,4},{13,5},{14,6},{15,7},{0,8},{1,9},{2... | collective-permute-start | bytes 589832 | tf_op jit(solution)/shard_map/ppermute | solution.py:893
  238.0 12.7 %collective-permute-start.46 = (bf16[1,48,1536]{2,1,0:T(8,128)(2,1)S(1)}, bf16[1,48,1536]{2,1,0:T(8,128)(2,1)S(1)}, u32[]{:S(2)}, u32[]{:S(2)}) collective-permute-start(bf16[1,48,1536]{2,1,0:T(8,128)(2,1)S(1)} %get-tuple-element.361), channel_id=1, source_target_pairs={{8,0},{9,1},{10,2},{11,3},{0,4},{1,5},{2,6},{3,7},{12,8},{13,9},{1... | collective-permute-start | bytes 442376 | tf_op jit(solution)/shard_map/ppermute | solution.py:893
  244.6 12.2 %collective-permute-start.49 = (bf16[1,48,2048]{2,1,0:T(8,128)(2,1)S(1)}, bf16[1,48,2048]{2,1,0:T(8,128)(2,1)S(1)}, u32[]{:S(2)}, u32[]{:S(2)}) collective-permute-start(bf16[1,48,2048]{2,1,0:T(8,128)(2,1)S(1)} %fusion.6), channel_id=1, source_target_pairs={{4,0},{5,1},{6,2},{7,3},{12,4},{13,5},{14,6},{15,7},{0,8},{1,9},{2... | collective-permute-start | bytes 589832 | tf_op jit(solution)/shard_map/ppermute | solution.py:893
  249.5 7.3 %collective-permute-start.47 = (bf16[1,48,1152]{2,1,0:T(8,128)(2,1)S(1)}, bf16[1,48,1152]{2,1,0:T(8,128)(2,1)S(1)}, u32[]{:S(2)}, u32[]{:S(2)}) collective-permute-start(bf16[1,48,1152]{2,1,0:T(8,128)(2,1)S(1)} %fusion.11), channel_id=1, source_target_pairs={{4,0},{5,1},{6,2},{7,3},{12,4},{13,5},{14,6},{15,7},{0,8},{1,9},{2... | collective-permute-start | bytes 331784 | tf_op jit(solution)/shard_map/ppermute | solution.py:893
  249.6 13.7 %collective-permute-start.50 = (bf16[1,192,768]{2,1,0:T(8,128)(2,1)S(1)}, bf16[1,192,768]{2,1,0:T(8,128)(2,1)S(1)}, u32[]{:S(2)}, u32[]{:S(2)}) collective-permute-start(bf16[1,192,768]{2,1,0:T(8,128)(2,1)S(1)} %slice.270), channel_id=1, source_target_pairs={{0,2},{1,3},{2,0},{3,1},{4,6},{5,7},{6,4},{7,5},{8,10},{9,11},{10,... | collective-permute-start | bytes 884744 | tf_op jit(solution)/shard_map/ppermute | solution.py:893
  259.8 9.3 %collective-permute-start.52 = (bf16[1,48,1152]{2,1,0:T(8,128)(2,1)S(1)}, bf16[1,48,1152]{2,1,0:T(8,128)(2,1)S(1)}, u32[]{:S(2)}, u32[]{:S(2)}) collective-permute-start(bf16[1,48,1152]{2,1,0:T(8,128)(2,1)S(1)} %fusion.10), channel_id=1, source_target_pairs={{4,0},{5,1},{6,2},{7,3},{12,4},{13,5},{14,6},{15,7},{0,8},{1,9},{2... | collective-permute-start | bytes 331784 | tf_op jit(solution)/shard_map/ppermute | solution.py:893
  263.4 21.3 %collective-permute-start.48 = (bf16[1,160,768]{2,1,0:T(8,128)(2,1)S(1)}, bf16[1,160,768]{2,1,0:T(8,128)(2,1)S(1)}, u32[]{:S(2)}, u32[]{:S(2)}) collective-permute-start(bf16[1,160,768]{2,1,0:T(8,128)(2,1)S(1)} %get-tuple-element.365), channel_id=1, source_target_pairs={{4,0},{5,1},{6,2},{7,3},{12,4},{13,5},{14,6},{15,7},{0,8},{1,9},{2... | collective-permute-start | bytes 737288 | tf_op jit(solution)/shard_map/ppermute | solution.py:893
  264.3 11.0 %collective-permute-start.55 = (bf16[1,48,2048]{2,1,0:T(8,128)(2,1)S(1)}, bf16[1,48,2048]{2,1,0:T(8,128)(2,1)S(1)}, u32[]{:S(2)}, u32[]{:S(2)}) collective-permute-start(bf16[1,48,2048]{2,1,0:T(8,128)(2,1)S(1)} %fusion.5), channel_id=1, source_target_pairs={{4,0},{5,1},{6,2},{7,3},{12,4},{13,5},{14,6},{15,7},{0,8},{1,9},{2... | collective-permute-start | bytes 589832 | tf_op jit(solution)/shard_map/ppermute | solution.py:893
  267.2 17.5 %collective-permute-start.51 = (bf16[1,160,768]{2,1,0:T(8,128)(2,1)S(1)}, bf16[1,160,768]{2,1,0:T(8,128)(2,1)S(1)}, u32[]{:S(2)}, u32[]{:S(2)}) collective-permute-start(bf16[1,160,768]{2,1,0:T(8,128)(2,1)S(1)} %get-tuple-element.368), channel_id=1, source_target_pairs={{12,0},{13,1},{14,2},{15,3},{8,4},{9,5},{10,6},{11,7},{4,8},{5,9},... | collective-permute-start | bytes 737288 | tf_op jit(solution)/shard_map/ppermute | solution.py:893
  267.8 12.1 %collective-permute-start.57 = (bf16[192,768]{1,0:T(8,128)(2,1)S(1)}, bf16[192,768]{1,0:T(8,128)(2,1)S(1)}, u32[]{:S(2)}, u32[]{:S(2)}) collective-permute-start(bf16[192,768]{1,0:T(8,128)(2,1)S(1)} %fusion.7), channel_id=1, source_target_pairs={{1,17},{3,19},{5,21},{7,23},{9,25},{11,27},{13,29},{15,31},{16,0},... | collective-permute-start | bytes 884744 | tf_op jit(solution)/shard_map/ppermute | solution.py:893
  269.2 6.8 %collective-permute-start.53 = (f32[24,1152]{1,0:T(8,128)S(1)}, f32[24,1152]{1,0:T(8,128)S(1)}, u32[]{:S(2)}, u32[]{:S(2)}) collective-permute-start(f32[24,1152]{1,0:T(8,128)S(1)} %get-tuple-element.370), channel_id=1, source_target_pairs={{0,1},{1,0},{2,3},{3,2},{4,5},{5,4},{6,7},{7,6},{8,9},{9,8},{10,11... | collective-permute-start | bytes 331784 | tf_op jit(solution)/shard_map/ppermute | solution.py:893
  276.0 15.1 %collective-permute-start.54 = (bf16[1,160,768]{2,1,0:T(8,128)(2,1)S(1)}, bf16[1,160,768]{2,1,0:T(8,128)(2,1)S(1)}, u32[]{:S(2)}, u32[]{:S(2)}) collective-permute-start(bf16[1,160,768]{2,1,0:T(8,128)(2,1)S(1)} %get-tuple-element.371), channel_id=1, source_target_pairs={{8,0},{9,1},{10,2},{11,3},{0,4},{1,5},{2,6},{3,7},{12,8},{13,9},{1... | collective-permute-start | bytes 737288 | tf_op jit(solution)/shard_map/ppermute | solution.py:893
  279.1 3.3 %collective-permute-start.56 = (f32[24,1920]{1,0:T(8,128)S(1)}, f32[24,1920]{1,0:T(8,128)S(1)}, u32[]{:S(2)}, u32[]{:S(2)}) collective-permute-start(f32[24,1920]{1,0:T(8,128)S(1)} %slice.212), channel_id=1, source_target_pairs={{0,1},{1,0},{2,3},{3,2},{4,5},{5,4},{6,7},{7,6},{8,9},{9,8},{10,11... | collective-permute-start | bytes 552968 | tf_op jit(solution)/shard_map/ppermute | solution.py:893
  280.0 12.0 %collective-permute-start.59 = (f32[96,768]{1,0:T(8,128)S(1)}, f32[96,768]{1,0:T(8,128)S(1)}, u32[]{:S(2)}, u32[]{:S(2)}) collective-permute-start(f32[96,768]{1,0:T(8,128)S(1)} %slice_select_fusion), channel_id=1, source_target_pairs={{0,1},{2,3},{4,5},{6,7},{8,9},{10,11},{12,13},{14,15},{17,16},{19,... | collective-permute-start | bytes 884744 | tf_op jit(solution)/shard_map/ppermute | solution.py:893
  282.5 1.5 collective-permute-start.58

commit v5 on v4

--- a/solution.py
+++ b/solution.py
@@ -22,14 +22,13 @@
 ORDERS = {"X": "zx", "x": "Z", "Q": "zxy", "U": "xzy", "G": "hyx", "D": "zx", "d": "zx", "g": "yxZ", "u": "xyz", "q": "yxz"}
 STREAMS = "XPQUGDCdguqx"
 SEQUENCE = [
-    1, 17, 18, -18, 33, 65, 81, 49, 34, 82, 2, -49, 43, 74, -33, -34, 83, -2,
-    3, -65, -35, 36, 50, 67, -36, 12, -66, -83, 37, -50, 51, -4, 5, -3, -67, 68,
-    84, -51, 60, -37, -84, 97, 85, -97, -52, 53, -5, 6, -85, -6, 94, 200, -68, -86,
-    87, 201, 202, 203, -203, -53, 54, 204, 205, 206, 207, -207, 208, 209, 211, 212, 129, 213,
-    145, -54, 210, 113, 214, -113, 161, -209, 130, -145, 114, 146, -130, 131, 177, -129, -114, 123,
-    -161, 162, -177, 132, -131, 178, -162, 163, -115, 147, -163, 141, -132, -146, 148, 164, 116, -133,
-    -178, -164, 179, -148, 173, 157, -116, 180, 117, 166, -166, 189, 150, -149, -117, 118, 134, -118,
-    -134, -180, -150,
+    17, 1, 18, -18, 33, 65, 81, 34, 49, 2, -49, 43, 82, 74, -33, 3, -34, 83,
+    -2, -65, -35, 36, 50, 67, 37, 12, -66, 51, -50, -4, 5, -3, -67, -36, 68, 84,
+    60, -37, -84, 97, 85, -97, -5, 53, 6, -85, -52, -6, 94, 200, -68, 87, 201, 202,
+    203, -203, -86, 54, -53, 204, 205, -87, 206, 207, 208, 209, 210, 211, 212, 129, 213, 113,
+    145, -54, -209, 214, -113, 161, 130, -145, 114, 146, -130, 131, 177, -129, -114, 123, -161, 162,
+    -177, 178, 163, 147, -162, -163, 132, 141, -147, -132, 148, 164, 116, -115, -178, -164, 179, -148,
+    173, 157, 117, -116, 180, 118, 166, -166, 189, 150, -149, 134, -118, -134, -180, -150,
 ]
 
 

time: 293 us -> 291 us (level)
  waiting for transfers between devices: 120 us -> 117 us
  transfers between devices with their start and end apart: 60 -> 60, of which waited for: 25 -> 30; matrix products, arithmetic and copies ran while one was open for 4% -> 4% of each run, Pallas kernels for 23% -> 23%
where the time goes in v5:
time: 291 us
  waiting for transfers between devices  117 us (40%)
  starting transfers between devices  84 us (29%)
  Pallas kernels  76.5 us (26%)
  other arithmetic  10.2 us (4%)
    ppermute x60, waiting for transfers between devices, move(): got = self.moved[self.label] = lax.ppermute(a, AXES, self.across[way])  117 us
    ppermute x60, starting transfers between devices, move(): got = self.moved[self.label] = lax.ppermute(a, AXES, self.across[way])  84 us
    pallas_call x1, Pallas kernels, attend_back(): pl.pallas_call(functools.partial(attend_back_kernel, places=places, per=p...  26.8 us
    pallas_call x1, Pallas kernels, attend(): pl.pallas_call(functools.partial(attend_kernel, chunk=512), grid=(3,), in...  10.3 us
    pallas_call x1, Pallas kernels, rank(): pl.pallas_call(functools.partial(rank_kernel, numbers=numbers, coarse=coa...  8.45 us
    pallas_call x1, Pallas kernels, project(): pl.pallas_call(functools.partial(project_kernel, places=places, per=per,...  8.17 us
  transfers between devices with their start and end apart: 60, of which 30 were waited for; matrix products, arithmetic and copies ran while one was open for 4% of the time, Pallas kernels for 23%

profile of v5, /device:TPU:0, one launch (start us, length us, event | category | flops | bytes accessed | tf_op | source)
XLA Modules:
  0.0 290.8 jit_solution(3643302930767774984)
XLA Ops:
  4.8 3.0 %collective-permute-start.1 = (bf16[1,48,1152]{2,1,0:T(8,128)(2,1)S(1)}, bf16[1,48,1152]{2,1,0:T(8,128)(2,1)S(1)}, u32[]{:S(2)}, u32[]{:S(2)}) collective-permute-start(bf16[1,48,1152]{2,1,0:T(8,128)(2,1)S(1)} %get-tuple-element.199), channel_id=1, source_target_pairs={{0,4},{1,5},{2,6},{3,7},{4,12},{5,13},{6,14},{7,15},{8,0},{9,1},{1... | collective-permute-start | bytes 331784 | tf_op jit(solution)/shard_map/ppermute | solution.py:892
  9.0 3.7 %collective-permute-done.1 = bf16[1,48,1152]{2,1,0:T(8,128)(2,1)S(1)} collective-permute-done((bf16[1,48,1152]{2,1,0:T(8,128)(2,1)S(1)}, bf16[1,48,1152]{2,1,0:T(8,128)(2,1)S(1)}, u32[]{:S(2)}, u32[]{:S(2)}) %collective-permute-start.1) | collective-permute-done | bytes 110624 | tf_op jit(solution)/shard_map/ppermute | solution.py:892
  12.6 4.1 %collective-permute-start.2 = (bf16[1,48,1152]{2,1,0:T(8,128)(2,1)S(1)}, bf16[1,48,1152]{2,1,0:T(8,128)(2,1)S(1)}, u32[]{:S(2)}, u32[]{:S(2)}) collective-permute-start(bf16[1,48,1152]{2,1,0:T(8,128)(2,1)S(1)} %collective-permute-done.1), channel_id=1, source_target_pairs={{0,4},{1,5},{2,6},{3,7},{4,12},{5,13},{6,14},{7,15},{8,0},{9,1},{1... | collective-permute-start | bytes 331784 | tf_op jit(solution)/shard_map/ppermute | solution.py:892
  16.8 1.5 collective-permute-start.3
  18.3 3.4 %collective-permute-start.5 = (bf16[1,176,768]{2,1,0:T(8,128)(2,1)S(1)}, bf16[1,176,768]{2,1,0:T(8,128)(2,1)S(1)}, u32[]{:S(2)}, u32[]{:S(2)}) collective-permute-start(bf16[1,176,768]{2,1,0:T(8,128)(2,1)S(1)} %bitcast.59), channel_id=1, source_target_pairs={{0,4},{1,5},{2,6},{3,7},{4,12},{5,13},{6,14},{7,15},{8,0},{9,1},{1... | collective-permute-start | bytes 811016 | tf_op jit(solution)/shard_map/ppermute | solution.py:892
  22.4 3.4 %collective-permute-start.9 = (bf16[1,48,1152]{2,1,0:T(8,128)(2,1)S(1)}, bf16[1,48,1152]{2,1,0:T(8,128)(2,1)S(1)}, u32[]{:S(2)}, u32[]{:S(2)}) collective-permute-start(bf16[1,48,1152]{2,1,0:T(8,128)(2,1)S(1)} %collective-permute-done.2), channel_id=1, source_target_pairs={{0,4},{1,5},{2,6},{3,7},{4,12},{5,13},{6,14},{7,15},{8,0},{9,1},{1... | collective-permute-start | bytes 331784 | tf_op jit(solution)/shard_map/ppermute | solution.py:892
  25.8 1.3 collective-permute-start.8
  27.8 1.7 collective-permute-start.11
  30.8 3.4 %collective-permute-start.7 = (bf16[192,768]{1,0:T(8,128)(2,1)S(1)}, bf16[192,768]{1,0:T(8,128)(2,1)S(1)}, u32[]{:S(2)}, u32[]{:S(2)}) collective-permute-start(bf16[192,768]{1,0:T(8,128)(2,1)S(1)} %maximum_select_fusion), channel_id=1, source_target_pairs={{0,16},{2,18},{4,20},{6,22},{8,24},{10,26},{12,28},{14,30},{17,1},... | collective-permute-start | bytes 884744 | tf_op jit(solution)/shard_map/ppermute | solution.py:892
  34.2 3.2 %collective-permute-start.14 = (bf16[2,48,2048]{2,1,0:T(8,128)(2,1)S(1)}, bf16[2,48,2048]{2,1,0:T(8,128)(2,1)S(1)}, u32[]{:S(2)}, u32[]{:S(2)}) collective-permute-start(bf16[2,48,2048]{2,1,0:T(8,128)(2,1)S(1)} %pad_maximum_fusion.6), channel_id=1, source_target_pairs={{0,4},{1,5},{2,6},{3,7},{4,12},{5,13},{6,14},{7,15},{8,0},{9,1},{1... | collective-permute-start | bytes 1179656 | tf_op jit(solution)/shard_map/ppermute | solution.py:892
  37.4 12.2 %collective-permute-done.8 = bf16[2,48,1536]{2,1,0:T(8,128)(2,1)S(1)} collective-permute-done((bf16[2,48,1536]{2,1,0:T(8,128)(2,1)S(1)}, bf16[2,48,1536]{2,1,0:T(8,128)(2,1)S(1)}, u32[]{:S(2)}, u32[]{:S(2)}) %collective-permute-start.8) | collective-permute-done | bytes 294944 | tf_op jit(solution)/shard_map/ppermute | solution.py:892
  49.6 1.6 collective-permute-start.10
  52.0 4.2 %collective-permute-start.16 = (bf16[2,48,2048]{2,1,0:T(8,128)(2,1)S(1)}, bf16[2,48,2048]{2,1,0:T(8,128)(2,1)S(1)}, u32[]{:S(2)}, u32[]{:S(2)}) collective-permute-start(bf16[2,48,2048]{2,1,0:T(8,128)(2,1)S(1)} %collective-permute-done.14), channel_id=1, source_target_pairs={{0,4},{1,5},{2,6},{3,7},{4,12},{5,13},{6,14},{7,15},{8,0},{9,1},{1... | collective-permute-start | bytes 1179656 | tf_op jit(solution)/shard_map/ppermute | solution.py:892
  56.2 5.4 %collective-permute-done.13 = bf16[1,176,768]{2,1,0:T(8,128)(2,1)S(1)} collective-permute-done((bf16[1,176,768]{2,1,0:T(8,128)(2,1)S(1)}, bf16[1,176,768]{2,1,0:T(8,128)(2,1)S(1)}, u32[]{:S(2)}, u32[]{:S(2)}) %collective-permute-start.13) | collective-permute-done | bytes 270368 | tf_op jit(solution)/shard_map/ppermute | solution.py:892
  61.8 1.6 collective-permute-start.19
  63.4 2.5 collective-permute-done.10
  66.1 3.7 %collective-permute-done.16 = bf16[2,48,2048]{2,1,0:T(8,128)(2,1)S(1)} collective-permute-done((bf16[2,48,2048]{2,1,0:T(8,128)(2,1)S(1)}, bf16[2,48,2048]{2,1,0:T(8,128)(2,1)S(1)}, u32[]{:S(2)}, u32[]{:S(2)}) %collective-permute-start.16) | collective-permute-done | bytes 393248 | tf_op jit(solution)/shard_map/ppermute | solution.py:892
  70.6 6.3 %collective-permute-done.15 = bf16[1,192,768]{2,1,0:T(8,128)(2,1)S(1)} collective-permute-done((bf16[1,192,768]{2,1,0:T(8,128)(2,1)S(1)}, bf16[1,192,768]{2,1,0:T(8,128)(2,1)S(1)}, u32[]{:S(2)}, u32[]{:S(2)}) %collective-permute-start.15) | collective-permute-done | bytes 294944 | tf_op jit(solution)/shard_map/ppermute | solution.py:892
  76.9 6.8 %collective-permute-done.17.refs_1_ = bf16[8,48,1152]{2,1,0:T(8,128)(2,1)S(1)} collective-permute-done((bf16[8,48,1152]{2,1,0:T(8,128)(2,1)S(1)}, bf16[8,48,1152]{2,1,0:T(8,128)(2,1)S(1)}, u32[]{:S(2)}, u32[]{:S(2)}) %collective-permute-start.17) | collective-permute-done | bytes 884768 | tf_op jit(solution)/shard_map/ppermute | solution.py:892
  83.8 1.4 collective-permute-done.21.cot_got_ref
  85.5 1.5 collective-permute-start.24
  87.0 1.5 collective-permute-start.26
  88.5 9.6 %collective-permute-done.18 = bf16[1,192,768]{2,1,0:T(8,128)(2,1)S(1)} collective-permute-done((bf16[1,192,768]{2,1,0:T(8,128)(2,1)S(1)}, bf16[1,192,768]{2,1,0:T(8,128)(2,1)S(1)}, u32[]{:S(2)}, u32[]{:S(2)}) %collective-permute-start.18) | collective-permute-done | bytes 294944 | tf_op jit(solution)/shard_map/ppermute | solution.py:892
  99.2 8.5 %rank.1 = (bf16[768,2560]{1,0:T(8,128)(2,1)}, f32[2560,128]{1,0:T(8,128)}, f32[2560,128]{1,0:T(8,128)}, bf16[2560,128]{1,0:T(8,128)(2,1)}, f32[320,128]{1,0:T(8,128)S(1)}) custom-call(s32[4]{0:T(128)S(1)} %pad_add_fusion.me_ref, bf16[8,176,768]{2,1,0:T(8,128)(2,1)S(1)} %constant_dynamic-update-slice_fusion.5.along_ref.note_a_ref.refs_2_.refs_5_, ...), custom_call_target="tpu_custom_call" | custom-call | flops 1 | bytes 1 | tf_op jit(solution)/shard_map/rank/pallas_call | solution.py:246
  107.8 5.9 %collective-permute-done.24.refs_1_ = bf16[8,48,1536]{2,1,0:T(8,128)(2,1)S(1)} collective-permute-done((bf16[8,48,1536]{2,1,0:T(8,128)(2,1)S(1)}, bf16[8,48,1536]{2,1,0:T(8,128)(2,1)S(1)}, u32[]{:S(2)}, u32[]{:S(2)}) %collective-permute-start.24) | collective-permute-done | bytes 1179680 | tf_op jit(solution)/shard_map/ppermute | solution.py:892
  113.7 1.5 collective-permute-start.25
  115.3 8.2 %project.1 = (bf16[320,384]{1,0:T(8,128)(2,1)}, bf16[3,2560,128]{2,1,0:T(8,128)(2,1)}, bf16[3,2560,128]{2,1,0:T(8,128)(2,1)}, bf16[768,1152]{1,0:T(8,128)(2,1)}) custom-call(s32[4]{0:T(128)S(1)} %pad_add_fusion.me_ref, bf16[8,48,1152]{2,1,0:T(8,128)(2,1)S(1)} %constant_dynamic-update-slice_fusion.refs_0_, ...), custom_call_target="tpu_custom_call" | custom-call | flops 1 | bytes 1 | tf_op jit(solution)/shard_map/project/pallas_call | solution.py:306
  123.4 10.3 %attend.1 = (f32[320,384]{1,0:T(8,128)}, bf16[320,384]{1,0:T(8,128)(2,1)S(1)}, bf16[6,320,128]{2,1,0:T(8,128)(2,1)}) custom-call(bf16[320,384]{1,0:T(8,128)(2,1)} %get-tuple-element.330.q_ref, bf16[3,2560,128]{2,1,0:T(8,128)(2,1)} %get-tuple-element.334.k_ref, bf16[3,2560,128]{2,1,0:T(8,128)(2,1)} %get-tuple-element.335.v_ref, ...), custom_call_target="tpu_custom_call" | custom-call | flops 5033164800 | bytes 7864320 | tf_op jit(solution)/shard_map/attend/pallas_call | solution.py:355
  133.9 1.4 collective-permute-done.27.refs_3_
  135.4 1.9 collective-permute-done.28.refs_4_
  137.3 2.8 mid.1
  140.0 1.8 gate_up.1
  141.8 1.6 down.1
  143.7 2.4 collective-permute-done.29.got_ref
  146.1 4.7 %turn.1 = (bf16[160,768]{1,0:T(8,128)(2,1)}, f32[320,768]{1,0:T(8,128)S(1)}, bf16[320,768]{1,0:T(8,128)(2,1)S(1)}, bf16[320,1536]{1,0:T(8,128)(2,1)S(1)}, bf16[3...) custom-call(f32[320,768]{1,0:T(8,128)S(1)} %get-tuple-element.275.part_ref, ...), custom_call_target="tpu_custom_call" | custom-call | flops 2264924160 | bytes 20971520 | tf_op jit(solution)/shard_map/turn/pallas_call | solution.py:555
  150.9 2.2 grad.2
  153.2 3.0 %grad.3 = (f32[8,48,1536]{2,1,0:T(8,128)S(1)}, bf16[8,48,1536]{2,1,0:T(8,128)(2,1)S(1)}) custom-call(s32[4]{0:T(128)S(1)} %pad_add_fusion.me_ref, bf16[320,768]{1,0:T(8,128)(2,1)S(1)} %get-tuple-element.319.refs_2_.left_ref.h1_ref, bf16[320,1536]{1,0:T(8,128)(2,1)S(1)} %get-tuple-element.299.right_ref), custom_call_target="tpu_custom_call" | custom-call | flops 754974720 | bytes 7077888 | tf_op jit(solution)/shard_map/grad/pallas_call | solution.py:622
  156.2 1.6 back.1
  157.9 1.6 collective-permute-start.31
  159.5 2.7 grad_up.1
  162.2 2.0 collective-permute-start.32
  165.0 26.8 %attend_back.1 = (f32[8,160,768]{2,1,0:T(8,128)S(1)}, bf16[8,160,768]{2,1,0:T(8,128)(2,1)S(1)}, f32[8,48,1152]{2,1,0:T(8,128)S(1)}, bf16[8,48,1152]{2,1,0:T(8,128)(2,1)S(1)}) custom-call(s32[4]{0:T(128)S(1)} %pad_add_fusion.me_ref, bf16[320,384]{1,0:T(8,128)(2,1)} %get-tuple-element.330.q_ref, bf16[6,320,128]{2,1,0:T(8,128)(2,1)} %get-tuple-element.331.lse_ref, ...), custom_call_target="tpu_custom_call" | custom-call | flops 20132659200 | bytes 12288000 | tf_op jit(solution)/shard_map/attend_back/pallas_call | solution.py:753
  194.3 7.3 %collective-permute-done.34 = bf16[8,48,2048]{2,1,0:T(8,128)(2,1)} collective-permute-done((bf16[8,48,2048]{2,1,0:T(8,128)(2,1)S(1)}, bf16[8,48,2048]{2,1,0:T(8,128)(2,1)}, u32[]{:S(2)}, u32[]{:S(2)}) %collective-permute-start.34) | collective-permute-done | bytes 1572896 | tf_op jit(solution)/shard_map/ppermute | solution.py:892
  201.6 2.5 collective-permute-start.37
  204.1 2.0 convert_add_fusion.1
  206.8 6.2 %collective-permute-done.33 = bf16[4,48,1536]{2,1,0:T(8,128)(2,1)S(1)} collective-permute-done((bf16[4,48,1536]{2,1,0:T(8,128)(2,1)S(1)}, bf16[4,48,1536]{2,1,0:T(8,128)(2,1)S(1)}, u32[]{:S(2)}, u32[]{:S(2)}) %collective-permute-start.33) | collective-permute-done | bytes 589856 | tf_op jit(solution)/shard_map/ppermute | solution.py:892
  214.8 2.8 collective-permute-start.56
  219.0 10.8 %collective-permute-done.42 = bf16[4,48,2048]{2,1,0:T(8,128)(2,1)S(1)} collective-permute-done((bf16[4,48,2048]{2,1,0:T(8,128)(2,1)S(1)}, bf16[4,48,2048]{2,1,0:T(8,128)(2,1)S(1)}, u32[]{:S(2)}, u32[]{:S(2)}) %collective-permute-start.42) | collective-permute-done | bytes 786464 | tf_op jit(solution)/shard_map/ppermute | solution.py:892
  230.8 2.5 collective-permute-start.41
  235.0 2.4 collective-permute-start.43
  237.4 1.3 collective-permute-start.44
  238.7 1.6 collective-permute-start.57
  240.3 2.4 collective-permute-done.43
  242.8 3.1 %collective-permute-done.44 = bf16[1,48,1536]{2,1,0:T(8,128)(2,1)S(1)} collective-permute-done((bf16[1,48,1536]{2,1,0:T(8,128)(2,1)S(1)}, bf16[1,48,1536]{2,1,0:T(8,128)(2,1)S(1)}, u32[]{:S(2)}, u32[]{:S(2)}) %collective-permute-start.44) | collective-permute-done | bytes 147488 | tf_op jit(solution)/shard_map/ppermute | solution.py:892
  245.9 3.7 %collective-permute-start.48 = (bf16[1,48,2048]{2,1,0:T(8,128)(2,1)S(1)}, bf16[1,48,2048]{2,1,0:T(8,128)(2,1)S(1)}, u32[]{:S(2)}, u32[]{:S(2)}) collective-permute-start(bf16[1,48,2048]{2,1,0:T(8,128)(2,1)S(1)} %fusion.6), channel_id=1, source_target_pairs={{4,0},{5,1},{6,2},{7,3},{12,4},{13,5},{14,6},{15,7},{0,8},{1,9},{2... | collective-permute-start | bytes 589832 | tf_op jit(solution)/shard_map/ppermute | solution.py:892
  251.4 5.2 %collective-permute-done.45 = bf16[1,48,1152]{2,1,0:T(8,128)(2,1)S(1)} collective-permute-done((bf16[1,48,1152]{2,1,0:T(8,128)(2,1)S(1)}, bf16[1,48,1152]{2,1,0:T(8,128)(2,1)S(1)}, u32[]{:S(2)}, u32[]{:S(2)}) %collective-permute-start.45) | collective-permute-done | bytes 110624 | tf_op jit(solution)/shard_map/ppermute | solution.py:892
  256.7 1.9 collective-permute-done.38
  258.9 3.0 %collective-permute-start.50 = (bf16[1,48,1152]{2,1,0:T(8,128)(2,1)S(1)}, bf16[1,48,1152]{2,1,0:T(8,128)(2,1)S(1)}, u32[]{:S(2)}, u32[]{:S(2)}) collective-permute-start(bf16[1,48,1152]{2,1,0:T(8,128)(2,1)S(1)} %fusion.10), channel_id=1, source_target_pairs={{4,0},{5,1},{6,2},{7,3},{12,4},{13,5},{14,6},{15,7},{0,8},{1,9},{2... | collective-permute-start | bytes 331784 | tf_op jit(solution)/shard_map/ppermute | solution.py:892
  262.1 2.6 collective-permute-start.46
  266.1 1.8 collective-permute-start.49
  268.0 7.0 %collective-permute-done.54 = bf16[1,48,2048]{2,1,0:T(8,128)(2,1)S(1)} collective-permute-done((bf16[1,48,2048]{2,1,0:T(8,128)(2,1)S(1)}, bf16[1,48,2048]{2,1,0:T(8,128)(2,1)S(1)}, u32[]{:S(2)}, u32[]{:S(2)}) %collective-permute-start.54) | collective-permute-done | bytes 196640 | tf_op jit(solution)/shard_map/ppermute | solution.py:892
  275.9 2.4 collective-permute-start.59
  280.0 1.9 collective-permute-start.53
  284.9 5.0 %collective-permute-done.53 = bf16[1,160,768]{2,1,0:T(8,128)(2,1)S(1)} collective-permute-done((bf16[1,160,768]{2,1,0:T(8,128)(2,1)S(1)}, bf16[1,160,768]{2,1,0:T(8,128)(2,1)S(1)}, u32[]{:S(2)}, u32[]{:S(2)}) %collective-permute-start.53) | collective-permute-done | bytes 245792 | tf_op jit(solution)/shard_map/ppermute | solution.py:892
  (161 shorter events, 32.0 us)
Async XLA Ops:
  3.1 1.6 collective-permute-start
  4.8 7.9 %collective-permute-start.1 = (bf16[1,48,1152]{2,1,0:T(8,128)(2,1)S(1)}, bf16[1,48,1152]{2,1,0:T(8,128)(2,1)S(1)}, u32[]{:S(2)}, u32[]{:S(2)}) collective-permute-start(bf16[1,48,1152]{2,1,0:T(8,128)(2,1)S(1)} %get-tuple-element.199), channel_id=1, source_target_pairs={{0,4},{1,5},{2,6},{3,7},{4,12},{5,13},{6,14},{7,15},{8,0},{9,1},{1... | collective-permute-start | bytes 331784 | tf_op jit(solution)/shard_map/ppermute | solution.py:892
  7.8 13.8 %collective-permute-start.6 = (bf16[1,48,1536]{2,1,0:T(8,128)(2,1)S(1)}, bf16[1,48,1536]{2,1,0:T(8,128)(2,1)S(1)}, u32[]{:S(2)}, u32[]{:S(2)}) collective-permute-start(bf16[1,48,1536]{2,1,0:T(8,128)(2,1)S(1)} %maximum_select_fusion.4), channel_id=1, source_target_pairs={{0,8},{1,9},{2,10},{3,11},{4,12},{5,13},{6,14},{7,15},{8,0},{9,1},... | collective-permute-start | bytes 442376 | tf_op jit(solution)/shard_map/ppermute | solution.py:892
  12.6 9.1 %collective-permute-start.2 = (bf16[1,48,1152]{2,1,0:T(8,128)(2,1)S(1)}, bf16[1,48,1152]{2,1,0:T(8,128)(2,1)S(1)}, u32[]{:S(2)}, u32[]{:S(2)}) collective-permute-start(bf16[1,48,1152]{2,1,0:T(8,128)(2,1)S(1)} %collective-permute-done.1), channel_id=1, source_target_pairs={{0,4},{1,5},{2,6},{3,7},{4,12},{5,13},{6,14},{7,15},{8,0},{9,1},{1... | collective-permute-start | bytes 331784 | tf_op jit(solution)/shard_map/ppermute | solution.py:892
  16.8 5.7 %collective-permute-start.3 = (bf16[1,48,2048]{2,1,0:T(8,128)(2,1)S(1)}, bf16[1,48,2048]{2,1,0:T(8,128)(2,1)S(1)}, u32[]{:S(2)}, u32[]{:S(2)}) collective-permute-start(bf16[1,48,2048]{2,1,0:T(8,128)(2,1)S(1)} %get-tuple-element.203), channel_id=1, source_target_pairs={{0,2},{1,3},{2,0},{3,1},{4,6},{5,7},{6,4},{7,5},{8,10},{9,11},{10,... | collective-permute-start | bytes 589832 | tf_op jit(solution)/shard_map/ppermute | solution.py:892
  18.3 9.6 %collective-permute-start.5 = (bf16[1,176,768]{2,1,0:T(8,128)(2,1)S(1)}, bf16[1,176,768]{2,1,0:T(8,128)(2,1)S(1)}, u32[]{:S(2)}, u32[]{:S(2)}) collective-permute-start(bf16[1,176,768]{2,1,0:T(8,128)(2,1)S(1)} %bitcast.59), channel_id=1, source_target_pairs={{0,4},{1,5},{2,6},{3,7},{4,12},{5,13},{6,14},{7,15},{8,0},{9,1},{1... | collective-permute-start | bytes 811016 | tf_op jit(solution)/shard_map/ppermute | solution.py:892
  22.4 7.1 %collective-permute-start.9 = (bf16[1,48,1152]{2,1,0:T(8,128)(2,1)S(1)}, bf16[1,48,1152]{2,1,0:T(8,128)(2,1)S(1)}, u32[]{:S(2)}, u32[]{:S(2)}) collective-permute-start(bf16[1,48,1152]{2,1,0:T(8,128)(2,1)S(1)} %collective-permute-done.2), channel_id=1, source_target_pairs={{0,4},{1,5},{2,6},{3,7},{4,12},{5,13},{6,14},{7,15},{8,0},{9,1},{1... | collective-permute-start | bytes 331784 | tf_op jit(solution)/shard_map/ppermute | solution.py:892
  25.8 3.8 %collective-permute-start.4 = (bf16[96,768]{1,0:T(8,128)(2,1)S(1)}, bf16[96,768]{1,0:T(8,128)(2,1)S(1)}, u32[]{:S(2)}, u32[]{:S(2)}) collective-permute-start(bf16[96,768]{1,0:T(8,128)(2,1)S(1)} %get-tuple-element.206), channel_id=1, source_target_pairs={{0,1},{1,0},{2,3},{3,2},{4,5},{5,4},{6,7},{7,6},{8,9},{9,8},{10,11... | collective-permute-start | bytes 442376 | tf_op jit(solution)/shard_map/ppermute | solution.py:892
  25.8 23.7 %collective-permute-start.8 = (bf16[2,48,1536]{2,1,0:T(8,128)(2,1)S(1)}, bf16[2,48,1536]{2,1,0:T(8,128)(2,1)S(1)}, u32[]{:S(2)}, u32[]{:S(2)}) collective-permute-start(bf16[2,48,1536]{2,1,0:T(8,128)(2,1)S(1)} %pad_maximum_fusion.7), channel_id=1, source_target_pairs={{0,4},{1,5},{2,6},{3,7},{4,0},{5,1},{6,2},{7,3},{8,12},{9,13},{10,... | collective-permute-start | bytes 884744 | tf_op jit(solution)/shard_map/ppermute | solution.py:892
  27.8 23.5 %collective-permute-start.11 = (bf16[1,176,768]{2,1,0:T(8,128)(2,1)S(1)}, bf16[1,176,768]{2,1,0:T(8,128)(2,1)S(1)}, u32[]{:S(2)}, u32[]{:S(2)}) collective-permute-start(bf16[1,176,768]{2,1,0:T(8,128)(2,1)S(1)} %collective-permute-done.5), channel_id=1, source_target_pairs={{0,4},{1,5},{2,6},{3,7},{4,12},{5,13},{6,14},{7,15},{8,0},{9,1},{1... | collective-permute-start | bytes 811016 | tf_op jit(solution)/shard_map/ppermute | solution.py:892
  29.7 21.5 %collective-permute-start.12 = (bf16[4,48,1152]{2,1,0:T(8,128)(2,1)S(1)}, bf16[4,48,1152]{2,1,0:T(8,128)(2,1)S(1)}, u32[]{:S(2)}, u32[]{:S(2)}) collective-permute-start(bf16[4,48,1152]{2,1,0:T(8,128)(2,1)S(1)} %pad_maximum_fusion.5), channel_id=1, source_target_pairs={{0,2},{1,3},{2,0},{3,1},{4,6},{5,7},{6,4},{7,5},{8,10},{9,11},{10,... | collective-permute-start | bytes 1327112 | tf_op jit(solution)/shard_map/ppermute | solution.py:892
  30.8 21.1 %collective-permute-start.7 = (bf16[192,768]{1,0:T(8,128)(2,1)S(1)}, bf16[192,768]{1,0:T(8,128)(2,1)S(1)}, u32[]{:S(2)}, u32[]{:S(2)}) collective-permute-start(bf16[192,768]{1,0:T(8,128)(2,1)S(1)} %maximum_select_fusion), channel_id=1, source_target_pairs={{0,16},{2,18},{4,20},{6,22},{8,24},{10,26},{12,28},{14,30},{17,1},... | collective-permute-start | bytes 884744 | tf_op jit(solution)/shard_map/ppermute | solution.py:892
  34.2 17.7 %collective-permute-start.14 = (bf16[2,48,2048]{2,1,0:T(8,128)(2,1)S(1)}, bf16[2,48,2048]{2,1,0:T(8,128)(2,1)S(1)}, u32[]{:S(2)}, u32[]{:S(2)}) collective-permute-start(bf16[2,48,2048]{2,1,0:T(8,128)(2,1)S(1)} %pad_maximum_fusion.6), channel_id=1, source_target_pairs={{0,4},{1,5},{2,6},{3,7},{4,12},{5,13},{6,14},{7,15},{8,0},{9,1},{1... | collective-permute-start | bytes 1179656 | tf_op jit(solution)/shard_map/ppermute | solution.py:892
  49.6 16.3 %collective-permute-start.10 = (bf16[4,48,1536]{2,1,0:T(8,128)(2,1)S(1)}, bf16[4,48,1536]{2,1,0:T(8,128)(2,1)S(1)}, u32[]{:S(2)}, u32[]{:S(2)}) collective-permute-start(bf16[4,48,1536]{2,1,0:T(8,128)(2,1)S(1)} %pad_maximum_fusion.3), channel_id=1, source_target_pairs={{0,16},{1,17},{2,18},{3,19},{4,20},{5,21},{6,22},{7,23},{8,24},{9,... | collective-permute-start | bytes 1769480 | tf_op jit(solution)/shard_map/ppermute | solution.py:892
  51.3 10.4 %collective-permute-start.13 = (bf16[1,176,768]{2,1,0:T(8,128)(2,1)S(1)}, bf16[1,176,768]{2,1,0:T(8,128)(2,1)S(1)}, u32[]{:S(2)}, u32[]{:S(2)}) collective-permute-start(bf16[1,176,768]{2,1,0:T(8,128)(2,1)S(1)} %collective-permute-done.11), channel_id=1, source_target_pairs={{0,4},{1,5},{2,6},{3,7},{4,12},{5,13},{6,14},{7,15},{8,0},{9,1},{1... | collective-permute-start | bytes 811016 | tf_op jit(solution)/shard_map/ppermute | solution.py:892
  51.4 32.3 %collective-permute-start.17 = (bf16[8,48,1152]{2,1,0:T(8,128)(2,1)S(1)}, bf16[8,48,1152]{2,1,0:T(8,128)(2,1)S(1)}, u32[]{:S(2)}, u32[]{:S(2)}) collective-permute-start(bf16[8,48,1152]{2,1,0:T(8,128)(2,1)S(1)} %constant_dynamic-update-slice_fusion.refs_0_), channel_id=1, source_target_pairs={{0,16},{1,17},{2,18},{3,19},{4,20},{5,21},{6,22},{7,23},{8,24},{9,... | collective-permute-start | bytes 2654216 | tf_op jit(solution)/shard_map/ppermute | solution.py:892
  52.0 17.8 %collective-permute-start.16 = (bf16[2,48,2048]{2,1,0:T(8,128)(2,1)S(1)}, bf16[2,48,2048]{2,1,0:T(8,128)(2,1)S(1)}, u32[]{:S(2)}, u32[]{:S(2)}) collective-permute-start(bf16[2,48,2048]{2,1,0:T(8,128)(2,1)S(1)} %collective-permute-done.14), channel_id=1, source_target_pairs={{0,4},{1,5},{2,6},{3,7},{4,12},{5,13},{6,14},{7,15},{8,0},{9,1},{1... | collective-permute-start | bytes 1179656 | tf_op jit(solution)/shard_map/ppermute | solution.py:892
  61.8 21.9 %copy-start = (bf16[160,768]{1,0:T(8,128)(2,1)S(1)}, bf16[160,768]{1,0:T(8,128)(2,1)}, u32[]{:S(2)}) copy-start(bf16[160,768]{1,0:T(8,128)(2,1)} %cot_ref) | copy-start | bytes 737284
  61.8 23.4 %collective-permute-start.19 = (bf16[4,176,768]{2,1,0:T(8,128)(2,1)S(1)}, bf16[4,176,768]{2,1,0:T(8,128)(2,1)S(1)}, u32[]{:S(2)}, u32[]{:S(2)}) collective-permute-start(bf16[4,176,768]{2,1,0:T(8,128)(2,1)S(1)} %pad_maximum_fusion.2), channel_id=1, source_target_pairs={{0,2},{1,3},{2,0},{3,1},{4,6},{5,7},{6,4},{7,5},{8,10},{9,11},{10,... | collective-permute-start | bytes 3244040 | tf_op jit(solution)/shard_map/ppermute | solution.py:892
  66.0 10.9 %collective-permute-start.15 = (bf16[1,192,768]{2,1,0:T(8,128)(2,1)S(1)}, bf16[1,192,768]{2,1,0:T(8,128)(2,1)S(1)}, u32[]{:S(2)}, u32[]{:S(2)}) collective-permute-start(bf16[1,192,768]{2,1,0:T(8,128)(2,1)S(1)} %select_bitcast_fusion.1), channel_id=1, source_target_pairs={{0,4},{1,5},{2,6},{3,7},{4,12},{5,13},{6,14},{7,15},{8,0},{9,1},{1... | collective-permute-start | bytes 884744 | tf_op jit(solution)/shard_map/ppermute | solution.py:892
  69.8 14.0 %collective-permute-start.20 = (bf16[2,48,2048]{2,1,0:T(8,128)(2,1)S(1)}, bf16[2,48,2048]{2,1,0:T(8,128)(2,1)S(1)}, u32[]{:S(2)}, u32[]{:S(2)}) collective-permute-start(bf16[2,48,2048]{2,1,0:T(8,128)(2,1)S(1)} %collective-permute-done.16), channel_id=1, source_target_pairs={{0,4},{1,5},{2,6},{3,7},{4,12},{5,13},{6,14},{7,15},{8,0},{9,1},{1... | collective-permute-start | bytes 1179656 | tf_op jit(solution)/shard_map/ppermute | solution.py:892
  83.7 1.5 collective-permute-start.21
  83.7 15.5 %copy-start.1 = (bf16[192,256]{1,0:T(8,128)(2,1)S(1)}, bf16[192,256]{1,0:T(8,128)(2,1)}, u32[]{:S(2)}) copy-start(bf16[192,256]{1,0:T(8,128)(2,1)} %constant.53.clone.coarse_ref) | copy-start | bytes 294916
  83.8 15.5 %copy-start.2 = (bf16[192,256]{1,0:T(8,128)(2,1)S(1)}, bf16[192,256]{1,0:T(8,128)(2,1)}, u32[]{:S(2)}) copy-start(bf16[192,256]{1,0:T(8,128)(2,1)} %constant.52.clone.fine_ref) | copy-start | bytes 294916
  85.3 12.9 %collective-permute-start.22 = (bf16[8,176,768]{2,1,0:T(8,128)(2,1)S(1)}, bf16[8,176,768]{2,1,0:T(8,128)(2,1)S(1)}, u32[]{:S(2)}, u32[]{:S(2)}) collective-permute-start(bf16[8,176,768]{2,1,0:T(8,128)(2,1)S(1)} %constant_dynamic-update-slice_fusion.5.along_ref.note_a_ref.refs_2_.refs_5_), channel_id=1, source_target_pairs={{0,1},{1,0},{2,3},{3,2},{4,5},{5,4},{6,7},{7,6},{8,9},{9,8},{10,11... | collective-permute-start | bytes 6488072 | tf_op jit(solution)/shard_map/ppermute | solution.py:892
  85.5 28.2 %collective-permute-start.24 = (bf16[8,48,1536]{2,1,0:T(8,128)(2,1)S(1)}, bf16[8,48,1536]{2,1,0:T(8,128)(2,1)S(1)}, u32[]{:S(2)}, u32[]{:S(2)}) collective-permute-start(bf16[8,48,1536]{2,1,0:T(8,128)(2,1)S(1)} %pad_maximum_fusion.refs_0_), channel_id=1, source_target_pairs={{0,2},{1,3},{2,0},{3,1},{4,6},{5,7},{6,4},{7,5},{8,10},{9,11},{10,... | collective-permute-start | bytes 3538952 | tf_op jit(solution)/shard_map/ppermute | solution.py:892
  87.0 46.8 %collective-permute-start.26 = (bf16[8,48,2048]{2,1,0:T(8,128)(2,1)S(1)}, bf16[8,48,2048]{2,1,0:T(8,128)(2,1)S(1)}, u32[]{:S(2)}, u32[]{:S(2)}) collective-permute-start(bf16[8,48,2048]{2,1,0:T(8,128)(2,1)S(1)} %constant_dynamic-update-slice_fusion.10.refs_0_), channel_id=1, source_target_pairs={{0,16},{1,17},{2,18},{3,19},{4,20},{5,21},{6,22},{7,23},{8,24},{9,... | collective-permute-start | bytes 4718600 | tf_op jit(solution)/shard_map/ppermute | solution.py:892
  88.5 9.6 %collective-permute-start.18 = (bf16[1,192,768]{2,1,0:T(8,128)(2,1)S(1)}, bf16[1,192,768]{2,1,0:T(8,128)(2,1)S(1)}, u32[]{:S(2)}, u32[]{:S(2)}) collective-permute-start(bf16[1,192,768]{2,1,0:T(8,128)(2,1)S(1)} %collective-permute-done.15), channel_id=1, source_target_pairs={{0,4},{1,5},{2,6},{3,7},{4,12},{5,13},{6,14},{7,15},{8,0},{9,1},{1... | collective-permute-start | bytes 884744 | tf_op jit(solution)/shard_map/ppermute | solution.py:892
  98.2 9.5 %collective-permute-start.23 = (bf16[1,192,768]{2,1,0:T(8,128)(2,1)S(1)}, bf16[1,192,768]{2,1,0:T(8,128)(2,1)S(1)}, u32[]{:S(2)}, u32[]{:S(2)}) collective-permute-start(bf16[1,192,768]{2,1,0:T(8,128)(2,1)S(1)} %collective-permute-done.18), channel_id=1, source_target_pairs={{0,4},{1,5},{2,6},{3,7},{4,12},{5,13},{6,14},{7,15},{8,0},{9,1},{1... | collective-permute-start | bytes 884744 | tf_op jit(solution)/shard_map/ppermute | solution.py:892
  113.7 28.1 %collective-permute-start.25 = (bf16[4,192,768]{2,1,0:T(8,128)(2,1)S(1)}, bf16[4,192,768]{2,1,0:T(8,128)(2,1)S(1)}, u32[]{:S(2)}, u32[]{:S(2)}) collective-permute-start(bf16[4,192,768]{2,1,0:T(8,128)(2,1)S(1)} %pad_maximum_fusion.1.refs_0_), channel_id=1, source_target_pairs={{0,2},{1,3},{2,0},{3,1},{4,6},{5,7},{6,4},{7,5},{8,10},{9,11},{10,... | collective-permute-start | bytes 3538952 | tf_op jit(solution)/shard_map/ppermute | solution.py:892
  133.7 1.5 collective-permute-start.27
  135.3 2.0 collective-permute-start.28
  143.5 2.6 collective-permute-start.29
  150.8 5.4 %collective-permute-start.30 = (f32[320,768]{1,0:T(8,128)S(1)}, f32[320,768]{1,0:T(8,128)S(1)}, u32[]{:S(2)}, u32[]{:S(2)}) collective-permute-start(f32[320,768]{1,0:T(8,128)S(1)} %get-tuple-element.302.part_ref), channel_id=1, source_target_pairs={{0,1},{1,0},{2,3},{3,2},{4,5},{5,4},{6,7},{7,6},{8,9},{9,8},{10,11... | collective-permute-start | bytes 2949128 | tf_op jit(solution)/shard_map/ppermute | solution.py:892
  157.9 34.7 %collective-permute-start.31 = (bf16[8,48,1536]{2,1,0:T(8,128)(2,1)S(1)}, bf16[8,48,1536]{2,1,0:T(8,128)(2,1)S(1)}, u32[]{:S(2)}, u32[]{:S(2)}) collective-permute-start(bf16[8,48,1536]{2,1,0:T(8,128)(2,1)S(1)} %get-tuple-element.318), channel_id=1, source_target_pairs={{0,16},{1,17},{2,18},{3,19},{4,20},{5,21},{6,22},{7,23},{8,24},{9,... | collective-permute-start | bytes 3538952 | tf_op jit(solution)/shard_map/ppermute | solution.py:892
  162.2 29.7 %collective-permute-start.32 = (bf16[2,192,768]{2,1,0:T(8,128)(2,1)S(1)}, bf16[2,192,768]{2,1,0:T(8,128)(2,1)S(1)}, u32[]{:S(2)}, u32[]{:S(2)}) collective-permute-start(bf16[2,192,768]{2,1,0:T(8,128)(2,1)S(1)} %split.68), channel_id=1, source_target_pairs={{4,0},{5,1},{6,2},{7,3},{12,4},{13,5},{14,6},{15,7},{0,8},{1,9},{2... | collective-permute-start | bytes 1769480 | tf_op jit(solution)/shard_map/ppermute | solution.py:892
  164.2 37.4 %collective-permute-start.34 = (bf16[8,48,2048]{2,1,0:T(8,128)(2,1)S(1)}, bf16[8,48,2048]{2,1,0:T(8,128)(2,1)}, u32[]{:S(2)}, u32[]{:S(2)}) collective-permute-start(bf16[8,48,2048]{2,1,0:T(8,128)(2,1)S(1)} %get-tuple-element.329), channel_id=1, source_target_pairs={{0,2},{1,3},{2,0},{3,1},{4,6},{5,7},{6,4},{7,5},{8,10},{9,11},{10,... | collective-permute-start | bytes 4718600 | tf_op jit(solution)/shard_map/ppermute | solution.py:892
  191.9 22.6 %collective-permute-start.36 = (bf16[8,48,1152]{2,1,0:T(8,128)(2,1)S(1)}, bf16[8,48,1152]{2,1,0:T(8,128)(2,1)S(1)}, u32[]{:S(2)}, u32[]{:S(2)}) collective-permute-start(bf16[8,48,1152]{2,1,0:T(8,128)(2,1)S(1)} %get-tuple-element.344), channel_id=1, source_target_pairs={{0,16},{1,17},{2,18},{3,19},{4,20},{5,21},{6,22},{7,23},{8,24},{9,... | collective-permute-start | bytes 2654216 | tf_op jit(solution)/shard_map/ppermute | solution.py:892
  193.1 19.9 %collective-permute-start.33 = (bf16[4,48,1536]{2,1,0:T(8,128)(2,1)S(1)}, bf16[4,48,1536]{2,1,0:T(8,128)(2,1)S(1)}, u32[]{:S(2)}, u32[]{:S(2)}) collective-permute-start(bf16[4,48,1536]{2,1,0:T(8,128)(2,1)S(1)} %slice.268), channel_id=1, source_target_pairs={{0,2},{1,3},{2,0},{3,1},{4,6},{5,7},{6,4},{7,5},{8,10},{9,11},{10,... | collective-permute-start | bytes 1769480 | tf_op jit(solution)/shard_map/ppermute | solution.py:892
  201.6 16.0 %collective-permute-start.37 = (bf16[2,192,768]{2,1,0:T(8,128)(2,1)S(1)}, bf16[2,192,768]{2,1,0:T(8,128)(2,1)S(1)}, u32[]{:S(2)}, u32[]{:S(2)}) collective-permute-start(bf16[2,192,768]{2,1,0:T(8,128)(2,1)S(1)} %add_convert_fusion.1), channel_id=1, source_target_pairs={{4,0},{5,1},{6,2},{7,3},{12,4},{13,5},{14,6},{15,7},{0,8},{1,9},{2... | collective-permute-start | bytes 1769480 | tf_op jit(solution)/shard_map/ppermute | solution.py:892
  206.2 23.6 %collective-permute-start.42 = (bf16[4,48,2048]{2,1,0:T(8,128)(2,1)S(1)}, bf16[4,48,2048]{2,1,0:T(8,128)(2,1)S(1)}, u32[]{:S(2)}, u32[]{:S(2)}) collective-permute-start(bf16[4,48,2048]{2,1,0:T(8,128)(2,1)S(1)} %slice.267), channel_id=1, source_target_pairs={{0,16},{1,17},{2,18},{3,19},{4,20},{5,21},{6,22},{7,23},{8,24},{9,... | collective-permute-start | bytes 2359304 | tf_op jit(solution)/shard_map/ppermute | solution.py:892
  213.2 17.1 %collective-permute-start.35 = (bf16[8,160,768]{2,1,0:T(8,128)(2,1)S(1)}, bf16[8,160,768]{2,1,0:T(8,128)(2,1)S(1)}, u32[]{:S(2)}, u32[]{:S(2)}) collective-permute-start(bf16[8,160,768]{2,1,0:T(8,128)(2,1)S(1)} %get-tuple-element.349), channel_id=1, source_target_pairs={{0,1},{1,0},{2,3},{3,2},{4,5},{5,4},{6,7},{7,6},{8,9},{9,8},{10,11... | collective-permute-start | bytes 5898248 | tf_op jit(solution)/shard_map/ppermute | solution.py:892
  214.8 34.9 %collective-permute-start.56 = (bf16[1,48,1536]{2,1,0:T(8,128)(2,1)S(1)}, bf16[1,48,1536]{2,1,0:T(8,128)(2,1)S(1)}, u32[]{:S(2)}, u32[]{:S(2)}) collective-permute-start(bf16[1,48,1536]{2,1,0:T(8,128)(2,1)S(1)} %get-tuple-element.348), channel_id=1, source_target_pairs={{4,0},{5,1},{6,2},{7,3},{12,4},{13,5},{14,6},{15,7},{0,8},{1,9},{2... | collective-permute-start | bytes 442376 | tf_op jit(solution)/shard_map/ppermute | solution.py:892
  217.7 15.9 %collective-permute-start.39 = (bf16[2,192,768]{2,1,0:T(8,128)(2,1)S(1)}, bf16[2,192,768]{2,1,0:T(8,128)(2,1)S(1)}, u32[]{:S(2)}, u32[]{:S(2)}) collective-permute-start(bf16[2,192,768]{2,1,0:T(8,128)(2,1)S(1)} %add_convert_fusion), channel_id=1, source_target_pairs={{4,0},{5,1},{6,2},{7,3},{12,4},{13,5},{14,6},{15,7},{0,8},{1,9},{2... | collective-permute-start | bytes 1769480 | tf_op jit(solution)/shard_map/ppermute | solution.py:892
  218.1 12.0 %collective-permute-start.40 = (bf16[4,48,1152]{2,1,0:T(8,128)(2,1)S(1)}, bf16[4,48,1152]{2,1,0:T(8,128)(2,1)S(1)}, u32[]{:S(2)}, u32[]{:S(2)}) collective-permute-start(bf16[4,48,1152]{2,1,0:T(8,128)(2,1)S(1)} %slice.269), channel_id=1, source_target_pairs={{0,2},{1,3},{2,0},{3,1},{4,6},{5,7},{6,4},{7,5},{8,10},{9,11},{10,... | collective-permute-start | bytes 1327112 | tf_op jit(solution)/shard_map/ppermute | solution.py:892
  230.8 6.6 %collective-permute-start.41 = (bf16[1,48,1152]{2,1,0:T(8,128)(2,1)S(1)}, bf16[1,48,1152]{2,1,0:T(8,128)(2,1)S(1)}, u32[]{:S(2)}, u32[]{:S(2)}) collective-permute-start(bf16[1,48,1152]{2,1,0:T(8,128)(2,1)S(1)} %split.138), channel_id=1, source_target_pairs={{4,0},{5,1},{6,2},{7,3},{12,4},{13,5},{14,6},{15,7},{0,8},{1,9},{2... | collective-permute-start | bytes 331784 | tf_op jit(solution)/shard_map/ppermute | solution.py:892
  233.8 24.8 %collective-permute-start.38 = (bf16[4,160,768]{2,1,0:T(8,128)(2,1)S(1)}, bf16[4,160,768]{2,1,0:T(8,128)(2,1)S(1)}, u32[]{:S(2)}, u32[]{:S(2)}) collective-permute-start(bf16[4,160,768]{2,1,0:T(8,128)(2,1)S(1)} %slice.266), channel_id=1, source_target_pairs={{0,2},{1,3},{2,0},{3,1},{4,6},{5,7},{6,4},{7,5},{8,10},{9,11},{10,... | collective-permute-start | bytes 2949128 | tf_op jit(solution)/shard_map/ppermute | solution.py:892
  235.0 7.7 %collective-permute-start.43 = (bf16[1,48,2048]{2,1,0:T(8,128)(2,1)S(1)}, bf16[1,48,2048]{2,1,0:T(8,128)(2,1)S(1)}, u32[]{:S(2)}, u32[]{:S(2)}) collective-permute-start(bf16[1,48,2048]{2,1,0:T(8,128)(2,1)S(1)} %split.137), channel_id=1, source_target_pairs={{4,0},{5,1},{6,2},{7,3},{12,4},{13,5},{14,6},{15,7},{0,8},{1,9},{2... | collective-permute-start | bytes 589832 | tf_op jit(solution)/shard_map/ppermute | solution.py:892
  237.4 8.5 %collective-permute-start.44 = (bf16[1,48,1536]{2,1,0:T(8,128)(2,1)S(1)}, bf16[1,48,1536]{2,1,0:T(8,128)(2,1)S(1)}, u32[]{:S(2)}, u32[]{:S(2)}) collective-permute-start(bf16[1,48,1536]{2,1,0:T(8,128)(2,1)S(1)} %get-tuple-element.356), channel_id=1, source_target_pairs={{12,0},{13,1},{14,2},{15,3},{8,4},{9,5},{10,6},{11,7},{4,8},{5,9},... | collective-permute-start | bytes 442376 | tf_op jit(solution)/shard_map/ppermute | solution.py:892
  238.7 11.4 %collective-permute-start.57 = (bf16[1,48,1536]{2,1,0:T(8,128)(2,1)S(1)}, bf16[1,48,1536]{2,1,0:T(8,128)(2,1)S(1)}, u32[]{:S(2)}, u32[]{:S(2)}) collective-permute-start(bf16[1,48,1536]{2,1,0:T(8,128)(2,1)S(1)} %get-tuple-element.357), channel_id=1, source_target_pairs={{8,0},{9,1},{10,2},{11,3},{0,4},{1,5},{2,6},{3,7},{12,8},{13,9},{1... | collective-permute-start | bytes 442376 | tf_op jit(solution)/shard_map/ppermute | solution.py:892
  245.9 10.7 %collective-permute-start.48 = (bf16[1,48,2048]{2,1,0:T(8,128)(2,1)S(1)}, bf16[1,48,2048]{2,1,0:T(8,128)(2,1)S(1)}, u32[]{:S(2)}, u32[]{:S(2)}) collective-permute-start(bf16[1,48,2048]{2,1,0:T(8,128)(2,1)S(1)} %fusion.6), channel_id=1, source_target_pairs={{4,0},{5,1},{6,2},{7,3},{12,4},{13,5},{14,6},{15,7},{0,8},{1,9},{2... | collective-permute-start | bytes 589832 | tf_op jit(solution)/shard_map/ppermute | solution.py:892
  249.6 7.0 %collective-permute-start.45 = (bf16[1,48,1152]{2,1,0:T(8,128)(2,1)S(1)}, bf16[1,48,1152]{2,1,0:T(8,128)(2,1)S(1)}, u32[]{:S(2)}, u32[]{:S(2)}) collective-permute-start(bf16[1,48,1152]{2,1,0:T(8,128)(2,1)S(1)} %fusion.11), channel_id=1, source_target_pairs={{4,0},{5,1},{6,2},{7,3},{12,4},{13,5},{14,6},{15,7},{0,8},{1,9},{2... | collective-permute-start | bytes 331784 | tf_op jit(solution)/shard_map/ppermute | solution.py:892
  250.2 11.8 %collective-permute-start.47 = (bf16[1,192,768]{2,1,0:T(8,128)(2,1)S(1)}, bf16[1,192,768]{2,1,0:T(8,128)(2,1)S(1)}, u32[]{:S(2)}, u32[]{:S(2)}) collective-permute-start(bf16[1,192,768]{2,1,0:T(8,128)(2,1)S(1)} %slice.270), channel_id=1, source_target_pairs={{0,2},{1,3},{2,0},{3,1},{4,6},{5,7},{6,4},{7,5},{8,10},{9,11},{10,... | collective-permute-start | bytes 884744 | tf_op jit(solution)/shard_map/ppermute | solution.py:892
  258.9 9.0 %collective-permute-start.50 = (bf16[1,48,1152]{2,1,0:T(8,128)(2,1)S(1)}, bf16[1,48,1152]{2,1,0:T(8,128)(2,1)S(1)}, u32[]{:S(2)}, u32[]{:S(2)}) collective-permute-start(bf16[1,48,1152]{2,1,0:T(8,128)(2,1)S(1)} %fusion.10), channel_id=1, source_target_pairs={{4,0},{5,1},{6,2},{7,3},{12,4},{13,5},{14,6},{15,7},{0,8},{1,9},{2... | collective-permute-start | bytes 331784 | tf_op jit(solution)/shard_map/ppermute | solution.py:892
  262.1 22.8 %collective-permute-start.46 = (bf16[1,160,768]{2,1,0:T(8,128)(2,1)S(1)}, bf16[1,160,768]{2,1,0:T(8,128)(2,1)S(1)}, u32[]{:S(2)}, u32[]{:S(2)}) collective-permute-start(bf16[1,160,768]{2,1,0:T(8,128)(2,1)S(1)} %get-tuple-element.361), channel_id=1, source_target_pairs={{4,0},{5,1},{6,2},{7,3},{12,4},{13,5},{14,6},{15,7},{0,8},{1,9},{2... | collective-permute-start | bytes 737288 | tf_op jit(solution)/shard_map/ppermute | solution.py:892
  264.7 10.3 %collective-permute-start.54 = (bf16[1,48,2048]{2,1,0:T(8,128)(2,1)S(1)}, bf16[1,48,2048]{2,1,0:T(8,128)(2,1)S(1)}, u32[]{:S(2)}, u32[]{:S(2)}) collective-permute-start(bf16[1,48,2048]{2,1,0:T(8,128)(2,1)S(1)} %fusion.5), channel_id=1, source_target_pairs={{4,0},{5,1},{6,2},{7,3},{12,4},{13,5},{14,6},{15,7},{0,8},{1,9},{2... | collective-permute-start | bytes 589832 | tf_op jit(solution)/shard_map/ppermute | solution.py:892
  264.8 10.3 %collective-permute-start.51 = (bf16[192,768]{1,0:T(8,128)(2,1)S(1)}, bf16[192,768]{1,0:T(8,128)(2,1)S(1)}, u32[]{:S(2)}, u32[]{:S(2)}) collective-permute-start(bf16[192,768]{1,0:T(8,128)(2,1)S(1)} %fusion.7), channel_id=1, source_target_pairs={{1,17},{3,19},{5,21},{7,23},{9,25},{11,27},{13,29},{15,31},{16,0},... | collective-permute-start | bytes 884744 | tf_op jit(solution)/shard_map/ppermute | solution.py:892
  266.1 18.8 %collective-permute-start.49 = (bf16[1,160,768]{2,1,0:T(8,128)(2,1)S(1)}, bf16[1,160,768]{2,1,0:T(8,128)(2,1)S(1)}, u32[]{:S(2)}, u32[]{:S(2)}) collective-permute-start(bf16[1,160,768]{2,1,0:T(8,128)(2,1)S(1)} %get-tuple-element.365), channel_id=1, source_target_pairs={{12,0},{13,1},{14,2},{15,3},{8,4},{9,5},{10,6},{11,7},{4,8},{5,9},... | collective-permute-start | bytes 737288 | tf_op jit(solution)/shard_map/ppermute | solution.py:892
  275.2 3.1 %collective-permute-start.52 = (f32[24,1152]{1,0:T(8,128)S(1)}, f32[24,1152]{1,0:T(8,128)S(1)}, u32[]{:S(2)}, u32[]{:S(2)}) collective-permute-start(f32[24,1152]{1,0:T(8,128)S(1)} %get-tuple-element.367), channel_id=1, source_target_pairs={{0,1},{1,0},{2,3},{3,2},{4,5},{5,4},{6,7},{7,6},{8,9},{9,8},{10,11... | collective-permute-start | bytes 331784 | tf_op jit(solution)/shard_map/ppermute | solution.py:892
  275.9 8.2 %collective-permute-start.59 = (f32[96,768]{1,0:T(8,128)S(1)}, f32[96,768]{1,0:T(8,128)S(1)}, u32[]{:S(2)}, u32[]{:S(2)}) collective-permute-start(f32[96,768]{1,0:T(8,128)S(1)} %slice_select_fusion), channel_id=1, source_target_pairs={{0,1},{2,3},{4,5},{6,7},{8,9},{10,11},{12,13},{14,15},{17,16},{19,... | collective-permute-start | bytes 884744 | tf_op jit(solution)/shard_map/ppermute | solution.py:892
  278.3 4.4 %collective-permute-start.55 = (f32[24,1920]{1,0:T(8,128)S(1)}, f32[24,1920]{1,0:T(8,128)S(1)}, u32[]{:S(2)}, u32[]{:S(2)}) collective-permute-start(f32[24,1920]{1,0:T(8,128)S(1)} %slice.214), channel_id=1, source_target_pairs={{0,1},{1,0},{2,3},{3,2},{4,5},{5,4},{6,7},{7,6},{8,9},{9,8},{10,11... | collective-permute-start | bytes 552968 | tf_op jit(solution)/shard_map/ppermute | solution.py:892
  278.4 1.6 collective-permute-start.58
  280.0 9.9 %collective-permute-start.53 = (bf16[1,160,768]{2,1,0:T(8,128)(2,1)S(1)}, bf16[1,160,768]{2,1,0:T(8,128)(2,1)S(1)}, u32[]{:S(2)}, u32[]{:S(2)}) collective-permute-start(bf16[1,160,768]{2,1,0:T(8,128)(2,1)S(1)} %get-tuple-element.368), channel_id=1, source_target_pairs={{8,0},{9,1},{10,2},{11,3},{0,4},{1,5},{2,6},{3,7},{12,8},{13,9},{1... | collective-permute-start | bytes 737288 | tf_op jit(solution)/shard_map/ppermute | solution.py:892

commit v6 on v5

--- a/solution.py
+++ b/solution.py
@@ -494,9 +494,11 @@
 
 def down_kernel(me_ref, *refs, places, per, n):
     pieces = refs[:n]
-    hidden_ref, part_ref, w_ref = refs[n:]
+    hidden_ref, part_ref, w_ref, low_ref = refs[n:]
     fill(w_ref, pieces, places(me_ref), per)
-    part_ref[...] = dot(hidden_ref[...], w_ref[...])
+    part = dot(hidden_ref[...], w_ref[...])
+    part_ref[...] = part
+    low_ref[...] = part.astype(BF)
 
 
 def down(me, pieces, places, per, hidden):
@@ -506,8 +508,8 @@
         functools.partial(down_kernel, places=places, per=per, n=len(pieces)),
         grid=(1,),
         in_specs=[scalars()] + [whole(a.shape) for a in [*pieces, hidden]],
-        out_specs=[whole((own, width)), whole((ff, width))],
-        out_shape=[like(own, width), like(ff, width, dtype=BF)],
+        out_specs=[whole((own, width)), whole((ff, width)), whole((own, width))],
+        out_shape=[like(own, width), like(ff, width, dtype=BF), like(own, width, dtype=BF)],
         compiler_params=params(14),
         cost_estimate=pl.CostEstimate(flops=2 * own * width * ff, bytes_accessed=8 << 20, transcendentals=0),
         name="down",
@@ -516,11 +518,11 @@
 
 def turn_kernel(
     part_ref, got_ref, n1_ref, norm_ref, cot_ref, cot_got_ref, keep_ref, gate_ref, up_ref, gate_w_ref, up_w_ref, down_w_ref,
-    out_ref, dr2_ref, dm_ref, dgate_ref, dup_ref, back_ref, sums_ref,
+    out_ref, dr2_ref, dm_ref, dgate_ref, dup_ref, back_ref, sums_ref, low_ref,
 ):
     local = out_ref.shape[0]
     h1 = n1_ref[...] * norm_ref[0:1] + norm_ref[2:3]
-    n2, f2 = normalize(h1 + part_ref[...] + turned(got_ref[...]))
+    n2, f2 = normalize(h1 + part_ref[...] + turned(got_ref[...]).astype(F32))
     keep = keep_ref[:, :1]
     gain = norm_ref[1:2]
     out_ref[...] = ((n2[:local] * gain + norm_ref[3:4]) * keep[:local]).astype(BF)
@@ -546,6 +548,7 @@
         dup_ref[:, at] = dup
         back = back + dot_t(dgate, gate_w_ref[:, at]) + dot_t(dup, up_w_ref[:, at])
     back_ref[...] = back
+    low_ref[...] = back.astype(BF)
 
 
 def turn(part, got, n1, norm, cot, cot_got, keep, gate, up, gate_w, up_w, down_w):
@@ -558,11 +561,11 @@
         in_specs=[whole(a.shape) for a in args],
         out_specs=[
             whole((own // 2, width)), whole((own, width)), whole((own, width)), whole((own, ff)),
-            whole((own, ff)), whole((own, width)), whole((8, width)),
+            whole((own, ff)), whole((own, width)), whole((8, width)), whole((own, width)),
         ],
         out_shape=[
             like(own // 2, width, dtype=BF), like(own, width), like(own, width, dtype=BF),
-            like(own, ff, dtype=BF), like(own, ff, dtype=BF), like(own, width), like(8, width),
+            like(own, ff, dtype=BF), like(own, ff, dtype=BF), like(own, width), like(8, width), like(own, width, dtype=BF),
         ],
         compiler_params=params(34),
         cost_estimate=pl.CostEstimate(flops=6 * own * width * ff, bytes_accessed=20 << 20, transcendentals=own * ff),
@@ -571,7 +574,7 @@
 
 
 def back_kernel(me_ref, dr2_ref, part_ref, got_ref, n1_ref, f1_ref, norm_ref, w_ref, dr1_ref, da_ref, dob_ref, sums_ref):
-    dh1 = dr2_ref[...] + part_ref[...] + turned(got_ref[...])
+    dh1 = dr2_ref[...] + part_ref[...] + turned(got_ref[...]).astype(F32)
     n1 = n1_ref[...]
     sums_ref[0:1] = jnp.sum(dh1 * n1, axis=0, keepdims=True)
     sums_ref[1:2] = jnp.sum(dh1, axis=0, keepdims=True)
@@ -1120,18 +1123,18 @@
         got["down"] = grid.work(lambda *a: down(me, list(a[:-1]), at, per, a[-1]), *pieces, got["gate"][1])
 
     def part_move():
-        got["part"] = grid.move("c", got["down"][0])
+        got["part"] = grid.move("c", got["down"][2])
 
     def turn_():
         n1, _, _, up, _, _, up_w, _ = got["mid"]
         gate, _, gate_w = got["gate"]
-        part, down_w = got["down"]
+        part, down_w, _ = got["down"]
         got["turn"] = grid.work(
             turn, part, got["part"], n1, got["norm"], cotangent, got["C"], got["rank"][4], gate, up, gate_w, up_w, down_w
         )
 
     def back_move():
-        got["back_part"] = grid.move("c", got["turn"][5])
+        got["back_part"] = grid.move("c", got["turn"][7])
 
     def grad_d():
         order = orders["d"]

time: 291 us -> 290 us (level)
  no operation moved by 1% of the time
where the time goes in v6:
time: 290 us
  waiting for transfers between devices  116 us (40%)
  starting transfers between devices  84 us (29%)
  Pallas kernels  76.1 us (26%)
  other arithmetic  10.2 us (4%)
    ppermute x60, waiting for transfers between devices, move(): got = self.moved[self.label] = lax.ppermute(a, AXES, self.across[way])  116 us
    ppermute x60, starting transfers between devices, move(): got = self.moved[self.label] = lax.ppermute(a, AXES, self.across[way])  84 us
    pallas_call x1, Pallas kernels, attend_back(): pl.pallas_call(functools.partial(attend_back_kernel, places=places, per=p...  26.8 us
    pallas_call x1, Pallas kernels, attend(): pl.pallas_call(functools.partial(attend_kernel, chunk=512), grid=(3,), in...  10.3 us
    pallas_call x1, Pallas kernels, rank(): pl.pallas_call(functools.partial(rank_kernel, numbers=numbers, coarse=coa...  8.46 us
    pallas_call x1, Pallas kernels, project(): pl.pallas_call(functools.partial(project_kernel, places=places, per=per,...  8.17 us
  transfers between devices with their start and end apart: 60, of which 30 were waited for; matrix products, arithmetic and copies ran while one was open for 4% of the time, Pallas kernels for 23%

profile of v6, /device:TPU:0, one launch (start us, length us, event | category | flops | bytes accessed | tf_op | source)
XLA Modules:
  0.0 289.7 jit_solution(7213613798836941124)
XLA Ops:
  4.8 3.0 %collective-permute-start.1 = (bf16[1,48,1152]{2,1,0:T(8,128)(2,1)S(1)}, bf16[1,48,1152]{2,1,0:T(8,128)(2,1)S(1)}, u32[]{:S(2)}, u32[]{:S(2)}) collective-permute-start(bf16[1,48,1152]{2,1,0:T(8,128)(2,1)S(1)} %get-tuple-element.201), channel_id=1, source_target_pairs={{0,4},{1,5},{2,6},{3,7},{4,12},{5,13},{6,14},{7,15},{8,0},{9,1},{1... | collective-permute-start | bytes 331784 | tf_op jit(solution)/shard_map/ppermute | solution.py:895
  9.0 3.7 %collective-permute-done.1 = bf16[1,48,1152]{2,1,0:T(8,128)(2,1)S(1)} collective-permute-done((bf16[1,48,1152]{2,1,0:T(8,128)(2,1)S(1)}, bf16[1,48,1152]{2,1,0:T(8,128)(2,1)S(1)}, u32[]{:S(2)}, u32[]{:S(2)}) %collective-permute-start.1) | collective-permute-done | bytes 110624 | tf_op jit(solution)/shard_map/ppermute | solution.py:895
  12.6 4.1 %collective-permute-start.2 = (bf16[1,48,1152]{2,1,0:T(8,128)(2,1)S(1)}, bf16[1,48,1152]{2,1,0:T(8,128)(2,1)S(1)}, u32[]{:S(2)}, u32[]{:S(2)}) collective-permute-start(bf16[1,48,1152]{2,1,0:T(8,128)(2,1)S(1)} %collective-permute-done.1), channel_id=1, source_target_pairs={{0,4},{1,5},{2,6},{3,7},{4,12},{5,13},{6,14},{7,15},{8,0},{9,1},{1... | collective-permute-start | bytes 331784 | tf_op jit(solution)/shard_map/ppermute | solution.py:895
  16.8 1.5 collective-permute-start.3
  18.3 3.4 %collective-permute-start.5 = (bf16[1,176,768]{2,1,0:T(8,128)(2,1)S(1)}, bf16[1,176,768]{2,1,0:T(8,128)(2,1)S(1)}, u32[]{:S(2)}, u32[]{:S(2)}) collective-permute-start(bf16[1,176,768]{2,1,0:T(8,128)(2,1)S(1)} %bitcast.59), channel_id=1, source_target_pairs={{0,4},{1,5},{2,6},{3,7},{4,12},{5,13},{6,14},{7,15},{8,0},{9,1},{1... | collective-permute-start | bytes 811016 | tf_op jit(solution)/shard_map/ppermute | solution.py:895
  22.4 3.4 %collective-permute-start.9 = (bf16[1,48,1152]{2,1,0:T(8,128)(2,1)S(1)}, bf16[1,48,1152]{2,1,0:T(8,128)(2,1)S(1)}, u32[]{:S(2)}, u32[]{:S(2)}) collective-permute-start(bf16[1,48,1152]{2,1,0:T(8,128)(2,1)S(1)} %collective-permute-done.2), channel_id=1, source_target_pairs={{0,4},{1,5},{2,6},{3,7},{4,12},{5,13},{6,14},{7,15},{8,0},{9,1},{1... | collective-permute-start | bytes 331784 | tf_op jit(solution)/shard_map/ppermute | solution.py:895
  25.8 1.3 collective-permute-start.8
  27.8 1.7 collective-permute-start.11
  30.8 3.4 %collective-permute-start.7 = (bf16[192,768]{1,0:T(8,128)(2,1)S(1)}, bf16[192,768]{1,0:T(8,128)(2,1)S(1)}, u32[]{:S(2)}, u32[]{:S(2)}) collective-permute-start(bf16[192,768]{1,0:T(8,128)(2,1)S(1)} %maximum_select_fusion), channel_id=1, source_target_pairs={{0,16},{2,18},{4,20},{6,22},{8,24},{10,26},{12,28},{14,30},{17,1},... | collective-permute-start | bytes 884744 | tf_op jit(solution)/shard_map/ppermute | solution.py:895
  34.2 3.2 %collective-permute-start.14 = (bf16[2,48,2048]{2,1,0:T(8,128)(2,1)S(1)}, bf16[2,48,2048]{2,1,0:T(8,128)(2,1)S(1)}, u32[]{:S(2)}, u32[]{:S(2)}) collective-permute-start(bf16[2,48,2048]{2,1,0:T(8,128)(2,1)S(1)} %pad_maximum_fusion.6), channel_id=1, source_target_pairs={{0,4},{1,5},{2,6},{3,7},{4,12},{5,13},{6,14},{7,15},{8,0},{9,1},{1... | collective-permute-start | bytes 1179656 | tf_op jit(solution)/shard_map/ppermute | solution.py:895
  37.4 12.2 %collective-permute-done.8 = bf16[2,48,1536]{2,1,0:T(8,128)(2,1)S(1)} collective-permute-done((bf16[2,48,1536]{2,1,0:T(8,128)(2,1)S(1)}, bf16[2,48,1536]{2,1,0:T(8,128)(2,1)S(1)}, u32[]{:S(2)}, u32[]{:S(2)}) %collective-permute-start.8) | collective-permute-done | bytes 294944 | tf_op jit(solution)/shard_map/ppermute | solution.py:895
  49.6 1.6 collective-permute-start.10
  52.0 4.2 %collective-permute-start.16 = (bf16[2,48,2048]{2,1,0:T(8,128)(2,1)S(1)}, bf16[2,48,2048]{2,1,0:T(8,128)(2,1)S(1)}, u32[]{:S(2)}, u32[]{:S(2)}) collective-permute-start(bf16[2,48,2048]{2,1,0:T(8,128)(2,1)S(1)} %collective-permute-done.14), channel_id=1, source_target_pairs={{0,4},{1,5},{2,6},{3,7},{4,12},{5,13},{6,14},{7,15},{8,0},{9,1},{1... | collective-permute-start | bytes 1179656 | tf_op jit(solution)/shard_map/ppermute | solution.py:895
  56.2 5.4 %collective-permute-done.13 = bf16[1,176,768]{2,1,0:T(8,128)(2,1)S(1)} collective-permute-done((bf16[1,176,768]{2,1,0:T(8,128)(2,1)S(1)}, bf16[1,176,768]{2,1,0:T(8,128)(2,1)S(1)}, u32[]{:S(2)}, u32[]{:S(2)}) %collective-permute-start.13) | collective-permute-done | bytes 270368 | tf_op jit(solution)/shard_map/ppermute | solution.py:895
  61.8 1.6 collective-permute-start.19
  63.4 2.5 collective-permute-done.10
  66.1 3.7 %collective-permute-done.16 = bf16[2,48,2048]{2,1,0:T(8,128)(2,1)S(1)} collective-permute-done((bf16[2,48,2048]{2,1,0:T(8,128)(2,1)S(1)}, bf16[2,48,2048]{2,1,0:T(8,128)(2,1)S(1)}, u32[]{:S(2)}, u32[]{:S(2)}) %collective-permute-start.16) | collective-permute-done | bytes 393248 | tf_op jit(solution)/shard_map/ppermute | solution.py:895
  70.6 6.3 %collective-permute-done.15 = bf16[1,192,768]{2,1,0:T(8,128)(2,1)S(1)} collective-permute-done((bf16[1,192,768]{2,1,0:T(8,128)(2,1)S(1)}, bf16[1,192,768]{2,1,0:T(8,128)(2,1)S(1)}, u32[]{:S(2)}, u32[]{:S(2)}) %collective-permute-start.15) | collective-permute-done | bytes 294944 | tf_op jit(solution)/shard_map/ppermute | solution.py:895
  76.9 6.8 %collective-permute-done.17.refs_1_ = bf16[8,48,1152]{2,1,0:T(8,128)(2,1)S(1)} collective-permute-done((bf16[8,48,1152]{2,1,0:T(8,128)(2,1)S(1)}, bf16[8,48,1152]{2,1,0:T(8,128)(2,1)S(1)}, u32[]{:S(2)}, u32[]{:S(2)}) %collective-permute-start.17) | collective-permute-done | bytes 884768 | tf_op jit(solution)/shard_map/ppermute | solution.py:895
  83.8 1.4 collective-permute-done.21.cot_got_ref
  85.5 1.5 collective-permute-start.24
  87.0 1.5 collective-permute-start.26
  88.5 9.6 %collective-permute-done.18 = bf16[1,192,768]{2,1,0:T(8,128)(2,1)S(1)} collective-permute-done((bf16[1,192,768]{2,1,0:T(8,128)(2,1)S(1)}, bf16[1,192,768]{2,1,0:T(8,128)(2,1)S(1)}, u32[]{:S(2)}, u32[]{:S(2)}) %collective-permute-start.18) | collective-permute-done | bytes 294944 | tf_op jit(solution)/shard_map/ppermute | solution.py:895
  99.2 8.5 %rank.1 = (bf16[768,2560]{1,0:T(8,128)(2,1)}, f32[2560,128]{1,0:T(8,128)}, f32[2560,128]{1,0:T(8,128)}, bf16[2560,128]{1,0:T(8,128)(2,1)}, f32[320,128]{1,0:T(8,128)S(1)}) custom-call(s32[4]{0:T(128)S(1)} %pad_add_fusion.me_ref, bf16[8,176,768]{2,1,0:T(8,128)(2,1)S(1)} %constant_dynamic-update-slice_fusion.5.along_ref.note_a_ref.refs_2_.refs_5_, ...), custom_call_target="tpu_custom_call" | custom-call | flops 1 | bytes 1 | tf_op jit(solution)/shard_map/rank/pallas_call | solution.py:246
  107.8 5.9 %collective-permute-done.24.refs_1_ = bf16[8,48,1536]{2,1,0:T(8,128)(2,1)S(1)} collective-permute-done((bf16[8,48,1536]{2,1,0:T(8,128)(2,1)S(1)}, bf16[8,48,1536]{2,1,0:T(8,128)(2,1)S(1)}, u32[]{:S(2)}, u32[]{:S(2)}) %collective-permute-start.24) | collective-permute-done | bytes 1179680 | tf_op jit(solution)/shard_map/ppermute | solution.py:895
  113.7 1.5 collective-permute-start.25
  115.3 8.2 %project.1 = (bf16[320,384]{1,0:T(8,128)(2,1)}, bf16[3,2560,128]{2,1,0:T(8,128)(2,1)}, bf16[3,2560,128]{2,1,0:T(8,128)(2,1)}, bf16[768,1152]{1,0:T(8,128)(2,1)}) custom-call(s32[4]{0:T(128)S(1)} %pad_add_fusion.me_ref, bf16[8,48,1152]{2,1,0:T(8,128)(2,1)S(1)} %constant_dynamic-update-slice_fusion.refs_0_, ...), custom_call_target="tpu_custom_call" | custom-call | flops 1 | bytes 1 | tf_op jit(solution)/shard_map/project/pallas_call | solution.py:306
  123.4 10.3 %attend.1 = (f32[320,384]{1,0:T(8,128)}, bf16[320,384]{1,0:T(8,128)(2,1)S(1)}, bf16[6,320,128]{2,1,0:T(8,128)(2,1)}) custom-call(bf16[320,384]{1,0:T(8,128)(2,1)} %get-tuple-element.334.q_ref, bf16[3,2560,128]{2,1,0:T(8,128)(2,1)} %get-tuple-element.338.k_ref, bf16[3,2560,128]{2,1,0:T(8,128)(2,1)} %get-tuple-element.339.v_ref, ...), custom_call_target="tpu_custom_call" | custom-call | flops 5033164800 | bytes 7864320 | tf_op jit(solution)/shard_map/attend/pallas_call | solution.py:355
  133.9 1.4 collective-permute-done.27.refs_3_
  135.4 1.9 collective-permute-done.28.refs_4_
  137.3 2.8 mid.1
  140.0 1.8 gate_up.1
  141.8 1.6 down.1
  143.7 1.7 collective-permute-done.29.got_ref
  145.4 4.3 %turn.1 = (bf16[160,768]{1,0:T(8,128)(2,1)}, f32[320,768]{1,0:T(8,128)S(1)}, bf16[320,768]{1,0:T(8,128)(2,1)S(1)}, bf16[320,1536]{1,0:T(8,128)(2,1)S(1)}, bf16[3...) custom-call(f32[320,768]{1,0:T(8,128)S(1)} %get-tuple-element.278.part_re, ...), custom_call_target="tpu_custom_call" | custom-call | flops 2264924160 | bytes 20971520 | tf_op jit(solution)/shard_map/turn/pallas_call | solution.py:558
  149.9 2.2 grad.2
  152.2 3.0 %grad.3 = (f32[8,48,1536]{2,1,0:T(8,128)S(1)}, bf16[8,48,1536]{2,1,0:T(8,128)(2,1)S(1)}) custom-call(s32[4]{0:T(128)S(1)} %pad_add_fusion.me_ref, bf16[320,768]{1,0:T(8,128)(2,1)S(1)} %get-tuple-element.323.refs_2_.left_ref.h1_ref, bf16[320,1536]{1,0:T(8,128)(2,1)S(1)} %get-tuple-element.303.right_ref), custom_call_target="tpu_custom_call" | custom-call | flops 754974720 | bytes 7077888 | tf_op jit(solution)/shard_map/grad/pallas_call | solution.py:625
  155.2 1.6 back.1
  156.8 1.6 collective-permute-start.31
  158.4 2.7 grad_up.1
  161.1 2.0 collective-permute-start.32
  164.0 26.8 %attend_back.1 = (f32[8,160,768]{2,1,0:T(8,128)S(1)}, bf16[8,160,768]{2,1,0:T(8,128)(2,1)S(1)}, f32[8,48,1152]{2,1,0:T(8,128)S(1)}, bf16[8,48,1152]{2,1,0:T(8,128)(2,1)S(1)}) custom-call(s32[4]{0:T(128)S(1)} %pad_add_fusion.me_ref, bf16[320,384]{1,0:T(8,128)(2,1)} %get-tuple-element.334.q_ref, bf16[6,320,128]{2,1,0:T(8,128)(2,1)} %get-tuple-element.335.lse_ref, ...), custom_call_target="tpu_custom_call" | custom-call | flops 20132659200 | bytes 12288000 | tf_op jit(solution)/shard_map/attend_back/pallas_call | solution.py:756
  193.3 7.3 %collective-permute-done.34 = bf16[8,48,2048]{2,1,0:T(8,128)(2,1)} collective-permute-done((bf16[8,48,2048]{2,1,0:T(8,128)(2,1)S(1)}, bf16[8,48,2048]{2,1,0:T(8,128)(2,1)}, u32[]{:S(2)}, u32[]{:S(2)}) %collective-permute-start.34) | collective-permute-done | bytes 1572896 | tf_op jit(solution)/shard_map/ppermute | solution.py:895
  200.5 2.5 collective-permute-start.37
  203.0 2.0 convert_add_fusion.1
  205.7 6.1 %collective-permute-done.33 = bf16[4,48,1536]{2,1,0:T(8,128)(2,1)S(1)} collective-permute-done((bf16[4,48,1536]{2,1,0:T(8,128)(2,1)S(1)}, bf16[4,48,1536]{2,1,0:T(8,128)(2,1)S(1)}, u32[]{:S(2)}, u32[]{:S(2)}) %collective-permute-start.33) | collective-permute-done | bytes 589856 | tf_op jit(solution)/shard_map/ppermute | solution.py:895
  213.7 2.8 collective-permute-start.56
  217.9 10.9 %collective-permute-done.42 = bf16[4,48,2048]{2,1,0:T(8,128)(2,1)S(1)} collective-permute-done((bf16[4,48,2048]{2,1,0:T(8,128)(2,1)S(1)}, bf16[4,48,2048]{2,1,0:T(8,128)(2,1)S(1)}, u32[]{:S(2)}, u32[]{:S(2)}) %collective-permute-start.42) | collective-permute-done | bytes 786464 | tf_op jit(solution)/shard_map/ppermute | solution.py:895
  229.7 2.5 collective-permute-start.41
  232.7 1.3 collective-permute-start.38
  234.0 2.3 collective-permute-start.43
  237.6 1.6 collective-permute-start.57
  239.2 2.4 collective-permute-done.43
  241.7 3.1 %collective-permute-done.44 = bf16[1,48,1536]{2,1,0:T(8,128)(2,1)S(1)} collective-permute-done((bf16[1,48,1536]{2,1,0:T(8,128)(2,1)S(1)}, bf16[1,48,1536]{2,1,0:T(8,128)(2,1)S(1)}, u32[]{:S(2)}, u32[]{:S(2)}) %collective-permute-start.44) | collective-permute-done | bytes 147488 | tf_op jit(solution)/shard_map/ppermute | solution.py:895
  244.8 3.7 %collective-permute-start.48 = (bf16[1,48,2048]{2,1,0:T(8,128)(2,1)S(1)}, bf16[1,48,2048]{2,1,0:T(8,128)(2,1)S(1)}, u32[]{:S(2)}, u32[]{:S(2)}) collective-permute-start(bf16[1,48,2048]{2,1,0:T(8,128)(2,1)S(1)} %fusion.6), channel_id=1, source_target_pairs={{4,0},{5,1},{6,2},{7,3},{12,4},{13,5},{14,6},{15,7},{0,8},{1,9},{2... | collective-permute-start | bytes 589832 | tf_op jit(solution)/shard_map/ppermute | solution.py:895
  250.3 5.2 %collective-permute-done.45 = bf16[1,48,1152]{2,1,0:T(8,128)(2,1)S(1)} collective-permute-done((bf16[1,48,1152]{2,1,0:T(8,128)(2,1)S(1)}, bf16[1,48,1152]{2,1,0:T(8,128)(2,1)S(1)}, u32[]{:S(2)}, u32[]{:S(2)}) %collective-permute-start.45) | collective-permute-done | bytes 110624 | tf_op jit(solution)/shard_map/ppermute | solution.py:895
  255.6 1.9 collective-permute-done.38
  257.8 3.0 %collective-permute-start.50 = (bf16[1,48,1152]{2,1,0:T(8,128)(2,1)S(1)}, bf16[1,48,1152]{2,1,0:T(8,128)(2,1)S(1)}, u32[]{:S(2)}, u32[]{:S(2)}) collective-permute-start(bf16[1,48,1152]{2,1,0:T(8,128)(2,1)S(1)} %fusion.10), channel_id=1, source_target_pairs={{4,0},{5,1},{6,2},{7,3},{12,4},{13,5},{14,6},{15,7},{0,8},{1,9},{2... | collective-permute-start | bytes 331784 | tf_op jit(solution)/shard_map/ppermute | solution.py:895
  261.0 2.6 collective-permute-start.46
  265.0 1.8 collective-permute-start.49
  266.9 7.0 %collective-permute-done.54 = bf16[1,48,2048]{2,1,0:T(8,128)(2,1)S(1)} collective-permute-done((bf16[1,48,2048]{2,1,0:T(8,128)(2,1)S(1)}, bf16[1,48,2048]{2,1,0:T(8,128)(2,1)S(1)}, u32[]{:S(2)}, u32[]{:S(2)}) %collective-permute-start.54) | collective-permute-done | bytes 196640 | tf_op jit(solution)/shard_map/ppermute | solution.py:895
  274.8 2.4 collective-permute-start.59
  278.9 2.0 collective-permute-start.53
  283.8 5.0 %collective-permute-done.53 = bf16[1,160,768]{2,1,0:T(8,128)(2,1)S(1)} collective-permute-done((bf16[1,160,768]{2,1,0:T(8,128)(2,1)S(1)}, bf16[1,160,768]{2,1,0:T(8,128)(2,1)S(1)}, u32[]{:S(2)}, u32[]{:S(2)}) %collective-permute-start.53) | collective-permute-done | bytes 245792 | tf_op jit(solution)/shard_map/ppermute | solution.py:895
  (161 shorter events, 32.1 us)
Async XLA Ops:
  3.1 1.6 collective-permute-start
  4.8 7.9 %collective-permute-start.1 = (bf16[1,48,1152]{2,1,0:T(8,128)(2,1)S(1)}, bf16[1,48,1152]{2,1,0:T(8,128)(2,1)S(1)}, u32[]{:S(2)}, u32[]{:S(2)}) collective-permute-start(bf16[1,48,1152]{2,1,0:T(8,128)(2,1)S(1)} %get-tuple-element.201), channel_id=1, source_target_pairs={{0,4},{1,5},{2,6},{3,7},{4,12},{5,13},{6,14},{7,15},{8,0},{9,1},{1... | collective-permute-start | bytes 331784 | tf_op jit(solution)/shard_map/ppermute | solution.py:895
  7.8 13.8 %collective-permute-start.6 = (bf16[1,48,1536]{2,1,0:T(8,128)(2,1)S(1)}, bf16[1,48,1536]{2,1,0:T(8,128)(2,1)S(1)}, u32[]{:S(2)}, u32[]{:S(2)}) collective-permute-start(bf16[1,48,1536]{2,1,0:T(8,128)(2,1)S(1)} %maximum_select_fusion.4), channel_id=1, source_target_pairs={{0,8},{1,9},{2,10},{3,11},{4,12},{5,13},{6,14},{7,15},{8,0},{9,1},... | collective-permute-start | bytes 442376 | tf_op jit(solution)/shard_map/ppermute | solution.py:895
  12.6 9.1 %collective-permute-start.2 = (bf16[1,48,1152]{2,1,0:T(8,128)(2,1)S(1)}, bf16[1,48,1152]{2,1,0:T(8,128)(2,1)S(1)}, u32[]{:S(2)}, u32[]{:S(2)}) collective-permute-start(bf16[1,48,1152]{2,1,0:T(8,128)(2,1)S(1)} %collective-permute-done.1), channel_id=1, source_target_pairs={{0,4},{1,5},{2,6},{3,7},{4,12},{5,13},{6,14},{7,15},{8,0},{9,1},{1... | collective-permute-start | bytes 331784 | tf_op jit(solution)/shard_map/ppermute | solution.py:895
  16.8 5.7 %collective-permute-start.3 = (bf16[1,48,2048]{2,1,0:T(8,128)(2,1)S(1)}, bf16[1,48,2048]{2,1,0:T(8,128)(2,1)S(1)}, u32[]{:S(2)}, u32[]{:S(2)}) collective-permute-start(bf16[1,48,2048]{2,1,0:T(8,128)(2,1)S(1)} %get-tuple-element.205), channel_id=1, source_target_pairs={{0,2},{1,3},{2,0},{3,1},{4,6},{5,7},{6,4},{7,5},{8,10},{9,11},{10,... | collective-permute-start | bytes 589832 | tf_op jit(solution)/shard_map/ppermute | solution.py:895
  18.3 9.6 %collective-permute-start.5 = (bf16[1,176,768]{2,1,0:T(8,128)(2,1)S(1)}, bf16[1,176,768]{2,1,0:T(8,128)(2,1)S(1)}, u32[]{:S(2)}, u32[]{:S(2)}) collective-permute-start(bf16[1,176,768]{2,1,0:T(8,128)(2,1)S(1)} %bitcast.59), channel_id=1, source_target_pairs={{0,4},{1,5},{2,6},{3,7},{4,12},{5,13},{6,14},{7,15},{8,0},{9,1},{1... | collective-permute-start | bytes 811016 | tf_op jit(solution)/shard_map/ppermute | solution.py:895
  22.4 7.1 %collective-permute-start.9 = (bf16[1,48,1152]{2,1,0:T(8,128)(2,1)S(1)}, bf16[1,48,1152]{2,1,0:T(8,128)(2,1)S(1)}, u32[]{:S(2)}, u32[]{:S(2)}) collective-permute-start(bf16[1,48,1152]{2,1,0:T(8,128)(2,1)S(1)} %collective-permute-done.2), channel_id=1, source_target_pairs={{0,4},{1,5},{2,6},{3,7},{4,12},{5,13},{6,14},{7,15},{8,0},{9,1},{1... | collective-permute-start | bytes 331784 | tf_op jit(solution)/shard_map/ppermute | solution.py:895
  25.8 3.8 %collective-permute-start.4 = (bf16[96,768]{1,0:T(8,128)(2,1)S(1)}, bf16[96,768]{1,0:T(8,128)(2,1)S(1)}, u32[]{:S(2)}, u32[]{:S(2)}) collective-permute-start(bf16[96,768]{1,0:T(8,128)(2,1)S(1)} %get-tuple-element.208), channel_id=1, source_target_pairs={{0,1},{1,0},{2,3},{3,2},{4,5},{5,4},{6,7},{7,6},{8,9},{9,8},{10,11... | collective-permute-start | bytes 442376 | tf_op jit(solution)/shard_map/ppermute | solution.py:895
  25.8 23.7 %collective-permute-start.8 = (bf16[2,48,1536]{2,1,0:T(8,128)(2,1)S(1)}, bf16[2,48,1536]{2,1,0:T(8,128)(2,1)S(1)}, u32[]{:S(2)}, u32[]{:S(2)}) collective-permute-start(bf16[2,48,1536]{2,1,0:T(8,128)(2,1)S(1)} %pad_maximum_fusion.7), channel_id=1, source_target_pairs={{0,4},{1,5},{2,6},{3,7},{4,0},{5,1},{6,2},{7,3},{8,12},{9,13},{10,... | collective-permute-start | bytes 884744 | tf_op jit(solution)/shard_map/ppermute | solution.py:895
  27.8 23.5 %collective-permute-start.11 = (bf16[1,176,768]{2,1,0:T(8,128)(2,1)S(1)}, bf16[1,176,768]{2,1,0:T(8,128)(2,1)S(1)}, u32[]{:S(2)}, u32[]{:S(2)}) collective-permute-start(bf16[1,176,768]{2,1,0:T(8,128)(2,1)S(1)} %collective-permute-done.5), channel_id=1, source_target_pairs={{0,4},{1,5},{2,6},{3,7},{4,12},{5,13},{6,14},{7,15},{8,0},{9,1},{1... | collective-permute-start | bytes 811016 | tf_op jit(solution)/shard_map/ppermute | solution.py:895
  29.7 21.5 %collective-permute-start.12 = (bf16[4,48,1152]{2,1,0:T(8,128)(2,1)S(1)}, bf16[4,48,1152]{2,1,0:T(8,128)(2,1)S(1)}, u32[]{:S(2)}, u32[]{:S(2)}) collective-permute-start(bf16[4,48,1152]{2,1,0:T(8,128)(2,1)S(1)} %pad_maximum_fusion.5), channel_id=1, source_target_pairs={{0,2},{1,3},{2,0},{3,1},{4,6},{5,7},{6,4},{7,5},{8,10},{9,11},{10,... | collective-permute-start | bytes 1327112 | tf_op jit(solution)/shard_map/ppermute | solution.py:895
  30.8 21.1 %collective-permute-start.7 = (bf16[192,768]{1,0:T(8,128)(2,1)S(1)}, bf16[192,768]{1,0:T(8,128)(2,1)S(1)}, u32[]{:S(2)}, u32[]{:S(2)}) collective-permute-start(bf16[192,768]{1,0:T(8,128)(2,1)S(1)} %maximum_select_fusion), channel_id=1, source_target_pairs={{0,16},{2,18},{4,20},{6,22},{8,24},{10,26},{12,28},{14,30},{17,1},... | collective-permute-start | bytes 884744 | tf_op jit(solution)/shard_map/ppermute | solution.py:895
  34.2 17.7 %collective-permute-start.14 = (bf16[2,48,2048]{2,1,0:T(8,128)(2,1)S(1)}, bf16[2,48,2048]{2,1,0:T(8,128)(2,1)S(1)}, u32[]{:S(2)}, u32[]{:S(2)}) collective-permute-start(bf16[2,48,2048]{2,1,0:T(8,128)(2,1)S(1)} %pad_maximum_fusion.6), channel_id=1, source_target_pairs={{0,4},{1,5},{2,6},{3,7},{4,12},{5,13},{6,14},{7,15},{8,0},{9,1},{1... | collective-permute-start | bytes 1179656 | tf_op jit(solution)/shard_map/ppermute | solution.py:895
  49.6 16.3 %collective-permute-start.10 = (bf16[4,48,1536]{2,1,0:T(8,128)(2,1)S(1)}, bf16[4,48,1536]{2,1,0:T(8,128)(2,1)S(1)}, u32[]{:S(2)}, u32[]{:S(2)}) collective-permute-start(bf16[4,48,1536]{2,1,0:T(8,128)(2,1)S(1)} %pad_maximum_fusion.3), channel_id=1, source_target_pairs={{0,16},{1,17},{2,18},{3,19},{4,20},{5,21},{6,22},{7,23},{8,24},{9,... | collective-permute-start | bytes 1769480 | tf_op jit(solution)/shard_map/ppermute | solution.py:895
  51.3 10.4 %collective-permute-start.13 = (bf16[1,176,768]{2,1,0:T(8,128)(2,1)S(1)}, bf16[1,176,768]{2,1,0:T(8,128)(2,1)S(1)}, u32[]{:S(2)}, u32[]{:S(2)}) collective-permute-start(bf16[1,176,768]{2,1,0:T(8,128)(2,1)S(1)} %collective-permute-done.11), channel_id=1, source_target_pairs={{0,4},{1,5},{2,6},{3,7},{4,12},{5,13},{6,14},{7,15},{8,0},{9,1},{1... | collective-permute-start | bytes 811016 | tf_op jit(solution)/shard_map/ppermute | solution.py:895
  51.4 32.3 %collective-permute-start.17 = (bf16[8,48,1152]{2,1,0:T(8,128)(2,1)S(1)}, bf16[8,48,1152]{2,1,0:T(8,128)(2,1)S(1)}, u32[]{:S(2)}, u32[]{:S(2)}) collective-permute-start(bf16[8,48,1152]{2,1,0:T(8,128)(2,1)S(1)} %constant_dynamic-update-slice_fusion.refs_0_), channel_id=1, source_target_pairs={{0,16},{1,17},{2,18},{3,19},{4,20},{5,21},{6,22},{7,23},{8,24},{9,... | collective-permute-start | bytes 2654216 | tf_op jit(solution)/shard_map/ppermute | solution.py:895
  52.0 17.8 %collective-permute-start.16 = (bf16[2,48,2048]{2,1,0:T(8,128)(2,1)S(1)}, bf16[2,48,2048]{2,1,0:T(8,128)(2,1)S(1)}, u32[]{:S(2)}, u32[]{:S(2)}) collective-permute-start(bf16[2,48,2048]{2,1,0:T(8,128)(2,1)S(1)} %collective-permute-done.14), channel_id=1, source_target_pairs={{0,4},{1,5},{2,6},{3,7},{4,12},{5,13},{6,14},{7,15},{8,0},{9,1},{1... | collective-permute-start | bytes 1179656 | tf_op jit(solution)/shard_map/ppermute | solution.py:895
  61.8 21.9 %copy-start = (bf16[160,768]{1,0:T(8,128)(2,1)S(1)}, bf16[160,768]{1,0:T(8,128)(2,1)}, u32[]{:S(2)}) copy-start(bf16[160,768]{1,0:T(8,128)(2,1)} %cot_ref) | copy-start | bytes 737284
  61.8 23.4 %collective-permute-start.19 = (bf16[4,176,768]{2,1,0:T(8,128)(2,1)S(1)}, bf16[4,176,768]{2,1,0:T(8,128)(2,1)S(1)}, u32[]{:S(2)}, u32[]{:S(2)}) collective-permute-start(bf16[4,176,768]{2,1,0:T(8,128)(2,1)S(1)} %pad_maximum_fusion.2), channel_id=1, source_target_pairs={{0,2},{1,3},{2,0},{3,1},{4,6},{5,7},{6,4},{7,5},{8,10},{9,11},{10,... | collective-permute-start | bytes 3244040 | tf_op jit(solution)/shard_map/ppermute | solution.py:895
  66.0 10.9 %collective-permute-start.15 = (bf16[1,192,768]{2,1,0:T(8,128)(2,1)S(1)}, bf16[1,192,768]{2,1,0:T(8,128)(2,1)S(1)}, u32[]{:S(2)}, u32[]{:S(2)}) collective-permute-start(bf16[1,192,768]{2,1,0:T(8,128)(2,1)S(1)} %select_bitcast_fusion.1), channel_id=1, source_target_pairs={{0,4},{1,5},{2,6},{3,7},{4,12},{5,13},{6,14},{7,15},{8,0},{9,1},{1... | collective-permute-start | bytes 884744 | tf_op jit(solution)/shard_map/ppermute | solution.py:895
  69.8 14.0 %collective-permute-start.20 = (bf16[2,48,2048]{2,1,0:T(8,128)(2,1)S(1)}, bf16[2,48,2048]{2,1,0:T(8,128)(2,1)S(1)}, u32[]{:S(2)}, u32[]{:S(2)}) collective-permute-start(bf16[2,48,2048]{2,1,0:T(8,128)(2,1)S(1)} %collective-permute-done.16), channel_id=1, source_target_pairs={{0,4},{1,5},{2,6},{3,7},{4,12},{5,13},{6,14},{7,15},{8,0},{9,1},{1... | collective-permute-start | bytes 1179656 | tf_op jit(solution)/shard_map/ppermute | solution.py:895
  83.7 1.5 collective-permute-start.21
  83.7 15.5 %copy-start.1 = (bf16[192,256]{1,0:T(8,128)(2,1)S(1)}, bf16[192,256]{1,0:T(8,128)(2,1)}, u32[]{:S(2)}) copy-start(bf16[192,256]{1,0:T(8,128)(2,1)} %constant.53.clone.coarse_ref) | copy-start | bytes 294916
  83.8 15.5 %copy-start.2 = (bf16[192,256]{1,0:T(8,128)(2,1)S(1)}, bf16[192,256]{1,0:T(8,128)(2,1)}, u32[]{:S(2)}) copy-start(bf16[192,256]{1,0:T(8,128)(2,1)} %constant.52.clone.fine_ref) | copy-start | bytes 294916
  85.3 12.9 %collective-permute-start.22 = (bf16[8,176,768]{2,1,0:T(8,128)(2,1)S(1)}, bf16[8,176,768]{2,1,0:T(8,128)(2,1)S(1)}, u32[]{:S(2)}, u32[]{:S(2)}) collective-permute-start(bf16[8,176,768]{2,1,0:T(8,128)(2,1)S(1)} %constant_dynamic-update-slice_fusion.5.along_ref.note_a_ref.refs_2_.refs_5_), channel_id=1, source_target_pairs={{0,1},{1,0},{2,3},{3,2},{4,5},{5,4},{6,7},{7,6},{8,9},{9,8},{10,11... | collective-permute-start | bytes 6488072 | tf_op jit(solution)/shard_map/ppermute | solution.py:895
  85.5 28.2 %collective-permute-start.24 = (bf16[8,48,1536]{2,1,0:T(8,128)(2,1)S(1)}, bf16[8,48,1536]{2,1,0:T(8,128)(2,1)S(1)}, u32[]{:S(2)}, u32[]{:S(2)}) collective-permute-start(bf16[8,48,1536]{2,1,0:T(8,128)(2,1)S(1)} %pad_maximum_fusion.refs_0_), channel_id=1, source_target_pairs={{0,2},{1,3},{2,0},{3,1},{4,6},{5,7},{6,4},{7,5},{8,10},{9,11},{10,... | collective-permute-start | bytes 3538952 | tf_op jit(solution)/shard_map/ppermute | solution.py:895
  87.0 46.8 %collective-permute-start.26 = (bf16[8,48,2048]{2,1,0:T(8,128)(2,1)S(1)}, bf16[8,48,2048]{2,1,0:T(8,128)(2,1)S(1)}, u32[]{:S(2)}, u32[]{:S(2)}) collective-permute-start(bf16[8,48,2048]{2,1,0:T(8,128)(2,1)S(1)} %constant_dynamic-update-slice_fusion.10.refs_0_), channel_id=1, source_target_pairs={{0,16},{1,17},{2,18},{3,19},{4,20},{5,21},{6,22},{7,23},{8,24},{9,... | collective-permute-start | bytes 4718600 | tf_op jit(solution)/shard_map/ppermute | solution.py:895
  88.5 9.6 %collective-permute-start.18 = (bf16[1,192,768]{2,1,0:T(8,128)(2,1)S(1)}, bf16[1,192,768]{2,1,0:T(8,128)(2,1)S(1)}, u32[]{:S(2)}, u32[]{:S(2)}) collective-permute-start(bf16[1,192,768]{2,1,0:T(8,128)(2,1)S(1)} %collective-permute-done.15), channel_id=1, source_target_pairs={{0,4},{1,5},{2,6},{3,7},{4,12},{5,13},{6,14},{7,15},{8,0},{9,1},{1... | collective-permute-start | bytes 884744 | tf_op jit(solution)/shard_map/ppermute | solution.py:895
  98.2 9.5 %collective-permute-start.23 = (bf16[1,192,768]{2,1,0:T(8,128)(2,1)S(1)}, bf16[1,192,768]{2,1,0:T(8,128)(2,1)S(1)}, u32[]{:S(2)}, u32[]{:S(2)}) collective-permute-start(bf16[1,192,768]{2,1,0:T(8,128)(2,1)S(1)} %collective-permute-done.18), channel_id=1, source_target_pairs={{0,4},{1,5},{2,6},{3,7},{4,12},{5,13},{6,14},{7,15},{8,0},{9,1},{1... | collective-permute-start | bytes 884744 | tf_op jit(solution)/shard_map/ppermute | solution.py:895
  113.7 28.1 %collective-permute-start.25 = (bf16[4,192,768]{2,1,0:T(8,128)(2,1)S(1)}, bf16[4,192,768]{2,1,0:T(8,128)(2,1)S(1)}, u32[]{:S(2)}, u32[]{:S(2)}) collective-permute-start(bf16[4,192,768]{2,1,0:T(8,128)(2,1)S(1)} %pad_maximum_fusion.1.refs_0_), channel_id=1, source_target_pairs={{0,2},{1,3},{2,0},{3,1},{4,6},{5,7},{6,4},{7,5},{8,10},{9,11},{10,... | collective-permute-start | bytes 3538952 | tf_op jit(solution)/shard_map/ppermute | solution.py:895
  133.7 1.5 collective-permute-start.27
  135.3 2.0 collective-permute-start.28
  143.5 1.9 collective-permute-start.29
  149.7 5.5 %collective-permute-start.30 = (bf16[320,768]{1,0:T(8,128)(2,1)S(1)}, bf16[320,768]{1,0:T(8,128)(2,1)S(1)}, u32[]{:S(2)}, u32[]{:S(2)}) collective-permute-start(bf16[320,768]{1,0:T(8,128)(2,1)S(1)} %get-tuple-element.294), channel_id=1, source_target_pairs={{0,1},{1,0},{2,3},{3,2},{4,5},{5,4},{6,7},{7,6},{8,9},{9,8},{10,11... | collective-permute-start | bytes 1474568 | tf_op jit(solution)/shard_map/ppermute | solution.py:895
  156.8 34.7 %collective-permute-start.31 = (bf16[8,48,1536]{2,1,0:T(8,128)(2,1)S(1)}, bf16[8,48,1536]{2,1,0:T(8,128)(2,1)S(1)}, u32[]{:S(2)}, u32[]{:S(2)}) collective-permute-start(bf16[8,48,1536]{2,1,0:T(8,128)(2,1)S(1)} %get-tuple-element.322), channel_id=1, source_target_pairs={{0,16},{1,17},{2,18},{3,19},{4,20},{5,21},{6,22},{7,23},{8,24},{9,... | collective-permute-start | bytes 3538952 | tf_op jit(solution)/shard_map/ppermute | solution.py:895
  161.1 29.7 %collective-permute-start.32 = (bf16[2,192,768]{2,1,0:T(8,128)(2,1)S(1)}, bf16[2,192,768]{2,1,0:T(8,128)(2,1)S(1)}, u32[]{:S(2)}, u32[]{:S(2)}) collective-permute-start(bf16[2,192,768]{2,1,0:T(8,128)(2,1)S(1)} %split.68), channel_id=1, source_target_pairs={{4,0},{5,1},{6,2},{7,3},{12,4},{13,5},{14,6},{15,7},{0,8},{1,9},{2... | collective-permute-start | bytes 1769480 | tf_op jit(solution)/shard_map/ppermute | solution.py:895
  163.1 37.4 %collective-permute-start.34 = (bf16[8,48,2048]{2,1,0:T(8,128)(2,1)S(1)}, bf16[8,48,2048]{2,1,0:T(8,128)(2,1)}, u32[]{:S(2)}, u32[]{:S(2)}) collective-permute-start(bf16[8,48,2048]{2,1,0:T(8,128)(2,1)S(1)} %get-tuple-element.333), channel_id=1, source_target_pairs={{0,2},{1,3},{2,0},{3,1},{4,6},{5,7},{6,4},{7,5},{8,10},{9,11},{10,... | collective-permute-start | bytes 4718600 | tf_op jit(solution)/shard_map/ppermute | solution.py:895
  190.8 22.6 %collective-permute-start.36 = (bf16[8,48,1152]{2,1,0:T(8,128)(2,1)S(1)}, bf16[8,48,1152]{2,1,0:T(8,128)(2,1)S(1)}, u32[]{:S(2)}, u32[]{:S(2)}) collective-permute-start(bf16[8,48,1152]{2,1,0:T(8,128)(2,1)S(1)} %get-tuple-element.348), channel_id=1, source_target_pairs={{0,16},{1,17},{2,18},{3,19},{4,20},{5,21},{6,22},{7,23},{8,24},{9,... | collective-permute-start | bytes 2654216 | tf_op jit(solution)/shard_map/ppermute | solution.py:895
  192.0 19.9 %collective-permute-start.33 = (bf16[4,48,1536]{2,1,0:T(8,128)(2,1)S(1)}, bf16[4,48,1536]{2,1,0:T(8,128)(2,1)S(1)}, u32[]{:S(2)}, u32[]{:S(2)}) collective-permute-start(bf16[4,48,1536]{2,1,0:T(8,128)(2,1)S(1)} %slice.268), channel_id=1, source_target_pairs={{0,2},{1,3},{2,0},{3,1},{4,6},{5,7},{6,4},{7,5},{8,10},{9,11},{10,... | collective-permute-start | bytes 1769480 | tf_op jit(solution)/shard_map/ppermute | solution.py:895
  200.5 16.0 %collective-permute-start.37 = (bf16[2,192,768]{2,1,0:T(8,128)(2,1)S(1)}, bf16[2,192,768]{2,1,0:T(8,128)(2,1)S(1)}, u32[]{:S(2)}, u32[]{:S(2)}) collective-permute-start(bf16[2,192,768]{2,1,0:T(8,128)(2,1)S(1)} %add_convert_fusion.1), channel_id=1, source_target_pairs={{4,0},{5,1},{6,2},{7,3},{12,4},{13,5},{14,6},{15,7},{0,8},{1,9},{2... | collective-permute-start | bytes 1769480 | tf_op jit(solution)/shard_map/ppermute | solution.py:895
  205.1 23.7 %collective-permute-start.42 = (bf16[4,48,2048]{2,1,0:T(8,128)(2,1)S(1)}, bf16[4,48,2048]{2,1,0:T(8,128)(2,1)S(1)}, u32[]{:S(2)}, u32[]{:S(2)}) collective-permute-start(bf16[4,48,2048]{2,1,0:T(8,128)(2,1)S(1)} %slice.267), channel_id=1, source_target_pairs={{0,16},{1,17},{2,18},{3,19},{4,20},{5,21},{6,22},{7,23},{8,24},{9,... | collective-permute-start | bytes 2359304 | tf_op jit(solution)/shard_map/ppermute | solution.py:895
  212.1 17.1 %collective-permute-start.35 = (bf16[8,160,768]{2,1,0:T(8,128)(2,1)S(1)}, bf16[8,160,768]{2,1,0:T(8,128)(2,1)S(1)}, u32[]{:S(2)}, u32[]{:S(2)}) collective-permute-start(bf16[8,160,768]{2,1,0:T(8,128)(2,1)S(1)} %get-tuple-element.353), channel_id=1, source_target_pairs={{0,1},{1,0},{2,3},{3,2},{4,5},{5,4},{6,7},{7,6},{8,9},{9,8},{10,11... | collective-permute-start | bytes 5898248 | tf_op jit(solution)/shard_map/ppermute | solution.py:895
  213.7 34.9 %collective-permute-start.56 = (bf16[1,48,1536]{2,1,0:T(8,128)(2,1)S(1)}, bf16[1,48,1536]{2,1,0:T(8,128)(2,1)S(1)}, u32[]{:S(2)}, u32[]{:S(2)}) collective-permute-start(bf16[1,48,1536]{2,1,0:T(8,128)(2,1)S(1)} %get-tuple-element.352), channel_id=1, source_target_pairs={{4,0},{5,1},{6,2},{7,3},{12,4},{13,5},{14,6},{15,7},{0,8},{1,9},{2... | collective-permute-start | bytes 442376 | tf_op jit(solution)/shard_map/ppermute | solution.py:895
  216.6 15.9 %collective-permute-start.39 = (bf16[2,192,768]{2,1,0:T(8,128)(2,1)S(1)}, bf16[2,192,768]{2,1,0:T(8,128)(2,1)S(1)}, u32[]{:S(2)}, u32[]{:S(2)}) collective-permute-start(bf16[2,192,768]{2,1,0:T(8,128)(2,1)S(1)} %add_convert_fusion), channel_id=1, source_target_pairs={{4,0},{5,1},{6,2},{7,3},{12,4},{13,5},{14,6},{15,7},{0,8},{1,9},{2... | collective-permute-start | bytes 1769480 | tf_op jit(solution)/shard_map/ppermute | solution.py:895
  217.0 12.0 %collective-permute-start.40 = (bf16[4,48,1152]{2,1,0:T(8,128)(2,1)S(1)}, bf16[4,48,1152]{2,1,0:T(8,128)(2,1)S(1)}, u32[]{:S(2)}, u32[]{:S(2)}) collective-permute-start(bf16[4,48,1152]{2,1,0:T(8,128)(2,1)S(1)} %slice.269), channel_id=1, source_target_pairs={{0,2},{1,3},{2,0},{3,1},{4,6},{5,7},{6,4},{7,5},{8,10},{9,11},{10,... | collective-permute-start | bytes 1327112 | tf_op jit(solution)/shard_map/ppermute | solution.py:895
  229.7 6.6 %collective-permute-start.41 = (bf16[1,48,1152]{2,1,0:T(8,128)(2,1)S(1)}, bf16[1,48,1152]{2,1,0:T(8,128)(2,1)S(1)}, u32[]{:S(2)}, u32[]{:S(2)}) collective-permute-start(bf16[1,48,1152]{2,1,0:T(8,128)(2,1)S(1)} %split.138), channel_id=1, source_target_pairs={{4,0},{5,1},{6,2},{7,3},{12,4},{13,5},{14,6},{15,7},{0,8},{1,9},{2... | collective-permute-start | bytes 331784 | tf_op jit(solution)/shard_map/ppermute | solution.py:895
  232.7 24.8 %collective-permute-start.38 = (bf16[4,160,768]{2,1,0:T(8,128)(2,1)S(1)}, bf16[4,160,768]{2,1,0:T(8,128)(2,1)S(1)}, u32[]{:S(2)}, u32[]{:S(2)}) collective-permute-start(bf16[4,160,768]{2,1,0:T(8,128)(2,1)S(1)} %slice.266), channel_id=1, source_target_pairs={{0,2},{1,3},{2,0},{3,1},{4,6},{5,7},{6,4},{7,5},{8,10},{9,11},{10,... | collective-permute-start | bytes 2949128 | tf_op jit(solution)/shard_map/ppermute | solution.py:895
  234.0 7.7 %collective-permute-start.43 = (bf16[1,48,2048]{2,1,0:T(8,128)(2,1)S(1)}, bf16[1,48,2048]{2,1,0:T(8,128)(2,1)S(1)}, u32[]{:S(2)}, u32[]{:S(2)}) collective-permute-start(bf16[1,48,2048]{2,1,0:T(8,128)(2,1)S(1)} %split.137), channel_id=1, source_target_pairs={{4,0},{5,1},{6,2},{7,3},{12,4},{13,5},{14,6},{15,7},{0,8},{1,9},{2... | collective-permute-start | bytes 589832 | tf_op jit(solution)/shard_map/ppermute | solution.py:895
  236.3 8.5 %collective-permute-start.44 = (bf16[1,48,1536]{2,1,0:T(8,128)(2,1)S(1)}, bf16[1,48,1536]{2,1,0:T(8,128)(2,1)S(1)}, u32[]{:S(2)}, u32[]{:S(2)}) collective-permute-start(bf16[1,48,1536]{2,1,0:T(8,128)(2,1)S(1)} %get-tuple-element.360), channel_id=1, source_target_pairs={{12,0},{13,1},{14,2},{15,3},{8,4},{9,5},{10,6},{11,7},{4,8},{5,9},... | collective-permute-start | bytes 442376 | tf_op jit(solution)/shard_map/ppermute | solution.py:895
  237.6 11.4 %collective-permute-start.57 = (bf16[1,48,1536]{2,1,0:T(8,128)(2,1)S(1)}, bf16[1,48,1536]{2,1,0:T(8,128)(2,1)S(1)}, u32[]{:S(2)}, u32[]{:S(2)}) collective-permute-start(bf16[1,48,1536]{2,1,0:T(8,128)(2,1)S(1)} %get-tuple-element.361), channel_id=1, source_target_pairs={{8,0},{9,1},{10,2},{11,3},{0,4},{1,5},{2,6},{3,7},{12,8},{13,9},{1... | collective-permute-start | bytes 442376 | tf_op jit(solution)/shard_map/ppermute | solution.py:895
  244.8 10.7 %collective-permute-start.48 = (bf16[1,48,2048]{2,1,0:T(8,128)(2,1)S(1)}, bf16[1,48,2048]{2,1,0:T(8,128)(2,1)S(1)}, u32[]{:S(2)}, u32[]{:S(2)}) collective-permute-start(bf16[1,48,2048]{2,1,0:T(8,128)(2,1)S(1)} %fusion.6), channel_id=1, source_target_pairs={{4,0},{5,1},{6,2},{7,3},{12,4},{13,5},{14,6},{15,7},{0,8},{1,9},{2... | collective-permute-start | bytes 589832 | tf_op jit(solution)/shard_map/ppermute | solution.py:895
  248.5 7.0 %collective-permute-start.45 = (bf16[1,48,1152]{2,1,0:T(8,128)(2,1)S(1)}, bf16[1,48,1152]{2,1,0:T(8,128)(2,1)S(1)}, u32[]{:S(2)}, u32[]{:S(2)}) collective-permute-start(bf16[1,48,1152]{2,1,0:T(8,128)(2,1)S(1)} %fusion.11), channel_id=1, source_target_pairs={{4,0},{5,1},{6,2},{7,3},{12,4},{13,5},{14,6},{15,7},{0,8},{1,9},{2... | collective-permute-start | bytes 331784 | tf_op jit(solution)/shard_map/ppermute | solution.py:895
  249.1 11.8 %collective-permute-start.47 = (bf16[1,192,768]{2,1,0:T(8,128)(2,1)S(1)}, bf16[1,192,768]{2,1,0:T(8,128)(2,1)S(1)}, u32[]{:S(2)}, u32[]{:S(2)}) collective-permute-start(bf16[1,192,768]{2,1,0:T(8,128)(2,1)S(1)} %slice.270), channel_id=1, source_target_pairs={{0,2},{1,3},{2,0},{3,1},{4,6},{5,7},{6,4},{7,5},{8,10},{9,11},{10,... | collective-permute-start | bytes 884744 | tf_op jit(solution)/shard_map/ppermute | solution.py:895
  257.8 9.0 %collective-permute-start.50 = (bf16[1,48,1152]{2,1,0:T(8,128)(2,1)S(1)}, bf16[1,48,1152]{2,1,0:T(8,128)(2,1)S(1)}, u32[]{:S(2)}, u32[]{:S(2)}) collective-permute-start(bf16[1,48,1152]{2,1,0:T(8,128)(2,1)S(1)} %fusion.10), channel_id=1, source_target_pairs={{4,0},{5,1},{6,2},{7,3},{12,4},{13,5},{14,6},{15,7},{0,8},{1,9},{2... | collective-permute-start | bytes 331784 | tf_op jit(solution)/shard_map/ppermute | solution.py:895
  261.0 22.8 %collective-permute-start.46 = (bf16[1,160,768]{2,1,0:T(8,128)(2,1)S(1)}, bf16[1,160,768]{2,1,0:T(8,128)(2,1)S(1)}, u32[]{:S(2)}, u32[]{:S(2)}) collective-permute-start(bf16[1,160,768]{2,1,0:T(8,128)(2,1)S(1)} %get-tuple-element.365), channel_id=1, source_target_pairs={{4,0},{5,1},{6,2},{7,3},{12,4},{13,5},{14,6},{15,7},{0,8},{1,9},{2... | collective-permute-start | bytes 737288 | tf_op jit(solution)/shard_map/ppermute | solution.py:895
  263.6 10.2 %collective-permute-start.54 = (bf16[1,48,2048]{2,1,0:T(8,128)(2,1)S(1)}, bf16[1,48,2048]{2,1,0:T(8,128)(2,1)S(1)}, u32[]{:S(2)}, u32[]{:S(2)}) collective-permute-start(bf16[1,48,2048]{2,1,0:T(8,128)(2,1)S(1)} %fusion.5), channel_id=1, source_target_pairs={{4,0},{5,1},{6,2},{7,3},{12,4},{13,5},{14,6},{15,7},{0,8},{1,9},{2... | collective-permute-start | bytes 589832 | tf_op jit(solution)/shard_map/ppermute | solution.py:895
  263.7 10.3 %collective-permute-start.51 = (bf16[192,768]{1,0:T(8,128)(2,1)S(1)}, bf16[192,768]{1,0:T(8,128)(2,1)S(1)}, u32[]{:S(2)}, u32[]{:S(2)}) collective-permute-start(bf16[192,768]{1,0:T(8,128)(2,1)S(1)} %fusion.7), channel_id=1, source_target_pairs={{1,17},{3,19},{5,21},{7,23},{9,25},{11,27},{13,29},{15,31},{16,0},... | collective-permute-start | bytes 884744 | tf_op jit(solution)/shard_map/ppermute | solution.py:895
  265.0 18.8 %collective-permute-start.49 = (bf16[1,160,768]{2,1,0:T(8,128)(2,1)S(1)}, bf16[1,160,768]{2,1,0:T(8,128)(2,1)S(1)}, u32[]{:S(2)}, u32[]{:S(2)}) collective-permute-start(bf16[1,160,768]{2,1,0:T(8,128)(2,1)S(1)} %get-tuple-element.369), channel_id=1, source_target_pairs={{12,0},{13,1},{14,2},{15,3},{8,4},{9,5},{10,6},{11,7},{4,8},{5,9},... | collective-permute-start | bytes 737288 | tf_op jit(solution)/shard_map/ppermute | solution.py:895
  274.1 3.1 %collective-permute-start.52 = (f32[24,1152]{1,0:T(8,128)S(1)}, f32[24,1152]{1,0:T(8,128)S(1)}, u32[]{:S(2)}, u32[]{:S(2)}) collective-permute-start(f32[24,1152]{1,0:T(8,128)S(1)} %get-tuple-element.371), channel_id=1, source_target_pairs={{0,1},{1,0},{2,3},{3,2},{4,5},{5,4},{6,7},{7,6},{8,9},{9,8},{10,11... | collective-permute-start | bytes 331784 | tf_op jit(solution)/shard_map/ppermute | solution.py:895
  274.8 8.2 %collective-permute-start.59 = (f32[96,768]{1,0:T(8,128)S(1)}, f32[96,768]{1,0:T(8,128)S(1)}, u32[]{:S(2)}, u32[]{:S(2)}) collective-permute-start(f32[96,768]{1,0:T(8,128)S(1)} %slice_select_fusion), channel_id=1, source_target_pairs={{0,1},{2,3},{4,5},{6,7},{8,9},{10,11},{12,13},{14,15},{17,16},{19,... | collective-permute-start | bytes 884744 | tf_op jit(solution)/shard_map/ppermute | solution.py:895
  277.2 4.4 %collective-permute-start.55 = (f32[24,1920]{1,0:T(8,128)S(1)}, f32[24,1920]{1,0:T(8,128)S(1)}, u32[]{:S(2)}, u32[]{:S(2)}) collective-permute-start(f32[24,1920]{1,0:T(8,128)S(1)} %slice.214), channel_id=1, source_target_pairs={{0,1},{1,0},{2,3},{3,2},{4,5},{5,4},{6,7},{7,6},{8,9},{9,8},{10,11... | collective-permute-start | bytes 552968 | tf_op jit(solution)/shard_map/ppermute | solution.py:895
  277.3 1.6 collective-permute-start.58
  278.9 9.9 %collective-permute-start.53 = (bf16[1,160,768]{2,1,0:T(8,128)(2,1)S(1)}, bf16[1,160,768]{2,1,0:T(8,128)(2,1)S(1)}, u32[]{:S(2)}, u32[]{:S(2)}) collective-permute-start(bf16[1,160,768]{2,1,0:T(8,128)(2,1)S(1)} %get-tuple-element.372), channel_id=1, source_target_pairs={{8,0},{9,1},{10,2},{11,3},{0,4},{1,5},{2,6},{3,7},{12,8},{13,9},{1... | collective-permute-start | bytes 737288 | tf_op jit(solution)/shard_map/ppermute | solution.py:895
